TPU v7x, 256 devices: a whole 4x4x8 slice. The times are simulated.
256 devices in a mesh: dp: 128 (over y_lo, z, x, core), section: 2 (over y_hi).
Axes of the slice: x: 4, y: 4 (y_hi: 2, y_lo: 2; y = y_hi * 2 + y_lo), z: 8, core: 2. Of those that a mesh axis runs over, the one named last changes fastest.
Arguments:
- teacher_image: bfloat16 [65536, 1536], P(('dp', 'section')), may hold values from -6 to 6
- teacher_proj: bfloat16 [1536, 1536], replicated, may hold values from -0.15625 to 0.15625
- teacher_text: bfloat16 [65536, 1536], P(('dp', 'section')), may hold values from -6 to 6
- image_feats: bfloat16 [65536, 768], P(('dp', 'section')), may hold values from -6 to 6
- text_feats: bfloat16 [65536, 768], P(('dp', 'section')), may hold values from -6 to 6
- image_proj: bfloat16 [768, 768], replicated, may hold values from -0.21875 to 0.21875
- text_proj: bfloat16 [768, 768], replicated, may hold values from -0.21875 to 0.21875
- class_ids: int32 [65536], P(('dp', 'section')), may hold values from 0 to 255
Outputs:
- grad_image_proj: float32 [768, 768], replicated
- grad_text_proj: float32 [768, 768], replicated
All inputs are finite; a program needn't handle non-finite values.
Results may differ from a plain program's by a relative error of at most 0.005.
Values may be sent and summed in bfloat16 or wider, within the bound.
No kernel may reach another device: no remote copies, remote signals or barrier semaphores. Data moves between devices by JAX's collectives and lax.ppermute only.
A program may use at most 128 MiB of HBM per device.

v0:
```python
import jax
import jax.numpy as jnp
from jax import lax
from jax.sharding import PartitionSpec as P

WINDOW = 4


epsilon = 1e-06
teacher_scale = 20.0
teacher_shift = -1.0
student_scale = 20.0
student_shift = -1.0


def passed_along(block, axis, distance):
    devices = range(lax.axis_size(axis))
    route = [((i - distance) % len(devices), i) for i in devices]
    return lax.ppermute(block, axis, route)


def unit_rows(raw_rows):
    row_len = jnp.sqrt(jnp.sum(raw_rows * raw_rows, axis=1, keepdims=True) + epsilon)
    return (raw_rows / row_len, row_len)


def pair_tile(teach_rows, image_rows, row_ids, teach_cols, text_cols, col_ids):
    teacher_dot = lax.dot_general(
        teach_rows, teach_cols, (((1,), (1,)), ((), ())), preferred_element_type=jnp.float32
    )
    labels = (row_ids[:, None] == col_ids[None, :]).astype(jnp.float32)
    target = 0.5 * jax.nn.sigmoid(teacher_scale * teacher_dot + teacher_shift) + 0.5 * labels
    logits = (
        student_scale
        * lax.dot_general(
            image_rows, text_cols, (((1,), (1,)), ((), ())), preferred_element_type=jnp.float32
        )
        + student_shift
    )
    scaled = ((jax.nn.sigmoid(logits) - target) / text_cols.shape[0]).astype(jnp.bfloat16)
    row_part = student_scale * jnp.dot(scaled, text_cols, preferred_element_type=jnp.float32)
    col_part = student_scale * lax.dot_general(
        scaled, image_rows, (((0,), (0,)), ((), ())), preferred_element_type=jnp.float32
    )
    return (row_part, col_part)


def weight_grad(feats, unit, length, grad):
    direction = (grad - unit * jnp.sum(unit * grad, axis=1, keepdims=True)) / length
    high = direction.astype(jnp.bfloat16)
    low = (direction - high.astype(jnp.float32)).astype(jnp.bfloat16)
    dims = (((0,), (0,)), ((), ()))
    first = lax.dot_general(feats, high, dims, preferred_element_type=jnp.float32)
    second = lax.dot_general(feats, low, dims, preferred_element_type=jnp.float32)
    return first + second


def local(
    teacher_image,
    teacher_proj,
    teacher_text,
    image_feats,
    text_feats,
    image_proj,
    text_proj,
    class_ids,
):
    teacher_unit, teacher_len = unit_rows(
        jnp.dot(teacher_image, teacher_proj, preferred_element_type=jnp.float32)
    )
    teacher_img = teacher_unit.astype(jnp.bfloat16)
    written_unit, written_len = unit_rows(teacher_text.astype(jnp.float32))
    teacher_txt = written_unit.astype(jnp.bfloat16)
    own_ids = class_ids.astype(jnp.bfloat16)
    image_unit, image_len = unit_rows(
        jnp.dot(image_feats, image_proj, preferred_element_type=jnp.float32)
    )
    image_emb = image_unit.astype(jnp.bfloat16)
    teach_rows, image_rows, row_ids = (
        lax.all_gather(teacher_img, "section", axis=0, tiled=True),
        lax.all_gather(image_emb, "section", axis=0, tiled=True),
        lax.all_gather(own_ids, "section", axis=0, tiled=True),
    )
    grad_rows = jnp.zeros((image_rows.shape[0], image_rows.shape[1]), jnp.float32)
    text_unit, text_len = unit_rows(
        jnp.dot(text_feats, text_proj, preferred_element_type=jnp.float32)
    )
    text_emb = text_unit.astype(jnp.bfloat16)
    panels = (teacher_txt, text_emb, own_ids)
    carried = jnp.zeros(text_unit.shape, jnp.float32)
    for offset in range(WINDOW):
        if offset > 0:
            panels = passed_along((panels[0], panels[1], panels[2]), "dp", 1)
            carried = passed_along(carried, "dp", 1)
        row_part, col_part = pair_tile(
            teach_rows, image_rows, row_ids, panels[0], panels[1], panels[2]
        )
        grad_rows = grad_rows + row_part
        carried = carried + col_part
    grad_txt = passed_along(carried, "dp", 1 - WINDOW)
    text_part = weight_grad(text_feats, text_unit, text_len, grad_txt)
    own_grads = lax.psum_scatter(
        grad_rows.astype(jnp.bfloat16), "section", scatter_dimension=0, tiled=True
    ).astype(jnp.float32)
    image_part = weight_grad(image_feats, image_unit, image_len, own_grads)
    image_total, text_total = lax.psum((image_part, text_part), ("dp", "section"))
    return (image_total, text_total)


def solution(mesh):
    in_specs = (
        P(("dp", "section"), None),
        P(),
        P(("dp", "section"), None),
        P(("dp", "section"), None),
        P(("dp", "section"), None),
        P(),
        P(),
        P(("dp", "section")),
    )
    out_specs = (P(), P())
    return jax.shard_map(local, mesh=mesh, in_specs=in_specs, out_specs=out_specs, check_vma=False)
```

profile of v0, /device:TPU:1, one launch (start us, length us, event | category | flops | bytes accessed | tf_op | source)
XLA Modules:
  0.0 432.7 jit_solution(15911521493191360860)
XLA Ops:
  7.2 4.1 multiply_reduce_fusion
  11.4 1.1 divide_convert_fusion
  12.6 2.7 collective-permute-start.2
  15.5 1.2 fusion.1
  16.7 0.6 multiply_reduce_fusion.2
  17.4 1.7 collective-permute-start
  19.1 0.6 multiply_reduce_fusion.3
  19.8 10.3 %collective-permute-done = bf16[256,768]{1,0:T(8,128)(2,1)} collective-permute-done((bf16[256,768]{1,0:T(8,128)(2,1)S(1)}, bf16[256,768]{1,0:T(8,128)(2,1)}, u32[]{:S(2)}, u32[]{:S(2)}) %collective-permute-start) | collective-permute-done | bytes 393248 | tf_op jit(solution)/shard_map/ppermute | solution.py:19
  30.1 2.6 collective-permute-start.3
  32.7 26.6 %all_gather.9 = bf16[512,768]{1,0:T(8,128)(2,1)S(1)} all-gather(bf16[256,768]{1,0:T(8,128)(2,1)S(1)} %fusion.74), channel_id=1, replica_groups=mesh['dp'=128,'section'=2] {'section'}, dimensions={0}, use_global_device_ids=true | all-gather | bytes 1179648 | tf_op jit(solution)/shard_map/all_gather | solution.py:81
  59.3 1.2 fusion.7
  60.5 5.0 %all-gather = bf16[2,1,256]{2,1,0:T(2,128)(2,1)S(1)} all-gather(bf16[1,1,256]{2,1,0:T(2,128)(2,1)S(1)} %reshape.35), channel_id=1, replica_groups=mesh['dp'=128,'section'=2] {'section'}, dimensions={0}, use_global_device_ids=true | all-gather | bytes 1536 | tf_op jit(solution)/shard_map/all_gather | solution.py:82
  65.9 3.2 all-gather.3.cloned.1.call-done
  69.1 2.4 fusion.62
  72.1 0.5 copy-done.4
  73.0 0.5 copy-done.14
  73.4 1.8 fusion.43
  75.2 1.8 fusion.36
  77.0 2.6 collective-permute-start.7
  79.6 1.4 fusion.60
  81.1 1.5 fusion.77
  82.5 1.4 fusion.59
  84.0 1.4 fusion.76
  85.3 2.3 collective-permute-done.9
  87.6 1.3 fusion.2
  88.9 2.5 collective-permute-start.10
  91.4 4.8 %collective-permute-done.7 = bf16[256,1536]{1,0:T(8,128)(2,1)S(1)} collective-permute-done((bf16[256,1536]{1,0:T(8,128)(2,1)}, bf16[256,1536]{1,0:T(8,128)(2,1)S(1)}, u32[]{:S(2)}, u32[]{:S(2)}) %collective-permute-start.7) | collective-permute-done | bytes 786464 | tf_op jit(solution)/shard_map/ppermute | solution.py:19
  96.1 0.7 fusion.29
  96.8 1.4 fusion.61
  98.3 0.7 copy-done.7
  98.9 2.3 multiply_convert_fusion
  101.3 1.3 convolution_multiply_fusion.1
  102.7 1.9 collective-permute-done.10
  104.6 1.2 add.158
  105.8 2.6 collective-permute-start.11
  108.7 12.3 %collective-permute-done.11 = f32[256,768]{1,0:T(8,128)S(1)} collective-permute-done((f32[256,768]{1,0:T(8,128)S(1)}, f32[256,768]{1,0:T(8,128)S(1)}, u32[]{:S(2)}, u32[]{:S(2)}) %collective-permute-start.11) | collective-permute-done | bytes 786464 | tf_op jit(solution)/shard_map/ppermute | solution.py:19
  121.0 1.0 add.159
  122.0 10.2 %collective-permute-start.12 = (f32[256,768]{1,0:T(8,128)}, f32[256,768]{1,0:T(8,128)S(1)}, u32[]{:S(2)}, u32[]{:S(2)}) collective-permute-start(f32[256,768]{1,0:T(8,128)} %add.159), channel_id=1, source_target_pairs={{6,0},{8,2},{10,4},{12,6},{14,8},{16,10},{18,12},{20,14},{22,16},{... | collective-permute-start | bytes 2359304 | tf_op jit(solution)/shard_map/ppermute | solution.py:19
  132.2 3.6 reduce-scatter.2.cloned.1.call-done
  135.8 1.3 fusion.63
  137.1 1.8 fusion.69
  138.9 2.1 add_bitcast_fusion.1
  141.0 0.6 collective-permute-done.12
  142.0 0.7 fusion.65
  142.7 2.1 add_bitcast_fusion
  144.8 276.3 %all-reduce.3.cloned.1.call-done = (f32[768,768]{0,1:T(8,128)}, f32[768,768]{0,1:T(8,128)}) async-done(((f32[768,768]{0,1:T(8,128)}, f32[768,768]{0,1:T(8,128)}), (f32[768,768]{0,1:T(8,128)}, f32[768,768]{0,1:T(8,128)})) %all-reduce.3.cloned.1.call-update) | async-done | bytes 4718608 | tf_op jit(solution)/shard_map/psum | solution.py:106
  421.1 3.2 copy.14
  424.3 1.9 copy.15
  (65 shorter events, 2.8 us)
Async XLA Ops:
  7.2 9.5 %copy-start = (bf16[768,768]{1,0:T(8,128)(2,1)S(1)}, bf16[768,768]{1,0:T(8,128)(2,1)}, u32[]{:S(2)}) copy-start(bf16[768,768]{1,0:T(8,128)(2,1)} %param.14) | copy-start | bytes 3538948
  7.2 61.9 %all-gather.3.cloned.1.call-start = ((), (), s32[]{:S(2)}) async-start(), calls=%async_computation.1 | async-start | bytes 2359296 | tf_op jit(solution)/shard_map/all_gather | solution.py:80
  11.4 1.2 copy-start.15
  11.4 3.9 copy-start.1
  12.5 4.3 copy-start.12
  12.5 123.3 %reduce-scatter.2.cloned.1.call-start = ((), (), s32[]{:S(2)}) async-start(), calls=%async_computation.2 | async-start | bytes 1179648 | tf_op jit(solution)/shard_map/reduce_scatter | solution.py:102
  12.6 47.9 %copy-start.16 = (bf16[256]{0:T(256)(128)(2,1)}, bf16[256]{0:T(256)(128)(2,1)S(1)}, u32[]{:S(2)}) copy-start(bf16[256]{0:T(256)(128)(2,1)S(1)} %convert_element_type.63) | copy-start | bytes 1540
  12.6 47.9 %collective-permute-start.2 = (bf16[256]{0:T(256)(128)(2,1)S(1)}, bf16[256]{0:T(256)(128)(2,1)}, u32[]{:S(2)}, u32[]{:S(2)}) collective-permute-start(bf16[256]{0:T(256)(128)(2,1)S(1)} %convert_element_type.63), channel_id=1, source_target_pairs={{254,0},{0,2},{2,4},{4,6},{6,8},{8,10},{10,12},{12,14},{14,16},{16... | collective-permute-start | bytes 1544 | tf_op jit(solution)/shard_map/ppermute | solution.py:19
  16.7 2.4 copy-start.5
  16.7 2.4 copy-start.10
  16.7 49.1 %collective-permute-start.1 = (bf16[256,1536]{1,0:T(8,128)(2,1)}, bf16[256,1536]{1,0:T(8,128)(2,1)}, u32[]{:S(2)}, u32[]{:S(2)}) collective-permute-start(bf16[256,1536]{1,0:T(8,128)(2,1)} %fusion.1), channel_id=1, source_target_pairs={{254,0},{0,2},{2,4},{4,6},{6,8},{8,10},{10,12},{12,14},{14,16},{16... | collective-permute-start | bytes 2359304 | tf_op jit(solution)/shard_map/ppermute | solution.py:19
  17.4 41.8 %copy-start.3 = (bf16[256,768]{1,0:T(8,128)(2,1)}, bf16[256,768]{1,0:T(8,128)(2,1)S(1)}, u32[]{:S(2)}) copy-start(bf16[256,768]{1,0:T(8,128)(2,1)S(1)} %fusion.73) | copy-start | bytes 1179652
  17.4 12.6 %collective-permute-start = (bf16[256,768]{1,0:T(8,128)(2,1)S(1)}, bf16[256,768]{1,0:T(8,128)(2,1)}, u32[]{:S(2)}, u32[]{:S(2)}) collective-permute-start(bf16[256,768]{1,0:T(8,128)(2,1)S(1)} %fusion.73), channel_id=1, source_target_pairs={{254,0},{0,2},{2,4},{4,6},{6,8},{8,10},{10,12},{12,14},{14,16},{16... | collective-permute-start | bytes 1179656 | tf_op jit(solution)/shard_map/ppermute | solution.py:19
  30.1 35.7 %collective-permute-start.3 = (bf16[256,768]{1,0:T(8,128)(2,1)}, bf16[256,768]{1,0:T(8,128)(2,1)}, u32[]{:S(2)}, u32[]{:S(2)}) collective-permute-start(bf16[256,768]{1,0:T(8,128)(2,1)} %collective-permute-done), channel_id=1, source_target_pairs={{254,0},{0,2},{2,4},{4,6},{6,8},{8,10},{10,12},{12,14},{14,16},{16... | collective-permute-start | bytes 1179656 | tf_op jit(solution)/shard_map/ppermute | solution.py:19
  60.5 5.3 %collective-permute-start.5 = (bf16[256]{0:T(256)(128)(2,1)}, bf16[256]{0:T(256)(128)(2,1)}, u32[]{:S(2)}, u32[]{:S(2)}) collective-permute-start(bf16[256]{0:T(256)(128)(2,1)} %collective-permute-done.2), channel_id=1, source_target_pairs={{254,0},{0,2},{2,4},{4,6},{6,8},{8,10},{10,12},{12,14},{14,16},{16... | collective-permute-start | bytes 1544 | tf_op jit(solution)/shard_map/ppermute | solution.py:19
  65.8 25.6 %collective-permute-start.8 = (bf16[256]{0:T(256)(128)(2,1)}, bf16[256]{0:T(256)(128)(2,1)S(1)}, u32[]{:S(2)}, u32[]{:S(2)}) collective-permute-start(bf16[256]{0:T(256)(128)(2,1)} %collective-permute-done.5), channel_id=1, source_target_pairs={{254,0},{0,2},{2,4},{4,6},{6,8},{8,10},{10,12},{12,14},{14,16},{16... | collective-permute-start | bytes 1544 | tf_op jit(solution)/shard_map/ppermute | solution.py:19
  65.8 9.4 %collective-permute-start.4 = (bf16[256,1536]{1,0:T(8,128)(2,1)}, bf16[256,1536]{1,0:T(8,128)(2,1)}, u32[]{:S(2)}, u32[]{:S(2)}) collective-permute-start(bf16[256,1536]{1,0:T(8,128)(2,1)} %collective-permute-done.1), channel_id=1, source_target_pairs={{254,0},{0,2},{2,4},{4,6},{6,8},{8,10},{10,12},{12,14},{14,16},{16... | collective-permute-start | bytes 2359304 | tf_op jit(solution)/shard_map/ppermute | solution.py:19
  65.8 31.0 %collective-permute-start.6 = (bf16[256,768]{1,0:T(8,128)(2,1)}, bf16[256,768]{1,0:T(8,128)(2,1)}, u32[]{:S(2)}, u32[]{:S(2)}) collective-permute-start(bf16[256,768]{1,0:T(8,128)(2,1)} %collective-permute-done.3), channel_id=1, source_target_pairs={{254,0},{0,2},{2,4},{4,6},{6,8},{8,10},{10,12},{12,14},{14,16},{16... | collective-permute-start | bytes 1179656 | tf_op jit(solution)/shard_map/ppermute | solution.py:19
  71.6 1.0 copy-start.4
  72.0 1.4 copy-start.14
  72.0 15.6 %collective-permute-start.9 = (f32[256,768]{1,0:T(8,128)S(1)}, f32[256,768]{1,0:T(8,128)S(1)}, u32[]{:S(2)}, u32[]{:S(2)}) collective-permute-start(f32[256,768]{1,0:T(8,128)S(1)} %convolution_multiply_fusion.3), channel_id=1, source_target_pairs={{254,0},{0,2},{2,4},{4,6},{6,8},{8,10},{10,12},{12,14},{14,16},{16... | collective-permute-start | bytes 2359304 | tf_op jit(solution)/shard_map/ppermute | solution.py:19
  77.0 19.1 %collective-permute-start.7 = (bf16[256,1536]{1,0:T(8,128)(2,1)}, bf16[256,1536]{1,0:T(8,128)(2,1)S(1)}, u32[]{:S(2)}, u32[]{:S(2)}) collective-permute-start(bf16[256,1536]{1,0:T(8,128)(2,1)} %collective-permute-done.4), channel_id=1, source_target_pairs={{254,0},{0,2},{2,4},{4,6},{6,8},{8,10},{10,12},{12,14},{14,16},{16... | collective-permute-start | bytes 2359304 | tf_op jit(solution)/shard_map/ppermute | solution.py:19
  81.0 7.8 %copy-start.6 = (bf16[512,256]{1,0:T(8,128)(2,1)}, bf16[512,256]{1,0:T(8,128)(2,1)S(1)}, u32[]{:S(2)}) copy-start(bf16[512,256]{1,0:T(8,128)(2,1)S(1)} %fusion.60) | copy-start | bytes 786436
  88.9 15.7 %collective-permute-start.10 = (f32[256,768]{1,0:T(8,128)}, f32[256,768]{1,0:T(8,128)}, u32[]{:S(2)}, u32[]{:S(2)}) collective-permute-start(f32[256,768]{1,0:T(8,128)} %fusion.2), channel_id=1, source_target_pairs={{254,0},{0,2},{2,4},{4,6},{6,8},{8,10},{10,12},{12,14},{14,16},{16... | collective-permute-start | bytes 2359304 | tf_op jit(solution)/shard_map/ppermute | solution.py:19
  98.2 0.7 copy-start.7
  101.3 319.8 %all-reduce.3.cloned.1.call-start = ((), (), s32[]{:S(2)}) async-start(), calls=%async_computation.3 | async-start | bytes 9437184 | tf_op jit(solution)/shard_map/psum | solution.py:106
  102.7 5.7 %copy-start.8 = (bf16[512,256]{1,0:T(8,128)(2,1)S(1)}, bf16[512,256]{1,0:T(8,128)(2,1)}, u32[]{:S(2)}) copy-start(bf16[512,256]{1,0:T(8,128)(2,1)} %copy-done.7) | copy-start | bytes 786436
  105.8 15.3 %collective-permute-start.11 = (f32[256,768]{1,0:T(8,128)S(1)}, f32[256,768]{1,0:T(8,128)S(1)}, u32[]{:S(2)}, u32[]{:S(2)}) collective-permute-start(f32[256,768]{1,0:T(8,128)S(1)} %add.158), channel_id=1, source_target_pairs={{254,0},{0,2},{2,4},{4,6},{6,8},{8,10},{10,12},{12,14},{14,16},{16... | collective-permute-start | bytes 2359304 | tf_op jit(solution)/shard_map/ppermute | solution.py:19
  122.0 19.7 %collective-permute-start.12 = (f32[256,768]{1,0:T(8,128)}, f32[256,768]{1,0:T(8,128)S(1)}, u32[]{:S(2)}, u32[]{:S(2)}) collective-permute-start(f32[256,768]{1,0:T(8,128)} %add.159), channel_id=1, source_target_pairs={{6,0},{8,2},{10,4},{12,6},{14,8},{16,10},{18,12},{20,14},{22,16},{... | collective-permute-start | bytes 2359304 | tf_op jit(solution)/shard_map/ppermute | solution.py:19
  137.0 1.9 copy-start.9
  137.1 1.9 copy-start.11
  141.0 1.0 copy-start.13
  421.1 3.2 copy-start.2
Sparse Core Ops, SparseCore 0:
  12.6 56.4 all-gather.2
  101.4 34.3 reduce-scatter.1
  144.9 276.0 all-reduce.2
where the time goes:
time: 434 us; the launch traced here: 433 us
  waiting for transfers between devices  315 us (73%)
  matrix products  33 us (8%)
  blocking collectives  31.6 us (7%)
  starting transfers between devices  25.1 us (6%)
  between operations  14.1 us (3%)
  local copies, waits for them, and re-layouts  7.01 us (2%)
  other arithmetic  6.48 us (1%)
    psum x1, waiting for transfers between devices, local(): lax.psum((image_part, text_part), ('dp', 'section'))  276 us
    ppermute x13, waiting for transfers between devices, passed_along(): return lax.ppermute(block, axis, route)  32.4 us
    all_gather x1, blocking collectives, local(): lax.all_gather(image_emb, 'section', axis=0, tiled=True)  26.6 us
    ppermute x13, starting transfers between devices, passed_along(): return lax.ppermute(block, axis, route)  24.9 us
  transfers between devices with their start and end apart: 16, of which 10 were waited for; matrix products, arithmetic and copies ran while one was open for 7% of the time, Pallas kernels for 0%

commit v1 on v0

v1 whole, which is shorter than its diff:
```python
import jax
import jax.numpy as jnp
from jax import lax
from jax.sharding import Mesh
from jax.sharding import PartitionSpec as P

epsilon = 1e-06
scale = 20.0
shift = -1.0

AXES = ("yl", "z", "x", "core", "yh")
DP = ("yl", "z", "x", "core")
N_DP = 128

f32 = jnp.float32
bf16 = jnp.bfloat16


def unit_rows(raw_rows):
    row_len = jnp.sqrt(jnp.sum(raw_rows * raw_rows, axis=1, keepdims=True) + epsilon)
    return (raw_rows / row_len, row_len)


def swap(block, axis):
    return lax.ppermute(block, axis, [(0, 1), (1, 0)])


def along_dp(block, route):
    return lax.ppermute(block, DP, route)


def chip_shift(block, step):
    return along_dp(block, [(i, (i + 2 * step) % N_DP) for i in range(N_DP)])


def pair_tile(target_rows, image_rows, row_ids, target_cols, text_cols, col_ids):
    teacher_dot = lax.dot_general(
        target_rows, target_cols, (((1,), (1,)), ((), ())), preferred_element_type=f32
    )
    labels = (row_ids[:, None] == col_ids[None, :]).astype(f32)
    target = 0.5 * jax.nn.sigmoid(scale * teacher_dot + shift) + 0.5 * labels
    logits = (
        scale
        * lax.dot_general(
            image_rows, text_cols, (((1,), (1,)), ((), ())), preferred_element_type=f32
        )
        + shift
    )
    scaled = ((jax.nn.sigmoid(logits) - target) / text_cols.shape[0]).astype(bf16)
    row_part = scale * jnp.dot(scaled, text_cols, preferred_element_type=f32)
    col_part = scale * lax.dot_general(
        scaled, image_rows, (((0,), (0,)), ((), ())), preferred_element_type=f32
    )
    return (row_part, col_part)


def direction(unit, length, grad):
    d = (grad - unit * jnp.sum(unit * grad, axis=1, keepdims=True)) / length
    high = d.astype(bf16)
    low = (d - high.astype(f32)).astype(bf16)
    return high, low


def local(
    teacher_image,
    teacher_proj,
    teacher_text,
    image_feats,
    text_feats,
    image_proj,
    text_proj,
    class_ids,
):
    core = lax.axis_index("core")
    first = core == 0
    back_route = [(i, i - 1 if i % 2 else (i - 3) % N_DP) for i in range(N_DP)]
    step_route = [(i, (i + 1) % N_DP) for i in range(N_DP)]

    ids_y = swap(class_ids, "yh")
    ids1 = along_dp(class_ids, step_route)
    ids2 = along_dp(class_ids, [(i, (i + 2) % N_DP) for i in range(N_DP)])
    ids3 = along_dp(class_ids, [(i, (i + 3) % N_DP) for i in range(N_DP)])

    text_unit, text_len = unit_rows(jnp.dot(text_feats, text_proj, preferred_element_type=f32))
    text_emb = text_unit.astype(bf16)
    text_recv = chip_shift(text_emb, 1)
    image_unit, image_len = unit_rows(
        jnp.dot(image_feats, image_proj, preferred_element_type=f32)
    )
    image_emb = image_unit.astype(bf16)
    image_y = swap(image_emb, "yh")
    written_unit, _ = unit_rows(teacher_text.astype(f32))
    teacher_txt = written_unit.astype(bf16)
    teach_recv = chip_shift(teacher_txt, 1)
    teacher_unit, _ = unit_rows(jnp.dot(teacher_image, teacher_proj, preferred_element_type=f32))
    teacher_img = teacher_unit.astype(bf16)
    teach_y = swap(teacher_img, "yh")
    text_exch = swap(text_recv, "core")
    text_far = along_dp(jnp.where(first, text_emb, text_recv), step_route)
    teach_exch = swap(teach_recv, "core")
    teach_far = along_dp(jnp.where(first, teacher_txt, teach_recv), step_route)

    sent_feats = jnp.where(first, text_feats, image_feats)
    kept_feats = jnp.where(first, image_feats, text_feats)
    feats_in = swap(sent_feats, "core")

    image_rows = jnp.concatenate([image_emb, image_y], axis=0)
    teach_rows = jnp.concatenate([teacher_img, teach_y], axis=0)
    row_ids = jnp.concatenate([class_ids, ids_y], axis=0)
    row0, col0 = pair_tile(teach_rows, image_rows, row_ids, teacher_txt, text_emb, class_ids)
    row1, col1 = pair_tile(teach_rows, image_rows, row_ids, teach_recv, text_recv, ids2)
    ids_exch = jnp.where(first, ids1, ids3)
    row2, col2 = pair_tile(teach_rows, image_rows, row_ids, teach_exch, text_exch, ids_exch)
    both = col1 + swap(col2.astype(bf16), "core").astype(f32)
    both_back = chip_shift(both.astype(bf16), -1)
    ids_far = jnp.where(first, ids3, ids1)
    row3, col3 = pair_tile(teach_rows, image_rows, row_ids, teach_far, text_far, ids_far)
    far_back = along_dp(col3.astype(bf16), back_route)
    grad_rows = row0 + row1 + row2 + row3
    half = text_emb.shape[0]
    rows_y = swap(grad_rows[half:].astype(bf16), "yh")
    grad_img = grad_rows[:half] + rows_y.astype(f32)
    grad_txt = col0 + both_back.astype(f32) + far_back.astype(f32)

    img_high, img_low = direction(image_unit, image_len, grad_img)
    txt_high, txt_low = direction(text_unit, text_len, grad_txt)
    high_in = swap(jnp.where(first, txt_high, img_high), "core")
    low_in = swap(jnp.where(first, txt_low, img_low), "core")
    high_own = jnp.where(first, img_high, txt_high)
    low_own = jnp.where(first, img_low, txt_low)
    feats2 = jnp.concatenate([kept_feats, feats_in], axis=0)
    high2 = jnp.concatenate([high_own, high_in], axis=0)
    low2 = jnp.concatenate([low_own, low_in], axis=0)
    dims = (((0,), (0,)), ((), ()))
    part = lax.dot_general(feats2, high2, dims, preferred_element_type=f32) + lax.dot_general(
        feats2, low2, dims, preferred_element_type=f32
    )
    ds = part.shape[0]
    parts = lax.all_to_all(part.reshape(4, ds // 4, ds), "x", 0, 0, tiled=True)
    summed = parts.sum(axis=0)
    parts = lax.all_to_all(summed.reshape(8, ds // 32, ds), "z", 0, 0, tiled=True)
    summed = parts.sum(axis=0)
    other_l = swap(summed, "yl")
    other_h = swap(summed, "yh")
    other_b = lax.ppermute(summed, ("yl", "yh"), [(0, 3), (1, 2), (2, 1), (3, 0)])
    summed = (summed + other_l) + (other_h + other_b)
    spread = jnp.broadcast_to(summed[None], (8,) + summed.shape)
    gathered = lax.all_to_all(spread, "z", 0, 0, tiled=True).reshape(ds // 4, ds)
    spread = jnp.broadcast_to(gathered[None], (4,) + gathered.shape)
    own_total = lax.all_to_all(spread, "x", 0, 0, tiled=True).reshape(ds, ds)
    other_total = swap(own_total, "core")
    return (
        jnp.where(first, own_total, other_total),
        jnp.where(first, other_total, own_total),
    )


def solution(mesh):
    fine = Mesh(mesh.devices.reshape(2, 8, 4, 2, 2), AXES)
    rows = P(AXES, None)
    in_specs = (rows, P(), rows, rows, rows, P(), P(), P(AXES))
    return jax.shard_map(
        local, mesh=fine, in_specs=in_specs, out_specs=(P(), P()), check_vma=False
    )
```

time: 434 us -> 229 us (0.53)
  waiting for transfers between devices: 315 us -> 65.8 us
  blocking collectives: 31.6 us -> 94.7 us
  matrix products: 33 us -> 18.1 us
  between operations: 14.1 us -> 1 us
  other arithmetic: 6.48 us -> 15.3 us
  starting transfers between devices: 25.1 us -> 32.9 us
  local copies, waits for them, and re-layouts: 7.01 us -> 0.32 us
    psum x1 -> x0, waiting for transfers between devices: 276 us -> none  [local(): lax.psum((image_part, text_part), ('dp', 'section'))]
    all_to_all x0 -> x4, blocking collectives: none -> 94.7 us  [the longest x1 31.4 us: local(): parts = lax.all_to_all(part.reshape(4, ds // 4, ds), 'x', 0, 0, tiled=True)]
    ppermute x13 -> x23, waiting for transfers between devices: 32.4 us -> 65.8 us  [the longest x13 45.2 us: swap(): return lax.ppermute(block, axis, [(0, 1), (1, 0)])]
    all_gather x2 -> x0, blocking collectives: 31.6 us -> none  [the longest x1 26.6 us: local(): lax.all_gather(image_emb, 'section', axis=0, tiled=True)]
    dot_general x15 -> x13, matrix products: 24.1 us -> 12.6 us  [the longest x4 4.9 us: pair_tile(): lax.dot_general(target_rows, target_cols, (((1,), (1,)), ((), ())), prefe...]
    ppermute x13 -> x23, starting transfers between devices: 24.9 us -> 32.9 us  [the longest x13 24.3 us: swap(): return lax.ppermute(block, axis, [(0, 1), (1, 0)])]
    unnamed x38 -> x24, local copies, waits for them, and re-layouts: 7.01 us -> 0.06 us
    select_n x0 -> x7, other arithmetic: none -> 6.6 us  [the longest x1 2.49 us: local(): jnp.where(first, other_total, own_total)]
  transfers between devices with their start and end apart: 16 -> 23, of which waited for: 10 -> 9; matrix products, arithmetic and copies ran while one was open for 7% -> 13% of each run, Pallas kernels for 0% -> 0%
where the time goes in v1:
time: 229 us; the launch traced here: 228 us
  blocking collectives  94.7 us (41%)
  waiting for transfers between devices  65.8 us (29%)
  starting transfers between devices  32.9 us (14%)
  matrix products  18.1 us (8%)
  other arithmetic  15.3 us (7%)
    ppermute x13, waiting for transfers between devices, swap(): return lax.ppermute(block, axis, [(0, 1), (1, 0)])  45.2 us
    all_to_all x1, blocking collectives, local(): parts = lax.all_to_all(part.reshape(4, ds // 4, ds), 'x', 0, 0, tiled=True)  31.4 us
    all_to_all x1, blocking collectives, local(): own_total = lax.all_to_all(spread, 'x', 0, 0, tiled=True).reshape(ds, ds)  25.7 us
    ppermute x13, starting transfers between devices, swap(): return lax.ppermute(block, axis, [(0, 1), (1, 0)])  24.3 us
    ppermute x9, waiting for transfers between devices, along_dp(): return lax.ppermute(block, DP, route)  19.4 us
    all_to_all x1, blocking collectives, local(): lax.all_to_all(summed.reshape(8, ds // 32, ds), 'z', 0, 0, tiled=True)  19.3 us
    all_to_all x1, blocking collectives, local(): lax.all_to_all(spread, 'z', 0, 0, tiled=True).reshape(ds // 4, ds)  18.2 us
    ppermute x9, starting transfers between devices, along_dp(): return lax.ppermute(block, DP, route)  7.56 us
  transfers between devices with their start and end apart: 23, of which 9 were waited for; matrix products, arithmetic and copies ran while one was open for 13% of the time, Pallas kernels for 0%

profile of v1, /device:TPU:1, one launch (start us, length us, event | category | flops | bytes accessed | tf_op | source)
XLA Modules:
  0.0 228.1 jit_solution(2588581385261548673)
XLA Ops:
  0.7 4.2 %collective-permute-start.10 = (s32[256]{0:T(256)}, s32[256]{0:T(256)}, u32[]{:S(2)}, u32[]{:S(2)}) collective-permute-start(s32[256]{0:T(256)} %param.15), channel_id=1, source_target_pairs={{0,6},{2,8},{4,10},{6,12},{8,14},{10,16},{12,18},{14,20},{16,22},{... | collective-permute-start | bytes 3080 | tf_op jit(solution)/shard_map/ppermute | solution.py:29
  4.9 2.9 %collective-permute-start.3 = (s32[256]{0:T(256)}, s32[256]{0:T(256)}, u32[]{:S(2)}, u32[]{:S(2)}) collective-permute-start(s32[256]{0:T(256)} %param.15), channel_id=1, source_target_pairs={{0,1},{1,0},{2,3},{3,2},{4,5},{5,4},{6,7},{7,6},{8,9},{9,8},{10,11... | collective-permute-start | bytes 3080 | tf_op jit(solution)/shard_map/ppermute | solution.py:25
  7.8 1.4 fusion
  9.2 2.5 %fusion.1 = bf16[256,1536]{1,0:T(8,128)(2,1)} fusion(bf16[256,1536]{1,0:T(8,128)(2,1)} %param.10, f32[256]{0:T(256)S(1)} %add_sqrt_fusion), kind=kLoop, calls=%fused_computation.4 | loop fusion | flops 1179648 | bytes 1573888 | tf_op jit(solution)/shard_map/convert_element_type | solution.py:93
  12.6 0.9 fusion.78
  13.5 1.6 collective-permute-start.4
  15.0 1.5 multiply_reduce_fusion
  17.1 1.1 divide_convert_fusion
  18.2 0.9 fusion.77
  19.1 1.2 collective-permute-start.6
  20.3 0.6 pad_add_fusion
  21.1 2.9 %collective-permute-start.1 = (bf16[256,768]{1,0:T(8,128)(2,1)}, bf16[256,768]{1,0:T(8,128)(2,1)S(1)}, u32[]{:S(2)}, u32[]{:S(2)}) collective-permute-start(bf16[256,768]{1,0:T(8,128)(2,1)} %fusion.77), channel_id=1, source_target_pairs={{0,1},{1,0},{2,3},{3,2},{4,5},{5,4},{6,7},{7,6},{8,9},{9,8},{10,11... | collective-permute-start | bytes 1179656 | tf_op jit(solution)/shard_map/ppermute | solution.py:25
  24.0 0.7 broadcast_select_fusion.11
  24.7 18.3 %collective-permute-done.4 = bf16[256,768]{1,0:T(8,128)(2,1)} collective-permute-done((bf16[256,768]{1,0:T(8,128)(2,1)}, bf16[256,768]{1,0:T(8,128)(2,1)}, u32[]{:S(2)}, u32[]{:S(2)}) %collective-permute-start.4) | collective-permute-done | bytes 393248 | tf_op jit(solution)/shard_map/ppermute | solution.py:29
  42.9 1.2 broadcast_select_fusion.7
  44.2 0.9 collective-permute-start.7
  45.1 1.6 broadcast_select_fusion.2
  46.7 18.9 %collective-permute-done.2 = bf16[256,1536]{1,0:T(8,128)(2,1)S(1)} collective-permute-done((bf16[256,1536]{1,0:T(8,128)(2,1)}, bf16[256,1536]{1,0:T(8,128)(2,1)S(1)}, u32[]{:S(2)}, u32[]{:S(2)}) %collective-permute-start.2) | collective-permute-done | bytes 786464 | tf_op jit(solution)/shard_map/ppermute | solution.py:25
  65.6 1.8 fusion.55
  67.4 0.9 collective-permute-start.8
  68.3 1.8 fusion.48
  70.1 10.2 %collective-permute-done.1 = bf16[256,768]{1,0:T(8,128)(2,1)S(1)} collective-permute-done((bf16[256,768]{1,0:T(8,128)(2,1)}, bf16[256,768]{1,0:T(8,128)(2,1)S(1)}, u32[]{:S(2)}, u32[]{:S(2)}) %collective-permute-start.1) | collective-permute-done | bytes 393248 | tf_op jit(solution)/shard_map/ppermute | solution.py:25
  80.3 1.4 fusion.65
  81.7 1.4 fusion.64
  83.2 1.4 fusion.79
  84.5 1.4 fusion.80
  85.9 0.7 fusion.41
  88.0 0.7 fusion.34
  90.5 3.7 %collective-permute-start.13 = (bf16[256,768]{1,0:T(8,128)(2,1)S(1)}, bf16[256,768]{1,0:T(8,128)(2,1)S(1)}, u32[]{:S(2)}, u32[]{:S(2)}) collective-permute-start(bf16[256,768]{1,0:T(8,128)(2,1)S(1)} %slice.17), channel_id=1, source_target_pairs={{0,1},{1,0},{2,3},{3,2},{4,5},{5,4},{6,7},{7,6},{8,9},{9,8},{10,11... | collective-permute-start | bytes 1179656 | tf_op jit(solution)/shard_map/ppermute | solution.py:25
  95.2 8.5 %collective-permute-done.13 = bf16[256,768]{1,0:T(8,128)(2,1)S(1)} collective-permute-done((bf16[256,768]{1,0:T(8,128)(2,1)S(1)}, bf16[256,768]{1,0:T(8,128)(2,1)S(1)}, u32[]{:S(2)}, u32[]{:S(2)}) %collective-permute-start.13) | collective-permute-done | bytes 393248 | tf_op jit(solution)/shard_map/ppermute | solution.py:25
  103.9 1.1 collective-permute-done.15
  106.3 1.2 collective-permute-start.18
  107.6 1.2 collective-permute-done.18
  108.9 0.8 fusion.71
  109.7 0.8 convolution_add_fusion
  110.5 31.4 %all_to_all.20 = f32[4,192,768]{2,1,0:T(8,128)S(1)} all-to-all(f32[4,192,768]{2,1,0:T(8,128)S(1)} %bitcast.32), channel_id=1, replica_groups=mesh['yl'=2,'z'=8,'x'=4,'core'=2,'yh'=2] {'x'}, dimensions={0} | all-to-all | bytes 4718592 | tf_op jit(solution)/shard_map/all_to_all | solution.py:139
  141.9 1.0 reduce_sum.78
  142.9 19.3 %all_to_all.21 = f32[8,24,768]{2,1,0:T(8,128)S(1)} all-to-all(f32[8,24,768]{2,1,0:T(8,128)} %bitcast.34), channel_id=1, replica_groups=mesh['yl'=2,'z'=8,'x'=4,'core'=2,'yh'=2] {'z'}, dimensions={0} | all-to-all | bytes 1179648 | tf_op jit(solution)/shard_map/all_to_all | solution.py:141
  162.2 2.3 %collective-permute-start.19 = (f32[24,768]{1,0:T(8,128)S(1)}, f32[24,768]{1,0:T(8,128)S(1)}, u32[]{:S(2)}, u32[]{:S(2)}) collective-permute-start(f32[24,768]{1,0:T(8,128)S(1)} %reduce_sum.79), channel_id=1, source_target_pairs={{0,128},{128,0},{1,129},{129,1},{2,130},{130,2},{3,131},{131,3},{4... | collective-permute-start | bytes 221192 | tf_op jit(solution)/shard_map/ppermute | solution.py:25
  164.6 1.4 collective-permute-start.20
  166.0 1.1 collective-permute-start.21
  167.1 2.2 collective-permute-done.20
  169.3 1.1 collective-permute-done.21
  170.5 18.2 %all_to_all.22 = f32[8,24,768]{2,1,0:T(8,128)S(1)} all-to-all(f32[8,24,768]{2,1,0:T(8,128)S(1)} %broadcast_in_dim.6), channel_id=1, replica_groups=mesh['yl'=2,'z'=8,'x'=4,'core'=2,'yh'=2] {'z'}, dimensions={0} | all-to-all | bytes 1179648 | tf_op jit(solution)/shard_map/all_to_all | solution.py:148
  188.9 25.7 %all_to_all.23 = f32[4,192,768]{2,1,0:T(8,128)S(1)} all-to-all(f32[4,192,768]{2,1,0:T(8,128)S(1)} %broadcast_in_dim.8), channel_id=1, replica_groups=mesh['yl'=2,'z'=8,'x'=4,'core'=2,'yh'=2] {'x'}, dimensions={0} | all-to-all | bytes 4718592 | tf_op jit(solution)/shard_map/all_to_all | solution.py:150
  214.6 6.8 %collective-permute-start.22 = (f32[768,768]{1,0:T(8,128)S(1)}, f32[768,768]{1,0:T(8,128)S(1)}, u32[]{:S(2)}, u32[]{:S(2)}) collective-permute-start(f32[768,768]{1,0:T(8,128)S(1)} %bitcast.33), channel_id=1, source_target_pairs={{0,2},{2,0},{1,3},{3,1},{4,6},{6,4},{5,7},{7,5},{8,10},{10,8},{9,1... | collective-permute-start | bytes 7077896 | tf_op jit(solution)/shard_map/ppermute | solution.py:25
  221.5 4.2 %collective-permute-done.22 = f32[768,768]{1,0:T(8,128)S(1)} collective-permute-done((f32[768,768]{1,0:T(8,128)S(1)}, f32[768,768]{1,0:T(8,128)S(1)}, u32[]{:S(2)}, u32[]{:S(2)}) %collective-permute-start.22) | collective-permute-done | bytes 2359328 | tf_op jit(solution)/shard_map/ppermute | solution.py:25
  225.6 2.5 %broadcast_select_fusion = (f32[768,768]{1,0:T(8,128)}, f32[768,768]{1,0:T(8,128)}) fusion(f32[768,768]{1,0:T(8,128)S(1)} %collective-permute-done.22, pred[]{:T(512)S(6)} %eq.20, f32[4,192,768]{2,1,0:T(8,128)S(1)} %all_to_all.23), kind=kLoop, calls=%fused_computation.87 | loop fusion | flops 1179648 | bytes 9437185 | tf_op jit(solution)/shard_map/jit(_where)/select_n | solution.py:154
  (71 shorter events, 7.7 us)
Async XLA Ops:
  0.6 11.4 %copy-start = (bf16[768,768]{1,0:T(8,128)(2,1)S(1)}, bf16[768,768]{1,0:T(8,128)(2,1)}, u32[]{:S(2)}) copy-start(bf16[768,768]{1,0:T(8,128)(2,1)} %param.14) | copy-start | bytes 3538948
  0.6 11.4 %copy-start.2 = (bf16[256,768]{1,0:T(8,128)(2,1)S(1)}, bf16[256,768]{1,0:T(8,128)(2,1)}, u32[]{:S(2)}) copy-start(bf16[256,768]{1,0:T(8,128)(2,1)} %param.12) | copy-start | bytes 1179652
  0.7 20.3 %collective-permute-start.10 = (s32[256]{0:T(256)}, s32[256]{0:T(256)}, u32[]{:S(2)}, u32[]{:S(2)}) collective-permute-start(s32[256]{0:T(256)} %param.15), channel_id=1, source_target_pairs={{0,6},{2,8},{4,10},{6,12},{8,14},{10,16},{12,18},{14,20},{16,22},{... | collective-permute-start | bytes 3080 | tf_op jit(solution)/shard_map/ppermute | solution.py:29
  4.9 16.2 %collective-permute-start.9 = (s32[256]{0:T(256)}, s32[256]{0:T(256)}, u32[]{:S(2)}, u32[]{:S(2)}) collective-permute-start(s32[256]{0:T(256)} %param.15), channel_id=1, source_target_pairs={{0,2},{2,4},{4,6},{6,8},{8,10},{10,12},{12,14},{14,16},{16,18},{18... | collective-permute-start | bytes 3080 | tf_op jit(solution)/shard_map/ppermute | solution.py:29
  4.9 14.2 %collective-permute-start.3 = (s32[256]{0:T(256)}, s32[256]{0:T(256)}, u32[]{:S(2)}, u32[]{:S(2)}) collective-permute-start(s32[256]{0:T(256)} %param.15), channel_id=1, source_target_pairs={{0,1},{1,0},{2,3},{3,2},{4,5},{5,4},{6,7},{7,6},{8,9},{9,8},{10,11... | collective-permute-start | bytes 3080 | tf_op jit(solution)/shard_map/ppermute | solution.py:25
  7.8 7.2 %copy-start.11 = (bf16[256,1536]{1,0:T(8,128)(2,1)S(1)}, bf16[256,1536]{1,0:T(8,128)(2,1)}, u32[]{:S(2)}) copy-start(bf16[256,1536]{1,0:T(8,128)(2,1)} %param.8) | copy-start | bytes 2359300
  9.2 5.8 %copy-start.10 = (bf16[1536,1536]{1,0:T(8,128)(2,1)S(1)}, bf16[1536,1536]{1,0:T(8,128)(2,1)}, u32[]{:S(2)}) copy-start(bf16[1536,1536]{1,0:T(8,128)(2,1)} %param.9) | copy-start | bytes 14155780
  11.7 32.5 %collective-permute-start.5 = (bf16[256,1536]{1,0:T(8,128)(2,1)}, bf16[256,1536]{1,0:T(8,128)(2,1)}, u32[]{:S(2)}, u32[]{:S(2)}) collective-permute-start(bf16[256,1536]{1,0:T(8,128)(2,1)} %fusion.1), channel_id=1, source_target_pairs={{0,4},{2,6},{4,8},{6,10},{8,12},{10,14},{12,16},{14,18},{16,20},{1... | collective-permute-start | bytes 2359304 | tf_op jit(solution)/shard_map/ppermute | solution.py:29
  13.5 3.1 %copy-start.4 = (bf16[256,768]{1,0:T(8,128)(2,1)S(1)}, bf16[256,768]{1,0:T(8,128)(2,1)}, u32[]{:S(2)}) copy-start(bf16[256,768]{1,0:T(8,128)(2,1)} %param.11) | copy-start | bytes 1179652
  13.5 3.1 %copy-start.6 = (bf16[768,768]{1,0:T(8,128)(2,1)S(1)}, bf16[768,768]{1,0:T(8,128)(2,1)}, u32[]{:S(2)}) copy-start(bf16[768,768]{1,0:T(8,128)(2,1)} %param.13) | copy-start | bytes 3538948
  13.5 29.5 %collective-permute-start.4 = (bf16[256,768]{1,0:T(8,128)(2,1)}, bf16[256,768]{1,0:T(8,128)(2,1)}, u32[]{:S(2)}, u32[]{:S(2)}) collective-permute-start(bf16[256,768]{1,0:T(8,128)(2,1)} %fusion.78), channel_id=1, source_target_pairs={{0,4},{2,6},{4,8},{6,10},{8,12},{10,14},{12,16},{14,18},{16,20},{1... | collective-permute-start | bytes 1179656 | tf_op jit(solution)/shard_map/ppermute | solution.py:29
  17.1 2.0 copy-start.9
  18.2 26.9 %copy-start.1 = (bf16[256,1536]{1,0:T(8,128)(2,1)S(1)}, bf16[256,1536]{1,0:T(8,128)(2,1)}, u32[]{:S(2)}) copy-start(bf16[256,1536]{1,0:T(8,128)(2,1)} %param.10) | copy-start | bytes 2359300
  19.1 48.3 %collective-permute-start.6 = (s32[256]{0:T(256)S(1)}, s32[256]{0:T(256)S(1)}, u32[]{:S(2)}, u32[]{:S(2)}) collective-permute-start(s32[256]{0:T(256)S(1)} %copy-done.9), channel_id=1, source_target_pairs={{0,4},{2,6},{4,8},{6,10},{8,12},{10,14},{12,16},{14,18},{16,20},{1... | collective-permute-start | bytes 3080 | tf_op jit(solution)/shard_map/ppermute | solution.py:29
  21.0 44.7 %collective-permute-start.2 = (bf16[256,1536]{1,0:T(8,128)(2,1)}, bf16[256,1536]{1,0:T(8,128)(2,1)S(1)}, u32[]{:S(2)}, u32[]{:S(2)}) collective-permute-start(bf16[256,1536]{1,0:T(8,128)(2,1)} %divide_convert_fusion), channel_id=1, source_target_pairs={{0,1},{1,0},{2,3},{3,2},{4,5},{5,4},{6,7},{7,6},{8,9},{9,8},{10,11... | collective-permute-start | bytes 2359304 | tf_op jit(solution)/shard_map/ppermute | solution.py:25
  21.1 59.2 %collective-permute-start.1 = (bf16[256,768]{1,0:T(8,128)(2,1)}, bf16[256,768]{1,0:T(8,128)(2,1)S(1)}, u32[]{:S(2)}, u32[]{:S(2)}) collective-permute-start(bf16[256,768]{1,0:T(8,128)(2,1)} %fusion.77), channel_id=1, source_target_pairs={{0,1},{1,0},{2,3},{3,2},{4,5},{5,4},{6,7},{7,6},{8,9},{9,8},{10,11... | collective-permute-start | bytes 1179656 | tf_op jit(solution)/shard_map/ppermute | solution.py:25
  44.1 21.5 %copy-start.7 = (bf16[256,1536]{1,0:T(8,128)(2,1)S(1)}, bf16[256,1536]{1,0:T(8,128)(2,1)}, u32[]{:S(2)}) copy-start(bf16[256,1536]{1,0:T(8,128)(2,1)} %divide_convert_fusion) | copy-start | bytes 2359300
  44.1 44.6 %collective-permute-start.11 = (bf16[256,768]{1,0:T(8,128)(2,1)S(1)}, bf16[256,768]{1,0:T(8,128)(2,1)S(1)}, u32[]{:S(2)}, u32[]{:S(2)}) collective-permute-start(bf16[256,768]{1,0:T(8,128)(2,1)S(1)} %broadcast_select_fusion.7), channel_id=1, source_target_pairs={{0,2},{2,4},{4,6},{6,8},{8,10},{10,12},{12,14},{14,16},{16,18},{18... | collective-permute-start | bytes 1179656 | tf_op jit(solution)/shard_map/ppermute | solution.py:29
  44.2 42.4 %collective-permute-start.7 = (bf16[256,768]{1,0:T(8,128)(2,1)}, bf16[256,768]{1,0:T(8,128)(2,1)S(1)}, u32[]{:S(2)}, u32[]{:S(2)}) collective-permute-start(bf16[256,768]{1,0:T(8,128)(2,1)} %collective-permute-done.4), channel_id=1, source_target_pairs={{0,2},{2,0},{1,3},{3,1},{4,6},{6,4},{5,7},{7,5},{8,10},{10,8},{9,1... | collective-permute-start | bytes 1179656 | tf_op jit(solution)/shard_map/ppermute | solution.py:25
  65.6 22.4 %collective-permute-start.12 = (bf16[256,1536]{1,0:T(8,128)(2,1)S(1)}, bf16[256,1536]{1,0:T(8,128)(2,1)S(1)}, u32[]{:S(2)}, u32[]{:S(2)}) collective-permute-start(bf16[256,1536]{1,0:T(8,128)(2,1)S(1)} %broadcast_select_fusion.2), channel_id=1, source_target_pairs={{0,2},{2,4},{4,6},{6,8},{8,10},{10,12},{12,14},{14,16},{16,18},{18... | collective-permute-start | bytes 2359304 | tf_op jit(solution)/shard_map/ppermute | solution.py:29
  67.4 12.9 %copy-start.8 = (bf16[256,768]{1,0:T(8,128)(2,1)S(1)}, bf16[256,768]{1,0:T(8,128)(2,1)}, u32[]{:S(2)}) copy-start(bf16[256,768]{1,0:T(8,128)(2,1)} %fusion.77) | copy-start | bytes 1179652
  67.4 18.5 %collective-permute-start.8 = (bf16[256,1536]{1,0:T(8,128)(2,1)}, bf16[256,1536]{1,0:T(8,128)(2,1)S(1)}, u32[]{:S(2)}, u32[]{:S(2)}) collective-permute-start(bf16[256,1536]{1,0:T(8,128)(2,1)} %collective-permute-done.5), channel_id=1, source_target_pairs={{0,2},{2,0},{1,3},{3,1},{4,6},{6,4},{5,7},{7,5},{8,10},{10,8},{9,1... | collective-permute-start | bytes 2359304 | tf_op jit(solution)/shard_map/ppermute | solution.py:25
  87.4 6.8 %collective-permute-start.14 = (bf16[256,768]{1,0:T(8,128)(2,1)S(1)}, bf16[256,768]{1,0:T(8,128)(2,1)S(1)}, u32[]{:S(2)}, u32[]{:S(2)}) collective-permute-start(bf16[256,768]{1,0:T(8,128)(2,1)S(1)} %fusion.6), channel_id=1, source_target_pairs={{0,2},{2,0},{1,3},{3,1},{4,6},{6,4},{5,7},{7,5},{8,10},{10,8},{9,1... | collective-permute-start | bytes 1179656 | tf_op jit(solution)/shard_map/ppermute | solution.py:25
  89.5 14.4 %collective-permute-start.16 = (bf16[256,768]{1,0:T(8,128)(2,1)S(1)}, bf16[256,768]{1,0:T(8,128)(2,1)S(1)}, u32[]{:S(2)}, u32[]{:S(2)}) collective-permute-start(bf16[256,768]{1,0:T(8,128)(2,1)S(1)} %fusion.7), channel_id=1, source_target_pairs={{0,250},{2,0},{4,254},{6,4},{8,2},{10,8},{12,6},{14,12},{16,10},{1... | collective-permute-start | bytes 1179656 | tf_op jit(solution)/shard_map/ppermute | solution.py:29
  90.4 4.3 %copy-start.3 = (bf16[256,768]{1,0:T(8,128)(2,1)S(1)}, bf16[256,768]{1,0:T(8,128)(2,1)}, u32[]{:S(2)}) copy-start(bf16[256,768]{1,0:T(8,128)(2,1)} %param.12) | copy-start | bytes 1179652
  90.4 4.3 %copy-start.5 = (bf16[256,768]{1,0:T(8,128)(2,1)S(1)}, bf16[256,768]{1,0:T(8,128)(2,1)}, u32[]{:S(2)}) copy-start(bf16[256,768]{1,0:T(8,128)(2,1)} %param.11) | copy-start | bytes 1179652
  90.5 13.2 %collective-permute-start.13 = (bf16[256,768]{1,0:T(8,128)(2,1)S(1)}, bf16[256,768]{1,0:T(8,128)(2,1)S(1)}, u32[]{:S(2)}, u32[]{:S(2)}) collective-permute-start(bf16[256,768]{1,0:T(8,128)(2,1)S(1)} %slice.17), channel_id=1, source_target_pairs={{0,1},{1,0},{2,3},{3,2},{4,5},{5,4},{6,7},{7,6},{8,9},{9,8},{10,11... | collective-permute-start | bytes 1179656 | tf_op jit(solution)/shard_map/ppermute | solution.py:25
  94.6 10.5 %collective-permute-start.15 = (bf16[256,768]{1,0:T(8,128)(2,1)S(1)}, bf16[256,768]{1,0:T(8,128)(2,1)S(1)}, u32[]{:S(2)}, u32[]{:S(2)}) collective-permute-start(bf16[256,768]{1,0:T(8,128)(2,1)S(1)} %fusion.5), channel_id=1, source_target_pairs={{0,252},{2,254},{4,0},{6,2},{8,4},{10,6},{12,8},{14,10},{16,12},{1... | collective-permute-start | bytes 1179656 | tf_op jit(solution)/shard_map/ppermute | solution.py:29
  94.8 12.8 %collective-permute-start = (bf16[256,768]{1,0:T(8,128)(2,1)S(1)}, bf16[256,768]{1,0:T(8,128)(2,1)S(1)}, u32[]{:S(2)}, u32[]{:S(2)}) collective-permute-start(bf16[256,768]{1,0:T(8,128)(2,1)S(1)} %get-tuple-element.11), channel_id=1, source_target_pairs={{0,2},{2,0},{1,3},{3,1},{4,6},{6,4},{5,7},{7,5},{8,10},{10,8},{9,1... | collective-permute-start | bytes 1179656 | tf_op jit(solution)/shard_map/ppermute | solution.py:25
  106.3 2.6 %collective-permute-start.18 = (bf16[256,768]{1,0:T(8,128)(2,1)S(1)}, bf16[256,768]{1,0:T(8,128)(2,1)S(1)}, u32[]{:S(2)}, u32[]{:S(2)}) collective-permute-start(bf16[256,768]{1,0:T(8,128)(2,1)S(1)} %get-tuple-element.9), channel_id=1, source_target_pairs={{0,2},{2,0},{1,3},{3,1},{4,6},{6,4},{5,7},{7,5},{8,10},{10,8},{9,1... | collective-permute-start | bytes 1179656 | tf_op jit(solution)/shard_map/ppermute | solution.py:25
  107.5 2.2 collective-permute-start.17
  162.2 4.8 %collective-permute-start.19 = (f32[24,768]{1,0:T(8,128)S(1)}, f32[24,768]{1,0:T(8,128)S(1)}, u32[]{:S(2)}, u32[]{:S(2)}) collective-permute-start(f32[24,768]{1,0:T(8,128)S(1)} %reduce_sum.79), channel_id=1, source_target_pairs={{0,128},{128,0},{1,129},{129,1},{2,130},{130,2},{3,131},{131,3},{4... | collective-permute-start | bytes 221192 | tf_op jit(solution)/shard_map/ppermute | solution.py:25
  164.6 4.7 %collective-permute-start.20 = (f32[24,768]{1,0:T(8,128)S(1)}, f32[24,768]{1,0:T(8,128)S(1)}, u32[]{:S(2)}, u32[]{:S(2)}) collective-permute-start(f32[24,768]{1,0:T(8,128)S(1)} %reduce_sum.79), channel_id=1, source_target_pairs={{0,1},{1,0},{2,3},{3,2},{4,5},{5,4},{6,7},{7,6},{8,9},{9,8},{10,11... | collective-permute-start | bytes 221192 | tf_op jit(solution)/shard_map/ppermute | solution.py:25
  166.0 4.4 %collective-permute-start.21 = (f32[24,768]{1,0:T(8,128)S(1)}, f32[24,768]{1,0:T(8,128)S(1)}, u32[]{:S(2)}, u32[]{:S(2)}) collective-permute-start(f32[24,768]{1,0:T(8,128)S(1)} %reduce_sum.79), channel_id=1, source_target_pairs={{0,129},{1,128},{128,1},{129,0},{2,131},{3,130},{130,3},{131,2},{4... | collective-permute-start | bytes 221192 | tf_op jit(solution)/shard_map/ppermute | solution.py:145
  214.6 11.0 %collective-permute-start.22 = (f32[768,768]{1,0:T(8,128)S(1)}, f32[768,768]{1,0:T(8,128)S(1)}, u32[]{:S(2)}, u32[]{:S(2)}) collective-permute-start(f32[768,768]{1,0:T(8,128)S(1)} %bitcast.33), channel_id=1, source_target_pairs={{0,2},{2,0},{1,3},{3,1},{4,6},{6,4},{5,7},{7,5},{8,10},{10,8},{9,1... | collective-permute-start | bytes 7077896 | tf_op jit(solution)/shard_map/ppermute | solution.py:25

commit v2 on v1

--- a/solution.py
+++ b/solution.py
@@ -14,6 +14,7 @@
 
 f32 = jnp.float32
 bf16 = jnp.bfloat16
+f16 = jnp.float16
 
 
 def unit_rows(raw_rows):
@@ -59,6 +60,44 @@
     high = d.astype(bf16)
     low = (d - high.astype(f32)).astype(bf16)
     return high, low
+
+
+def packed(values, exponent):
+    scaled = (values * jnp.exp2(-exponent)).astype(f16)
+    note = jnp.full((values.shape[0], 8, values.shape[2]), exponent, f32).astype(f16)
+    return jnp.concatenate([scaled, note], axis=1)
+
+
+def unpacked_sum(blocks):
+    exponents = blocks[:, -8, 0].astype(f32)
+    scales = jnp.exp2(exponents)[:, None, None]
+    return (blocks[:, :-8].astype(f32) * scales).sum(axis=0), exponents.max()
+
+
+def sum_everywhere(part):
+    ds = part.shape[0]
+    biggest = jnp.log2(jnp.maximum(jnp.max(jnp.abs(part)), 1e-30))
+    exponent = jnp.clip(jnp.ceil(biggest) - 14.0, -110.0, 110.0)
+    blocks = lax.all_to_all(packed(part.reshape(4, ds // 4, ds), exponent), "x", 0, 0, tiled=True)
+    summed, exponent = unpacked_sum(blocks)
+    exponent = exponent + 2.0
+    blocks = packed(summed.reshape(8, ds // 32, ds), exponent)
+    blocks = lax.all_to_all(blocks, "z", 0, 0, tiled=True)
+    summed, exponent = unpacked_sum(blocks)
+    noted = jnp.concatenate([summed, jnp.full((8, ds), exponent, f32)], axis=0)
+    other_l = swap(noted, "yl")
+    other_h = swap(noted, "yh")
+    other_b = lax.ppermute(noted, ("yl", "yh"), [(0, 3), (1, 2), (2, 1), (3, 0)])
+    summed = ((noted + other_l) + (other_h + other_b))[:-8]
+    exponent = jnp.maximum(exponent, jnp.maximum(other_l[-8, 0], other_h[-8, 0]))
+    exponent = jnp.maximum(exponent, other_b[-8, 0]) + 5.0
+    other_e = swap(jnp.full((8, 128), exponent, f32), "core")[0, 0]
+    block = (summed * jnp.exp2(-exponent)).astype(f16)
+    spread = jnp.broadcast_to(block[None], (8,) + block.shape)
+    gathered = lax.all_to_all(spread, "z", 0, 0, tiled=True).reshape(ds // 4, ds)
+    spread = jnp.broadcast_to(gathered[None], (4,) + gathered.shape)
+    own_total = lax.all_to_all(spread, "x", 0, 0, tiled=True).reshape(ds, ds)
+    return own_total, swap(own_total, "core"), exponent, other_e
 
 
 def local(
@@ -135,20 +174,9 @@
     part = lax.dot_general(feats2, high2, dims, preferred_element_type=f32) + lax.dot_general(
         feats2, low2, dims, preferred_element_type=f32
     )
-    ds = part.shape[0]
-    parts = lax.all_to_all(part.reshape(4, ds // 4, ds), "x", 0, 0, tiled=True)
-    summed = parts.sum(axis=0)
-    parts = lax.all_to_all(summed.reshape(8, ds // 32, ds), "z", 0, 0, tiled=True)
-    summed = parts.sum(axis=0)
-    other_l = swap(summed, "yl")
-    other_h = swap(summed, "yh")
-    other_b = lax.ppermute(summed, ("yl", "yh"), [(0, 3), (1, 2), (2, 1), (3, 0)])
-    summed = (summed + other_l) + (other_h + other_b)
-    spread = jnp.broadcast_to(summed[None], (8,) + summed.shape)
-    gathered = lax.all_to_all(spread, "z", 0, 0, tiled=True).reshape(ds // 4, ds)
-    spread = jnp.broadcast_to(gathered[None], (4,) + gathered.shape)
-    own_total = lax.all_to_all(spread, "x", 0, 0, tiled=True).reshape(ds, ds)
-    other_total = swap(own_total, "core")
+    own_total, other_total, own_e, other_e = sum_everywhere(part)
+    own_total = own_total.astype(f32) * jnp.exp2(own_e)
+    other_total = other_total.astype(f32) * jnp.exp2(other_e)
     return (
         jnp.where(first, own_total, other_total),
         jnp.where(first, other_total, own_total),

time: 229 us -> 203 us (0.89)
  blocking collectives: 94.7 us -> 64.2 us
  between operations: 1 us -> 5.86 us
  waiting for transfers between devices: 65.8 us -> 62.7 us
  local copies, waits for them, and re-layouts: 0.32 us -> 3.27 us
  starting transfers between devices: 32.9 us -> 30.1 us
    all_to_all x4, blocking collectives: 94.7 us -> 64.2 us  [the longest x1 18.9 us: sum_everywhere(): lax.all_to_all(packed(part.reshape(4, ds // 4, ds), exponent), 'x', 0, 0,...]
    ppermute x13 -> x14, waiting for transfers between devices: 45.2 us -> 43.3 us  [swap(): return lax.ppermute(block, axis, [(0, 1), (1, 0)])]
    ppermute x13 -> x14, starting transfers between devices: 24.3 us -> 22.4 us  [swap(): return lax.ppermute(block, axis, [(0, 1), (1, 0)])]
  transfers between devices with their start and end apart: 23 -> 24, of which waited for: 9 -> 8; matrix products, arithmetic and copies ran while one was open for 13% -> 15% of each run, Pallas kernels for 0% -> 0%
where the time goes in v2:
time: 203 us; the launch traced here: 202 us
  blocking collectives  64.2 us (32%)
  waiting for transfers between devices  62.7 us (31%)
  starting transfers between devices  30.1 us (15%)
  matrix products  18.8 us (9%)
  other arithmetic  17.2 us (8%)
  between operations  5.86 us (3%)
  local copies, waits for them, and re-layouts  3.27 us (2%)
    ppermute x14, waiting for transfers between devices, swap(): return lax.ppermute(block, axis, [(0, 1), (1, 0)])  43.3 us
    ppermute x14, starting transfers between devices, swap(): return lax.ppermute(block, axis, [(0, 1), (1, 0)])  22.4 us
    ppermute x9, waiting for transfers between devices, along_dp(): return lax.ppermute(block, DP, route)  19.4 us
    all_to_all x1, blocking collectives, sum_everywhere(): lax.all_to_all(packed(part.reshape(4, ds // 4, ds), exponent), 'x', 0, 0,...  18.9 us
    all_to_all x1, blocking collectives, sum_everywhere(): blocks = lax.all_to_all(blocks, 'z', 0, 0, tiled=True)  16.5 us
    all_to_all x1, blocking collectives, sum_everywhere(): own_total = lax.all_to_all(spread, 'x', 0, 0, tiled=True).reshape(ds, ds)  15.1 us
    all_to_all x1, blocking collectives, sum_everywhere(): lax.all_to_all(spread, 'z', 0, 0, tiled=True).reshape(ds // 4, ds)  13.7 us
    ppermute x9, starting transfers between devices, along_dp(): return lax.ppermute(block, DP, route)  7.56 us
  transfers between devices with their start and end apart: 24, of which 8 were waited for; matrix products, arithmetic and copies ran while one was open for 15% of the time, Pallas kernels for 0%

profile of v2, /device:TPU:1, one launch (start us, length us, event | category | flops | bytes accessed | tf_op | source)
XLA Modules:
  0.0 202.1 jit_solution(17347840275903210865)
XLA Ops:
  0.7 4.2 %collective-permute-start.10 = (s32[256]{0:T(256)}, s32[256]{0:T(256)}, u32[]{:S(2)}, u32[]{:S(2)}) collective-permute-start(s32[256]{0:T(256)} %param.15), channel_id=1, source_target_pairs={{0,6},{2,8},{4,10},{6,12},{8,14},{10,16},{12,18},{14,20},{16,22},{... | collective-permute-start | bytes 3080 | tf_op jit(solution)/shard_map/ppermute | solution.py:30
  4.9 2.9 %collective-permute-start.3 = (s32[256]{0:T(256)}, s32[256]{0:T(256)}, u32[]{:S(2)}, u32[]{:S(2)}) collective-permute-start(s32[256]{0:T(256)} %param.15), channel_id=1, source_target_pairs={{0,1},{1,0},{2,3},{3,2},{4,5},{5,4},{6,7},{7,6},{8,9},{9,8},{10,11... | collective-permute-start | bytes 3080 | tf_op jit(solution)/shard_map/ppermute | solution.py:26
  7.8 1.4 fusion.2
  9.2 2.5 %fusion.3 = bf16[256,1536]{1,0:T(8,128)(2,1)} fusion(bf16[256,1536]{1,0:T(8,128)(2,1)} %param.10, f32[256]{0:T(256)S(1)} %add_sqrt_fusion), kind=kLoop, calls=%fused_computation.11 | loop fusion | flops 1179648 | bytes 1573888 | tf_op jit(solution)/shard_map/convert_element_type | solution.py:132
  12.6 0.9 fusion.85
  13.5 1.6 collective-permute-start.4
  15.1 1.5 multiply_reduce_fusion.1
  17.1 1.1 divide_convert_fusion
  18.2 0.9 fusion.84
  19.1 1.2 collective-permute-start.6
  20.3 0.7 pad_add_fusion
  21.1 2.9 %collective-permute-start.1 = (bf16[256,768]{1,0:T(8,128)(2,1)}, bf16[256,768]{1,0:T(8,128)(2,1)S(1)}, u32[]{:S(2)}, u32[]{:S(2)}) collective-permute-start(bf16[256,768]{1,0:T(8,128)(2,1)} %fusion.84), channel_id=1, source_target_pairs={{0,1},{1,0},{2,3},{3,2},{4,5},{5,4},{6,7},{7,6},{8,9},{9,8},{10,11... | collective-permute-start | bytes 1179656 | tf_op jit(solution)/shard_map/ppermute | solution.py:26
  24.0 0.7 broadcast_select_fusion.9
  24.7 18.2 %collective-permute-done.4 = bf16[256,768]{1,0:T(8,128)(2,1)} collective-permute-done((bf16[256,768]{1,0:T(8,128)(2,1)}, bf16[256,768]{1,0:T(8,128)(2,1)}, u32[]{:S(2)}, u32[]{:S(2)}) %collective-permute-start.4) | collective-permute-done | bytes 393248 | tf_op jit(solution)/shard_map/ppermute | solution.py:30
  42.9 1.2 broadcast_select_fusion.5
  44.2 0.9 collective-permute-start.7
  45.1 1.6 broadcast_select_fusion
  46.7 18.9 %collective-permute-done.2 = bf16[256,1536]{1,0:T(8,128)(2,1)S(1)} collective-permute-done((bf16[256,1536]{1,0:T(8,128)(2,1)}, bf16[256,1536]{1,0:T(8,128)(2,1)S(1)}, u32[]{:S(2)}, u32[]{:S(2)}) %collective-permute-start.2) | collective-permute-done | bytes 786464 | tf_op jit(solution)/shard_map/ppermute | solution.py:26
  65.6 1.8 fusion.57
  67.4 0.9 collective-permute-start.8
  68.3 1.8 fusion.50
  70.1 10.2 %collective-permute-done.1 = bf16[256,768]{1,0:T(8,128)(2,1)S(1)} collective-permute-done((bf16[256,768]{1,0:T(8,128)(2,1)}, bf16[256,768]{1,0:T(8,128)(2,1)S(1)}, u32[]{:S(2)}, u32[]{:S(2)}) %collective-permute-start.1) | collective-permute-done | bytes 393248 | tf_op jit(solution)/shard_map/ppermute | solution.py:26
  80.3 1.4 fusion.67
  81.7 1.4 fusion.66
  83.2 1.4 fusion.86
  84.5 1.4 fusion.87
  85.9 0.6 fusion.43
  88.0 0.7 fusion.36
  90.5 3.7 %collective-permute-start.13 = (bf16[256,768]{1,0:T(8,128)(2,1)S(1)}, bf16[256,768]{1,0:T(8,128)(2,1)S(1)}, u32[]{:S(2)}, u32[]{:S(2)}) collective-permute-start(bf16[256,768]{1,0:T(8,128)(2,1)S(1)} %slice.86), channel_id=1, source_target_pairs={{0,1},{1,0},{2,3},{3,2},{4,5},{5,4},{6,7},{7,6},{8,9},{9,8},{10,11... | collective-permute-start | bytes 1179656 | tf_op jit(solution)/shard_map/ppermute | solution.py:26
  95.1 8.5 %collective-permute-done.13 = bf16[256,768]{1,0:T(8,128)(2,1)S(1)} collective-permute-done((bf16[256,768]{1,0:T(8,128)(2,1)S(1)}, bf16[256,768]{1,0:T(8,128)(2,1)S(1)}, u32[]{:S(2)}, u32[]{:S(2)}) %collective-permute-start.13) | collective-permute-done | bytes 393248 | tf_op jit(solution)/shard_map/ppermute | solution.py:26
  103.9 1.1 collective-permute-done.15
  106.3 1.2 collective-permute-start.18
  107.8 1.0 collective-permute-done.18
  108.8 0.8 fusion.73
  109.7 1.5 abs_reduce_fusion
  112.3 18.9 %all_to_all.20 = f16[4,200,768]{2,1,0:T(8,128)(2,1)S(1)} all-to-all(f16[4,200,768]{2,1,0:T(8,128)(2,1)S(1)} %concatenate.33), channel_id=1, replica_groups=mesh['yl'=2,'z'=8,'x'=4,'core'=2,'yh'=2] {'x'}, dimensions={0} | all-to-all | bytes 2457600 | tf_op jit(solution)/shard_map/all_to_all | solution.py:81
  131.2 0.6 fusion.81
  133.1 16.5 %all_to_all.21 = f16[8,32,768]{2,1,0:T(8,128)(2,1)S(1)} all-to-all(f16[8,32,768]{2,1,0:T(8,128)(2,1)S(1)} %concatenate.34), channel_id=1, replica_groups=mesh['yl'=2,'z'=8,'x'=4,'core'=2,'yh'=2] {'z'}, dimensions={0} | all-to-all | bytes 786432 | tf_op jit(solution)/shard_map/all_to_all | solution.py:85
  149.5 0.6 fusion.80
  150.3 0.7 concatenate.35
  151.5 3.2 %collective-permute-start.20 = (f32[32,768]{1,0:T(8,128)S(1)}, f32[32,768]{1,0:T(8,128)S(1)}, u32[]{:S(2)}, u32[]{:S(2)}) collective-permute-start(f32[32,768]{1,0:T(8,128)S(1)} %concatenate.35), channel_id=1, source_target_pairs={{0,1},{1,0},{2,3},{3,2},{4,5},{5,4},{6,7},{7,6},{8,9},{9,8},{10,11... | collective-permute-start | bytes 294920 | tf_op jit(solution)/shard_map/ppermute | solution.py:26
  155.4 2.3 %collective-permute-done.20 = f32[32,768]{1,0:T(8,128)S(1)} collective-permute-done((f32[32,768]{1,0:T(8,128)S(1)}, f32[32,768]{1,0:T(8,128)S(1)}, u32[]{:S(2)}, u32[]{:S(2)}) %collective-permute-start.20) | collective-permute-done | bytes 98336 | tf_op jit(solution)/shard_map/ppermute | solution.py:26
  161.4 0.7 fusion.79
  162.1 13.7 %all_to_all.22 = f16[8,24,768]{2,1,0:T(8,128)(2,1)S(1)} all-to-all(f16[8,24,768]{2,1,0:T(8,128)(2,1)S(1)} %broadcast_in_dim.8), channel_id=1, replica_groups=mesh['yl'=2,'z'=8,'x'=4,'core'=2,'yh'=2] {'z'}, dimensions={0} | all-to-all | bytes 589824 | tf_op jit(solution)/shard_map/all_to_all | solution.py:97
  175.8 15.1 %all_to_all.23 = f16[4,192,768]{2,1,0:T(8,128)(2,1)S(1)} all-to-all(f16[4,192,768]{2,1,0:T(8,128)(2,1)S(1)} %broadcast_in_dim.10), channel_id=1, replica_groups=mesh['yl'=2,'z'=8,'x'=4,'core'=2,'yh'=2] {'x'}, dimensions={0} | all-to-all | bytes 2359296 | tf_op jit(solution)/shard_map/all_to_all | solution.py:99
  190.9 4.7 %collective-permute-start.22 = (f16[768,768]{1,0:T(8,128)(2,1)S(1)}, f16[768,768]{1,0:T(8,128)(2,1)S(1)}, u32[]{:S(2)}, u32[]{:S(2)}) collective-permute-start(f16[768,768]{1,0:T(8,128)(2,1)S(1)} %bitcast.36), channel_id=1, source_target_pairs={{0,2},{2,0},{1,3},{3,1},{4,6},{6,4},{5,7},{7,5},{8,10},{10,8},{9,1... | collective-permute-start | bytes 3538952 | tf_op jit(solution)/shard_map/ppermute | solution.py:26
  195.7 2.4 %collective-permute-done.23 = f32[8,128]{1,0:T(8,128)S(1)} collective-permute-done((f32[8,128]{1,0:T(8,128)S(1)}, f32[8,128]{1,0:T(8,128)S(1)}, u32[]{:S(2)}, u32[]{:S(2)}) %collective-permute-start.23) | collective-permute-done | bytes 4128 | tf_op jit(solution)/shard_map/ppermute | solution.py:26
  199.4 2.7 %fusion = (f32[768,768]{1,0:T(8,128)}, f32[768,768]{1,0:T(8,128)}) fusion(f16[768,768]{1,0:T(8,128)(2,1)S(1)} %collective-permute-done.22, f32[]{:T(128)} %bitcast.6, f32[]{:T(128)S(6)} %exp2.61, pred[]{:T(512)S(6)} %eq.20, f16[4,192,768]{2,1,0:T(8,128)(2,1)S(1)} %all_to_all.23), kind=kLoop, calls=%fused_computation.1 | loop fusion | flops 3538944 | bytes 7077897 | tf_op jit(solution)/shard_map/jit(_where)/select_n | solution.py:182
  (85 shorter events, 11.7 us)
Async XLA Ops:
  0.6 11.4 %copy-start = (bf16[768,768]{1,0:T(8,128)(2,1)S(1)}, bf16[768,768]{1,0:T(8,128)(2,1)}, u32[]{:S(2)}) copy-start(bf16[768,768]{1,0:T(8,128)(2,1)} %param.14) | copy-start | bytes 3538948
  0.6 11.4 %copy-start.2 = (bf16[256,768]{1,0:T(8,128)(2,1)S(1)}, bf16[256,768]{1,0:T(8,128)(2,1)}, u32[]{:S(2)}) copy-start(bf16[256,768]{1,0:T(8,128)(2,1)} %param.12) | copy-start | bytes 1179652
  0.7 20.3 %collective-permute-start.10 = (s32[256]{0:T(256)}, s32[256]{0:T(256)}, u32[]{:S(2)}, u32[]{:S(2)}) collective-permute-start(s32[256]{0:T(256)} %param.15), channel_id=1, source_target_pairs={{0,6},{2,8},{4,10},{6,12},{8,14},{10,16},{12,18},{14,20},{16,22},{... | collective-permute-start | bytes 3080 | tf_op jit(solution)/shard_map/ppermute | solution.py:30
  4.9 16.3 %collective-permute-start.9 = (s32[256]{0:T(256)}, s32[256]{0:T(256)}, u32[]{:S(2)}, u32[]{:S(2)}) collective-permute-start(s32[256]{0:T(256)} %param.15), channel_id=1, source_target_pairs={{0,2},{2,4},{4,6},{6,8},{8,10},{10,12},{12,14},{14,16},{16,18},{18... | collective-permute-start | bytes 3080 | tf_op jit(solution)/shard_map/ppermute | solution.py:30
  4.9 14.2 %collective-permute-start.3 = (s32[256]{0:T(256)}, s32[256]{0:T(256)}, u32[]{:S(2)}, u32[]{:S(2)}) collective-permute-start(s32[256]{0:T(256)} %param.15), channel_id=1, source_target_pairs={{0,1},{1,0},{2,3},{3,2},{4,5},{5,4},{6,7},{7,6},{8,9},{9,8},{10,11... | collective-permute-start | bytes 3080 | tf_op jit(solution)/shard_map/ppermute | solution.py:26
  7.8 7.3 %copy-start.11 = (bf16[256,1536]{1,0:T(8,128)(2,1)S(1)}, bf16[256,1536]{1,0:T(8,128)(2,1)}, u32[]{:S(2)}) copy-start(bf16[256,1536]{1,0:T(8,128)(2,1)} %param.8) | copy-start | bytes 2359300
  9.2 5.8 %copy-start.10 = (bf16[1536,1536]{1,0:T(8,128)(2,1)S(1)}, bf16[1536,1536]{1,0:T(8,128)(2,1)}, u32[]{:S(2)}) copy-start(bf16[1536,1536]{1,0:T(8,128)(2,1)} %param.9) | copy-start | bytes 14155780
  11.7 32.5 %collective-permute-start.5 = (bf16[256,1536]{1,0:T(8,128)(2,1)}, bf16[256,1536]{1,0:T(8,128)(2,1)}, u32[]{:S(2)}, u32[]{:S(2)}) collective-permute-start(bf16[256,1536]{1,0:T(8,128)(2,1)} %fusion.3), channel_id=1, source_target_pairs={{0,4},{2,6},{4,8},{6,10},{8,12},{10,14},{12,16},{14,18},{16,20},{1... | collective-permute-start | bytes 2359304 | tf_op jit(solution)/shard_map/ppermute | solution.py:30
  13.5 3.1 %copy-start.4 = (bf16[256,768]{1,0:T(8,128)(2,1)S(1)}, bf16[256,768]{1,0:T(8,128)(2,1)}, u32[]{:S(2)}) copy-start(bf16[256,768]{1,0:T(8,128)(2,1)} %param.11) | copy-start | bytes 1179652
  13.5 3.1 %copy-start.6 = (bf16[768,768]{1,0:T(8,128)(2,1)S(1)}, bf16[768,768]{1,0:T(8,128)(2,1)}, u32[]{:S(2)}) copy-start(bf16[768,768]{1,0:T(8,128)(2,1)} %param.13) | copy-start | bytes 3538948
  13.5 29.5 %collective-permute-start.4 = (bf16[256,768]{1,0:T(8,128)(2,1)}, bf16[256,768]{1,0:T(8,128)(2,1)}, u32[]{:S(2)}, u32[]{:S(2)}) collective-permute-start(bf16[256,768]{1,0:T(8,128)(2,1)} %fusion.85), channel_id=1, source_target_pairs={{0,4},{2,6},{4,8},{6,10},{8,12},{10,14},{12,16},{14,18},{16,20},{1... | collective-permute-start | bytes 1179656 | tf_op jit(solution)/shard_map/ppermute | solution.py:30
  17.1 2.0 copy-start.9
  18.2 26.9 %copy-start.1 = (bf16[256,1536]{1,0:T(8,128)(2,1)S(1)}, bf16[256,1536]{1,0:T(8,128)(2,1)}, u32[]{:S(2)}) copy-start(bf16[256,1536]{1,0:T(8,128)(2,1)} %param.10) | copy-start | bytes 2359300
  19.1 48.3 %collective-permute-start.6 = (s32[256]{0:T(256)S(1)}, s32[256]{0:T(256)S(1)}, u32[]{:S(2)}, u32[]{:S(2)}) collective-permute-start(s32[256]{0:T(256)S(1)} %copy-done.9), channel_id=1, source_target_pairs={{0,4},{2,6},{4,8},{6,10},{8,12},{10,14},{12,16},{14,18},{16,20},{1... | collective-permute-start | bytes 3080 | tf_op jit(solution)/shard_map/ppermute | solution.py:30
  21.0 44.6 %collective-permute-start.2 = (bf16[256,1536]{1,0:T(8,128)(2,1)}, bf16[256,1536]{1,0:T(8,128)(2,1)S(1)}, u32[]{:S(2)}, u32[]{:S(2)}) collective-permute-start(bf16[256,1536]{1,0:T(8,128)(2,1)} %divide_convert_fusion), channel_id=1, source_target_pairs={{0,1},{1,0},{2,3},{3,2},{4,5},{5,4},{6,7},{7,6},{8,9},{9,8},{10,11... | collective-permute-start | bytes 2359304 | tf_op jit(solution)/shard_map/ppermute | solution.py:26
  21.1 59.1 %collective-permute-start.1 = (bf16[256,768]{1,0:T(8,128)(2,1)}, bf16[256,768]{1,0:T(8,128)(2,1)S(1)}, u32[]{:S(2)}, u32[]{:S(2)}) collective-permute-start(bf16[256,768]{1,0:T(8,128)(2,1)} %fusion.84), channel_id=1, source_target_pairs={{0,1},{1,0},{2,3},{3,2},{4,5},{5,4},{6,7},{7,6},{8,9},{9,8},{10,11... | collective-permute-start | bytes 1179656 | tf_op jit(solution)/shard_map/ppermute | solution.py:26
  44.1 21.5 %copy-start.7 = (bf16[256,1536]{1,0:T(8,128)(2,1)S(1)}, bf16[256,1536]{1,0:T(8,128)(2,1)}, u32[]{:S(2)}) copy-start(bf16[256,1536]{1,0:T(8,128)(2,1)} %divide_convert_fusion) | copy-start | bytes 2359300
  44.1 44.6 %collective-permute-start.11 = (bf16[256,768]{1,0:T(8,128)(2,1)S(1)}, bf16[256,768]{1,0:T(8,128)(2,1)S(1)}, u32[]{:S(2)}, u32[]{:S(2)}) collective-permute-start(bf16[256,768]{1,0:T(8,128)(2,1)S(1)} %broadcast_select_fusion.5), channel_id=1, source_target_pairs={{0,2},{2,4},{4,6},{6,8},{8,10},{10,12},{12,14},{14,16},{16,18},{18... | collective-permute-start | bytes 1179656 | tf_op jit(solution)/shard_map/ppermute | solution.py:30
  44.2 42.3 %collective-permute-start.7 = (bf16[256,768]{1,0:T(8,128)(2,1)}, bf16[256,768]{1,0:T(8,128)(2,1)S(1)}, u32[]{:S(2)}, u32[]{:S(2)}) collective-permute-start(bf16[256,768]{1,0:T(8,128)(2,1)} %collective-permute-done.4), channel_id=1, source_target_pairs={{0,2},{2,0},{1,3},{3,1},{4,6},{6,4},{5,7},{7,5},{8,10},{10,8},{9,1... | collective-permute-start | bytes 1179656 | tf_op jit(solution)/shard_map/ppermute | solution.py:26
  65.6 22.4 %collective-permute-start.12 = (bf16[256,1536]{1,0:T(8,128)(2,1)S(1)}, bf16[256,1536]{1,0:T(8,128)(2,1)S(1)}, u32[]{:S(2)}, u32[]{:S(2)}) collective-permute-start(bf16[256,1536]{1,0:T(8,128)(2,1)S(1)} %broadcast_select_fusion), channel_id=1, source_target_pairs={{0,2},{2,4},{4,6},{6,8},{8,10},{10,12},{12,14},{14,16},{16,18},{18... | collective-permute-start | bytes 2359304 | tf_op jit(solution)/shard_map/ppermute | solution.py:30
  67.4 12.9 %copy-start.8 = (bf16[256,768]{1,0:T(8,128)(2,1)S(1)}, bf16[256,768]{1,0:T(8,128)(2,1)}, u32[]{:S(2)}) copy-start(bf16[256,768]{1,0:T(8,128)(2,1)} %fusion.84) | copy-start | bytes 1179652
  67.4 18.5 %collective-permute-start.8 = (bf16[256,1536]{1,0:T(8,128)(2,1)}, bf16[256,1536]{1,0:T(8,128)(2,1)S(1)}, u32[]{:S(2)}, u32[]{:S(2)}) collective-permute-start(bf16[256,1536]{1,0:T(8,128)(2,1)} %collective-permute-done.5), channel_id=1, source_target_pairs={{0,2},{2,0},{1,3},{3,1},{4,6},{6,4},{5,7},{7,5},{8,10},{10,8},{9,1... | collective-permute-start | bytes 2359304 | tf_op jit(solution)/shard_map/ppermute | solution.py:26
  87.4 6.8 %collective-permute-start.14 = (bf16[256,768]{1,0:T(8,128)(2,1)S(1)}, bf16[256,768]{1,0:T(8,128)(2,1)S(1)}, u32[]{:S(2)}, u32[]{:S(2)}) collective-permute-start(bf16[256,768]{1,0:T(8,128)(2,1)S(1)} %fusion.8), channel_id=1, source_target_pairs={{0,2},{2,0},{1,3},{3,1},{4,6},{6,4},{5,7},{7,5},{8,10},{10,8},{9,1... | collective-permute-start | bytes 1179656 | tf_op jit(solution)/shard_map/ppermute | solution.py:26
  89.5 14.4 %collective-permute-start.16 = (bf16[256,768]{1,0:T(8,128)(2,1)S(1)}, bf16[256,768]{1,0:T(8,128)(2,1)S(1)}, u32[]{:S(2)}, u32[]{:S(2)}) collective-permute-start(bf16[256,768]{1,0:T(8,128)(2,1)S(1)} %fusion.9), channel_id=1, source_target_pairs={{0,250},{2,0},{4,254},{6,4},{8,2},{10,8},{12,6},{14,12},{16,10},{1... | collective-permute-start | bytes 1179656 | tf_op jit(solution)/shard_map/ppermute | solution.py:30
  90.4 4.3 %copy-start.3 = (bf16[256,768]{1,0:T(8,128)(2,1)S(1)}, bf16[256,768]{1,0:T(8,128)(2,1)}, u32[]{:S(2)}) copy-start(bf16[256,768]{1,0:T(8,128)(2,1)} %param.12) | copy-start | bytes 1179652
  90.4 4.3 %copy-start.5 = (bf16[256,768]{1,0:T(8,128)(2,1)S(1)}, bf16[256,768]{1,0:T(8,128)(2,1)}, u32[]{:S(2)}) copy-start(bf16[256,768]{1,0:T(8,128)(2,1)} %param.11) | copy-start | bytes 1179652
  90.5 13.2 %collective-permute-start.13 = (bf16[256,768]{1,0:T(8,128)(2,1)S(1)}, bf16[256,768]{1,0:T(8,128)(2,1)S(1)}, u32[]{:S(2)}, u32[]{:S(2)}) collective-permute-start(bf16[256,768]{1,0:T(8,128)(2,1)S(1)} %slice.86), channel_id=1, source_target_pairs={{0,1},{1,0},{2,3},{3,2},{4,5},{5,4},{6,7},{7,6},{8,9},{9,8},{10,11... | collective-permute-start | bytes 1179656 | tf_op jit(solution)/shard_map/ppermute | solution.py:26
  94.6 10.5 %collective-permute-start.15 = (bf16[256,768]{1,0:T(8,128)(2,1)S(1)}, bf16[256,768]{1,0:T(8,128)(2,1)S(1)}, u32[]{:S(2)}, u32[]{:S(2)}) collective-permute-start(bf16[256,768]{1,0:T(8,128)(2,1)S(1)} %fusion.7), channel_id=1, source_target_pairs={{0,252},{2,254},{4,0},{6,2},{8,4},{10,6},{12,8},{14,10},{16,12},{1... | collective-permute-start | bytes 1179656 | tf_op jit(solution)/shard_map/ppermute | solution.py:30
  94.8 13.0 %collective-permute-start = (bf16[256,768]{1,0:T(8,128)(2,1)S(1)}, bf16[256,768]{1,0:T(8,128)(2,1)S(1)}, u32[]{:S(2)}, u32[]{:S(2)}) collective-permute-start(bf16[256,768]{1,0:T(8,128)(2,1)S(1)} %get-tuple-element.15), channel_id=1, source_target_pairs={{0,2},{2,0},{1,3},{3,1},{4,6},{6,4},{5,7},{7,5},{8,10},{10,8},{9,1... | collective-permute-start | bytes 1179656 | tf_op jit(solution)/shard_map/ppermute | solution.py:26
  106.3 2.6 %collective-permute-start.18 = (bf16[256,768]{1,0:T(8,128)(2,1)S(1)}, bf16[256,768]{1,0:T(8,128)(2,1)S(1)}, u32[]{:S(2)}, u32[]{:S(2)}) collective-permute-start(bf16[256,768]{1,0:T(8,128)(2,1)S(1)} %get-tuple-element.13), channel_id=1, source_target_pairs={{0,2},{2,0},{1,3},{3,1},{4,6},{6,4},{5,7},{7,5},{8,10},{10,8},{9,1... | collective-permute-start | bytes 1179656 | tf_op jit(solution)/shard_map/ppermute | solution.py:26
  107.5 2.2 %collective-permute-start.17 = (bf16[256,768]{1,0:T(8,128)(2,1)S(1)}, bf16[256,768]{1,0:T(8,128)(2,1)S(1)}, u32[]{:S(2)}, u32[]{:S(2)}) collective-permute-start(bf16[256,768]{1,0:T(8,128)(2,1)S(1)} %get-tuple-element.11), channel_id=1, source_target_pairs={{0,2},{2,0},{1,3},{3,1},{4,6},{6,4},{5,7},{7,5},{8,10},{10,8},{9,1... | collective-permute-start | bytes 1179656 | tf_op jit(solution)/shard_map/ppermute | solution.py:26
  150.9 4.0 %collective-permute-start.19 = (f32[32,768]{1,0:T(8,128)S(1)}, f32[32,768]{1,0:T(8,128)S(1)}, u32[]{:S(2)}, u32[]{:S(2)}) collective-permute-start(f32[32,768]{1,0:T(8,128)S(1)} %concatenate.35), channel_id=1, source_target_pairs={{0,128},{128,0},{1,129},{129,1},{2,130},{130,2},{3,131},{131,3},{4... | collective-permute-start | bytes 294920 | tf_op jit(solution)/shard_map/ppermute | solution.py:26
  151.5 6.1 %collective-permute-start.20 = (f32[32,768]{1,0:T(8,128)S(1)}, f32[32,768]{1,0:T(8,128)S(1)}, u32[]{:S(2)}, u32[]{:S(2)}) collective-permute-start(f32[32,768]{1,0:T(8,128)S(1)} %concatenate.35), channel_id=1, source_target_pairs={{0,1},{1,0},{2,3},{3,2},{4,5},{5,4},{6,7},{7,6},{8,9},{9,8},{10,11... | collective-permute-start | bytes 294920 | tf_op jit(solution)/shard_map/ppermute | solution.py:26
  154.7 5.4 %collective-permute-start.21 = (f32[32,768]{1,0:T(8,128)S(1)}, f32[32,768]{1,0:T(8,128)S(1)}, u32[]{:S(2)}, u32[]{:S(2)}) collective-permute-start(f32[32,768]{1,0:T(8,128)S(1)} %concatenate.35), channel_id=1, source_target_pairs={{0,129},{1,128},{128,1},{129,0},{2,131},{3,130},{130,3},{131,2},{4... | collective-permute-start | bytes 294920 | tf_op jit(solution)/shard_map/ppermute | solution.py:90
  190.9 8.4 %collective-permute-start.22 = (f16[768,768]{1,0:T(8,128)(2,1)S(1)}, f16[768,768]{1,0:T(8,128)(2,1)S(1)}, u32[]{:S(2)}, u32[]{:S(2)}) collective-permute-start(f16[768,768]{1,0:T(8,128)(2,1)S(1)} %bitcast.36), channel_id=1, source_target_pairs={{0,2},{2,0},{1,3},{3,1},{4,6},{6,4},{5,7},{7,5},{8,10},{10,8},{9,1... | collective-permute-start | bytes 3538952 | tf_op jit(solution)/shard_map/ppermute | solution.py:26
  195.7 2.5 %collective-permute-start.23 = (f32[8,128]{1,0:T(8,128)S(1)}, f32[8,128]{1,0:T(8,128)S(1)}, u32[]{:S(2)}, u32[]{:S(2)}) collective-permute-start(f32[8,128]{1,0:T(8,128)S(1)} %broadcast_in_dim.11), channel_id=1, source_target_pairs={{0,2},{2,0},{1,3},{3,1},{4,6},{6,4},{5,7},{7,5},{8,10},{10,8},{9,1... | collective-permute-start | bytes 12296 | tf_op jit(solution)/shard_map/ppermute | solution.py:26

commit v3 on v2

--- a/solution.py
+++ b/solution.py
@@ -34,11 +34,14 @@
     return along_dp(block, [(i, (i + 2 * step) % N_DP) for i in range(N_DP)])
 
 
-def pair_tile(target_rows, image_rows, row_ids, target_cols, text_cols, col_ids):
-    teacher_dot = lax.dot_general(
-        target_rows, target_cols, (((1,), (1,)), ((), ())), preferred_element_type=f32
-    )
-    labels = (row_ids[:, None] == col_ids[None, :]).astype(f32)
+def pair_tile(teach_rows, image_rows, row_ids, teach_cols, text_cols, notes):
+    teacher_dot = (
+        lax.dot_general(
+            teach_rows, teach_cols, (((1,), (1,)), ((), ())), preferred_element_type=f32
+        )
+        * notes[1:2, :]
+    )
+    labels = (row_ids == notes[0:1, :]).astype(f32)
     target = 0.5 * jax.nn.sigmoid(scale * teacher_dot + shift) + 0.5 * labels
     logits = (
         scale
@@ -64,34 +67,37 @@
 
 def packed(values, exponent):
     scaled = (values * jnp.exp2(-exponent)).astype(f16)
-    note = jnp.full((values.shape[0], 8, values.shape[2]), exponent, f32).astype(f16)
+    shape = (values.shape[0], 8, values.shape[2])
+    note = jnp.broadcast_to(exponent.astype(f16), shape)
     return jnp.concatenate([scaled, note], axis=1)
 
 
 def unpacked_sum(blocks):
-    exponents = blocks[:, -8, 0].astype(f32)
-    scales = jnp.exp2(exponents)[:, None, None]
-    return (blocks[:, :-8].astype(f32) * scales).sum(axis=0), exponents.max()
+    exponents = blocks[:, -8:-7, :].astype(f32)
+    summed = (blocks[:, :-8].astype(f32) * jnp.exp2(exponents)).sum(axis=0)
+    return summed, exponents.max(axis=0)
 
 
 def sum_everywhere(part):
     ds = part.shape[0]
     biggest = jnp.log2(jnp.maximum(jnp.max(jnp.abs(part)), 1e-30))
     exponent = jnp.clip(jnp.ceil(biggest) - 14.0, -110.0, 110.0)
-    blocks = lax.all_to_all(packed(part.reshape(4, ds // 4, ds), exponent), "x", 0, 0, tiled=True)
+    blocks = packed(part.reshape(4, ds // 4, ds), exponent)
+    blocks = lax.all_to_all(blocks, "x", 0, 0, tiled=True)
     summed, exponent = unpacked_sum(blocks)
     exponent = exponent + 2.0
     blocks = packed(summed.reshape(8, ds // 32, ds), exponent)
     blocks = lax.all_to_all(blocks, "z", 0, 0, tiled=True)
     summed, exponent = unpacked_sum(blocks)
-    noted = jnp.concatenate([summed, jnp.full((8, ds), exponent, f32)], axis=0)
+    noted = jnp.concatenate([summed, jnp.broadcast_to(exponent, (8, ds))], axis=0)
     other_l = swap(noted, "yl")
     other_h = swap(noted, "yh")
     other_b = lax.ppermute(noted, ("yl", "yh"), [(0, 3), (1, 2), (2, 1), (3, 0)])
     summed = ((noted + other_l) + (other_h + other_b))[:-8]
-    exponent = jnp.maximum(exponent, jnp.maximum(other_l[-8, 0], other_h[-8, 0]))
-    exponent = jnp.maximum(exponent, other_b[-8, 0]) + 5.0
-    other_e = swap(jnp.full((8, 128), exponent, f32), "core")[0, 0]
+    exponent = jnp.maximum(
+        jnp.maximum(noted, other_l), jnp.maximum(other_h, other_b)
+    )[-8:-7] + 5.0
+    other_e = swap(jnp.broadcast_to(exponent, (8, ds)), "core")[0:1]
     block = (summed * jnp.exp2(-exponent)).astype(f16)
     spread = jnp.broadcast_to(block[None], (8,) + block.shape)
     gathered = lax.all_to_all(spread, "z", 0, 0, tiled=True).reshape(ds // 4, ds)
@@ -115,45 +121,54 @@
     back_route = [(i, i - 1 if i % 2 else (i - 3) % N_DP) for i in range(N_DP)]
     step_route = [(i, (i + 1) % N_DP) for i in range(N_DP)]
 
-    ids_y = swap(class_ids, "yh")
-    ids1 = along_dp(class_ids, step_route)
-    ids2 = along_dp(class_ids, [(i, (i + 2) % N_DP) for i in range(N_DP)])
-    ids3 = along_dp(class_ids, [(i, (i + 3) % N_DP) for i in range(N_DP)])
-
+    teach_recv = chip_shift(teacher_text, 1)
+    teach_y = swap(teacher_image, "yh")
     text_unit, text_len = unit_rows(jnp.dot(text_feats, text_proj, preferred_element_type=f32))
     text_emb = text_unit.astype(bf16)
     text_recv = chip_shift(text_emb, 1)
+    image_first, _ = lax.optimization_barrier((image_feats, text_emb))
     image_unit, image_len = unit_rows(
-        jnp.dot(image_feats, image_proj, preferred_element_type=f32)
+        jnp.dot(image_first, image_proj, preferred_element_type=f32)
     )
     image_emb = image_unit.astype(bf16)
     image_y = swap(image_emb, "yh")
-    written_unit, _ = unit_rows(teacher_text.astype(f32))
-    teacher_txt = written_unit.astype(bf16)
-    teach_recv = chip_shift(teacher_txt, 1)
-    teacher_unit, _ = unit_rows(jnp.dot(teacher_image, teacher_proj, preferred_element_type=f32))
-    teacher_img = teacher_unit.astype(bf16)
-    teach_y = swap(teacher_img, "yh")
+    class_ids, teacher_later, text_later, _ = lax.optimization_barrier(
+        (class_ids, teacher_image, teacher_text, image_emb)
+    )
+    wide = text_later.astype(f32)
+    inverse = 1.0 / jnp.sqrt(jnp.sum(wide * wide, axis=1) + epsilon)
+    ids = class_ids.astype(f32)
+    notes = jnp.stack([ids, inverse] + [ids] * 6)
+    ids_y = swap(ids, "yh")
+    notes_recv = chip_shift(notes, 1)
+    teach_exch = swap(teach_recv, "core")
+    teach_far = along_dp(jnp.where(first, teacher_text, teach_recv), step_route)
     text_exch = swap(text_recv, "core")
     text_far = along_dp(jnp.where(first, text_emb, text_recv), step_route)
-    teach_exch = swap(teach_recv, "core")
-    teach_far = along_dp(jnp.where(first, teacher_txt, teach_recv), step_route)
+    notes_exch = swap(notes_recv, "core")
+    notes_far = along_dp(jnp.where(first, notes, notes_recv), step_route)
+
+    def teacher_rows(rows):
+        unit, _ = unit_rows(jnp.dot(rows, teacher_proj, preferred_element_type=f32))
+        return unit.astype(bf16)
+
+    teacher_img = teacher_rows(teacher_later)
+    teacher_img_y = teacher_rows(teach_y)
 
     sent_feats = jnp.where(first, text_feats, image_feats)
     kept_feats = jnp.where(first, image_feats, text_feats)
     feats_in = swap(sent_feats, "core")
 
     image_rows = jnp.concatenate([image_emb, image_y], axis=0)
-    teach_rows = jnp.concatenate([teacher_img, teach_y], axis=0)
-    row_ids = jnp.concatenate([class_ids, ids_y], axis=0)
-    row0, col0 = pair_tile(teach_rows, image_rows, row_ids, teacher_txt, text_emb, class_ids)
-    row1, col1 = pair_tile(teach_rows, image_rows, row_ids, teach_recv, text_recv, ids2)
-    ids_exch = jnp.where(first, ids1, ids3)
-    row2, col2 = pair_tile(teach_rows, image_rows, row_ids, teach_exch, text_exch, ids_exch)
+    teach_rows = jnp.concatenate([teacher_img, teacher_img_y], axis=0)
+    row_ids = jnp.concatenate([ids, ids_y], axis=0)[:, None]
+    rows = (teach_rows, image_rows, row_ids)
+    row0, col0 = pair_tile(*rows, teacher_text, text_emb, notes)
+    row1, col1 = pair_tile(*rows, teach_recv, text_recv, notes_recv)
+    row2, col2 = pair_tile(*rows, teach_exch, text_exch, notes_exch)
     both = col1 + swap(col2.astype(bf16), "core").astype(f32)
     both_back = chip_shift(both.astype(bf16), -1)
-    ids_far = jnp.where(first, ids3, ids1)
-    row3, col3 = pair_tile(teach_rows, image_rows, row_ids, teach_far, text_far, ids_far)
+    row3, col3 = pair_tile(*rows, teach_far, text_far, notes_far)
     far_back = along_dp(col3.astype(bf16), back_route)
     grad_rows = row0 + row1 + row2 + row3
     half = text_emb.shape[0]

time: 203 us -> 217 us (1.069)
  matrix products: 18.8 us -> 31.1 us
  starting transfers between devices: 30.1 us -> 40.5 us
  blocking collectives: 64.2 us -> 72.5 us
  other arithmetic: 17.2 us -> 11.2 us
  waiting for transfers between devices: 62.7 us -> 57.7 us
  between operations: 5.86 us -> 1.83 us
    all_to_all x1, blocking collectives: 16.5 us -> 25.2 us  [sum_everywhere(): blocks = lax.all_to_all(blocks, 'z', 0, 0, tiled=True)]
    ppermute x14 -> x15, starting transfers between devices: 22.4 us -> 30.9 us  [swap(): return lax.ppermute(block, axis, [(0, 1), (1, 0)])]
    ppermute x9 -> x8, waiting for transfers between devices: 19.4 us -> 13.3 us  [along_dp(): return lax.ppermute(block, DP, route)]
    dot_general x4, matrix products: 1.74 us -> 6.22 us  [pair_tile(): lax.dot_general(scaled, image_rows, (((0,), (0,)), ((), ())), preferred_e...]
    dot_general x6 -> x7, matrix products: 6.92 us -> 10.9 us  [the longest x2 6.58 us: teacher_rows(): unit, _ = unit_rows(jnp.dot(rows, teacher_proj, preferred_element_type=f32))]
    convert_element_type x2, other arithmetic: 3.54 us -> 0.45 us  [the longest x1 0.45 us: teacher_rows(): return unit.astype(bf16)]
    dot_general x4, matrix products: 3.78 us -> 6.51 us  [pair_tile(): lax.dot_general(image_rows, text_cols, (((1,), (1,)), ((), ())), preferre...]
    ppermute x9 -> x8, starting transfers between devices: 7.56 us -> 8.87 us  [along_dp(): return lax.ppermute(block, DP, route)]
  transfers between devices with their start and end apart: 24 -> 24, of which waited for: 8 -> 9; matrix products, arithmetic and copies ran while one was open for 15% -> 18% of each run, Pallas kernels for 0% -> 0%
where the time goes in v3:
time: 217 us
  blocking collectives  72.5 us (33%)
  waiting for transfers between devices  57.7 us (27%)
  starting transfers between devices  40.5 us (19%)
  matrix products  31.1 us (14%)
  other arithmetic  11.2 us (5%)
    ppermute x15, waiting for transfers between devices, swap(): return lax.ppermute(block, axis, [(0, 1), (1, 0)])  42.8 us
    ppermute x15, starting transfers between devices, swap(): return lax.ppermute(block, axis, [(0, 1), (1, 0)])  30.9 us
    all_to_all x1, blocking collectives, sum_everywhere(): blocks = lax.all_to_all(blocks, 'z', 0, 0, tiled=True)  25.2 us
    all_to_all x1, blocking collectives, sum_everywhere(): blocks = lax.all_to_all(blocks, 'x', 0, 0, tiled=True)  18.9 us
    all_to_all x1, blocking collectives, sum_everywhere(): own_total = lax.all_to_all(spread, 'x', 0, 0, tiled=True).reshape(ds, ds)  14.5 us
    all_to_all x1, blocking collectives, sum_everywhere(): lax.all_to_all(spread, 'z', 0, 0, tiled=True).reshape(ds // 4, ds)  13.9 us
    ppermute x8, waiting for transfers between devices, along_dp(): return lax.ppermute(block, DP, route)  13.3 us
    ppermute x8, starting transfers between devices, along_dp(): return lax.ppermute(block, DP, route)  8.87 us
  transfers between devices with their start and end apart: 24, of which 9 were waited for; matrix products, arithmetic and copies ran while one was open for 18% of the time, Pallas kernels for 0%

profile of v3, /device:TPU:1, one launch (start us, length us, event | category | flops | bytes accessed | tf_op | source)
XLA Modules:
  0.0 216.5 jit_solution(7554469752142735222)
XLA Ops:
  0.7 3.8 %collective-permute-start.2 = (bf16[256,1536]{1,0:T(8,128)(2,1)}, bf16[256,1536]{1,0:T(8,128)(2,1)}, u32[]{:S(2)}, u32[]{:S(2)}) collective-permute-start(bf16[256,1536]{1,0:T(8,128)(2,1)} %param.8), channel_id=1, source_target_pairs={{0,1},{1,0},{2,3},{3,2},{4,5},{5,4},{6,7},{7,6},{8,9},{9,8},{10,11... | collective-permute-start | bytes 2359304 | tf_op jit(solution)/shard_map/ppermute | solution.py:26
  4.5 1.2 collective-permute-start.5
  5.7 1.6 multiply_reduce_fusion.7
  7.4 0.9 fusion.94
  8.2 1.2 collective-permute-start.4
  10.0 0.9 fusion.95
  11.0 3.0 %collective-permute-start.3 = (f32[256]{0:T(256)S(1)}, f32[256]{0:T(256)}, u32[]{:S(2)}, u32[]{:S(2)}) collective-permute-start(f32[256]{0:T(256)S(1)} %convert_element_type.118), channel_id=1, source_target_pairs={{0,1},{1,0},{2,3},{3,2},{4,5},{5,4},{6,7},{7,6},{8,9},{9,8},{10,11... | collective-permute-start | bytes 3080 | tf_op jit(solution)/shard_map/ppermute | solution.py:26
  14.0 2.5 %multiply_reduce_fusion.3 = (f32[256]{0:T(256)S(1)}, f32[256,1536]{1,0:T(8,128)}) fusion(bf16[256,1536]{1,0:T(8,128)(2,1)S(1)} %copy-done.13, bf16[1536,1536]{1,0:T(8,128)(2,1)S(1)} %copy-done.12), kind=kOutput, calls=%fused_computation.14 | convolution fusion | flops 1208745728 | bytes 7078912 | tf_op jit(solution)/shard_map/dot_general | solution.py:152
  18.6 36.1 %collective-permute-done.3 = f32[256]{0:T(256)} collective-permute-done((f32[256]{0:T(256)S(1)}, f32[256]{0:T(256)}, u32[]{:S(2)}, u32[]{:S(2)}) %collective-permute-start.3) | collective-permute-done | bytes 1056 | tf_op jit(solution)/shard_map/ppermute | solution.py:26
  55.4 6.1 %collective-permute-done.6 = f32[8,256]{1,0:T(8,128)S(1)} collective-permute-done((f32[8,256]{1,0:T(8,128)S(1)}, f32[8,256]{1,0:T(8,128)S(1)}, u32[]{:S(2)}, u32[]{:S(2)}) %collective-permute-start.6) | collective-permute-done | bytes 8224 | tf_op jit(solution)/shard_map/ppermute | solution.py:30
  61.5 3.5 %collective-permute-start.9 = (f32[8,256]{1,0:T(8,128)S(1)}, f32[8,256]{1,0:T(8,128)S(1)}, u32[]{:S(2)}, u32[]{:S(2)}) collective-permute-start(f32[8,256]{1,0:T(8,128)S(1)} %collective-permute-done.6), channel_id=1, source_target_pairs={{0,2},{2,0},{1,3},{3,1},{4,6},{6,4},{5,7},{7,5},{8,10},{10,8},{9,1... | collective-permute-start | bytes 24584 | tf_op jit(solution)/shard_map/ppermute | solution.py:26
  65.0 0.8 collective-permute-done.9
  65.8 1.2 collective-permute-done.12
  67.0 1.2 broadcast_select_fusion.5
  68.1 1.0 collective-permute-start.10
  69.1 4.7 %collective-permute-start.7 = (bf16[256,768]{1,0:T(8,128)(2,1)}, bf16[256,768]{1,0:T(8,128)(2,1)S(1)}, u32[]{:S(2)}, u32[]{:S(2)}) collective-permute-start(bf16[256,768]{1,0:T(8,128)(2,1)} %collective-permute-done.4), channel_id=1, source_target_pairs={{0,2},{2,0},{1,3},{3,1},{4,6},{6,4},{5,7},{7,5},{8,10},{10,8},{9,1... | collective-permute-start | bytes 1179656 | tf_op jit(solution)/shard_map/ppermute | solution.py:26
  73.8 4.0 %multiply_reduce_fusion.2 = (f32[256]{0:T(256)S(1)}, f32[256,1536]{1,0:T(8,128)S(1)}) fusion(bf16[256,1536]{1,0:T(8,128)(2,1)} %collective-permute-done.2, bf16[1536,1536]{1,0:T(8,128)(2,1)} %param.9), kind=kOutput, calls=%fused_computation.12 | convolution fusion | flops 1208745728 | bytes 7078912 | tf_op jit(solution)/shard_map/dot_general | solution.py:152
  77.9 1.3 broadcast_select_fusion
  81.4 1.8 fusion.51
  83.2 1.7 fusion.67
  84.9 1.7 fusion.68
  86.6 1.4 fusion.99
  88.0 1.4 fusion.100
  90.1 1.6 fusion.69
  91.6 1.5 fusion.6
  94.1 1.6 fusion.70
  95.7 1.5 fusion.7
  97.2 1.5 collective-permute-start.16
  99.6 3.0 %collective-permute-start.13 = (bf16[256,768]{1,0:T(8,128)(2,1)S(1)}, bf16[256,768]{1,0:T(8,128)(2,1)S(1)}, u32[]{:S(2)}, u32[]{:S(2)}) collective-permute-start(bf16[256,768]{1,0:T(8,128)(2,1)S(1)} %slice.148), channel_id=1, source_target_pairs={{0,1},{1,0},{2,3},{3,2},{4,5},{5,4},{6,7},{7,6},{8,9},{9,8},{10,11... | collective-permute-start | bytes 1179656 | tf_op jit(solution)/shard_map/ppermute | solution.py:26
  102.6 1.5 fusion.5
  104.1 3.9 %collective-permute-start.15 = (bf16[256,768]{1,0:T(8,128)(2,1)S(1)}, bf16[256,768]{1,0:T(8,128)(2,1)S(1)}, u32[]{:S(2)}, u32[]{:S(2)}) collective-permute-start(bf16[256,768]{1,0:T(8,128)(2,1)S(1)} %fusion.5), channel_id=1, source_target_pairs={{0,252},{2,254},{4,0},{6,2},{8,4},{10,6},{12,8},{14,10},{16,12},{1... | collective-permute-start | bytes 1179656 | tf_op jit(solution)/shard_map/ppermute | solution.py:30
  108.0 1.2 collective-permute-start
  109.5 6.1 %collective-permute-done.15 = bf16[256,768]{1,0:T(8,128)(2,1)S(1)} collective-permute-done((bf16[256,768]{1,0:T(8,128)(2,1)S(1)}, bf16[256,768]{1,0:T(8,128)(2,1)S(1)}, u32[]{:S(2)}, u32[]{:S(2)}) %collective-permute-start.15) | collective-permute-done | bytes 393248 | tf_op jit(solution)/shard_map/ppermute | solution.py:30
  115.6 1.7 multiply_reduce_fusion.4
  117.9 1.8 collective-permute-start.18
  120.0 1.0 collective-permute-done.18
  121.1 0.8 fusion.74
  121.9 1.5 abs_reduce_fusion
  124.6 18.9 %all_to_all.20 = f16[4,200,768]{2,1,0:T(8,128)(2,1)S(1)} all-to-all(f16[4,200,768]{2,1,0:T(8,128)(2,1)S(1)} %concatenate.33), channel_id=1, replica_groups=mesh['yl'=2,'z'=8,'x'=4,'core'=2,'yh'=2] {'x'}, dimensions={0} | all-to-all | bytes 2457600 | tf_op jit(solution)/shard_map/all_to_all | solution.py:86
  144.0 25.2 %all_to_all.21 = f16[8,32,768]{2,1,0:T(8,128)(2,1)S(1)} all-to-all(f16[8,32,768]{2,1,0:T(8,128)(2,1)S(1)} %pad_maximum_fusion.5), channel_id=1, replica_groups=mesh['yl'=2,'z'=8,'x'=4,'core'=2,'yh'=2] {'z'}, dimensions={0} | all-to-all | bytes 786432 | tf_op jit(solution)/shard_map/all_to_all | solution.py:90
  169.5 3.0 %collective-permute-start.20 = (f32[32,768]{1,0:T(8,128)S(1)}, f32[32,768]{1,0:T(8,128)S(1)}, u32[]{:S(2)}, u32[]{:S(2)}) collective-permute-start(f32[32,768]{1,0:T(8,128)S(1)} %pad_maximum_fusion.6), channel_id=1, source_target_pairs={{0,1},{1,0},{2,3},{3,2},{4,5},{5,4},{6,7},{7,6},{8,9},{9,8},{10,11... | collective-permute-start | bytes 294920 | tf_op jit(solution)/shard_map/ppermute | solution.py:26
  173.3 2.3 %collective-permute-done.20 = f32[32,768]{1,0:T(8,128)S(1)} collective-permute-done((f32[32,768]{1,0:T(8,128)S(1)}, f32[32,768]{1,0:T(8,128)S(1)}, u32[]{:S(2)}, u32[]{:S(2)}) %collective-permute-start.20) | collective-permute-done | bytes 98336 | tf_op jit(solution)/shard_map/ppermute | solution.py:26
  175.6 1.6 collective-permute-done.21
  177.3 13.9 %all_to_all.22 = f16[8,24,768]{2,1,0:T(8,128)(2,1)S(1)} all-to-all(f16[8,24,768]{2,1,0:T(8,128)(2,1)S(1)} %broadcast_in_dim.16), channel_id=1, replica_groups=mesh['yl'=2,'z'=8,'x'=4,'core'=2,'yh'=2] {'z'}, dimensions={0} | all-to-all | bytes 589824 | tf_op jit(solution)/shard_map/all_to_all | solution.py:103
  191.3 14.5 %all_to_all.23 = f16[4,192,768]{2,1,0:T(8,128)(2,1)S(1)} all-to-all(f16[4,192,768]{2,1,0:T(8,128)(2,1)S(1)} %broadcast_in_dim.18), channel_id=1, replica_groups=mesh['yl'=2,'z'=8,'x'=4,'core'=2,'yh'=2] {'x'}, dimensions={0} | all-to-all | bytes 2359296 | tf_op jit(solution)/shard_map/all_to_all | solution.py:105
  205.8 5.4 %collective-permute-start.22 = (f16[768,768]{1,0:T(8,128)(2,1)S(1)}, f16[768,768]{1,0:T(8,128)(2,1)S(1)}, u32[]{:S(2)}, u32[]{:S(2)}) collective-permute-start(f16[768,768]{1,0:T(8,128)(2,1)S(1)} %bitcast.47), channel_id=1, source_target_pairs={{0,2},{2,0},{1,3},{3,1},{4,6},{6,4},{5,7},{7,5},{8,10},{10,8},{9,1... | collective-permute-start | bytes 3538952 | tf_op jit(solution)/shard_map/ppermute | solution.py:26
  211.2 2.5 %collective-permute-done.23 = f32[8,768]{1,0:T(8,128)S(1)} collective-permute-done((f32[8,768]{1,0:T(8,128)S(1)}, f32[8,768]{1,0:T(8,128)S(1)}, u32[]{:S(2)}, u32[]{:S(2)}) %collective-permute-start.23) | collective-permute-done | bytes 24608 | tf_op jit(solution)/shard_map/ppermute | solution.py:26
  213.8 2.7 %fusion = (f32[768,768]{1,0:T(8,128)}, f32[768,768]{1,0:T(8,128)}) fusion(f16[768,768]{1,0:T(8,128)(2,1)S(1)} %collective-permute-done.22, f32[768]{0:T(1024)S(1)} %fusion.90, f32[768]{0:T(1024)S(1)} %get-tuple-element.10, pred[]{:T(512)S(6)} %eq.26, f16[4,192,768]{2,1,0:T(8,128)(2,1)S(1)} %all_to_all.23), kind=kLoop, calls=%fused_computation.1 | loop fusion | flops 3538944 | bytes 7084033 | tf_op jit(solution)/shard_map/jit(_where)/select_n | solution.py:197
  (98 shorter events, 11.5 us)
Async XLA Ops:
  0.6 5.1 %copy-start = (bf16[768,768]{1,0:T(8,128)(2,1)S(1)}, bf16[768,768]{1,0:T(8,128)(2,1)}, u32[]{:S(2)}) copy-start(bf16[768,768]{1,0:T(8,128)(2,1)} %param.14) | copy-start | bytes 3538948
  0.6 8.8 %copy-start.4 = (bf16[256,768]{1,0:T(8,128)(2,1)S(1)}, bf16[256,768]{1,0:T(8,128)(2,1)}, u32[]{:S(2)}) copy-start(bf16[256,768]{1,0:T(8,128)(2,1)} %param.11) | copy-start | bytes 1179652
  0.7 8.8 %copy-start.6 = (bf16[768,768]{1,0:T(8,128)(2,1)S(1)}, bf16[768,768]{1,0:T(8,128)(2,1)}, u32[]{:S(2)}) copy-start(bf16[768,768]{1,0:T(8,128)(2,1)} %param.13) | copy-start | bytes 3538948
  0.7 73.1 %collective-permute-start.2 = (bf16[256,1536]{1,0:T(8,128)(2,1)}, bf16[256,1536]{1,0:T(8,128)(2,1)}, u32[]{:S(2)}, u32[]{:S(2)}) collective-permute-start(bf16[256,1536]{1,0:T(8,128)(2,1)} %param.8), channel_id=1, source_target_pairs={{0,1},{1,0},{2,3},{3,2},{4,5},{5,4},{6,7},{7,6},{8,9},{9,8},{10,11... | collective-permute-start | bytes 2359304 | tf_op jit(solution)/shard_map/ppermute | solution.py:26
  4.5 73.4 %collective-permute-start.5 = (bf16[256,1536]{1,0:T(8,128)(2,1)}, bf16[256,1536]{1,0:T(8,128)(2,1)}, u32[]{:S(2)}, u32[]{:S(2)}) collective-permute-start(bf16[256,1536]{1,0:T(8,128)(2,1)} %param.10), channel_id=1, source_target_pairs={{0,4},{2,6},{4,8},{6,10},{8,12},{10,14},{12,16},{14,18},{16,20},{1... | collective-permute-start | bytes 2359304 | tf_op jit(solution)/shard_map/ppermute | solution.py:30
  5.7 8.3 %copy-start.13 = (bf16[256,1536]{1,0:T(8,128)(2,1)S(1)}, bf16[256,1536]{1,0:T(8,128)(2,1)}, u32[]{:S(2)}) copy-start(bf16[256,1536]{1,0:T(8,128)(2,1)} %param.8) | copy-start | bytes 2359300
  7.4 6.6 %copy-start.12 = (bf16[1536,1536]{1,0:T(8,128)(2,1)S(1)}, bf16[1536,1536]{1,0:T(8,128)(2,1)}, u32[]{:S(2)}) copy-start(bf16[1536,1536]{1,0:T(8,128)(2,1)} %param.9) | copy-start | bytes 14155780
  8.2 2.8 %copy-start.11 = (s32[256]{0:T(256)S(1)}, s32[256]{0:T(256)}, u32[]{:S(2)}) copy-start(s32[256]{0:T(256)} %param.15) | copy-start | bytes 3076
  8.2 58.7 %collective-permute-start.4 = (bf16[256,768]{1,0:T(8,128)(2,1)}, bf16[256,768]{1,0:T(8,128)(2,1)}, u32[]{:S(2)}, u32[]{:S(2)}) collective-permute-start(bf16[256,768]{1,0:T(8,128)(2,1)} %fusion.94), channel_id=1, source_target_pairs={{0,4},{2,6},{4,8},{6,10},{8,12},{10,14},{12,16},{14,18},{16,20},{1... | collective-permute-start | bytes 1179656 | tf_op jit(solution)/shard_map/ppermute | solution.py:30
  10.0 1.0 copy-start.7
  10.9 72.3 %collective-permute-start.1 = (bf16[256,768]{1,0:T(8,128)(2,1)}, bf16[256,768]{1,0:T(8,128)(2,1)}, u32[]{:S(2)}, u32[]{:S(2)}) collective-permute-start(bf16[256,768]{1,0:T(8,128)(2,1)} %fusion.95), channel_id=1, source_target_pairs={{0,1},{1,0},{2,3},{3,2},{4,5},{5,4},{6,7},{7,6},{8,9},{9,8},{10,11... | collective-permute-start | bytes 1179656 | tf_op jit(solution)/shard_map/ppermute | solution.py:26
  11.0 6.1 %copy-start.1 = (bf16[256,1536]{1,0:T(8,128)(2,1)S(1)}, bf16[256,1536]{1,0:T(8,128)(2,1)}, u32[]{:S(2)}) copy-start(bf16[256,1536]{1,0:T(8,128)(2,1)} %param.10) | copy-start | bytes 2359300
  11.0 43.7 %collective-permute-start.3 = (f32[256]{0:T(256)S(1)}, f32[256]{0:T(256)}, u32[]{:S(2)}, u32[]{:S(2)}) collective-permute-start(f32[256]{0:T(256)S(1)} %convert_element_type.118), channel_id=1, source_target_pairs={{0,1},{1,0},{2,3},{3,2},{4,5},{5,4},{6,7},{7,6},{8,9},{9,8},{10,11... | collective-permute-start | bytes 3080 | tf_op jit(solution)/shard_map/ppermute | solution.py:26
  54.7 6.7 %collective-permute-start.6 = (f32[8,256]{1,0:T(8,128)S(1)}, f32[8,256]{1,0:T(8,128)S(1)}, u32[]{:S(2)}, u32[]{:S(2)}) collective-permute-start(f32[8,256]{1,0:T(8,128)S(1)} %stack.5), channel_id=1, source_target_pairs={{0,4},{2,6},{4,8},{6,10},{8,12},{10,14},{12,16},{14,18},{16,20},{1... | collective-permute-start | bytes 24584 | tf_op jit(solution)/shard_map/ppermute | solution.py:30
  61.5 4.3 %collective-permute-start.9 = (f32[8,256]{1,0:T(8,128)S(1)}, f32[8,256]{1,0:T(8,128)S(1)}, u32[]{:S(2)}, u32[]{:S(2)}) collective-permute-start(f32[8,256]{1,0:T(8,128)S(1)} %collective-permute-done.6), channel_id=1, source_target_pairs={{0,2},{2,0},{1,3},{3,1},{4,6},{6,4},{5,7},{7,5},{8,10},{10,8},{9,1... | collective-permute-start | bytes 24584 | tf_op jit(solution)/shard_map/ppermute | solution.py:26
  65.8 1.2 collective-permute-start.12
  68.1 26.0 %collective-permute-start.10 = (bf16[256,768]{1,0:T(8,128)(2,1)S(1)}, bf16[256,768]{1,0:T(8,128)(2,1)S(1)}, u32[]{:S(2)}, u32[]{:S(2)}) collective-permute-start(bf16[256,768]{1,0:T(8,128)(2,1)S(1)} %broadcast_select_fusion.5), channel_id=1, source_target_pairs={{0,2},{2,4},{4,6},{6,8},{8,10},{10,12},{12,14},{14,16},{16,18},{18... | collective-permute-start | bytes 1179656 | tf_op jit(solution)/shard_map/ppermute | solution.py:30
  69.1 20.9 %collective-permute-start.7 = (bf16[256,768]{1,0:T(8,128)(2,1)}, bf16[256,768]{1,0:T(8,128)(2,1)S(1)}, u32[]{:S(2)}, u32[]{:S(2)}) collective-permute-start(bf16[256,768]{1,0:T(8,128)(2,1)} %collective-permute-done.4), channel_id=1, source_target_pairs={{0,2},{2,0},{1,3},{3,1},{4,6},{6,4},{5,7},{7,5},{8,10},{10,8},{9,1... | collective-permute-start | bytes 1179656 | tf_op jit(solution)/shard_map/ppermute | solution.py:26
  77.8 1.7 copy-start.2
  77.9 1.6 copy-start.10
  79.2 14.2 %collective-permute-start.11 = (bf16[256,1536]{1,0:T(8,128)(2,1)S(1)}, bf16[256,1536]{1,0:T(8,128)(2,1)S(1)}, u32[]{:S(2)}, u32[]{:S(2)}) collective-permute-start(bf16[256,1536]{1,0:T(8,128)(2,1)S(1)} %broadcast_select_fusion), channel_id=1, source_target_pairs={{0,2},{2,4},{4,6},{6,8},{8,10},{10,12},{12,14},{14,16},{16,18},{18... | collective-permute-start | bytes 2359304 | tf_op jit(solution)/shard_map/ppermute | solution.py:30
  79.5 0.7 copy-start.9
  80.8 8.6 %collective-permute-start.8 = (bf16[256,1536]{1,0:T(8,128)(2,1)}, bf16[256,1536]{1,0:T(8,128)(2,1)S(1)}, u32[]{:S(2)}, u32[]{:S(2)}) collective-permute-start(bf16[256,1536]{1,0:T(8,128)(2,1)} %collective-permute-done.5), channel_id=1, source_target_pairs={{0,2},{2,0},{1,3},{3,1},{4,6},{6,4},{5,7},{7,5},{8,10},{10,8},{9,1... | collective-permute-start | bytes 2359304 | tf_op jit(solution)/shard_map/ppermute | solution.py:26
  93.1 9.5 %collective-permute-start.14 = (bf16[256,768]{1,0:T(8,128)(2,1)S(1)}, bf16[256,768]{1,0:T(8,128)(2,1)S(1)}, u32[]{:S(2)}, u32[]{:S(2)}) collective-permute-start(bf16[256,768]{1,0:T(8,128)(2,1)S(1)} %fusion.6), channel_id=1, source_target_pairs={{0,2},{2,0},{1,3},{3,1},{4,6},{6,4},{5,7},{7,5},{8,10},{10,8},{9,1... | collective-permute-start | bytes 1179656 | tf_op jit(solution)/shard_map/ppermute | solution.py:26
  97.2 12.3 %collective-permute-start.16 = (bf16[256,768]{1,0:T(8,128)(2,1)S(1)}, bf16[256,768]{1,0:T(8,128)(2,1)S(1)}, u32[]{:S(2)}, u32[]{:S(2)}) collective-permute-start(bf16[256,768]{1,0:T(8,128)(2,1)S(1)} %fusion.7), channel_id=1, source_target_pairs={{0,250},{2,0},{4,254},{6,4},{8,2},{10,8},{12,6},{14,12},{16,10},{1... | collective-permute-start | bytes 1179656 | tf_op jit(solution)/shard_map/ppermute | solution.py:30
  99.5 8.5 %copy-start.3 = (bf16[256,768]{1,0:T(8,128)(2,1)S(1)}, bf16[256,768]{1,0:T(8,128)(2,1)}, u32[]{:S(2)}) copy-start(bf16[256,768]{1,0:T(8,128)(2,1)} %param.12) | copy-start | bytes 1179652
  99.5 8.5 %copy-start.5 = (bf16[256,768]{1,0:T(8,128)(2,1)S(1)}, bf16[256,768]{1,0:T(8,128)(2,1)}, u32[]{:S(2)}) copy-start(bf16[256,768]{1,0:T(8,128)(2,1)} %param.11) | copy-start | bytes 1179652
  99.5 9.7 %copy-start.8 = (f32[256]{0:T(256)S(1)}, f32[256]{0:T(256)}, u32[]{:S(2)}) copy-start(f32[256]{0:T(256)} %copy-done.7) | copy-start | bytes 3076
  99.6 9.7 %collective-permute-start.13 = (bf16[256,768]{1,0:T(8,128)(2,1)S(1)}, bf16[256,768]{1,0:T(8,128)(2,1)S(1)}, u32[]{:S(2)}, u32[]{:S(2)}) collective-permute-start(bf16[256,768]{1,0:T(8,128)(2,1)S(1)} %slice.148), channel_id=1, source_target_pairs={{0,1},{1,0},{2,3},{3,2},{4,5},{5,4},{6,7},{7,6},{8,9},{9,8},{10,11... | collective-permute-start | bytes 1179656 | tf_op jit(solution)/shard_map/ppermute | solution.py:26
  104.1 11.5 %collective-permute-start.15 = (bf16[256,768]{1,0:T(8,128)(2,1)S(1)}, bf16[256,768]{1,0:T(8,128)(2,1)S(1)}, u32[]{:S(2)}, u32[]{:S(2)}) collective-permute-start(bf16[256,768]{1,0:T(8,128)(2,1)S(1)} %fusion.5), channel_id=1, source_target_pairs={{0,252},{2,254},{4,0},{6,2},{8,4},{10,6},{12,8},{14,10},{16,12},{1... | collective-permute-start | bytes 1179656 | tf_op jit(solution)/shard_map/ppermute | solution.py:30
  108.0 12.0 %collective-permute-start = (bf16[256,768]{1,0:T(8,128)(2,1)S(1)}, bf16[256,768]{1,0:T(8,128)(2,1)S(1)}, u32[]{:S(2)}, u32[]{:S(2)}) collective-permute-start(bf16[256,768]{1,0:T(8,128)(2,1)S(1)} %get-tuple-element.24), channel_id=1, source_target_pairs={{0,2},{2,0},{1,3},{3,1},{4,6},{6,4},{5,7},{7,5},{8,10},{10,8},{9,1... | collective-permute-start | bytes 1179656 | tf_op jit(solution)/shard_map/ppermute | solution.py:26
  117.9 3.2 %collective-permute-start.18 = (bf16[256,768]{1,0:T(8,128)(2,1)S(1)}, bf16[256,768]{1,0:T(8,128)(2,1)S(1)}, u32[]{:S(2)}, u32[]{:S(2)}) collective-permute-start(bf16[256,768]{1,0:T(8,128)(2,1)S(1)} %get-tuple-element.20), channel_id=1, source_target_pairs={{0,2},{2,0},{1,3},{3,1},{4,6},{6,4},{5,7},{7,5},{8,10},{10,8},{9,1... | collective-permute-start | bytes 1179656 | tf_op jit(solution)/shard_map/ppermute | solution.py:26
  119.7 2.2 collective-permute-start.17
  169.3 3.9 %collective-permute-start.19 = (f32[32,768]{1,0:T(8,128)S(1)}, f32[32,768]{1,0:T(8,128)S(1)}, u32[]{:S(2)}, u32[]{:S(2)}) collective-permute-start(f32[32,768]{1,0:T(8,128)S(1)} %pad_maximum_fusion.6), channel_id=1, source_target_pairs={{0,128},{128,0},{1,129},{129,1},{2,130},{130,2},{3,131},{131,3},{4... | collective-permute-start | bytes 294920 | tf_op jit(solution)/shard_map/ppermute | solution.py:26
  169.5 6.0 %collective-permute-start.20 = (f32[32,768]{1,0:T(8,128)S(1)}, f32[32,768]{1,0:T(8,128)S(1)}, u32[]{:S(2)}, u32[]{:S(2)}) collective-permute-start(f32[32,768]{1,0:T(8,128)S(1)} %pad_maximum_fusion.6), channel_id=1, source_target_pairs={{0,1},{1,0},{2,3},{3,2},{4,5},{5,4},{6,7},{7,6},{8,9},{9,8},{10,11... | collective-permute-start | bytes 294920 | tf_op jit(solution)/shard_map/ppermute | solution.py:26
  172.5 4.7 %collective-permute-start.21 = (f32[32,768]{1,0:T(8,128)S(1)}, f32[32,768]{1,0:T(8,128)S(1)}, u32[]{:S(2)}, u32[]{:S(2)}) collective-permute-start(f32[32,768]{1,0:T(8,128)S(1)} %pad_maximum_fusion.6), channel_id=1, source_target_pairs={{0,129},{1,128},{128,1},{129,0},{2,131},{3,130},{130,3},{131,2},{4... | collective-permute-start | bytes 294920 | tf_op jit(solution)/shard_map/ppermute | solution.py:95
  205.8 8.0 %collective-permute-start.22 = (f16[768,768]{1,0:T(8,128)(2,1)S(1)}, f16[768,768]{1,0:T(8,128)(2,1)S(1)}, u32[]{:S(2)}, u32[]{:S(2)}) collective-permute-start(f16[768,768]{1,0:T(8,128)(2,1)S(1)} %bitcast.47), channel_id=1, source_target_pairs={{0,2},{2,0},{1,3},{3,1},{4,6},{6,4},{5,7},{7,5},{8,10},{10,8},{9,1... | collective-permute-start | bytes 3538952 | tf_op jit(solution)/shard_map/ppermute | solution.py:26
  211.2 2.5 %collective-permute-start.23 = (f32[8,768]{1,0:T(8,128)S(1)}, f32[8,768]{1,0:T(8,128)S(1)}, u32[]{:S(2)}, u32[]{:S(2)}) collective-permute-start(f32[8,768]{1,0:T(8,128)S(1)} %broadcast_in_dim.20), channel_id=1, source_target_pairs={{0,2},{2,0},{1,3},{3,1},{4,6},{6,4},{5,7},{7,5},{8,10},{10,8},{9,1... | collective-permute-start | bytes 73736 | tf_op jit(solution)/shard_map/ppermute | solution.py:26

commit v4 on v3

--- a/solution.py
+++ b/solution.py
@@ -34,14 +34,27 @@
     return along_dp(block, [(i, (i + 2 * step) % N_DP) for i in range(N_DP)])
 
 
-def pair_tile(teach_rows, image_rows, row_ids, teach_cols, text_cols, notes):
+def with_ids(rows, ids):
+    below = jnp.pad(ids.astype(rows.dtype)[None, :], ((0, 15), (0, rows.shape[1] - ids.shape[0])))
+    return jnp.concatenate([rows, below], axis=0)
+
+
+def without_ids(noted):
+    count = noted.shape[0] - 16
+    return noted[:count], noted[count, :count]
+
+
+def pair_tile(teach_rows, image_rows, row_ids, teach_cols, noted_cols):
+    text_cols, col_ids = without_ids(noted_cols)
+    wide = teach_cols.astype(f32)
+    inverse = 1.0 / jnp.sqrt(jnp.sum(wide * wide, axis=1) + epsilon)
     teacher_dot = (
         lax.dot_general(
             teach_rows, teach_cols, (((1,), (1,)), ((), ())), preferred_element_type=f32
         )
-        * notes[1:2, :]
-    )
-    labels = (row_ids == notes[0:1, :]).astype(f32)
+        * inverse[None, :]
+    )
+    labels = (row_ids == col_ids[None, :]).astype(f32)
     target = 0.5 * jax.nn.sigmoid(scale * teacher_dot + shift) + 0.5 * labels
     logits = (
         scale
@@ -124,29 +137,19 @@
     teach_recv = chip_shift(teacher_text, 1)
     teach_y = swap(teacher_image, "yh")
     text_unit, text_len = unit_rows(jnp.dot(text_feats, text_proj, preferred_element_type=f32))
-    text_emb = text_unit.astype(bf16)
-    text_recv = chip_shift(text_emb, 1)
-    image_first, _ = lax.optimization_barrier((image_feats, text_emb))
+    text_own = with_ids(text_unit.astype(bf16), class_ids)
+    image_first, text_own = lax.optimization_barrier((image_feats, text_own))
+    text_recv = chip_shift(text_own, 1)
     image_unit, image_len = unit_rows(
         jnp.dot(image_first, image_proj, preferred_element_type=f32)
     )
-    image_emb = image_unit.astype(bf16)
-    image_y = swap(image_emb, "yh")
-    class_ids, teacher_later, text_later, _ = lax.optimization_barrier(
-        (class_ids, teacher_image, teacher_text, image_emb)
-    )
-    wide = text_later.astype(f32)
-    inverse = 1.0 / jnp.sqrt(jnp.sum(wide * wide, axis=1) + epsilon)
-    ids = class_ids.astype(f32)
-    notes = jnp.stack([ids, inverse] + [ids] * 6)
-    ids_y = swap(ids, "yh")
-    notes_recv = chip_shift(notes, 1)
+    image_own = with_ids(image_unit.astype(bf16), class_ids)
+    teacher_later, image_own = lax.optimization_barrier((teacher_image, image_own))
+    image_y = swap(image_own, "yh")
     teach_exch = swap(teach_recv, "core")
     teach_far = along_dp(jnp.where(first, teacher_text, teach_recv), step_route)
     text_exch = swap(text_recv, "core")
-    text_far = along_dp(jnp.where(first, text_emb, text_recv), step_route)
-    notes_exch = swap(notes_recv, "core")
-    notes_far = along_dp(jnp.where(first, notes, notes_recv), step_route)
+    text_far = along_dp(jnp.where(first, text_own, text_recv), step_route)
 
     def teacher_rows(rows):
         unit, _ = unit_rows(jnp.dot(rows, teacher_proj, preferred_element_type=f32))
@@ -159,19 +162,21 @@
     kept_feats = jnp.where(first, image_feats, text_feats)
     feats_in = swap(sent_feats, "core")
 
-    image_rows = jnp.concatenate([image_emb, image_y], axis=0)
+    image_emb, ids = without_ids(image_own)
+    image_emb_y, ids_y = without_ids(image_y)
+    image_rows = jnp.concatenate([image_emb, image_emb_y], axis=0)
     teach_rows = jnp.concatenate([teacher_img, teacher_img_y], axis=0)
     row_ids = jnp.concatenate([ids, ids_y], axis=0)[:, None]
     rows = (teach_rows, image_rows, row_ids)
-    row0, col0 = pair_tile(*rows, teacher_text, text_emb, notes)
-    row1, col1 = pair_tile(*rows, teach_recv, text_recv, notes_recv)
-    row2, col2 = pair_tile(*rows, teach_exch, text_exch, notes_exch)
+    row0, col0 = pair_tile(*rows, teacher_text, text_own)
+    row1, col1 = pair_tile(*rows, teach_recv, text_recv)
+    row2, col2 = pair_tile(*rows, teach_exch, text_exch)
     both = col1 + swap(col2.astype(bf16), "core").astype(f32)
     both_back = chip_shift(both.astype(bf16), -1)
-    row3, col3 = pair_tile(*rows, teach_far, text_far, notes_far)
+    row3, col3 = pair_tile(*rows, teach_far, text_far)
     far_back = along_dp(col3.astype(bf16), back_route)
     grad_rows = row0 + row1 + row2 + row3
-    half = text_emb.shape[0]
+    half = image_emb.shape[0]
     rows_y = swap(grad_rows[half:].astype(bf16), "yh")
     grad_img = grad_rows[:half] + rows_y.astype(f32)
     grad_txt = col0 + both_back.astype(f32) + far_back.astype(f32)

time: 217 us -> 203 us (0.935)
  matrix products: 31.1 us -> 23 us
  starting transfers between devices: 40.5 us -> 32.5 us
  local copies, waits for them, and re-layouts: 1.58 us -> 6.62 us
  waiting for transfers between devices: 57.7 us -> 55.1 us
    ppermute x15 -> x13, starting transfers between devices: 30.9 us -> 23.4 us  [swap(): return lax.ppermute(block, axis, [(0, 1), (1, 0)])]
    slice x3 -> x8, local copies, waits for them, and re-layouts: 0.01 us -> 4.96 us  [without_ids(): return (noted[:count], noted[count, :count])]
    dot_general x4, matrix products: 6.22 us -> 1.76 us  [pair_tile(): lax.dot_general(scaled, image_rows, (((0,), (0,)), ((), ())), preferred_e...]
    ppermute x8 -> x6, waiting for transfers between devices: 13.3 us -> 9.42 us  [along_dp(): return lax.ppermute(block, DP, route)]
    dot_general x4, matrix products: 6.51 us -> 2.79 us  [pair_tile(): lax.dot_general(image_rows, text_cols, (((1,), (1,)), ((), ())), preferre...]
    reduce_sum x1 -> x4, other arithmetic: 0.23 us -> 3.35 us  [pair_tile(): inverse = 1.0 / jnp.sqrt(jnp.sum(wide * wide, axis=1) + epsilon)]
    ppermute x15 -> x13, waiting for transfers between devices: 42.8 us -> 44.1 us  [swap(): return lax.ppermute(block, axis, [(0, 1), (1, 0)])]
    ppermute x8 -> x6, starting transfers between devices: 8.87 us -> 8.35 us  [along_dp(): return lax.ppermute(block, DP, route)]
  transfers between devices with their start and end apart: 24 -> 20, of which waited for: 9 -> 8; matrix products, arithmetic and copies ran while one was open for 18% -> 17% of each run, Pallas kernels for 0% -> 0%
where the time goes in v4:
time: 203 us; the launch traced here: 202 us
  blocking collectives  71.3 us (35%)
  waiting for transfers between devices  55.1 us (27%)
  starting transfers between devices  32.5 us (16%)
  matrix products  23 us (11%)
  other arithmetic  11.7 us (6%)
  local copies, waits for them, and re-layouts  6.62 us (3%)
    ppermute x13, waiting for transfers between devices, swap(): return lax.ppermute(block, axis, [(0, 1), (1, 0)])  44.1 us
    all_to_all x1, blocking collectives, sum_everywhere(): blocks = lax.all_to_all(blocks, 'z', 0, 0, tiled=True)  24 us
    ppermute x13, starting transfers between devices, swap(): return lax.ppermute(block, axis, [(0, 1), (1, 0)])  23.4 us
    all_to_all x1, blocking collectives, sum_everywhere(): blocks = lax.all_to_all(blocks, 'x', 0, 0, tiled=True)  18.9 us
    all_to_all x1, blocking collectives, sum_everywhere(): own_total = lax.all_to_all(spread, 'x', 0, 0, tiled=True).reshape(ds, ds)  14.5 us
    all_to_all x1, blocking collectives, sum_everywhere(): lax.all_to_all(spread, 'z', 0, 0, tiled=True).reshape(ds // 4, ds)  13.9 us
    ppermute x6, waiting for transfers between devices, along_dp(): return lax.ppermute(block, DP, route)  9.42 us
    ppermute x6, starting transfers between devices, along_dp(): return lax.ppermute(block, DP, route)  8.35 us
  transfers between devices with their start and end apart: 20, of which 8 were waited for; matrix products, arithmetic and copies ran while one was open for 17% of the time, Pallas kernels for 0%

profile of v4, /device:TPU:1, one launch (start us, length us, event | category | flops | bytes accessed | tf_op | source)
XLA Modules:
  0.0 202.1 jit_solution(9185623261319334971)
XLA Ops:
  0.7 3.8 %collective-permute-start.2 = (bf16[256,1536]{1,0:T(8,128)(2,1)}, bf16[256,1536]{1,0:T(8,128)(2,1)}, u32[]{:S(2)}, u32[]{:S(2)}) collective-permute-start(bf16[256,1536]{1,0:T(8,128)(2,1)} %param.8), channel_id=1, source_target_pairs={{0,1},{1,0},{2,3},{3,2},{4,5},{5,4},{6,7},{7,6},{8,9},{9,8},{10,11... | collective-permute-start | bytes 2359304 | tf_op jit(solution)/shard_map/ppermute | solution.py:26
  4.5 1.6 multiply_reduce_fusion.10
  6.3 0.8 copy-done.3
  8.2 0.8 fusion.81
  8.9 1.2 collective-permute-start.1
  10.1 1.2 collective-permute-start.3
  11.3 1.2 collective-permute-start.4
  12.5 1.4 multiply_reduce_fusion.4
  13.9 2.5 %multiply_reduce_fusion.6 = (f32[256]{0:T(256)S(1)}, f32[256,1536]{1,0:T(8,128)}) fusion(bf16[256,1536]{1,0:T(8,128)(2,1)S(1)} %copy-done.8, bf16[1536,1536]{1,0:T(8,128)(2,1)S(1)} %copy-done.7), kind=kOutput, calls=%fused_computation.17 | convolution fusion | flops 1208745728 | bytes 7078912 | tf_op jit(solution)/shard_map/dot_general | solution.py:155
  16.5 0.7 slice_reduce_fusion.5
  17.2 1.8 slice.64
  19.0 8.1 %collective-permute-done.3 = bf16[272,768]{1,0:T(8,128)(2,1)} collective-permute-done((bf16[272,768]{1,0:T(8,128)(2,1)S(1)}, bf16[272,768]{1,0:T(8,128)(2,1)}, u32[]{:S(2)}, u32[]{:S(2)}) %collective-permute-start.3) | collective-permute-done | bytes 417824 | tf_op jit(solution)/shard_map/ppermute | solution.py:30
  27.0 1.1 broadcast_select_fusion.1
  28.2 2.1 %collective-permute-start.5 = (bf16[272,768]{1,0:T(8,128)(2,1)}, bf16[272,768]{1,0:T(8,128)(2,1)S(1)}, u32[]{:S(2)}, u32[]{:S(2)}) collective-permute-start(bf16[272,768]{1,0:T(8,128)(2,1)} %collective-permute-done.3), channel_id=1, source_target_pairs={{0,2},{2,0},{1,3},{3,1},{4,6},{6,4},{5,7},{7,5},{8,10},{10,8},{9,1... | collective-permute-start | bytes 1253384 | tf_op jit(solution)/shard_map/ppermute | solution.py:26
  30.3 30.0 %collective-permute-done.1 = bf16[272,768]{1,0:T(8,128)(2,1)} collective-permute-done((bf16[272,768]{1,0:T(8,128)(2,1)}, bf16[272,768]{1,0:T(8,128)(2,1)}, u32[]{:S(2)}, u32[]{:S(2)}) %collective-permute-start.1) | collective-permute-done | bytes 417824 | tf_op jit(solution)/shard_map/ppermute | solution.py:26
  60.2 1.0 slice.85
  61.3 0.7 slice_reduce_fusion.3
  62.0 0.7 slice_reduce_fusion.2
  62.7 4.0 %multiply_reduce_fusion.5 = (f32[256]{0:T(256)S(1)}, f32[256,1536]{1,0:T(8,128)S(1)}) fusion(bf16[256,1536]{1,0:T(8,128)(2,1)} %collective-permute-done.2, bf16[1536,1536]{1,0:T(8,128)(2,1)} %param.9), kind=kOutput, calls=%fused_computation.15 | convolution fusion | flops 1208745728 | bytes 7078912 | tf_op jit(solution)/shard_map/dot_general | solution.py:155
  66.8 1.5 multiply_reduce_fusion.3
  68.3 1.2 broadcast_select_fusion
  70.1 1.9 fusion.59
  72.4 2.5 %collective-permute-start.6 = (bf16[256,1536]{1,0:T(8,128)(2,1)}, bf16[256,1536]{1,0:T(8,128)(2,1)S(1)}, u32[]{:S(2)}, u32[]{:S(2)}) collective-permute-start(bf16[256,1536]{1,0:T(8,128)(2,1)} %collective-permute-done.4), channel_id=1, source_target_pairs={{0,2},{2,0},{1,3},{3,1},{4,6},{6,4},{5,7},{7,5},{8,10},{10,8},{9,1... | collective-permute-start | bytes 2359304 | tf_op jit(solution)/shard_map/ppermute | solution.py:26
  74.9 1.8 fusion.51
  77.1 1.4 fusion.69
  78.6 1.4 fusion.87
  80.2 0.7 fusion.43
  82.1 0.7 fusion.35
  83.7 5.7 %collective-permute-start.12 = (bf16[256,768]{1,0:T(8,128)(2,1)S(1)}, bf16[256,768]{1,0:T(8,128)(2,1)S(1)}, u32[]{:S(2)}, u32[]{:S(2)}) collective-permute-start(bf16[256,768]{1,0:T(8,128)(2,1)S(1)} %fusion.7), channel_id=1, source_target_pairs={{0,250},{2,0},{4,254},{6,4},{8,2},{10,8},{12,6},{14,12},{16,10},{1... | collective-permute-start | bytes 1179656 | tf_op jit(solution)/shard_map/ppermute | solution.py:30
  90.2 3.0 %collective-permute-start.9 = (bf16[256,768]{1,0:T(8,128)(2,1)S(1)}, bf16[256,768]{1,0:T(8,128)(2,1)S(1)}, u32[]{:S(2)}, u32[]{:S(2)}) collective-permute-start(bf16[256,768]{1,0:T(8,128)(2,1)S(1)} %slice.196), channel_id=1, source_target_pairs={{0,1},{1,0},{2,3},{3,2},{4,5},{5,4},{6,7},{7,6},{8,9},{9,8},{10,11... | collective-permute-start | bytes 1179656 | tf_op jit(solution)/shard_map/ppermute | solution.py:26
  94.3 8.2 %collective-permute-done.9 = bf16[256,768]{1,0:T(8,128)(2,1)S(1)} collective-permute-done((bf16[256,768]{1,0:T(8,128)(2,1)S(1)}, bf16[256,768]{1,0:T(8,128)(2,1)S(1)}, u32[]{:S(2)}, u32[]{:S(2)}) %collective-permute-start.9) | collective-permute-done | bytes 393248 | tf_op jit(solution)/shard_map/ppermute | solution.py:26
  102.8 1.3 collective-permute-done.11
  104.2 0.6 multiply_reduce_fusion.7
  105.4 1.2 collective-permute-start.14
  106.9 1.0 collective-permute-done.14
  107.9 0.8 fusion.76
  108.7 1.5 abs_reduce_fusion
  111.4 18.9 %all_to_all.20 = f16[4,200,768]{2,1,0:T(8,128)(2,1)S(1)} all-to-all(f16[4,200,768]{2,1,0:T(8,128)(2,1)S(1)} %concatenate.41), channel_id=1, replica_groups=mesh['yl'=2,'z'=8,'x'=4,'core'=2,'yh'=2] {'x'}, dimensions={0} | all-to-all | bytes 2457600 | tf_op jit(solution)/shard_map/all_to_all | solution.py:99
  130.8 24.0 %all_to_all.21 = f16[8,32,768]{2,1,0:T(8,128)(2,1)S(1)} all-to-all(f16[8,32,768]{2,1,0:T(8,128)(2,1)S(1)} %pad_maximum_fusion.5), channel_id=1, replica_groups=mesh['yl'=2,'z'=8,'x'=4,'core'=2,'yh'=2] {'z'}, dimensions={0} | all-to-all | bytes 786432 | tf_op jit(solution)/shard_map/all_to_all | solution.py:103
  155.2 3.0 %collective-permute-start.16 = (f32[32,768]{1,0:T(8,128)S(1)}, f32[32,768]{1,0:T(8,128)S(1)}, u32[]{:S(2)}, u32[]{:S(2)}) collective-permute-start(f32[32,768]{1,0:T(8,128)S(1)} %pad_maximum_fusion.6), channel_id=1, source_target_pairs={{0,1},{1,0},{2,3},{3,2},{4,5},{5,4},{6,7},{7,6},{8,9},{9,8},{10,11... | collective-permute-start | bytes 294920 | tf_op jit(solution)/shard_map/ppermute | solution.py:26
  158.1 0.7 collective-permute-start.17
  158.9 2.3 %collective-permute-done.16 = f32[32,768]{1,0:T(8,128)S(1)} collective-permute-done((f32[32,768]{1,0:T(8,128)S(1)}, f32[32,768]{1,0:T(8,128)S(1)}, u32[]{:S(2)}, u32[]{:S(2)}) %collective-permute-start.16) | collective-permute-done | bytes 98336 | tf_op jit(solution)/shard_map/ppermute | solution.py:26
  161.2 1.6 collective-permute-done.17
  162.9 13.9 %all_to_all.22 = f16[8,24,768]{2,1,0:T(8,128)(2,1)S(1)} all-to-all(f16[8,24,768]{2,1,0:T(8,128)(2,1)S(1)} %broadcast_in_dim.19), channel_id=1, replica_groups=mesh['yl'=2,'z'=8,'x'=4,'core'=2,'yh'=2] {'z'}, dimensions={0} | all-to-all | bytes 589824 | tf_op jit(solution)/shard_map/all_to_all | solution.py:116
  177.0 14.5 %all_to_all.23 = f16[4,192,768]{2,1,0:T(8,128)(2,1)S(1)} all-to-all(f16[4,192,768]{2,1,0:T(8,128)(2,1)S(1)} %broadcast_in_dim.21), channel_id=1, replica_groups=mesh['yl'=2,'z'=8,'x'=4,'core'=2,'yh'=2] {'x'}, dimensions={0} | all-to-all | bytes 2359296 | tf_op jit(solution)/shard_map/all_to_all | solution.py:118
  191.4 5.4 %collective-permute-start.18 = (f16[768,768]{1,0:T(8,128)(2,1)S(1)}, f16[768,768]{1,0:T(8,128)(2,1)S(1)}, u32[]{:S(2)}, u32[]{:S(2)}) collective-permute-start(f16[768,768]{1,0:T(8,128)(2,1)S(1)} %bitcast.31), channel_id=1, source_target_pairs={{0,2},{2,0},{1,3},{3,1},{4,6},{6,4},{5,7},{7,5},{8,10},{10,8},{9,1... | collective-permute-start | bytes 3538952 | tf_op jit(solution)/shard_map/ppermute | solution.py:26
  196.8 2.5 %collective-permute-done.19 = f32[8,768]{1,0:T(8,128)S(1)} collective-permute-done((f32[8,768]{1,0:T(8,128)S(1)}, f32[8,768]{1,0:T(8,128)S(1)}, u32[]{:S(2)}, u32[]{:S(2)}) %collective-permute-start.19) | collective-permute-done | bytes 24608 | tf_op jit(solution)/shard_map/ppermute | solution.py:26
  199.4 2.7 %fusion = (f32[768,768]{1,0:T(8,128)}, f32[768,768]{1,0:T(8,128)}) fusion(f16[768,768]{1,0:T(8,128)(2,1)S(1)} %collective-permute-done.18, f32[768]{0:T(1024)S(1)} %fusion.105, f32[768]{0:T(1024)S(1)} %get-tuple-element.10, pred[]{:T(512)S(6)} %eq.28, f16[4,192,768]{2,1,0:T(8,128)(2,1)S(1)} %all_to_all.23), kind=kLoop, calls=%fused_computation.1 | loop fusion | flops 3538944 | bytes 7084033 | tf_op jit(solution)/shard_map/jit(_where)/select_n | solution.py:202
  (94 shorter events, 9.6 us)
Async XLA Ops:
  0.6 3.9 %copy-start = (bf16[768,768]{1,0:T(8,128)(2,1)S(1)}, bf16[768,768]{1,0:T(8,128)(2,1)}, u32[]{:S(2)}) copy-start(bf16[768,768]{1,0:T(8,128)(2,1)} %param.14) | copy-start | bytes 3538948
  0.6 5.4 %copy-start.9 = (s32[256]{0:T(256)S(1)}, s32[256]{0:T(256)}, u32[]{:S(2)}) copy-start(s32[256]{0:T(256)} %param.15) | copy-start | bytes 3076
  0.7 62.0 %collective-permute-start.2 = (bf16[256,1536]{1,0:T(8,128)(2,1)}, bf16[256,1536]{1,0:T(8,128)(2,1)}, u32[]{:S(2)}, u32[]{:S(2)}) collective-permute-start(bf16[256,1536]{1,0:T(8,128)(2,1)} %param.8), channel_id=1, source_target_pairs={{0,1},{1,0},{2,3},{3,2},{4,5},{5,4},{6,7},{7,6},{8,9},{9,8},{10,11... | collective-permute-start | bytes 2359304 | tf_op jit(solution)/shard_map/ppermute | solution.py:26
  6.0 1.0 copy-start.3
  6.1 1.4 copy-start.5
  6.2 7.7 %copy-start.8 = (bf16[256,1536]{1,0:T(8,128)(2,1)S(1)}, bf16[256,1536]{1,0:T(8,128)(2,1)}, u32[]{:S(2)}) copy-start(bf16[256,1536]{1,0:T(8,128)(2,1)} %param.8) | copy-start | bytes 2359300
  7.4 6.5 %copy-start.7 = (bf16[1536,1536]{1,0:T(8,128)(2,1)S(1)}, bf16[1536,1536]{1,0:T(8,128)(2,1)}, u32[]{:S(2)}) copy-start(bf16[1536,1536]{1,0:T(8,128)(2,1)} %param.9) | copy-start | bytes 14155780
  8.9 51.3 %collective-permute-start.1 = (bf16[272,768]{1,0:T(8,128)(2,1)}, bf16[272,768]{1,0:T(8,128)(2,1)}, u32[]{:S(2)}, u32[]{:S(2)}) collective-permute-start(bf16[272,768]{1,0:T(8,128)(2,1)} %fusion.81), channel_id=1, source_target_pairs={{0,1},{1,0},{2,3},{3,2},{4,5},{5,4},{6,7},{7,6},{8,9},{9,8},{10,11... | collective-permute-start | bytes 1253384 | tf_op jit(solution)/shard_map/ppermute | solution.py:26
  10.1 16.9 %collective-permute-start.3 = (bf16[272,768]{1,0:T(8,128)(2,1)S(1)}, bf16[272,768]{1,0:T(8,128)(2,1)}, u32[]{:S(2)}, u32[]{:S(2)}) collective-permute-start(bf16[272,768]{1,0:T(8,128)(2,1)S(1)} %fusion.80), channel_id=1, source_target_pairs={{0,4},{2,6},{4,8},{6,10},{8,12},{10,14},{12,16},{14,18},{16,20},{1... | collective-permute-start | bytes 1253384 | tf_op jit(solution)/shard_map/ppermute | solution.py:30
  11.3 55.4 %collective-permute-start.4 = (bf16[256,1536]{1,0:T(8,128)(2,1)}, bf16[256,1536]{1,0:T(8,128)(2,1)}, u32[]{:S(2)}, u32[]{:S(2)}) collective-permute-start(bf16[256,1536]{1,0:T(8,128)(2,1)} %param.10), channel_id=1, source_target_pairs={{0,4},{2,6},{4,8},{6,10},{8,12},{10,14},{12,16},{14,18},{16,20},{1... | collective-permute-start | bytes 2359304 | tf_op jit(solution)/shard_map/ppermute | solution.py:30
  28.1 51.9 %collective-permute-start.7 = (bf16[272,768]{1,0:T(8,128)(2,1)S(1)}, bf16[272,768]{1,0:T(8,128)(2,1)S(1)}, u32[]{:S(2)}, u32[]{:S(2)}) collective-permute-start(bf16[272,768]{1,0:T(8,128)(2,1)S(1)} %broadcast_select_fusion.1), channel_id=1, source_target_pairs={{0,2},{2,4},{4,6},{6,8},{8,10},{10,12},{12,14},{14,16},{16,18},{18... | collective-permute-start | bytes 1253384 | tf_op jit(solution)/shard_map/ppermute | solution.py:30
  28.2 51.7 %collective-permute-start.5 = (bf16[272,768]{1,0:T(8,128)(2,1)}, bf16[272,768]{1,0:T(8,128)(2,1)S(1)}, u32[]{:S(2)}, u32[]{:S(2)}) collective-permute-start(bf16[272,768]{1,0:T(8,128)(2,1)} %collective-permute-done.3), channel_id=1, source_target_pairs={{0,2},{2,0},{1,3},{3,1},{4,6},{6,4},{5,7},{7,5},{8,10},{10,8},{9,1... | collective-permute-start | bytes 1253384 | tf_op jit(solution)/shard_map/ppermute | solution.py:26
  66.7 2.8 %copy-start.1 = (f32[256,1536]{1,0:T(8,128)S(1)}, f32[256,1536]{1,0:T(8,128)}, u32[]{:S(2)}) copy-start(f32[256,1536]{1,0:T(8,128)} %get-tuple-element.36) | copy-start | bytes 4718596
  69.5 12.4 %collective-permute-start.8 = (bf16[256,1536]{1,0:T(8,128)(2,1)S(1)}, bf16[256,1536]{1,0:T(8,128)(2,1)S(1)}, u32[]{:S(2)}, u32[]{:S(2)}) collective-permute-start(bf16[256,1536]{1,0:T(8,128)(2,1)S(1)} %broadcast_select_fusion), channel_id=1, source_target_pairs={{0,2},{2,4},{4,6},{6,8},{8,10},{10,12},{12,14},{14,16},{16,18},{18... | collective-permute-start | bytes 2359304 | tf_op jit(solution)/shard_map/ppermute | solution.py:30
  70.1 1.9 copy-start.6
  72.4 7.6 %collective-permute-start.6 = (bf16[256,1536]{1,0:T(8,128)(2,1)}, bf16[256,1536]{1,0:T(8,128)(2,1)S(1)}, u32[]{:S(2)}, u32[]{:S(2)}) collective-permute-start(bf16[256,1536]{1,0:T(8,128)(2,1)} %collective-permute-done.4), channel_id=1, source_target_pairs={{0,2},{2,0},{1,3},{3,1},{4,6},{6,4},{5,7},{7,5},{8,10},{10,8},{9,1... | collective-permute-start | bytes 2359304 | tf_op jit(solution)/shard_map/ppermute | solution.py:26
  81.8 11.5 %collective-permute-start.10 = (bf16[256,768]{1,0:T(8,128)(2,1)S(1)}, bf16[256,768]{1,0:T(8,128)(2,1)S(1)}, u32[]{:S(2)}, u32[]{:S(2)}) collective-permute-start(bf16[256,768]{1,0:T(8,128)(2,1)S(1)} %fusion.6), channel_id=1, source_target_pairs={{0,2},{2,0},{1,3},{3,1},{4,6},{6,4},{5,7},{7,5},{8,10},{10,8},{9,1... | collective-permute-start | bytes 1179656 | tf_op jit(solution)/shard_map/ppermute | solution.py:26
  83.7 19.1 %collective-permute-start.12 = (bf16[256,768]{1,0:T(8,128)(2,1)S(1)}, bf16[256,768]{1,0:T(8,128)(2,1)S(1)}, u32[]{:S(2)}, u32[]{:S(2)}) collective-permute-start(bf16[256,768]{1,0:T(8,128)(2,1)S(1)} %fusion.7), channel_id=1, source_target_pairs={{0,250},{2,0},{4,254},{6,4},{8,2},{10,8},{12,6},{14,12},{16,10},{1... | collective-permute-start | bytes 1179656 | tf_op jit(solution)/shard_map/ppermute | solution.py:30
  90.1 3.6 %copy-start.2 = (bf16[256,768]{1,0:T(8,128)(2,1)S(1)}, bf16[256,768]{1,0:T(8,128)(2,1)}, u32[]{:S(2)}) copy-start(bf16[256,768]{1,0:T(8,128)(2,1)} %param.12) | copy-start | bytes 1179652
  90.1 3.6 %copy-start.4 = (bf16[256,768]{1,0:T(8,128)(2,1)S(1)}, bf16[256,768]{1,0:T(8,128)(2,1)}, u32[]{:S(2)}) copy-start(bf16[256,768]{1,0:T(8,128)(2,1)} %param.11) | copy-start | bytes 1179652
  90.2 12.3 %collective-permute-start.9 = (bf16[256,768]{1,0:T(8,128)(2,1)S(1)}, bf16[256,768]{1,0:T(8,128)(2,1)S(1)}, u32[]{:S(2)}, u32[]{:S(2)}) collective-permute-start(bf16[256,768]{1,0:T(8,128)(2,1)S(1)} %slice.196), channel_id=1, source_target_pairs={{0,1},{1,0},{2,3},{3,2},{4,5},{5,4},{6,7},{7,6},{8,9},{9,8},{10,11... | collective-permute-start | bytes 1179656 | tf_op jit(solution)/shard_map/ppermute | solution.py:26
  93.7 10.5 %collective-permute-start.11 = (bf16[256,768]{1,0:T(8,128)(2,1)S(1)}, bf16[256,768]{1,0:T(8,128)(2,1)S(1)}, u32[]{:S(2)}, u32[]{:S(2)}) collective-permute-start(bf16[256,768]{1,0:T(8,128)(2,1)S(1)} %fusion.5), channel_id=1, source_target_pairs={{0,252},{2,254},{4,0},{6,2},{8,4},{10,6},{12,8},{14,10},{16,12},{1... | collective-permute-start | bytes 1179656 | tf_op jit(solution)/shard_map/ppermute | solution.py:30
  93.8 13.1 %collective-permute-start = (bf16[256,768]{1,0:T(8,128)(2,1)S(1)}, bf16[256,768]{1,0:T(8,128)(2,1)S(1)}, u32[]{:S(2)}, u32[]{:S(2)}) collective-permute-start(bf16[256,768]{1,0:T(8,128)(2,1)S(1)} %get-tuple-element.24), channel_id=1, source_target_pairs={{0,2},{2,0},{1,3},{3,1},{4,6},{6,4},{5,7},{7,5},{8,10},{10,8},{9,1... | collective-permute-start | bytes 1179656 | tf_op jit(solution)/shard_map/ppermute | solution.py:26
  105.4 2.5 %collective-permute-start.14 = (bf16[256,768]{1,0:T(8,128)(2,1)S(1)}, bf16[256,768]{1,0:T(8,128)(2,1)S(1)}, u32[]{:S(2)}, u32[]{:S(2)}) collective-permute-start(bf16[256,768]{1,0:T(8,128)(2,1)S(1)} %get-tuple-element.20), channel_id=1, source_target_pairs={{0,2},{2,0},{1,3},{3,1},{4,6},{6,4},{5,7},{7,5},{8,10},{10,8},{9,1... | collective-permute-start | bytes 1179656 | tf_op jit(solution)/shard_map/ppermute | solution.py:26
  106.6 2.2 %collective-permute-start.13 = (bf16[256,768]{1,0:T(8,128)(2,1)S(1)}, bf16[256,768]{1,0:T(8,128)(2,1)S(1)}, u32[]{:S(2)}, u32[]{:S(2)}) collective-permute-start(bf16[256,768]{1,0:T(8,128)(2,1)S(1)} %get-tuple-element.18), channel_id=1, source_target_pairs={{0,2},{2,0},{1,3},{3,1},{4,6},{6,4},{5,7},{7,5},{8,10},{10,8},{9,1... | collective-permute-start | bytes 1179656 | tf_op jit(solution)/shard_map/ppermute | solution.py:26
  154.9 3.9 %collective-permute-start.15 = (f32[32,768]{1,0:T(8,128)S(1)}, f32[32,768]{1,0:T(8,128)S(1)}, u32[]{:S(2)}, u32[]{:S(2)}) collective-permute-start(f32[32,768]{1,0:T(8,128)S(1)} %pad_maximum_fusion.6), channel_id=1, source_target_pairs={{0,128},{128,0},{1,129},{129,1},{2,130},{130,2},{3,131},{131,3},{4... | collective-permute-start | bytes 294920 | tf_op jit(solution)/shard_map/ppermute | solution.py:26
  155.2 6.0 %collective-permute-start.16 = (f32[32,768]{1,0:T(8,128)S(1)}, f32[32,768]{1,0:T(8,128)S(1)}, u32[]{:S(2)}, u32[]{:S(2)}) collective-permute-start(f32[32,768]{1,0:T(8,128)S(1)} %pad_maximum_fusion.6), channel_id=1, source_target_pairs={{0,1},{1,0},{2,3},{3,2},{4,5},{5,4},{6,7},{7,6},{8,9},{9,8},{10,11... | collective-permute-start | bytes 294920 | tf_op jit(solution)/shard_map/ppermute | solution.py:26
  158.1 4.7 %collective-permute-start.17 = (f32[32,768]{1,0:T(8,128)S(1)}, f32[32,768]{1,0:T(8,128)S(1)}, u32[]{:S(2)}, u32[]{:S(2)}) collective-permute-start(f32[32,768]{1,0:T(8,128)S(1)} %pad_maximum_fusion.6), channel_id=1, source_target_pairs={{0,129},{1,128},{128,1},{129,0},{2,131},{3,130},{130,3},{131,2},{4... | collective-permute-start | bytes 294920 | tf_op jit(solution)/shard_map/ppermute | solution.py:108
  191.4 8.0 %collective-permute-start.18 = (f16[768,768]{1,0:T(8,128)(2,1)S(1)}, f16[768,768]{1,0:T(8,128)(2,1)S(1)}, u32[]{:S(2)}, u32[]{:S(2)}) collective-permute-start(f16[768,768]{1,0:T(8,128)(2,1)S(1)} %bitcast.31), channel_id=1, source_target_pairs={{0,2},{2,0},{1,3},{3,1},{4,6},{6,4},{5,7},{7,5},{8,10},{10,8},{9,1... | collective-permute-start | bytes 3538952 | tf_op jit(solution)/shard_map/ppermute | solution.py:26
  196.8 2.5 %collective-permute-start.19 = (f32[8,768]{1,0:T(8,128)S(1)}, f32[8,768]{1,0:T(8,128)S(1)}, u32[]{:S(2)}, u32[]{:S(2)}) collective-permute-start(f32[8,768]{1,0:T(8,128)S(1)} %broadcast_in_dim.23), channel_id=1, source_target_pairs={{0,2},{2,0},{1,3},{3,1},{4,6},{6,4},{5,7},{7,5},{8,10},{10,8},{9,1... | collective-permute-start | bytes 73736 | tf_op jit(solution)/shard_map/ppermute | solution.py:26

commit v5 on v4

--- a/solution.py
+++ b/solution.py
@@ -1,6 +1,8 @@
 import jax
 import jax.numpy as jnp
 from jax import lax
+from jax.experimental import pallas as pl
+from jax.experimental.pallas import tpu as pltpu
 from jax.sharding import Mesh
 from jax.sharding import PartitionSpec as P
 
@@ -11,6 +13,8 @@
 AXES = ("yl", "z", "x", "core", "yh")
 DP = ("yl", "z", "x", "core")
 N_DP = 128
+COST1 = 10**10
+COST2 = 2 * 10**10
 
 f32 = jnp.float32
 bf16 = jnp.bfloat16
@@ -32,6 +36,29 @@
 
 def chip_shift(block, step):
     return along_dp(block, [(i, (i + 2 * step) % N_DP) for i in range(N_DP)])
+
+
+def forward(block):
+    direct = along_dp(block, [(i, (i + 2) % N_DP) for i in range(N_DP) if i not in (62, 126)])
+    aside = along_dp(block, [(126, 56), (62, 120)])
+    aside = along_dp(aside, [(56, 0), (120, 64)])
+    return direct, aside
+
+
+def hand_on_kernel(flag, own, got, onward):
+    onward[...] = jnp.where(flag[0] == 1, own[...], got[...])
+
+
+def hand_on(first, own, got, flops):
+    block = pl.BlockSpec((own.shape[0] // 2, own.shape[1]), lambda i, flag: (i, 0))
+    return pl.pallas_call(
+        hand_on_kernel,
+        grid_spec=pltpu.PrefetchScalarGridSpec(
+            num_scalar_prefetch=1, grid=(2,), in_specs=[block] * 2, out_specs=block
+        ),
+        out_shape=jax.ShapeDtypeStruct(own.shape, own.dtype),
+        cost_estimate=pl.CostEstimate(flops=flops, bytes_accessed=own.size * 6, transcendentals=0),
+    )(first.astype(jnp.int32)[None], own, got)
 
 
 def with_ids(rows, ids):
@@ -134,7 +161,7 @@
     back_route = [(i, i - 1 if i % 2 else (i - 3) % N_DP) for i in range(N_DP)]
     step_route = [(i, (i + 1) % N_DP) for i in range(N_DP)]
 
-    teach_recv = chip_shift(teacher_text, 1)
+    teach_direct, teach_aside = forward(teacher_text)
     teach_y = swap(teacher_image, "yh")
     text_unit, text_len = unit_rows(jnp.dot(text_feats, text_proj, preferred_element_type=f32))
     text_own = with_ids(text_unit.astype(bf16), class_ids)
@@ -146,10 +173,12 @@
     image_own = with_ids(image_unit.astype(bf16), class_ids)
     teacher_later, image_own = lax.optimization_barrier((teacher_image, image_own))
     image_y = swap(image_own, "yh")
+    teach_far = along_dp(hand_on(first, teacher_text, teach_direct, COST2), step_route)
+    text_far = along_dp(hand_on(first, text_own, text_recv, COST1), step_route)
+    crossed = lax.axis_index(DP) % 64 == 0
+    teach_recv = jnp.where(crossed, teach_aside, teach_direct)
+    text_exch = swap(text_recv, "core")
     teach_exch = swap(teach_recv, "core")
-    teach_far = along_dp(jnp.where(first, teacher_text, teach_recv), step_route)
-    text_exch = swap(text_recv, "core")
-    text_far = along_dp(jnp.where(first, text_own, text_recv), step_route)
 
     def teacher_rows(rows):
         unit, _ = unit_rows(jnp.dot(rows, teacher_proj, preferred_element_type=f32))

time: 203 us -> 205 us (level)
  waiting for transfers between devices: 55.1 us -> 43.4 us
  matrix products: 23 us -> 30.4 us
  starting transfers between devices: 32.5 us -> 39.8 us
  Pallas kernels: 0 us -> 4.1 us
  blocking collectives: 71.3 us -> 68.2 us
  other arithmetic: 11.7 us -> 9.41 us
    ppermute x13, waiting for transfers between devices: 44.1 us -> 33 us  [swap(): return lax.ppermute(block, axis, [(0, 1), (1, 0)])]
    all_to_all x1, blocking collectives: 24 us -> 15.6 us  [sum_everywhere(): blocks = lax.all_to_all(blocks, 'z', 0, 0, tiled=True)]
    pallas_call x0 -> x2, Pallas kernels: none -> 4.1 us  [hand_on(): pl.pallas_call(hand_on_kernel, grid_spec=pltpu.PrefetchScalarGridSpec(num...]
    dot_general x4, matrix products: 2.79 us -> 6.7 us  [pair_tile(): lax.dot_general(image_rows, text_cols, (((1,), (1,)), ((), ())), preferre...]
    ppermute x6 -> x8, starting transfers between devices: 8.35 us -> 11.6 us  [along_dp(): return lax.ppermute(block, DP, route)]
    ppermute x13, starting transfers between devices: 23.4 us -> 26.5 us  [swap(): return lax.ppermute(block, axis, [(0, 1), (1, 0)])]
    dot_general x4, matrix products: 2.5 us -> 5.54 us  [pair_tile(): row_part = scale * jnp.dot(scaled, text_cols, preferred_element_type=f32)]
    dot_general x2, matrix products: 6.58 us -> 9.27 us  [teacher_rows(): unit, _ = unit_rows(jnp.dot(rows, teacher_proj, preferred_element_type=f32))]
  transfers between devices with their start and end apart: 20 -> 22, of which waited for: 8 -> 8; matrix products, arithmetic and copies ran while one was open for 17% -> 20% of each run, Pallas kernels for 0% -> 2%
where the time goes in v5:
time: 205 us; the launch traced here: 204 us
  blocking collectives  68.2 us (33%)
  waiting for transfers between devices  43.4 us (21%)
  starting transfers between devices  39.8 us (19%)
  matrix products  30.4 us (15%)
  other arithmetic  9.41 us (5%)
  local copies, waits for them, and re-layouts  6.66 us (3%)
  Pallas kernels  4.1 us (2%)
    ppermute x13, waiting for transfers between devices, swap(): return lax.ppermute(block, axis, [(0, 1), (1, 0)])  33 us
    ppermute x13, starting transfers between devices, swap(): return lax.ppermute(block, axis, [(0, 1), (1, 0)])  26.5 us
    all_to_all x1, blocking collectives, sum_everywhere(): blocks = lax.all_to_all(blocks, 'x', 0, 0, tiled=True)  20.9 us
    all_to_all x1, blocking collectives, sum_everywhere(): own_total = lax.all_to_all(spread, 'x', 0, 0, tiled=True).reshape(ds, ds)  15.9 us
    all_to_all x1, blocking collectives, sum_everywhere(): lax.all_to_all(spread, 'z', 0, 0, tiled=True).reshape(ds // 4, ds)  15.8 us
    all_to_all x1, blocking collectives, sum_everywhere(): blocks = lax.all_to_all(blocks, 'z', 0, 0, tiled=True)  15.6 us
    ppermute x8, starting transfers between devices, along_dp(): return lax.ppermute(block, DP, route)  11.6 us
    dot_general x2, matrix products, teacher_rows(): unit, _ = unit_rows(jnp.dot(rows, teacher_proj, preferred_element_type=f32))  9.27 us
  transfers between devices with their start and end apart: 22, of which 8 were waited for; matrix products, arithmetic and copies ran while one was open for 20% of the time, Pallas kernels for 2%

profile of v5, /device:TPU:1, one launch (start us, length us, event | category | flops | bytes accessed | tf_op | source)
XLA Modules:
  0.0 204.0 jit_solution(15237504952547294155)
XLA Ops:
  0.7 4.1 %collective-permute-start.6 = (bf16[256,1536]{1,0:T(8,128)(2,1)}, bf16[256,1536]{1,0:T(8,128)(2,1)}, u32[]{:S(2)}, u32[]{:S(2)}) collective-permute-start(bf16[256,1536]{1,0:T(8,128)(2,1)} %own.1), channel_id=1, source_target_pairs={{0,4},{2,6},{4,8},{6,10},{8,12},{10,14},{12,16},{14,18},{16,20},{1... | collective-permute-start | bytes 2359304 | tf_op jit(solution)/shard_map/ppermute | solution.py:34
  4.7 1.6 collective-permute-start.4
  6.3 2.9 %collective-permute-start.2 = (bf16[256,1536]{1,0:T(8,128)(2,1)}, bf16[256,1536]{1,0:T(8,128)(2,1)}, u32[]{:S(2)}, u32[]{:S(2)}) collective-permute-start(bf16[256,1536]{1,0:T(8,128)(2,1)} %param.8), channel_id=1, source_target_pairs={{0,1},{1,0},{2,3},{3,2},{4,5},{5,4},{6,7},{7,6},{8,9},{9,8},{10,11... | collective-permute-start | bytes 2359304 | tf_op jit(solution)/shard_map/ppermute | solution.py:30
  9.2 1.6 multiply_reduce_fusion.10
  11.0 0.8 fusion.79.own
  13.2 1.2 collective-permute-start.3
  14.5 0.8 slice.64
  16.0 1.4 multiply_reduce_fusion.4
  17.3 5.1 %multiply_reduce_fusion.6 = (f32[256]{0:T(256)S(1)}, f32[256,1536]{1,0:T(8,128)}) fusion(bf16[256,1536]{1,0:T(8,128)(2,1)} %param.8, bf16[1536,1536]{1,0:T(8,128)(2,1)} %param.9), kind=kOutput, calls=%fused_computation.17 | convolution fusion | flops 1208745728 | bytes 7078912 | tf_op jit(solution)/shard_map/dot_general | solution.py:184
  22.5 7.7 %collective-permute-done.3.got = bf16[272,768]{1,0:T(8,128)(2,1)} collective-permute-done((bf16[272,768]{1,0:T(8,128)(2,1)}, bf16[272,768]{1,0:T(8,128)(2,1)}, u32[]{:S(2)}, u32[]{:S(2)}) %collective-permute-start.3) | collective-permute-done | bytes 417824 | tf_op jit(solution)/shard_map/ppermute | solution.py:34
  30.2 1.9 shard_map.95
  32.2 3.6 %collective-permute-start.9 = (bf16[272,768]{1,0:T(8,128)(2,1)}, bf16[272,768]{1,0:T(8,128)(2,1)}, u32[]{:S(2)}, u32[]{:S(2)}) collective-permute-start(bf16[272,768]{1,0:T(8,128)(2,1)} %shard_map.95), channel_id=1, source_target_pairs={{0,2},{2,4},{4,6},{6,8},{8,10},{10,12},{12,14},{14,16},{16,18},{18... | collective-permute-start | bytes 1253384 | tf_op jit(solution)/shard_map/ppermute | solution.py:34
  35.8 20.4 %collective-permute-done.1 = bf16[272,768]{1,0:T(8,128)(2,1)} collective-permute-done((bf16[272,768]{1,0:T(8,128)(2,1)S(1)}, bf16[272,768]{1,0:T(8,128)(2,1)}, u32[]{:S(2)}, u32[]{:S(2)}) %collective-permute-start.1) | collective-permute-done | bytes 417824 | tf_op jit(solution)/shard_map/ppermute | solution.py:30
  56.2 2.7 %collective-permute-start.7 = (bf16[272,768]{1,0:T(8,128)(2,1)}, bf16[272,768]{1,0:T(8,128)(2,1)}, u32[]{:S(2)}, u32[]{:S(2)}) collective-permute-start(bf16[272,768]{1,0:T(8,128)(2,1)} %collective-permute-done.3.got), channel_id=1, source_target_pairs={{0,2},{2,0},{1,3},{3,1},{4,6},{6,4},{5,7},{7,5},{8,10},{10,8},{9,1... | collective-permute-start | bytes 1253384 | tf_op jit(solution)/shard_map/ppermute | solution.py:30
  58.9 1.0 slice.85
  61.3 2.3 %fusion.17 = f32[512,256]{1,0:T(8,128)} fusion(bf16[272,768]{1,0:T(8,128)(2,1)} %collective-permute-done.3.got, bf16[256,768]{1,0:T(8,128)(2,1)S(1)} %slice.85, bf16[256,768]{1,0:T(8,128)(2,1)} %slice.64), kind=kOutput, calls=%fused_computation.41 | convolution fusion | flops 203554816 | bytes 1703936 | tf_op jit(solution)/shard_map/dot_general | solution.py:88
  63.7 2.1 %shard_map.96 = bf16[256,1536]{1,0:T(8,128)(2,1)} custom-call(s32[1]{0:T(128)} %bitcast.flag, bf16[256,1536]{1,0:T(8,128)(2,1)} %own.1, bf16[256,1536]{1,0:T(8,128)(2,1)} %collective-permute-done.6.got), custom_call_target="tpu_custom_call" | custom-call | flops 20000000000 | bytes 2359296 | tf_op jit(solution)/shard_map/pallas_call | solution.py:54
  65.8 4.2 %multiply_reduce_fusion.5 = (f32[256]{0:T(256)S(1)}, f32[256,1536]{1,0:T(8,128)S(1)}) fusion(bf16[256,1536]{1,0:T(8,128)(2,1)} %collective-permute-done.2, bf16[1536,1536]{1,0:T(8,128)(2,1)} %param.9), kind=kOutput, calls=%fused_computation.15 | convolution fusion | flops 1208745728 | bytes 7078912 | tf_op jit(solution)/shard_map/dot_general | solution.py:184
  70.5 0.7 collective-permute-start.5
  72.2 1.4 fusion.67
  73.7 1.4 fusion.89
  76.4 1.5 multiply_reduce_fusion.3
  77.9 8.7 %collective-permute-start.8 = (bf16[256,1536]{1,0:T(8,128)(2,1)S(1)}, bf16[256,1536]{1,0:T(8,128)(2,1)S(1)}, u32[]{:S(2)}, u32[]{:S(2)}) collective-permute-start(bf16[256,1536]{1,0:T(8,128)(2,1)S(1)} %get-tuple-element.17), channel_id=1, source_target_pairs={{0,2},{2,0},{1,3},{3,1},{4,6},{6,4},{5,7},{7,5},{8,10},{10,8},{9,1... | collective-permute-start | bytes 2359304 | tf_op jit(solution)/shard_map/ppermute | solution.py:30
  87.6 1.4 fusion.69
  89.7 1.4 fusion.81
  91.1 0.7 fusion.70
  91.8 1.4 fusion.86
  94.1 1.5 fusion.68
  96.1 1.5 add_multiply_fusion
  97.6 3.0 %collective-permute-start.11 = (bf16[256,768]{1,0:T(8,128)(2,1)S(1)}, bf16[256,768]{1,0:T(8,128)(2,1)S(1)}, u32[]{:S(2)}, u32[]{:S(2)}) collective-permute-start(bf16[256,768]{1,0:T(8,128)(2,1)S(1)} %slice.196), channel_id=1, source_target_pairs={{0,1},{1,0},{2,3},{3,2},{4,5},{5,4},{6,7},{7,6},{8,9},{9,8},{10,11... | collective-permute-start | bytes 1179656 | tf_op jit(solution)/shard_map/ppermute | solution.py:30
  101.2 0.9 collective-permute-start
  102.1 7.3 %collective-permute-done.11 = bf16[256,768]{1,0:T(8,128)(2,1)S(1)} collective-permute-done((bf16[256,768]{1,0:T(8,128)(2,1)S(1)}, bf16[256,768]{1,0:T(8,128)(2,1)S(1)}, u32[]{:S(2)}, u32[]{:S(2)}) %collective-permute-start.11) | collective-permute-done | bytes 393248 | tf_op jit(solution)/shard_map/ppermute | solution.py:30
  109.7 1.3 collective-permute-done.13
  112.2 1.8 collective-permute-start.16
  114.0 1.2 collective-permute-done.16
  115.3 0.8 fusion.75
  116.1 1.5 abs_reduce_fusion
  118.8 20.9 %all_to_all.20 = f16[4,200,768]{2,1,0:T(8,128)(2,1)S(1)} all-to-all(f16[4,200,768]{2,1,0:T(8,128)(2,1)S(1)} %concatenate.41), channel_id=1, replica_groups=mesh['yl'=2,'z'=8,'x'=4,'core'=2,'yh'=2] {'x'}, dimensions={0} | all-to-all | bytes 2457600 | tf_op jit(solution)/shard_map/all_to_all | solution.py:126
  140.1 15.6 %all_to_all.21 = f16[8,32,768]{2,1,0:T(8,128)(2,1)S(1)} all-to-all(f16[8,32,768]{2,1,0:T(8,128)(2,1)S(1)} %pad_maximum_fusion.5), channel_id=1, replica_groups=mesh['yl'=2,'z'=8,'x'=4,'core'=2,'yh'=2] {'z'}, dimensions={0} | all-to-all | bytes 786432 | tf_op jit(solution)/shard_map/all_to_all | solution.py:130
  156.4 1.7 collective-permute-start.18
  158.2 1.7 collective-permute-start.19
  159.9 1.5 collective-permute-done.18
  161.4 1.4 collective-permute-done.19
  162.9 15.8 %all_to_all.22 = f16[8,24,768]{2,1,0:T(8,128)(2,1)S(1)} all-to-all(f16[8,24,768]{2,1,0:T(8,128)(2,1)S(1)} %broadcast_in_dim.25), channel_id=1, replica_groups=mesh['yl'=2,'z'=8,'x'=4,'core'=2,'yh'=2] {'z'}, dimensions={0} | all-to-all | bytes 589824 | tf_op jit(solution)/shard_map/all_to_all | solution.py:143
  178.8 15.9 %all_to_all.23 = f16[4,192,768]{2,1,0:T(8,128)(2,1)S(1)} all-to-all(f16[4,192,768]{2,1,0:T(8,128)(2,1)S(1)} %broadcast_in_dim.27), channel_id=1, replica_groups=mesh['yl'=2,'z'=8,'x'=4,'core'=2,'yh'=2] {'x'}, dimensions={0} | all-to-all | bytes 2359296 | tf_op jit(solution)/shard_map/all_to_all | solution.py:145
  194.8 4.0 %collective-permute-start.20 = (f16[768,768]{1,0:T(8,128)(2,1)S(1)}, f16[768,768]{1,0:T(8,128)(2,1)S(1)}, u32[]{:S(2)}, u32[]{:S(2)}) collective-permute-start(f16[768,768]{1,0:T(8,128)(2,1)S(1)} %bitcast.32), channel_id=1, source_target_pairs={{0,2},{2,0},{1,3},{3,1},{4,6},{6,4},{5,7},{7,5},{8,10},{10,8},{9,1... | collective-permute-start | bytes 3538952 | tf_op jit(solution)/shard_map/ppermute | solution.py:30
  198.7 2.5 %collective-permute-done.21 = f32[8,768]{1,0:T(8,128)S(1)} collective-permute-done((f32[8,768]{1,0:T(8,128)S(1)}, f32[8,768]{1,0:T(8,128)S(1)}, u32[]{:S(2)}, u32[]{:S(2)}) %collective-permute-start.21) | collective-permute-done | bytes 24608 | tf_op jit(solution)/shard_map/ppermute | solution.py:30
  201.3 2.7 %fusion = (f32[768,768]{1,0:T(8,128)}, f32[768,768]{1,0:T(8,128)}) fusion(f16[768,768]{1,0:T(8,128)(2,1)S(1)} %collective-permute-done.20, f32[768]{0:T(1024)S(1)} %fusion.104, f32[768]{0:T(1024)S(1)} %get-tuple-element.10, pred[]{:T(512)S(6)} %eq.62, f16[4,192,768]{2,1,0:T(8,128)(2,1)S(1)} %all_to_all.23), kind=kLoop, calls=%fused_computation.1 | loop fusion | flops 3538944 | bytes 7084033 | tf_op jit(solution)/shard_map/jit(_where)/select_n | solution.py:231
  (98 shorter events, 13.4 us)
Async XLA Ops:
  0.6 8.6 %copy-start = (bf16[768,768]{1,0:T(8,128)(2,1)S(1)}, bf16[768,768]{1,0:T(8,128)(2,1)}, u32[]{:S(2)}) copy-start(bf16[768,768]{1,0:T(8,128)(2,1)} %param.14) | copy-start | bytes 3538948
  0.6 10.2 %copy-start.8 = (s32[256]{0:T(256)S(1)}, s32[256]{0:T(256)}, u32[]{:S(2)}) copy-start(s32[256]{0:T(256)} %param.15) | copy-start | bytes 3076
  0.7 63.0 %collective-permute-start.6 = (bf16[256,1536]{1,0:T(8,128)(2,1)}, bf16[256,1536]{1,0:T(8,128)(2,1)}, u32[]{:S(2)}, u32[]{:S(2)}) collective-permute-start(bf16[256,1536]{1,0:T(8,128)(2,1)} %own.1), channel_id=1, source_target_pairs={{0,4},{2,6},{4,8},{6,10},{8,12},{10,14},{12,16},{14,18},{16,20},{1... | collective-permute-start | bytes 2359304 | tf_op jit(solution)/shard_map/ppermute | solution.py:34
  4.7 65.7 %collective-permute-start.4 = (bf16[256,1536]{1,0:T(8,128)(2,1)}, bf16[256,1536]{1,0:T(8,128)(2,1)}, u32[]{:S(2)}, u32[]{:S(2)}) collective-permute-start(bf16[256,1536]{1,0:T(8,128)(2,1)} %own.1), channel_id=1, source_target_pairs={{252,112},{124,240},{253,113},{125,241}} | collective-permute-start | bytes 2359304 | tf_op jit(solution)/shard_map/ppermute | solution.py:34
  6.3 59.5 %collective-permute-start.2 = (bf16[256,1536]{1,0:T(8,128)(2,1)}, bf16[256,1536]{1,0:T(8,128)(2,1)}, u32[]{:S(2)}, u32[]{:S(2)}) collective-permute-start(bf16[256,1536]{1,0:T(8,128)(2,1)} %param.8), channel_id=1, source_target_pairs={{0,1},{1,0},{2,3},{3,2},{4,5},{5,4},{6,7},{7,6},{8,9},{9,8},{10,11... | collective-permute-start | bytes 2359304 | tf_op jit(solution)/shard_map/ppermute | solution.py:30
  10.8 1.0 copy-start.3
  10.8 1.5 copy-start.5
  13.1 43.1 %collective-permute-start.1 = (bf16[272,768]{1,0:T(8,128)(2,1)S(1)}, bf16[272,768]{1,0:T(8,128)(2,1)}, u32[]{:S(2)}, u32[]{:S(2)}) collective-permute-start(bf16[272,768]{1,0:T(8,128)(2,1)S(1)} %fusion.80), channel_id=1, source_target_pairs={{0,1},{1,0},{2,3},{3,2},{4,5},{5,4},{6,7},{7,6},{8,9},{9,8},{10,11... | collective-permute-start | bytes 1253384 | tf_op jit(solution)/shard_map/ppermute | solution.py:30
  13.2 17.0 %collective-permute-start.3 = (bf16[272,768]{1,0:T(8,128)(2,1)}, bf16[272,768]{1,0:T(8,128)(2,1)}, u32[]{:S(2)}, u32[]{:S(2)}) collective-permute-start(bf16[272,768]{1,0:T(8,128)(2,1)} %fusion.79.own), channel_id=1, source_target_pairs={{0,4},{2,6},{4,8},{6,10},{8,12},{10,14},{12,16},{14,18},{16,20},{1... | collective-permute-start | bytes 1253384 | tf_op jit(solution)/shard_map/ppermute | solution.py:34
  32.2 43.6 %collective-permute-start.9 = (bf16[272,768]{1,0:T(8,128)(2,1)}, bf16[272,768]{1,0:T(8,128)(2,1)}, u32[]{:S(2)}, u32[]{:S(2)}) collective-permute-start(bf16[272,768]{1,0:T(8,128)(2,1)} %shard_map.95), channel_id=1, source_target_pairs={{0,2},{2,4},{4,6},{6,8},{8,10},{10,12},{12,14},{14,16},{16,18},{18... | collective-permute-start | bytes 1253384 | tf_op jit(solution)/shard_map/ppermute | solution.py:34
  56.2 18.9 %collective-permute-start.7 = (bf16[272,768]{1,0:T(8,128)(2,1)}, bf16[272,768]{1,0:T(8,128)(2,1)}, u32[]{:S(2)}, u32[]{:S(2)}) collective-permute-start(bf16[272,768]{1,0:T(8,128)(2,1)} %collective-permute-done.3.got), channel_id=1, source_target_pairs={{0,2},{2,0},{1,3},{3,1},{4,6},{6,4},{5,7},{7,5},{8,10},{10,8},{9,1... | collective-permute-start | bytes 1253384 | tf_op jit(solution)/shard_map/ppermute | solution.py:30
  65.8 4.2 %copy-start.1 = (f32[256,1536]{1,0:T(8,128)S(1)}, f32[256,1536]{1,0:T(8,128)}, u32[]{:S(2)}) copy-start(f32[256,1536]{1,0:T(8,128)} %get-tuple-element.38) | copy-start | bytes 4718596
  65.8 20.8 %collective-permute-start.10 = (bf16[256,1536]{1,0:T(8,128)(2,1)}, bf16[256,1536]{1,0:T(8,128)(2,1)S(1)}, u32[]{:S(2)}, u32[]{:S(2)}) collective-permute-start(bf16[256,1536]{1,0:T(8,128)(2,1)} %shard_map.96), channel_id=1, source_target_pairs={{0,2},{2,4},{4,6},{6,8},{8,10},{10,12},{12,14},{14,16},{16,18},{18... | collective-permute-start | bytes 2359304 | tf_op jit(solution)/shard_map/ppermute | solution.py:34
  70.0 1.2 copy-start.6
  70.5 5.9 %collective-permute-start.5 = (bf16[256,1536]{1,0:T(8,128)(2,1)}, bf16[256,1536]{1,0:T(8,128)(2,1)S(1)}, u32[]{:S(2)}, u32[]{:S(2)}) collective-permute-start(bf16[256,1536]{1,0:T(8,128)(2,1)} %collective-permute-done.4), channel_id=1, source_target_pairs={{112,0},{240,128},{113,1},{241,129}} | collective-permute-start | bytes 2359304 | tf_op jit(solution)/shard_map/ppermute | solution.py:34
  71.2 1.0 copy-start.7
  77.9 15.2 %collective-permute-start.8 = (bf16[256,1536]{1,0:T(8,128)(2,1)S(1)}, bf16[256,1536]{1,0:T(8,128)(2,1)S(1)}, u32[]{:S(2)}, u32[]{:S(2)}) collective-permute-start(bf16[256,1536]{1,0:T(8,128)(2,1)S(1)} %get-tuple-element.17), channel_id=1, source_target_pairs={{0,2},{2,0},{1,3},{3,1},{4,6},{6,4},{5,7},{7,5},{8,10},{10,8},{9,1... | collective-permute-start | bytes 2359304 | tf_op jit(solution)/shard_map/ppermute | solution.py:30
  89.4 1.7 copy-start.9
  89.4 20.2 %collective-permute-start.14 = (bf16[256,768]{1,0:T(8,128)(2,1)S(1)}, bf16[256,768]{1,0:T(8,128)(2,1)S(1)}, u32[]{:S(2)}, u32[]{:S(2)}) collective-permute-start(bf16[256,768]{1,0:T(8,128)(2,1)S(1)} %fusion.7), channel_id=1, source_target_pairs={{0,250},{2,0},{4,254},{6,4},{8,2},{10,8},{12,6},{14,12},{16,10},{1... | collective-permute-start | bytes 1179656 | tf_op jit(solution)/shard_map/ppermute | solution.py:34
  96.0 4.7 %collective-permute-start.12 = (bf16[256,768]{1,0:T(8,128)(2,1)S(1)}, bf16[256,768]{1,0:T(8,128)(2,1)S(1)}, u32[]{:S(2)}, u32[]{:S(2)}) collective-permute-start(bf16[256,768]{1,0:T(8,128)(2,1)S(1)} %fusion.6), channel_id=1, source_target_pairs={{0,2},{2,0},{1,3},{3,1},{4,6},{6,4},{5,7},{7,5},{8,10},{10,8},{9,1... | collective-permute-start | bytes 1179656 | tf_op jit(solution)/shard_map/ppermute | solution.py:30
  97.5 3.6 %copy-start.2 = (bf16[256,768]{1,0:T(8,128)(2,1)S(1)}, bf16[256,768]{1,0:T(8,128)(2,1)}, u32[]{:S(2)}) copy-start(bf16[256,768]{1,0:T(8,128)(2,1)} %param.12) | copy-start | bytes 1179652
  97.5 3.6 %copy-start.4 = (bf16[256,768]{1,0:T(8,128)(2,1)S(1)}, bf16[256,768]{1,0:T(8,128)(2,1)}, u32[]{:S(2)}) copy-start(bf16[256,768]{1,0:T(8,128)(2,1)} %param.11) | copy-start | bytes 1179652
  97.6 11.8 %collective-permute-start.11 = (bf16[256,768]{1,0:T(8,128)(2,1)S(1)}, bf16[256,768]{1,0:T(8,128)(2,1)S(1)}, u32[]{:S(2)}, u32[]{:S(2)}) collective-permute-start(bf16[256,768]{1,0:T(8,128)(2,1)S(1)} %slice.196), channel_id=1, source_target_pairs={{0,1},{1,0},{2,3},{3,2},{4,5},{5,4},{6,7},{7,6},{8,9},{9,8},{10,11... | collective-permute-start | bytes 1179656 | tf_op jit(solution)/shard_map/ppermute | solution.py:30
  101.0 9.9 %collective-permute-start.13 = (bf16[256,768]{1,0:T(8,128)(2,1)S(1)}, bf16[256,768]{1,0:T(8,128)(2,1)S(1)}, u32[]{:S(2)}, u32[]{:S(2)}) collective-permute-start(bf16[256,768]{1,0:T(8,128)(2,1)S(1)} %fusion.5), channel_id=1, source_target_pairs={{0,252},{2,254},{4,0},{6,2},{8,4},{10,6},{12,8},{14,10},{16,12},{1... | collective-permute-start | bytes 1179656 | tf_op jit(solution)/shard_map/ppermute | solution.py:34
  101.2 12.8 %collective-permute-start = (bf16[256,768]{1,0:T(8,128)(2,1)S(1)}, bf16[256,768]{1,0:T(8,128)(2,1)S(1)}, u32[]{:S(2)}, u32[]{:S(2)}) collective-permute-start(bf16[256,768]{1,0:T(8,128)(2,1)S(1)} %get-tuple-element.26), channel_id=1, source_target_pairs={{0,2},{2,0},{1,3},{3,1},{4,6},{6,4},{5,7},{7,5},{8,10},{10,8},{9,1... | collective-permute-start | bytes 1179656 | tf_op jit(solution)/shard_map/ppermute | solution.py:30
  112.2 3.1 %collective-permute-start.16 = (bf16[256,768]{1,0:T(8,128)(2,1)S(1)}, bf16[256,768]{1,0:T(8,128)(2,1)S(1)}, u32[]{:S(2)}, u32[]{:S(2)}) collective-permute-start(bf16[256,768]{1,0:T(8,128)(2,1)S(1)} %get-tuple-element.22), channel_id=1, source_target_pairs={{0,2},{2,0},{1,3},{3,1},{4,6},{6,4},{5,7},{7,5},{8,10},{10,8},{9,1... | collective-permute-start | bytes 1179656 | tf_op jit(solution)/shard_map/ppermute | solution.py:30
  113.9 2.2 %collective-permute-start.15 = (bf16[256,768]{1,0:T(8,128)(2,1)S(1)}, bf16[256,768]{1,0:T(8,128)(2,1)S(1)}, u32[]{:S(2)}, u32[]{:S(2)}) collective-permute-start(bf16[256,768]{1,0:T(8,128)(2,1)S(1)} %get-tuple-element.20), channel_id=1, source_target_pairs={{0,2},{2,0},{1,3},{3,1},{4,6},{6,4},{5,7},{7,5},{8,10},{10,8},{9,1... | collective-permute-start | bytes 1179656 | tf_op jit(solution)/shard_map/ppermute | solution.py:30
  155.9 4.0 %collective-permute-start.17 = (f32[32,768]{1,0:T(8,128)S(1)}, f32[32,768]{1,0:T(8,128)S(1)}, u32[]{:S(2)}, u32[]{:S(2)}) collective-permute-start(f32[32,768]{1,0:T(8,128)S(1)} %pad_maximum_fusion.6), channel_id=1, source_target_pairs={{0,128},{128,0},{1,129},{129,1},{2,130},{130,2},{3,131},{131,3},{4... | collective-permute-start | bytes 294920 | tf_op jit(solution)/shard_map/ppermute | solution.py:30
  156.4 5.0 %collective-permute-start.18 = (f32[32,768]{1,0:T(8,128)S(1)}, f32[32,768]{1,0:T(8,128)S(1)}, u32[]{:S(2)}, u32[]{:S(2)}) collective-permute-start(f32[32,768]{1,0:T(8,128)S(1)} %pad_maximum_fusion.6), channel_id=1, source_target_pairs={{0,1},{1,0},{2,3},{3,2},{4,5},{5,4},{6,7},{7,6},{8,9},{9,8},{10,11... | collective-permute-start | bytes 294920 | tf_op jit(solution)/shard_map/ppermute | solution.py:30
  158.2 4.7 %collective-permute-start.19 = (f32[32,768]{1,0:T(8,128)S(1)}, f32[32,768]{1,0:T(8,128)S(1)}, u32[]{:S(2)}, u32[]{:S(2)}) collective-permute-start(f32[32,768]{1,0:T(8,128)S(1)} %pad_maximum_fusion.6), channel_id=1, source_target_pairs={{0,129},{1,128},{128,1},{129,0},{2,131},{3,130},{130,3},{131,2},{4... | collective-permute-start | bytes 294920 | tf_op jit(solution)/shard_map/ppermute | solution.py:135
  194.8 6.5 %collective-permute-start.20 = (f16[768,768]{1,0:T(8,128)(2,1)S(1)}, f16[768,768]{1,0:T(8,128)(2,1)S(1)}, u32[]{:S(2)}, u32[]{:S(2)}) collective-permute-start(f16[768,768]{1,0:T(8,128)(2,1)S(1)} %bitcast.32), channel_id=1, source_target_pairs={{0,2},{2,0},{1,3},{3,1},{4,6},{6,4},{5,7},{7,5},{8,10},{10,8},{9,1... | collective-permute-start | bytes 3538952 | tf_op jit(solution)/shard_map/ppermute | solution.py:30
  198.7 2.5 %collective-permute-start.21 = (f32[8,768]{1,0:T(8,128)S(1)}, f32[8,768]{1,0:T(8,128)S(1)}, u32[]{:S(2)}, u32[]{:S(2)}) collective-permute-start(f32[8,768]{1,0:T(8,128)S(1)} %broadcast_in_dim.29), channel_id=1, source_target_pairs={{0,2},{2,0},{1,3},{3,1},{4,6},{6,4},{5,7},{7,5},{8,10},{10,8},{9,1... | collective-permute-start | bytes 73736 | tf_op jit(solution)/shard_map/ppermute | solution.py:30

commit v6 on v3

--- a/solution.py
+++ b/solution.py
@@ -1,6 +1,8 @@
 import jax
 import jax.numpy as jnp
 from jax import lax
+from jax.experimental import pallas as pl
+from jax.experimental.pallas import tpu as pltpu
 from jax.sharding import Mesh
 from jax.sharding import PartitionSpec as P
 
@@ -34,28 +36,121 @@
     return along_dp(block, [(i, (i + 2 * step) % N_DP) for i in range(N_DP)])
 
 
-def pair_tile(teach_rows, image_rows, row_ids, teach_cols, text_cols, notes):
-    teacher_dot = (
-        lax.dot_general(
-            teach_rows, teach_cols, (((1,), (1,)), ((), ())), preferred_element_type=f32
-        )
-        * notes[1:2, :]
-    )
-    labels = (row_ids == notes[0:1, :]).astype(f32)
+VMEM = pl.BlockSpec(memory_space=pltpu.VMEM)
+SMEM = pl.BlockSpec(memory_space=pltpu.SMEM)
+ROWS = 256
+DT = 1536
+DS = 768
+PAD = 16
+
+
+def note_ids(ids, payload):
+    payload[ROWS:, :] = jnp.zeros((PAD, DT + DS), bf16)
+    payload[ROWS:, :ROWS] = jnp.broadcast_to(ids[...], (PAD, ROWS)).astype(f32).astype(bf16)
+
+
+def student(feats, proj, payload, unit_out, len_out):
+    unit, length = unit_rows(jnp.dot(feats[...], proj[...], preferred_element_type=f32))
+    payload[:ROWS, DT:] = unit.astype(bf16)
+    unit_out[...] = unit
+    len_out[...] = length
+
+
+def text_kernel(ids, feats, proj, teacher, payload, unit_out, len_out):
+    student(feats, proj, payload, unit_out, len_out)
+    unit, _ = unit_rows(teacher[...].astype(f32))
+    payload[:ROWS, :DT] = unit.astype(bf16)
+    note_ids(ids, payload)
+
+
+def image_kernel(ids, feats, proj, teacher, teacher_proj, payload, unit_out, len_out):
+    student(feats, proj, payload, unit_out, len_out)
+    unit, _ = unit_rows(jnp.dot(teacher[...], teacher_proj[...], preferred_element_type=f32))
+    payload[:ROWS, :DT] = unit.astype(bf16)
+    note_ids(ids, payload)
+
+
+def embed(kernel, flops, *args):
+    return pl.pallas_call(
+        kernel,
+        in_specs=[VMEM] * len(args),
+        out_specs=[VMEM] * 3,
+        out_shape=[
+            jax.ShapeDtypeStruct((ROWS + PAD, DT + DS), bf16),
+            jax.ShapeDtypeStruct((ROWS, DS), f32),
+            jax.ShapeDtypeStruct((ROWS, 1), f32),
+        ],
+        compiler_params=pltpu.CompilerParams(vmem_limit_bytes=48 * 2**20),
+        cost_estimate=pl.CostEstimate(flops=flops, bytes_accessed=5 * 2**20, transcendentals=0),
+    )(*args)
+
+
+CROSS = (((1,), (1,)), ((), ()))
+OVER_ROWS = (((0,), (0,)), ((), ()))
+
+
+def tile(image, text):
+    teacher_dot = lax.dot_general(
+        image[:ROWS, :DT], text[:ROWS, :DT], CROSS, preferred_element_type=f32
+    )
+    row_ids = jnp.broadcast_to(image[ROWS:, :ROWS].astype(f32)[:1], (ROWS, ROWS)).T
+    labels = (row_ids == text[ROWS:, :ROWS].astype(f32)[:1]).astype(f32)
     target = 0.5 * jax.nn.sigmoid(scale * teacher_dot + shift) + 0.5 * labels
     logits = (
         scale
         * lax.dot_general(
-            image_rows, text_cols, (((1,), (1,)), ((), ())), preferred_element_type=f32
+            image[:ROWS, DT:], text[:ROWS, DT:], CROSS, preferred_element_type=f32
         )
         + shift
     )
-    scaled = ((jax.nn.sigmoid(logits) - target) / text_cols.shape[0]).astype(bf16)
-    row_part = scale * jnp.dot(scaled, text_cols, preferred_element_type=f32)
+    resid = ((jax.nn.sigmoid(logits) - target) * (1.0 / ROWS)).astype(bf16)
+    row_part = scale * jnp.dot(resid, text[:ROWS, DT:], preferred_element_type=f32)
     col_part = scale * lax.dot_general(
-        scaled, image_rows, (((0,), (0,)), ((), ())), preferred_element_type=f32
-    )
-    return (row_part, col_part)
+        resid, image[:ROWS, DT:], OVER_ROWS, preferred_element_type=f32
+    )
+    return row_part, col_part
+
+
+def near_kernel(own, other, text, recv, rows, col0, col1):
+    row_a, col_a = tile(own, text)
+    row_b, col_b = tile(own, recv)
+    rows[:ROWS] = row_a + row_b
+    row_a, col_c = tile(other, text)
+    row_b, col_d = tile(other, recv)
+    rows[ROWS:] = row_a + row_b
+    col0[...] = col_a + col_c
+    col1[...] = col_b + col_d
+
+
+def exch_kernel(own, other, text, rows, col):
+    row_a, col_a = tile(own, text)
+    rows[:ROWS] = row_a
+    row_b, col_b = tile(other, text)
+    rows[ROWS:] = row_b
+    col[...] = (col_a + col_b).astype(bf16)
+
+
+def far_kernel(flag, own, other, beside, behind, rows, more_rows, own_rows, other_rows, col, text):
+    text[...] = jnp.where(flag[0] == 1, behind[...], beside[...])
+    row_a, col_a = tile(own, text)
+    row_b, col_b = tile(other, text)
+    col[...] = (col_a + col_b).astype(bf16)
+    own_rows[...] = row_a + rows[:ROWS] + more_rows[:ROWS]
+    other_rows[...] = (row_b + rows[ROWS:] + more_rows[ROWS:]).astype(bf16)
+
+
+def pairs(kernel, specs, outs, scratch, tiles, *args):
+    return pl.pallas_call(
+        kernel,
+        in_specs=specs,
+        out_specs=[VMEM] * len(outs),
+        out_shape=[jax.ShapeDtypeStruct(shape, dtype) for shape, dtype in outs],
+        scratch_shapes=scratch,
+        compiler_params=pltpu.CompilerParams(vmem_limit_bytes=48 * 2**20),
+        cost_estimate=pl.CostEstimate(
+            flops=tiles * 10**9, bytes_accessed=tiles * 3 * 2**20, transcendentals=0
+        ),
+    )(*args)
 
 
 def direction(unit, length, grad):
@@ -119,61 +214,54 @@
     core = lax.axis_index("core")
     first = core == 0
     back_route = [(i, i - 1 if i % 2 else (i - 3) % N_DP) for i in range(N_DP)]
-    step_route = [(i, (i + 1) % N_DP) for i in range(N_DP)]
-
-    teach_recv = chip_shift(teacher_text, 1)
-    teach_y = swap(teacher_image, "yh")
-    text_unit, text_len = unit_rows(jnp.dot(text_feats, text_proj, preferred_element_type=f32))
-    text_emb = text_unit.astype(bf16)
-    text_recv = chip_shift(text_emb, 1)
-    image_first, _ = lax.optimization_barrier((image_feats, text_emb))
-    image_unit, image_len = unit_rows(
-        jnp.dot(image_first, image_proj, preferred_element_type=f32)
-    )
-    image_emb = image_unit.astype(bf16)
-    image_y = swap(image_emb, "yh")
-    class_ids, teacher_later, text_later, _ = lax.optimization_barrier(
-        (class_ids, teacher_image, teacher_text, image_emb)
-    )
-    wide = text_later.astype(f32)
-    inverse = 1.0 / jnp.sqrt(jnp.sum(wide * wide, axis=1) + epsilon)
-    ids = class_ids.astype(f32)
-    notes = jnp.stack([ids, inverse] + [ids] * 6)
-    ids_y = swap(ids, "yh")
-    notes_recv = chip_shift(notes, 1)
-    teach_exch = swap(teach_recv, "core")
-    teach_far = along_dp(jnp.where(first, teacher_text, teach_recv), step_route)
-    text_exch = swap(text_recv, "core")
-    text_far = along_dp(jnp.where(first, text_emb, text_recv), step_route)
-    notes_exch = swap(notes_recv, "core")
-    notes_far = along_dp(jnp.where(first, notes, notes_recv), step_route)
-
-    def teacher_rows(rows):
-        unit, _ = unit_rows(jnp.dot(rows, teacher_proj, preferred_element_type=f32))
-        return unit.astype(bf16)
-
-    teacher_img = teacher_rows(teacher_later)
-    teacher_img_y = teacher_rows(teach_y)
+    ids = class_ids[None, :]
+    text_own, text_unit, text_len = embed(
+        text_kernel, 10**9, ids, text_feats, text_proj, teacher_text
+    )
+    ids, image_feats, teacher_image, text_own = lax.optimization_barrier(
+        (ids, image_feats, teacher_image, text_own)
+    )
+    recv = chip_shift(text_own, 1)
+    beside = along_dp(text_own, [(i, i + 1) for i in range(0, N_DP, 2)])
+    image_own, image_unit, image_len = embed(
+        image_kernel, 2 * 10**9, ids, image_feats, image_proj, teacher_image, teacher_proj
+    )
+    image_y = swap(image_own, "yh")
+    behind = along_dp(recv, [(i, (i + 1) % N_DP) for i in range(1, N_DP, 2)])
+    exch = swap(recv, "core")
 
     sent_feats = jnp.where(first, text_feats, image_feats)
     kept_feats = jnp.where(first, image_feats, text_feats)
     feats_in = swap(sent_feats, "core")
 
-    image_rows = jnp.concatenate([image_emb, image_y], axis=0)
-    teach_rows = jnp.concatenate([teacher_img, teacher_img_y], axis=0)
-    row_ids = jnp.concatenate([ids, ids_y], axis=0)[:, None]
-    rows = (teach_rows, image_rows, row_ids)
-    row0, col0 = pair_tile(*rows, teacher_text, text_emb, notes)
-    row1, col1 = pair_tile(*rows, teach_recv, text_recv, notes_recv)
-    row2, col2 = pair_tile(*rows, teach_exch, text_exch, notes_exch)
-    both = col1 + swap(col2.astype(bf16), "core").astype(f32)
-    both_back = chip_shift(both.astype(bf16), -1)
-    row3, col3 = pair_tile(*rows, teach_far, text_far, notes_far)
-    far_back = along_dp(col3.astype(bf16), back_route)
-    grad_rows = row0 + row1 + row2 + row3
-    half = text_emb.shape[0]
-    rows_y = swap(grad_rows[half:].astype(bf16), "yh")
-    grad_img = grad_rows[:half] + rows_y.astype(f32)
+    wide, narrow = ((2 * ROWS, DS), f32), ((ROWS, DS), bf16)
+    block = ((ROWS, DS), f32)
+    rows, col0, col1 = pairs(
+        near_kernel, [VMEM] * 4, [wide, block, block], [], 4, image_own, image_y, text_own, recv
+    )
+    more_rows, col2 = pairs(
+        exch_kernel, [VMEM] * 3, [wide, narrow], [], 2, image_own, image_y, exch
+    )
+    both = (col1 + swap(col2, "core").astype(f32)).astype(bf16)
+    both, behind = lax.optimization_barrier((both, behind))
+    both_back = chip_shift(both, -1)
+    own_rows, other_rows, col3 = pairs(
+        far_kernel,
+        [SMEM] + [VMEM] * 6,
+        [block, narrow, narrow],
+        [pltpu.VMEM((ROWS + PAD, DT + DS), bf16)],
+        2,
+        first.astype(jnp.int32)[None],
+        image_own,
+        image_y,
+        beside,
+        behind,
+        rows,
+        more_rows,
+    )
+    far_back = along_dp(col3, back_route)
+    rows_y = swap(other_rows, "yh")
+    grad_img = own_rows + rows_y.astype(f32)
     grad_txt = col0 + both_back.astype(f32) + far_back.astype(f32)
 
     img_high, img_low = direction(image_unit, image_len, grad_img)

time: 217 us -> 213 us (0.982)
  matrix products: 31.1 us -> 3.3 us
  Pallas kernels: 0 us -> 19.1 us
  waiting for transfers between devices: 57.7 us -> 76.3 us
  starting transfers between devices: 40.5 us -> 24.8 us
  local copies, waits for them, and re-layouts: 1.58 us -> 10.1 us
  blocking collectives: 72.5 us -> 65.6 us
    dot_general x20 -> x0, matrix products: 28.8 us -> none  [the longest x2 6.58 us: teacher_rows(): unit, _ = unit_rows(jnp.dot(rows, teacher_proj, preferred_element_type=f32))]
    pallas_call x0 -> x5, Pallas kernels: none -> 19.1 us  [the longest x3 13.1 us: pairs(): pl.pallas_call(kernel, in_specs=specs, out_specs=[VMEM] * len(outs), out_...]
    ppermute x8 -> x5, waiting for transfers between devices: 13.3 us -> 27.4 us  [along_dp(): return lax.ppermute(block, DP, route)]
    ppermute x15 -> x11, starting transfers between devices: 30.9 us -> 18.4 us  [swap(): return lax.ppermute(block, axis, [(0, 1), (1, 0)])]
    unnamed x29 -> x37, local copies, waits for them, and re-layouts: 0.45 us -> 9.72 us
    all_to_all x1, blocking collectives: 25.2 us -> 18.9 us  [sum_everywhere(): blocks = lax.all_to_all(blocks, 'z', 0, 0, tiled=True)]
    ppermute x15 -> x11, waiting for transfers between devices: 42.8 us -> 46.5 us  [swap(): return lax.ppermute(block, axis, [(0, 1), (1, 0)])]
    ppermute x8 -> x5, starting transfers between devices: 8.87 us -> 5.96 us  [along_dp(): return lax.ppermute(block, DP, route)]
  transfers between devices with their start and end apart: 24 -> 17, of which waited for: 9 -> 7; matrix products, arithmetic and copies ran while one was open for 18% -> 4% of each run, Pallas kernels for 0% -> 6%
where the time goes in v6:
time: 213 us
  waiting for transfers between devices  76.3 us (36%)
  blocking collectives  65.6 us (31%)
  starting transfers between devices  24.8 us (12%)
  Pallas kernels  19.1 us (9%)
  other arithmetic  11.7 us (5%)
  local copies, waits for them, and re-layouts  10.1 us (5%)
  matrix products  3.3 us (2%)
    ppermute x11, waiting for transfers between devices, swap(): return lax.ppermute(block, axis, [(0, 1), (1, 0)])  46.5 us
    ppermute x5, waiting for transfers between devices, along_dp(): return lax.ppermute(block, DP, route)  27.4 us
    all_to_all x1, blocking collectives, sum_everywhere(): blocks = lax.all_to_all(blocks, 'z', 0, 0, tiled=True)  18.9 us
    all_to_all x1, blocking collectives, sum_everywhere(): blocks = lax.all_to_all(blocks, 'x', 0, 0, tiled=True)  18.9 us
    ppermute x11, starting transfers between devices, swap(): return lax.ppermute(block, axis, [(0, 1), (1, 0)])  18.4 us
    all_to_all x1, blocking collectives, sum_everywhere(): own_total = lax.all_to_all(spread, 'x', 0, 0, tiled=True).reshape(ds, ds)  14.5 us
    all_to_all x1, blocking collectives, sum_everywhere(): lax.all_to_all(spread, 'z', 0, 0, tiled=True).reshape(ds // 4, ds)  13.4 us
    pallas_call x3, Pallas kernels, pairs(): pl.pallas_call(kernel, in_specs=specs, out_specs=[VMEM] * len(outs), out_...  13.1 us
  transfers between devices with their start and end apart: 17, of which 7 were waited for; matrix products, arithmetic and copies ran while one was open for 4% of the time, Pallas kernels for 6%

profile of v6, /device:TPU:1, one launch (start us, length us, event | category | flops | bytes accessed | tf_op | source)
XLA Modules:
  0.0 212.6 jit_solution(10421067685019451200)
XLA Ops:
  0.6 1.0 copy-done.7
  1.6 1.3 copy-done.11
  2.9 1.1 copy-done.13
  4.0 0.7 copy-done.15
  4.7 1.8 shard_map.95
  6.5 0.7 copy-done.9
  7.2 2.0 collective-permute-start.3
  9.2 4.2 %shard_map.96 = (bf16[272,2304]{1,0:T(8,128)(2,1)S(1)}, f32[256,768]{1,0:T(8,128)S(1)}, f32[256,1]{1,0:T(8,128)S(1)}) custom-call(s32[1,256]{1,0:T(1,128)S(1)} %bitcast.14, bf16[256,768]{1,0:T(8,128)(2,1)S(1)} %copy-done.6, bf16[768,768]{1,0:T(8,128)(2,1)S(1)} %copy-done.12, bf16[256,1536]{1,0:T(8,128)(2,1)S(1)} %copy-done.14, bf16[1536,1536]{1,0:T(8,128)(2,1)} %teacher_proj.1), custom_call_target="tpu_custom_call" | custom-call | flops 2000000000 | bytes 5242880 | tf_op jit(solution)/shard_map/pallas_call | solution.py:74
  13.5 0.6 copy-done.10
  14.1 2.9 %collective-permute-start.1 = (bf16[272,2304]{1,0:T(8,128)(2,1)S(1)}, bf16[272,2304]{1,0:T(8,128)(2,1)S(1)}, u32[]{:S(2)}, u32[]{:S(2)}) collective-permute-start(bf16[272,2304]{1,0:T(8,128)(2,1)S(1)} %get-tuple-element.26.own), channel_id=1, source_target_pairs={{0,1},{1,0},{2,3},{3,2},{4,5},{5,4},{6,7},{7,6},{8,9},{9,8},{10,11... | collective-permute-start | bytes 3760136 | tf_op jit(solution)/shard_map/ppermute | solution.py:28
  17.0 27.3 %collective-permute-done.3.recv = bf16[272,2304]{1,0:T(8,128)(2,1)} collective-permute-done((bf16[272,2304]{1,0:T(8,128)(2,1)}, bf16[272,2304]{1,0:T(8,128)(2,1)}, u32[]{:S(2)}, u32[]{:S(2)}) %collective-permute-start.3) | collective-permute-done | bytes 1253408 | tf_op jit(solution)/shard_map/ppermute | solution.py:32
  44.4 1.3 collective-permute-start.4
  45.7 2.3 %collective-permute-start.6 = (bf16[272,2304]{1,0:T(8,128)(2,1)}, bf16[272,2304]{1,0:T(8,128)(2,1)}, u32[]{:S(2)}, u32[]{:S(2)}) collective-permute-start(bf16[272,2304]{1,0:T(8,128)(2,1)} %collective-permute-done.3.recv), channel_id=1, source_target_pairs={{2,4},{6,8},{10,12},{14,16},{18,20},{22,24},{26,28},{30,32},{34,36... | collective-permute-start | bytes 3760136 | tf_op jit(solution)/shard_map/ppermute | solution.py:32
  48.0 1.3 collective-permute-start.2
  49.3 34.4 %collective-permute-done.1.other = bf16[272,2304]{1,0:T(8,128)(2,1)S(1)} collective-permute-done((bf16[272,2304]{1,0:T(8,128)(2,1)S(1)}, bf16[272,2304]{1,0:T(8,128)(2,1)S(1)}, u32[]{:S(2)}, u32[]{:S(2)}) %collective-permute-start.1) | collective-permute-done | bytes 1253408 | tf_op jit(solution)/shard_map/ppermute | solution.py:28
  83.8 1.7 shard_map.98
  85.5 1.1 copy-done
  86.7 2.1 collective-permute-start.5
  88.8 1.3 copy-done.2
  90.1 1.3 copy-done.4
  91.4 6.0 %shard_map.97 = (f32[512,768]{1,0:T(8,128)}, f32[256,768]{1,0:T(8,128)S(1)}, f32[256,768]{1,0:T(8,128)S(1)}) custom-call(bf16[272,2304]{1,0:T(8,128)(2,1)S(1)} %copy-done.2, bf16[272,2304]{1,0:T(8,128)(2,1)S(1)} %copy-done.4, bf16[272,2304]{1,0:T(8,128)(2,1)} %get-tuple-element.27.text, bf16[272,2304]{1,0:T(8,128)(2,1)} %collective-permute-done.3.recv), custom_call_target="tpu_custom_call" | custom-call | flops 4000000000 | bytes 12582912 | tf_op jit(solution)/shard_map/pallas_call | solution.py:143
  97.4 0.8 add_convert_fusion
  98.3 0.6 copy-done.5
  98.9 5.3 %shard_map.99 = (f32[256,768]{1,0:T(8,128)S(1)}, bf16[256,768]{1,0:T(8,128)(2,1)}, bf16[256,768]{1,0:T(8,128)(2,1)}) custom-call(s32[1]{0:T(128)} %bitcast.1.flag, bf16[272,2304]{1,0:T(8,128)(2,1)S(1)} %copy-done.2, bf16[272,2304]{1,0:T(8,128)(2,1)S(1)} %copy-done.5, bf16[272,2304]{1,0:T(8,128)(2,1)} %collective-permute-done.2.beside, ...), custom_call_target="tpu_custom_call" | custom-call | flops 2000000000 | bytes 6291456 | tf_op jit(solution)/shard_map/pallas_call | solution.py:143
  104.1 1.6 collective-permute-start.7
  106.0 0.9 broadcast_select_fusion.5
  107.0 1.0 reduce.2
  108.0 1.0 reduce.3
  109.0 7.7 %collective-permute-done.7 = bf16[256,768]{1,0:T(8,128)(2,1)} collective-permute-done((bf16[256,768]{1,0:T(8,128)(2,1)}, bf16[256,768]{1,0:T(8,128)(2,1)}, u32[]{:S(2)}, u32[]{:S(2)}) %collective-permute-start.7) | collective-permute-done | bytes 393248 | tf_op jit(solution)/shard_map/ppermute | solution.py:28
  116.7 1.2 multiply_reduce_fusion.2
  117.9 1.3 multiply_reduce_fusion.1
  119.2 1.6 broadcast_select_fusion.3
  121.1 2.1 collective-permute-start.11
  123.3 1.2 collective-permute-done.11
  124.5 0.8 fusion.5
  125.3 2.5 %abs_reduce_fusion = (f32[]{:T(128)}, f32[768,768]{1,0:T(8,128)S(1)}) fusion(f32[768,768]{1,0:T(8,128)S(1)} %fusion.5, bf16[256,768]{1,0:T(8,128)(2,1)S(1)} %collective-permute-done.10, bf16[256,768]{1,0:T(8,128)(2,1)S(1)} %get-tuple-element.45, bf16[256,768]{1,0:T(8,128)(2,1)} %copy-done.17, bf16[256,768]{1,0:T(8,128)(2,1)S(1)} %copy-done.16), kind=kOutput, calls=%fused_computation.6 | convolution fusion | flops 608894976 | bytes 6291460 | tf_op jit(solution)/shard_map/dot_general | solution.py:277
  129.0 18.9 %all_to_all.20 = f16[4,200,768]{2,1,0:T(8,128)(2,1)S(1)} all-to-all(f16[4,200,768]{2,1,0:T(8,128)(2,1)S(1)} %concatenate.21), channel_id=1, replica_groups=mesh['yl'=2,'z'=8,'x'=4,'core'=2,'yh'=2] {'x'}, dimensions={0} | all-to-all | bytes 2457600 | tf_op jit(solution)/shard_map/all_to_all | solution.py:181
  148.4 18.9 %all_to_all.21 = f16[8,32,768]{2,1,0:T(8,128)(2,1)S(1)} all-to-all(f16[8,32,768]{2,1,0:T(8,128)(2,1)S(1)} %pad_maximum_fusion.3), channel_id=1, replica_groups=mesh['yl'=2,'z'=8,'x'=4,'core'=2,'yh'=2] {'z'}, dimensions={0} | all-to-all | bytes 786432 | tf_op jit(solution)/shard_map/all_to_all | solution.py:185
  167.5 0.5 collective-permute-start.14
  167.9 1.7 collective-permute-start.13
  169.7 1.2 collective-permute-start.12
  170.8 2.5 %collective-permute-done.14 = f32[32,768]{1,0:T(8,128)S(1)} collective-permute-done((f32[32,768]{1,0:T(8,128)S(1)}, f32[32,768]{1,0:T(8,128)S(1)}, u32[]{:S(2)}, u32[]{:S(2)}) %collective-permute-start.14) | collective-permute-done | bytes 98336 | tf_op jit(solution)/shard_map/ppermute | solution.py:190
  173.3 0.6 collective-permute-done.12
  174.0 13.4 %all_to_all.22 = f16[8,24,768]{2,1,0:T(8,128)(2,1)S(1)} all-to-all(f16[8,24,768]{2,1,0:T(8,128)(2,1)S(1)} %broadcast_in_dim.47), channel_id=1, replica_groups=mesh['yl'=2,'z'=8,'x'=4,'core'=2,'yh'=2] {'z'}, dimensions={0} | all-to-all | bytes 589824 | tf_op jit(solution)/shard_map/all_to_all | solution.py:198
  187.4 14.5 %all_to_all.23 = f16[4,192,768]{2,1,0:T(8,128)(2,1)S(1)} all-to-all(f16[4,192,768]{2,1,0:T(8,128)(2,1)S(1)} %broadcast_in_dim.49), channel_id=1, replica_groups=mesh['yl'=2,'z'=8,'x'=4,'core'=2,'yh'=2] {'x'}, dimensions={0} | all-to-all | bytes 2359296 | tf_op jit(solution)/shard_map/all_to_all | solution.py:200
  201.9 5.4 %collective-permute-start.15 = (f16[768,768]{1,0:T(8,128)(2,1)S(1)}, f16[768,768]{1,0:T(8,128)(2,1)S(1)}, u32[]{:S(2)}, u32[]{:S(2)}) collective-permute-start(f16[768,768]{1,0:T(8,128)(2,1)S(1)} %bitcast.15), channel_id=1, source_target_pairs={{0,2},{2,0},{1,3},{3,1},{4,6},{6,4},{5,7},{7,5},{8,10},{10,8},{9,1... | collective-permute-start | bytes 3538952 | tf_op jit(solution)/shard_map/ppermute | solution.py:28
  207.3 2.5 %collective-permute-done.16 = f32[8,768]{1,0:T(8,128)S(1)} collective-permute-done((f32[8,768]{1,0:T(8,128)S(1)}, f32[8,768]{1,0:T(8,128)S(1)}, u32[]{:S(2)}, u32[]{:S(2)}) %collective-permute-start.16) | collective-permute-done | bytes 24608 | tf_op jit(solution)/shard_map/ppermute | solution.py:28
  209.9 2.7 %fusion = (f32[768,768]{1,0:T(8,128)}, f32[768,768]{1,0:T(8,128)}) fusion(f16[768,768]{1,0:T(8,128)(2,1)S(1)} %collective-permute-done.15, f32[768]{0:T(1024)S(1)} %fusion.21, f32[768]{0:T(1024)S(1)} %get-tuple-element.42, pred[]{:T(512)S(6)} %eq.3, f16[4,192,768]{2,1,0:T(8,128)(2,1)S(1)} %all_to_all.23), kind=kLoop, calls=%fused_computation.1 | loop fusion | flops 3538944 | bytes 7084033 | tf_op jit(solution)/shard_map/jit(_where)/select_n | solution.py:285
  (62 shorter events, 1.9 us)
Async XLA Ops:
  0.6 1.0 copy-start.7
  1.6 1.3 copy-start.11
  2.9 1.1 copy-start.13
  4.0 0.7 copy-start.15
  4.7 4.5 %copy-start.6 = (bf16[256,768]{1,0:T(8,128)(2,1)S(1)}, bf16[256,768]{1,0:T(8,128)(2,1)}, u32[]{:S(2)}) copy-start(bf16[256,768]{1,0:T(8,128)(2,1)} %feats.2) | copy-start | bytes 1179652
  4.7 4.5 %copy-start.12 = (bf16[768,768]{1,0:T(8,128)(2,1)S(1)}, bf16[768,768]{1,0:T(8,128)(2,1)}, u32[]{:S(2)}) copy-start(bf16[768,768]{1,0:T(8,128)(2,1)} %proj.3) | copy-start | bytes 3538948
  4.7 4.5 %copy-start.14 = (bf16[256,1536]{1,0:T(8,128)(2,1)S(1)}, bf16[256,1536]{1,0:T(8,128)(2,1)}, u32[]{:S(2)}) copy-start(bf16[256,1536]{1,0:T(8,128)(2,1)} %teacher.2) | copy-start | bytes 2359300
  6.5 0.7 copy-start.9
  7.2 37.2 %collective-permute-start.3 = (bf16[272,2304]{1,0:T(8,128)(2,1)}, bf16[272,2304]{1,0:T(8,128)(2,1)}, u32[]{:S(2)}, u32[]{:S(2)}) collective-permute-start(bf16[272,2304]{1,0:T(8,128)(2,1)} %get-tuple-element.27.text), channel_id=1, source_target_pairs={{0,4},{2,6},{4,8},{6,10},{8,12},{10,14},{12,16},{14,18},{16,20},{1... | collective-permute-start | bytes 3760136 | tf_op jit(solution)/shard_map/ppermute | solution.py:32
  13.5 0.6 copy-start.10
  14.1 71.4 %copy-start.1 = (bf16[272,2304]{1,0:T(8,128)(2,1)}, bf16[272,2304]{1,0:T(8,128)(2,1)S(1)}, u32[]{:S(2)}) copy-start(bf16[272,2304]{1,0:T(8,128)(2,1)S(1)} %get-tuple-element.26.own) | copy-start | bytes 3760132
  14.1 69.7 %collective-permute-start.1 = (bf16[272,2304]{1,0:T(8,128)(2,1)S(1)}, bf16[272,2304]{1,0:T(8,128)(2,1)S(1)}, u32[]{:S(2)}, u32[]{:S(2)}) collective-permute-start(bf16[272,2304]{1,0:T(8,128)(2,1)S(1)} %get-tuple-element.26.own), channel_id=1, source_target_pairs={{0,1},{1,0},{2,3},{3,2},{4,5},{5,4},{6,7},{7,6},{8,9},{9,8},{10,11... | collective-permute-start | bytes 3760136 | tf_op jit(solution)/shard_map/ppermute | solution.py:28
  44.4 39.4 %collective-permute-start.4 = (bf16[272,2304]{1,0:T(8,128)(2,1)}, bf16[272,2304]{1,0:T(8,128)(2,1)S(1)}, u32[]{:S(2)}, u32[]{:S(2)}) collective-permute-start(bf16[272,2304]{1,0:T(8,128)(2,1)} %collective-permute-done.3.recv), channel_id=1, source_target_pairs={{0,2},{2,0},{1,3},{3,1},{4,6},{6,4},{5,7},{7,5},{8,10},{10,8},{9,1... | collective-permute-start | bytes 3760136 | tf_op jit(solution)/shard_map/ppermute | solution.py:28
  45.7 52.6 %collective-permute-start.6 = (bf16[272,2304]{1,0:T(8,128)(2,1)}, bf16[272,2304]{1,0:T(8,128)(2,1)}, u32[]{:S(2)}, u32[]{:S(2)}) collective-permute-start(bf16[272,2304]{1,0:T(8,128)(2,1)} %collective-permute-done.3.recv), channel_id=1, source_target_pairs={{2,4},{6,8},{10,12},{14,16},{18,20},{22,24},{26,28},{30,32},{34,36... | collective-permute-start | bytes 3760136 | tf_op jit(solution)/shard_map/ppermute | solution.py:32
  48.0 50.2 %collective-permute-start.2 = (bf16[272,2304]{1,0:T(8,128)(2,1)}, bf16[272,2304]{1,0:T(8,128)(2,1)}, u32[]{:S(2)}, u32[]{:S(2)}) collective-permute-start(bf16[272,2304]{1,0:T(8,128)(2,1)} %get-tuple-element.27.text), channel_id=1, source_target_pairs={{0,2},{4,6},{8,10},{12,14},{16,18},{20,22},{24,26},{28,30},{32,34}... | collective-permute-start | bytes 3760136 | tf_op jit(solution)/shard_map/ppermute | solution.py:32
  83.8 1.8 copy-start.3
  85.5 1.1 copy-start
  86.7 10.7 %collective-permute-start.5 = (bf16[256,768]{1,0:T(8,128)(2,1)S(1)}, bf16[256,768]{1,0:T(8,128)(2,1)S(1)}, u32[]{:S(2)}, u32[]{:S(2)}) collective-permute-start(bf16[256,768]{1,0:T(8,128)(2,1)S(1)} %get-tuple-element.29), channel_id=1, source_target_pairs={{0,2},{2,0},{1,3},{3,1},{4,6},{6,4},{5,7},{7,5},{8,10},{10,8},{9,1... | collective-permute-start | bytes 1179656 | tf_op jit(solution)/shard_map/ppermute | solution.py:28
  88.8 1.3 copy-start.2
  90.1 1.3 copy-start.4
  97.4 1.4 copy-start.5
  98.8 7.2 %copy-start.8 = (bf16[256,768]{1,0:T(8,128)(2,1)S(1)}, bf16[256,768]{1,0:T(8,128)(2,1)}, u32[]{:S(2)}) copy-start(bf16[256,768]{1,0:T(8,128)(2,1)} %feats.1) | copy-start | bytes 1179652
  104.1 12.6 %collective-permute-start.7 = (bf16[256,768]{1,0:T(8,128)(2,1)}, bf16[256,768]{1,0:T(8,128)(2,1)}, u32[]{:S(2)}, u32[]{:S(2)}) collective-permute-start(bf16[256,768]{1,0:T(8,128)(2,1)} %get-tuple-element.34), channel_id=1, source_target_pairs={{0,1},{1,0},{2,3},{3,2},{4,5},{5,4},{6,7},{7,6},{8,9},{9,8},{10,11... | collective-permute-start | bytes 1179656 | tf_op jit(solution)/shard_map/ppermute | solution.py:28
  105.7 12.2 %collective-permute-start.9 = (bf16[256,768]{1,0:T(8,128)(2,1)}, bf16[256,768]{1,0:T(8,128)(2,1)}, u32[]{:S(2)}, u32[]{:S(2)}) collective-permute-start(bf16[256,768]{1,0:T(8,128)(2,1)} %get-tuple-element.39), channel_id=1, source_target_pairs={{0,250},{2,0},{4,254},{6,4},{8,2},{10,8},{12,6},{14,12},{16,10},{1... | collective-permute-start | bytes 1179656 | tf_op jit(solution)/shard_map/ppermute | solution.py:32
  106.0 11.9 %collective-permute-start.8 = (bf16[256,768]{1,0:T(8,128)(2,1)}, bf16[256,768]{1,0:T(8,128)(2,1)}, u32[]{:S(2)}, u32[]{:S(2)}) collective-permute-start(bf16[256,768]{1,0:T(8,128)(2,1)} %add_convert_fusion), channel_id=1, source_target_pairs={{0,252},{2,254},{4,0},{6,2},{8,4},{10,6},{12,8},{14,10},{16,12},{1... | collective-permute-start | bytes 1179656 | tf_op jit(solution)/shard_map/ppermute | solution.py:32
  106.9 16.3 %collective-permute-start = (bf16[256,768]{1,0:T(8,128)(2,1)}, bf16[256,768]{1,0:T(8,128)(2,1)S(1)}, u32[]{:S(2)}, u32[]{:S(2)}) collective-permute-start(bf16[256,768]{1,0:T(8,128)(2,1)} %get-tuple-element.56), channel_id=1, source_target_pairs={{0,2},{2,0},{1,3},{3,1},{4,6},{6,4},{5,7},{7,5},{8,10},{10,8},{9,1... | collective-permute-start | bytes 1179656 | tf_op jit(solution)/shard_map/ppermute | solution.py:28
  120.9 3.6 %copy-start.16 = (bf16[256,768]{1,0:T(8,128)(2,1)S(1)}, bf16[256,768]{1,0:T(8,128)(2,1)}, u32[]{:S(2)}) copy-start(bf16[256,768]{1,0:T(8,128)(2,1)} %get-tuple-element.55) | copy-start | bytes 1179652
  121.1 3.4 %collective-permute-start.11 = (bf16[256,768]{1,0:T(8,128)(2,1)S(1)}, bf16[256,768]{1,0:T(8,128)(2,1)S(1)}, u32[]{:S(2)}, u32[]{:S(2)}) collective-permute-start(bf16[256,768]{1,0:T(8,128)(2,1)S(1)} %get-tuple-element.52), channel_id=1, source_target_pairs={{0,2},{2,0},{1,3},{3,1},{4,6},{6,4},{5,7},{7,5},{8,10},{10,8},{9,1... | collective-permute-start | bytes 1179656 | tf_op jit(solution)/shard_map/ppermute | solution.py:28
  123.1 2.2 %collective-permute-start.10 = (bf16[256,768]{1,0:T(8,128)(2,1)S(1)}, bf16[256,768]{1,0:T(8,128)(2,1)S(1)}, u32[]{:S(2)}, u32[]{:S(2)}) collective-permute-start(bf16[256,768]{1,0:T(8,128)(2,1)S(1)} %get-tuple-element.50), channel_id=1, source_target_pairs={{0,2},{2,0},{1,3},{3,1},{4,6},{6,4},{5,7},{7,5},{8,10},{10,8},{9,1... | collective-permute-start | bytes 1179656 | tf_op jit(solution)/shard_map/ppermute | solution.py:28
  123.3 2.1 copy-start.17
  167.5 5.8 %collective-permute-start.14 = (f32[32,768]{1,0:T(8,128)S(1)}, f32[32,768]{1,0:T(8,128)S(1)}, u32[]{:S(2)}, u32[]{:S(2)}) collective-permute-start(f32[32,768]{1,0:T(8,128)S(1)} %pad_maximum_fusion.4), channel_id=1, source_target_pairs={{0,129},{1,128},{128,1},{129,0},{2,131},{3,130},{130,3},{131,2},{4... | collective-permute-start | bytes 294920 | tf_op jit(solution)/shard_map/ppermute | solution.py:190
  167.9 5.4 %collective-permute-start.13 = (f32[32,768]{1,0:T(8,128)S(1)}, f32[32,768]{1,0:T(8,128)S(1)}, u32[]{:S(2)}, u32[]{:S(2)}) collective-permute-start(f32[32,768]{1,0:T(8,128)S(1)} %pad_maximum_fusion.4), channel_id=1, source_target_pairs={{0,1},{1,0},{2,3},{3,2},{4,5},{5,4},{6,7},{7,6},{8,9},{9,8},{10,11... | collective-permute-start | bytes 294920 | tf_op jit(solution)/shard_map/ppermute | solution.py:28
  169.7 4.2 %collective-permute-start.12 = (f32[32,768]{1,0:T(8,128)S(1)}, f32[32,768]{1,0:T(8,128)S(1)}, u32[]{:S(2)}, u32[]{:S(2)}) collective-permute-start(f32[32,768]{1,0:T(8,128)S(1)} %pad_maximum_fusion.4), channel_id=1, source_target_pairs={{0,128},{128,0},{1,129},{129,1},{2,130},{130,2},{3,131},{131,3},{4... | collective-permute-start | bytes 294920 | tf_op jit(solution)/shard_map/ppermute | solution.py:28
  201.9 8.0 %collective-permute-start.15 = (f16[768,768]{1,0:T(8,128)(2,1)S(1)}, f16[768,768]{1,0:T(8,128)(2,1)S(1)}, u32[]{:S(2)}, u32[]{:S(2)}) collective-permute-start(f16[768,768]{1,0:T(8,128)(2,1)S(1)} %bitcast.15), channel_id=1, source_target_pairs={{0,2},{2,0},{1,3},{3,1},{4,6},{6,4},{5,7},{7,5},{8,10},{10,8},{9,1... | collective-permute-start | bytes 3538952 | tf_op jit(solution)/shard_map/ppermute | solution.py:28
  207.3 2.5 %collective-permute-start.16 = (f32[8,768]{1,0:T(8,128)S(1)}, f32[8,768]{1,0:T(8,128)S(1)}, u32[]{:S(2)}, u32[]{:S(2)}) collective-permute-start(f32[8,768]{1,0:T(8,128)S(1)} %broadcast_in_dim.51), channel_id=1, source_target_pairs={{0,2},{2,0},{1,3},{3,1},{4,6},{6,4},{5,7},{7,5},{8,10},{10,8},{9,1... | collective-permute-start | bytes 73736 | tf_op jit(solution)/shard_map/ppermute | solution.py:28

commit v7 on v6

--- a/solution.py
+++ b/solution.py
@@ -36,12 +36,20 @@
     return along_dp(block, [(i, (i + 2 * step) % N_DP) for i in range(N_DP)])
 
 
+def forward(block):
+    direct = along_dp(block, [(i, (i + 2) % N_DP) for i in range(N_DP) if i not in (62, 126)])
+    aside = along_dp(block, [(126, 56), (62, 120)])
+    return direct, aside
+
+
 VMEM = pl.BlockSpec(memory_space=pltpu.VMEM)
 SMEM = pl.BlockSpec(memory_space=pltpu.SMEM)
 ROWS = 256
 DT = 1536
 DS = 768
 PAD = 16
+FAR_COST = 40
+OWN_COST = 2
 
 
 def note_ids(ids, payload):
@@ -80,7 +88,7 @@
             jax.ShapeDtypeStruct((ROWS, DS), f32),
             jax.ShapeDtypeStruct((ROWS, 1), f32),
         ],
-        compiler_params=pltpu.CompilerParams(vmem_limit_bytes=48 * 2**20),
+        compiler_params=pltpu.CompilerParams(vmem_limit_bytes=28 * 2**20),
         cost_estimate=pl.CostEstimate(flops=flops, bytes_accessed=5 * 2**20, transcendentals=0),
     )(*args)
 
@@ -111,32 +119,36 @@
     return row_part, col_part
 
 
-def near_kernel(own, other, text, recv, rows, col0, col1):
-    row_a, col_a = tile(own, text)
-    row_b, col_b = tile(own, recv)
-    rows[:ROWS] = row_a + row_b
-    row_a, col_c = tile(other, text)
-    row_b, col_d = tile(other, recv)
-    rows[ROWS:] = row_a + row_b
-    col0[...] = col_a + col_c
-    col1[...] = col_b + col_d
-
-
-def exch_kernel(own, other, text, rows, col):
+def own_kernel(own, other, text, rows, col):
     row_a, col_a = tile(own, text)
     rows[:ROWS] = row_a
     row_b, col_b = tile(other, text)
     rows[ROWS:] = row_b
-    col[...] = (col_a + col_b).astype(bf16)
-
-
-def far_kernel(flag, own, other, beside, behind, rows, more_rows, own_rows, other_rows, col, text):
+    col[...] = col_a + col_b
+
+
+def near_kernel(
+    flags, own, other, direct, aside, exch, aside_exch, before, rows, col1, col2, recv, swapped
+):
+    recv[...] = jnp.where(flags[0] == 1, aside[...], direct[...])
+    swapped[...] = jnp.where(flags[1] == 1, aside_exch[...], exch[...])
+    row_a, col_a = tile(own, swapped)
+    row_b, col_b = tile(own, recv)
+    rows[:ROWS] = row_a + row_b + before[:ROWS]
+    row_a, col_c = tile(other, swapped)
+    row_b, col_d = tile(other, recv)
+    rows[ROWS:] = row_a + row_b + before[ROWS:]
+    col2[...] = (col_a + col_c).astype(bf16)
+    col1[...] = col_b + col_d
+
+
+def far_kernel(flag, own, other, beside, behind, rows, own_rows, other_rows, col, text):
     text[...] = jnp.where(flag[0] == 1, behind[...], beside[...])
     row_a, col_a = tile(own, text)
     row_b, col_b = tile(other, text)
     col[...] = (col_a + col_b).astype(bf16)
-    own_rows[...] = row_a + rows[:ROWS] + more_rows[:ROWS]
-    other_rows[...] = (row_b + rows[ROWS:] + more_rows[ROWS:]).astype(bf16)
+    own_rows[...] = row_a + rows[:ROWS]
+    other_rows[...] = (row_b + rows[ROWS:]).astype(bf16)
 
 
 def pairs(kernel, specs, outs, scratch, tiles, *args):
@@ -146,7 +158,7 @@
         out_specs=[VMEM] * len(outs),
         out_shape=[jax.ShapeDtypeStruct(shape, dtype) for shape, dtype in outs],
         scratch_shapes=scratch,
-        compiler_params=pltpu.CompilerParams(vmem_limit_bytes=48 * 2**20),
+        compiler_params=pltpu.CompilerParams(vmem_limit_bytes=28 * 2**20),
         cost_estimate=pl.CostEstimate(
             flops=tiles * 10**9, bytes_accessed=tiles * 3 * 2**20, transcendentals=0
         ),
@@ -221,14 +233,17 @@
     ids, image_feats, teacher_image, text_own = lax.optimization_barrier(
         (ids, image_feats, teacher_image, text_own)
     )
-    recv = chip_shift(text_own, 1)
+    recv, aside = forward(text_own)
     beside = along_dp(text_own, [(i, i + 1) for i in range(0, N_DP, 2)])
     image_own, image_unit, image_len = embed(
         image_kernel, 2 * 10**9, ids, image_feats, image_proj, teacher_image, teacher_proj
     )
     image_y = swap(image_own, "yh")
+    recv, aside, beside, image_later = lax.optimization_barrier((recv, aside, beside, image_own))
+    aside_exch = along_dp(aside, [(56, 1), (120, 65)])
+    aside = along_dp(aside, [(56, 0), (120, 64)])
     behind = along_dp(recv, [(i, (i + 1) % N_DP) for i in range(1, N_DP, 2)])
-    exch = swap(recv, "core")
+    exch = along_dp(recv, [(i, i ^ 1) for i in range(N_DP) if i not in (0, 64)])
 
     sent_feats = jnp.where(first, text_feats, image_feats)
     kept_feats = jnp.where(first, image_feats, text_feats)
@@ -236,28 +251,38 @@
 
     wide, narrow = ((2 * ROWS, DS), f32), ((ROWS, DS), bf16)
     block = ((ROWS, DS), f32)
-    rows, col0, col1 = pairs(
-        near_kernel, [VMEM] * 4, [wide, block, block], [], 4, image_own, image_y, text_own, recv
-    )
-    more_rows, col2 = pairs(
-        exch_kernel, [VMEM] * 3, [wide, narrow], [], 2, image_own, image_y, exch
+    rows, col0 = pairs(own_kernel, [VMEM] * 3, [wide, block], [], OWN_COST, image_later, image_y, text_own)
+    dp = lax.axis_index(DP) % 64
+    place = pltpu.VMEM((ROWS + PAD, DT + DS), bf16)
+    rows, col1, col2 = pairs(
+        near_kernel,
+        [SMEM] + [VMEM] * 7,
+        [wide, block, narrow],
+        [place] * 2,
+        4,
+        jnp.stack([dp == 0, dp == 1]).astype(jnp.int32),
+        image_later,
+        image_y,
+        recv,
+        aside,
+        exch,
+        aside_exch,
+        rows,
     )
     both = (col1 + swap(col2, "core").astype(f32)).astype(bf16)
-    both, behind = lax.optimization_barrier((both, behind))
     both_back = chip_shift(both, -1)
     own_rows, other_rows, col3 = pairs(
         far_kernel,
-        [SMEM] + [VMEM] * 6,
+        [SMEM] + [VMEM] * 5,
         [block, narrow, narrow],
-        [pltpu.VMEM((ROWS + PAD, DT + DS), bf16)],
-        2,
+        [place],
+        FAR_COST,
         first.astype(jnp.int32)[None],
-        image_own,
+        image_later,
         image_y,
         beside,
         behind,
         rows,
-        more_rows,
     )
     far_back = along_dp(col3, back_route)
     rows_y = swap(other_rows, "yh")

time: 213 us -> 214 us (level)
  starting transfers between devices: 24.8 us -> 36.1 us
  waiting for transfers between devices: 76.3 us -> 67.5 us
  Pallas kernels: 19.1 us -> 16.3 us
  local copies, waits for them, and re-layouts: 10.1 us -> 12.8 us
    ppermute x11 -> x10, waiting for transfers between devices: 46.5 us -> 24 us  [swap(): return lax.ppermute(block, axis, [(0, 1), (1, 0)])]
    ppermute x5 -> x9, waiting for transfers between devices: 27.4 us -> 41.8 us  [along_dp(): return lax.ppermute(block, DP, route)]
    ppermute x5 -> x9, starting transfers between devices: 5.96 us -> 19.5 us  [along_dp(): return lax.ppermute(block, DP, route)]
    pallas_call x2, Pallas kernels: 6.02 us -> 2.62 us  [embed(): pl.pallas_call(kernel, in_specs=[VMEM] * len(args), out_specs=[VMEM] * 3,...]
    unnamed x37 -> x43, local copies, waits for them, and re-layouts: 9.72 us -> 12.4 us
    all_to_all x1, blocking collectives: 18.9 us -> 16.5 us  [sum_everywhere(): blocks = lax.all_to_all(blocks, 'z', 0, 0, tiled=True)]
    ppermute x11 -> x10, starting transfers between devices: 18.4 us -> 16.7 us  [swap(): return lax.ppermute(block, axis, [(0, 1), (1, 0)])]
  transfers between devices with their start and end apart: 17 -> 20, of which waited for: 7 -> 9; matrix products, arithmetic and copies ran while one was open for 4% -> 4% of each run, Pallas kernels for 6% -> 7%
where the time goes in v7:
time: 214 us; the launch traced here: 213 us
  waiting for transfers between devices  67.5 us (32%)
  blocking collectives  63.8 us (30%)
  starting transfers between devices  36.1 us (17%)
  Pallas kernels  16.3 us (8%)
  local copies, waits for them, and re-layouts  12.8 us (6%)
  other arithmetic  11.8 us (6%)
  matrix products  3.3 us (2%)
    ppermute x9, waiting for transfers between devices, along_dp(): return lax.ppermute(block, DP, route)  41.8 us
    ppermute x10, waiting for transfers between devices, swap(): return lax.ppermute(block, axis, [(0, 1), (1, 0)])  24 us
    ppermute x9, starting transfers between devices, along_dp(): return lax.ppermute(block, DP, route)  19.5 us
    all_to_all x1, blocking collectives, sum_everywhere(): blocks = lax.all_to_all(blocks, 'x', 0, 0, tiled=True)  18.9 us
    ppermute x10, starting transfers between devices, swap(): return lax.ppermute(block, axis, [(0, 1), (1, 0)])  16.7 us
    all_to_all x1, blocking collectives, sum_everywhere(): blocks = lax.all_to_all(blocks, 'z', 0, 0, tiled=True)  16.5 us
    all_to_all x1, blocking collectives, sum_everywhere(): own_total = lax.all_to_all(spread, 'x', 0, 0, tiled=True).reshape(ds, ds)  14.5 us
    all_to_all x1, blocking collectives, sum_everywhere(): lax.all_to_all(spread, 'z', 0, 0, tiled=True).reshape(ds // 4, ds)  14 us
  transfers between devices with their start and end apart: 20, of which 9 were waited for; matrix products, arithmetic and copies ran while one was open for 4% of the time, Pallas kernels for 7%

profile of v7, /device:TPU:1, one launch (start us, length us, event | category | flops | bytes accessed | tf_op | source)
XLA Modules:
  0.0 213.4 jit_solution(7797144975438170680)
XLA Ops:
  0.6 1.0 copy-done.1
  1.6 1.3 copy-done.13
  2.9 1.1 copy-done.15
  4.7 0.7 shard_map.95
  6.1 3.9 %collective-permute-start.1 = (bf16[272,2304]{1,0:T(8,128)(2,1)S(1)}, bf16[272,2304]{1,0:T(8,128)(2,1)}, u32[]{:S(2)}, u32[]{:S(2)}) collective-permute-start(bf16[272,2304]{1,0:T(8,128)(2,1)S(1)} %get-tuple-element.26.text), channel_id=1, source_target_pairs={{0,4},{2,6},{4,8},{6,10},{8,12},{10,14},{12,16},{14,18},{16,20},{1... | collective-permute-start | bytes 3760136 | tf_op jit(solution)/shard_map/ppermute | solution.py:32
  10.1 1.8 collective-permute-start.2
  11.8 1.3 collective-permute-start.3
  13.2 2.3 %copy-done.5 = bf16[1536,1536]{1,0:T(8,128)(2,1)S(1)} copy-done((bf16[1536,1536]{1,0:T(8,128)(2,1)S(1)}, bf16[1536,1536]{1,0:T(8,128)(2,1)}, u32[]{:S(2)}) %copy-start.5) | copy-done | bytes 4718616
  15.5 1.9 shard_map.96
  18.1 2.9 %collective-permute-start.4 = (bf16[272,2304]{1,0:T(8,128)(2,1)S(1)}, bf16[272,2304]{1,0:T(8,128)(2,1)}, u32[]{:S(2)}, u32[]{:S(2)}) collective-permute-start(bf16[272,2304]{1,0:T(8,128)(2,1)S(1)} %get-tuple-element.30.own), channel_id=1, source_target_pairs={{0,1},{1,0},{2,3},{3,2},{4,5},{5,4},{6,7},{7,6},{8,9},{9,8},{10,11... | collective-permute-start | bytes 3760136 | tf_op jit(solution)/shard_map/ppermute | solution.py:28
  21.0 1.0 copy-done.8
  22.0 14.3 %collective-permute-done.1.direct = bf16[272,2304]{1,0:T(8,128)(2,1)} collective-permute-done((bf16[272,2304]{1,0:T(8,128)(2,1)S(1)}, bf16[272,2304]{1,0:T(8,128)(2,1)}, u32[]{:S(2)}, u32[]{:S(2)}) %collective-permute-start.1) | collective-permute-done | bytes 1253408 | tf_op jit(solution)/shard_map/ppermute | solution.py:32
  36.3 1.0 copy-done.6
  37.3 4.6 %collective-permute-start.7 = (bf16[272,2304]{1,0:T(8,128)(2,1)}, bf16[272,2304]{1,0:T(8,128)(2,1)}, u32[]{:S(2)}, u32[]{:S(2)}) collective-permute-start(bf16[272,2304]{1,0:T(8,128)(2,1)} %collective-permute-done.1.direct), channel_id=1, source_target_pairs={{2,0},{4,6},{6,4},{8,10},{10,8},{12,14},{14,12},{16,18},{18,16},{2... | collective-permute-start | bytes 3760136 | tf_op jit(solution)/shard_map/ppermute | solution.py:32
  41.9 1.7 collective-permute-start.6
  43.6 1.3 collective-permute-start.8
  44.9 4.4 %collective-permute-start.5 = (bf16[272,2304]{1,0:T(8,128)(2,1)}, bf16[272,2304]{1,0:T(8,128)(2,1)}, u32[]{:S(2)}, u32[]{:S(2)}) collective-permute-start(bf16[272,2304]{1,0:T(8,128)(2,1)} %collective-permute-done.1.direct), channel_id=1, source_target_pairs={{2,4},{6,8},{10,12},{14,16},{18,20},{22,24},{26,28},{30,32},{34,36... | collective-permute-start | bytes 3760136 | tf_op jit(solution)/shard_map/ppermute | solution.py:32
  49.4 11.4 %collective-permute-done.4.other = bf16[272,2304]{1,0:T(8,128)(2,1)} collective-permute-done((bf16[272,2304]{1,0:T(8,128)(2,1)S(1)}, bf16[272,2304]{1,0:T(8,128)(2,1)}, u32[]{:S(2)}, u32[]{:S(2)}) %collective-permute-start.4) | collective-permute-done | bytes 1253408 | tf_op jit(solution)/shard_map/ppermute | solution.py:28
  60.8 1.3 copy-done.9
  62.1 1.3 copy-done.12
  63.4 3.1 %shard_map.97 = (f32[512,768]{1,0:T(8,128)S(1)}, f32[256,768]{1,0:T(8,128)S(1)}) custom-call(bf16[272,2304]{1,0:T(8,128)(2,1)S(1)} %copy-done.9, bf16[272,2304]{1,0:T(8,128)(2,1)} %collective-permute-done.4.other, bf16[272,2304]{1,0:T(8,128)(2,1)S(1)} %copy-done.12), custom_call_target="tpu_custom_call" | custom-call | flops 2000000000 | bytes 6291456 | tf_op jit(solution)/shard_map/pallas_call | solution.py:155
  66.6 27.1 %collective-permute-done.8.aside_exch = bf16[272,2304]{1,0:T(8,128)(2,1)} collective-permute-done((bf16[272,2304]{1,0:T(8,128)(2,1)}, bf16[272,2304]{1,0:T(8,128)(2,1)}, u32[]{:S(2)}, u32[]{:S(2)}) %collective-permute-start.8) | collective-permute-done | bytes 1253408 | tf_op jit(solution)/shard_map/ppermute | solution.py:32
  93.7 6.3 %shard_map.98 = (f32[512,768]{1,0:T(8,128)S(1)}, f32[256,768]{1,0:T(8,128)S(1)}, bf16[256,768]{1,0:T(8,128)(2,1)S(1)}) custom-call(s32[2]{0:T(128)S(1)} %add_convert_fusion.2.flags, bf16[272,2304]{1,0:T(8,128)(2,1)S(1)} %copy-done.10, bf16[272,2304]{1,0:T(8,128)(2,1)} %collective-permute-done.4.other, bf16[272,2304]{1,0:T(8,128)(2,1)} %collective-permute-done.1.direct, ...), custom_call_target="tpu_custom_call" | custom-call | flops 4000000000 | bytes 12582912 | tf_op jit(solution)/shard_map/pallas_call | solution.py:155
  100.1 4.2 %shard_map.99 = (f32[256,768]{1,0:T(8,128)S(1)}, bf16[256,768]{1,0:T(8,128)(2,1)}, bf16[256,768]{1,0:T(8,128)(2,1)}) custom-call(s32[1]{0:T(128)} %bitcast.1.flag, bf16[272,2304]{1,0:T(8,128)(2,1)S(1)} %copy-done.10, bf16[272,2304]{1,0:T(8,128)(2,1)} %collective-permute-done.4.other, bf16[272,2304]{1,0:T(8,128)(2,1)S(1)} %copy-done.7, ...), custom_call_target="tpu_custom_call" | custom-call | flops 40000000000 | bytes 125829120 | tf_op jit(solution)/shard_map/pallas_call | solution.py:155
  104.8 2.6 %collective-permute-start.9 = (bf16[256,768]{1,0:T(8,128)(2,1)}, bf16[256,768]{1,0:T(8,128)(2,1)}, u32[]{:S(2)}, u32[]{:S(2)}) collective-permute-start(bf16[256,768]{1,0:T(8,128)(2,1)} %get-tuple-element.37), channel_id=1, source_target_pairs={{0,1},{1,0},{2,3},{3,2},{4,5},{5,4},{6,7},{7,6},{8,9},{9,8},{10,11... | collective-permute-start | bytes 1179656 | tf_op jit(solution)/shard_map/ppermute | solution.py:28
  107.5 0.8 add_convert_fusion
  108.3 1.0 broadcast_select_fusion.5
  109.6 1.0 reduce.2
  110.6 1.0 reduce.3
  111.6 5.8 %collective-permute-done.9 = bf16[256,768]{1,0:T(8,128)(2,1)} collective-permute-done((bf16[256,768]{1,0:T(8,128)(2,1)}, bf16[256,768]{1,0:T(8,128)(2,1)}, u32[]{:S(2)}, u32[]{:S(2)}) %collective-permute-start.9) | collective-permute-done | bytes 393248 | tf_op jit(solution)/shard_map/ppermute | solution.py:28
  117.4 1.2 multiply_reduce_fusion.2
  119.0 1.3 multiply_reduce_fusion.1
  120.4 1.6 broadcast_select_fusion.3
  122.2 1.2 collective-permute-start.14
  123.5 1.2 collective-permute-done.14
  124.8 0.8 fusion.5
  125.6 2.5 %abs_reduce_fusion = (f32[]{:T(128)}, f32[768,768]{1,0:T(8,128)S(1)}) fusion(f32[768,768]{1,0:T(8,128)S(1)} %fusion.5, bf16[256,768]{1,0:T(8,128)(2,1)S(1)} %collective-permute-done.13, bf16[256,768]{1,0:T(8,128)(2,1)S(1)} %get-tuple-element.49, bf16[256,768]{1,0:T(8,128)(2,1)} %copy-done.20, bf16[256,768]{1,0:T(8,128)(2,1)S(1)} %copy-done.19), kind=kOutput, calls=%fused_computation.6 | convolution fusion | flops 608894976 | bytes 6291460 | tf_op jit(solution)/shard_map/dot_general | solution.py:302
  129.3 18.9 %all_to_all.20 = f16[4,200,768]{2,1,0:T(8,128)(2,1)S(1)} all-to-all(f16[4,200,768]{2,1,0:T(8,128)(2,1)S(1)} %concatenate.21), channel_id=1, replica_groups=mesh['yl'=2,'z'=8,'x'=4,'core'=2,'yh'=2] {'x'}, dimensions={0} | all-to-all | bytes 2457600 | tf_op jit(solution)/shard_map/all_to_all | solution.py:193
  148.7 16.5 %all_to_all.21 = f16[8,32,768]{2,1,0:T(8,128)(2,1)S(1)} all-to-all(f16[8,32,768]{2,1,0:T(8,128)(2,1)S(1)} %pad_maximum_fusion.3), channel_id=1, replica_groups=mesh['yl'=2,'z'=8,'x'=4,'core'=2,'yh'=2] {'z'}, dimensions={0} | all-to-all | bytes 786432 | tf_op jit(solution)/shard_map/all_to_all | solution.py:197
  165.4 1.4 collective-permute-start.15
  166.7 2.6 %collective-permute-start.16 = (f32[32,768]{1,0:T(8,128)S(1)}, f32[32,768]{1,0:T(8,128)S(1)}, u32[]{:S(2)}, u32[]{:S(2)}) collective-permute-start(f32[32,768]{1,0:T(8,128)S(1)} %pad_maximum_fusion.4), channel_id=1, source_target_pairs={{0,1},{1,0},{2,3},{3,2},{4,5},{5,4},{6,7},{7,6},{8,9},{9,8},{10,11... | collective-permute-start | bytes 294920 | tf_op jit(solution)/shard_map/ppermute | solution.py:28
  169.4 3.0 %collective-permute-done.16 = f32[32,768]{1,0:T(8,128)S(1)} collective-permute-done((f32[32,768]{1,0:T(8,128)S(1)}, f32[32,768]{1,0:T(8,128)S(1)}, u32[]{:S(2)}, u32[]{:S(2)}) %collective-permute-start.16) | collective-permute-done | bytes 98336 | tf_op jit(solution)/shard_map/ppermute | solution.py:28
  172.4 1.6 collective-permute-done.17
  174.1 14.0 %all_to_all.22 = f16[8,24,768]{2,1,0:T(8,128)(2,1)S(1)} all-to-all(f16[8,24,768]{2,1,0:T(8,128)(2,1)S(1)} %broadcast_in_dim.47), channel_id=1, replica_groups=mesh['yl'=2,'z'=8,'x'=4,'core'=2,'yh'=2] {'z'}, dimensions={0} | all-to-all | bytes 589824 | tf_op jit(solution)/shard_map/all_to_all | solution.py:210
  188.2 14.5 %all_to_all.23 = f16[4,192,768]{2,1,0:T(8,128)(2,1)S(1)} all-to-all(f16[4,192,768]{2,1,0:T(8,128)(2,1)S(1)} %broadcast_in_dim.49), channel_id=1, replica_groups=mesh['yl'=2,'z'=8,'x'=4,'core'=2,'yh'=2] {'x'}, dimensions={0} | all-to-all | bytes 2359296 | tf_op jit(solution)/shard_map/all_to_all | solution.py:212
  202.7 5.4 %collective-permute-start.18 = (f16[768,768]{1,0:T(8,128)(2,1)S(1)}, f16[768,768]{1,0:T(8,128)(2,1)S(1)}, u32[]{:S(2)}, u32[]{:S(2)}) collective-permute-start(f16[768,768]{1,0:T(8,128)(2,1)S(1)} %bitcast.17), channel_id=1, source_target_pairs={{0,2},{2,0},{1,3},{3,1},{4,6},{6,4},{5,7},{7,5},{8,10},{10,8},{9,1... | collective-permute-start | bytes 3538952 | tf_op jit(solution)/shard_map/ppermute | solution.py:28
  208.1 2.5 %collective-permute-done.19 = f32[8,768]{1,0:T(8,128)S(1)} collective-permute-done((f32[8,768]{1,0:T(8,128)S(1)}, f32[8,768]{1,0:T(8,128)S(1)}, u32[]{:S(2)}, u32[]{:S(2)}) %collective-permute-start.19) | collective-permute-done | bytes 24608 | tf_op jit(solution)/shard_map/ppermute | solution.py:28
  210.6 2.7 %fusion = (f32[768,768]{1,0:T(8,128)}, f32[768,768]{1,0:T(8,128)}) fusion(f16[768,768]{1,0:T(8,128)(2,1)S(1)} %collective-permute-done.18, f32[768]{0:T(1024)S(1)} %fusion.21, f32[768]{0:T(1024)S(1)} %get-tuple-element.46, pred[]{:T(512)S(6)} %eq.11, f16[4,192,768]{2,1,0:T(8,128)(2,1)S(1)} %all_to_all.23), kind=kLoop, calls=%fused_computation.1 | loop fusion | flops 3538944 | bytes 7084033 | tf_op jit(solution)/shard_map/jit(_where)/select_n | solution.py:310
  (75 shorter events, 5.0 us)
Async XLA Ops:
  0.6 1.0 copy-start.1
  1.6 1.3 copy-start.13
  2.9 1.1 copy-start.15
  4.0 0.7 copy-start.17
  4.7 8.4 %copy-start = (bf16[256,768]{1,0:T(8,128)(2,1)S(1)}, bf16[256,768]{1,0:T(8,128)(2,1)}, u32[]{:S(2)}) copy-start(bf16[256,768]{1,0:T(8,128)(2,1)} %feats.2) | copy-start | bytes 1179652
  4.7 8.4 %copy-start.14 = (bf16[768,768]{1,0:T(8,128)(2,1)S(1)}, bf16[768,768]{1,0:T(8,128)(2,1)}, u32[]{:S(2)}) copy-start(bf16[768,768]{1,0:T(8,128)(2,1)} %proj.3) | copy-start | bytes 3538948
  4.7 8.4 %copy-start.16 = (bf16[256,1536]{1,0:T(8,128)(2,1)S(1)}, bf16[256,1536]{1,0:T(8,128)(2,1)}, u32[]{:S(2)}) copy-start(bf16[256,1536]{1,0:T(8,128)(2,1)} %teacher.2) | copy-start | bytes 2359300
  4.7 8.4 %copy-start.18 = (s32[256]{0:T(256)S(1)}, s32[256]{0:T(256)}, u32[]{:S(2)}) copy-start(s32[256]{0:T(256)} %param.15) | copy-start | bytes 3076
  5.5 0.7 copy-start.3
  6.1 11.3 %copy-start.11 = (bf16[272,2304]{1,0:T(8,128)(2,1)}, bf16[272,2304]{1,0:T(8,128)(2,1)S(1)}, u32[]{:S(2)}) copy-start(bf16[272,2304]{1,0:T(8,128)(2,1)S(1)} %get-tuple-element.26.text) | copy-start | bytes 3760132
  6.1 30.1 %collective-permute-start.1 = (bf16[272,2304]{1,0:T(8,128)(2,1)S(1)}, bf16[272,2304]{1,0:T(8,128)(2,1)}, u32[]{:S(2)}, u32[]{:S(2)}) collective-permute-start(bf16[272,2304]{1,0:T(8,128)(2,1)S(1)} %get-tuple-element.26.text), channel_id=1, source_target_pairs={{0,4},{2,6},{4,8},{6,10},{8,12},{10,14},{12,16},{14,18},{16,20},{1... | collective-permute-start | bytes 3760136 | tf_op jit(solution)/shard_map/ppermute | solution.py:32
  10.1 26.2 %collective-permute-start.2 = (bf16[272,2304]{1,0:T(8,128)(2,1)S(1)}, bf16[272,2304]{1,0:T(8,128)(2,1)}, u32[]{:S(2)}, u32[]{:S(2)}) collective-permute-start(bf16[272,2304]{1,0:T(8,128)(2,1)S(1)} %get-tuple-element.26.text), channel_id=1, source_target_pairs={{252,112},{124,240},{253,113},{125,241}} | collective-permute-start | bytes 3760136 | tf_op jit(solution)/shard_map/ppermute | solution.py:32
  11.8 24.4 %collective-permute-start.3 = (bf16[272,2304]{1,0:T(8,128)(2,1)S(1)}, bf16[272,2304]{1,0:T(8,128)(2,1)S(1)}, u32[]{:S(2)}, u32[]{:S(2)}) collective-permute-start(bf16[272,2304]{1,0:T(8,128)(2,1)S(1)} %get-tuple-element.26.text), channel_id=1, source_target_pairs={{0,2},{4,6},{8,10},{12,14},{16,18},{20,22},{24,26},{28,30},{32,34}... | collective-permute-start | bytes 3760136 | tf_op jit(solution)/shard_map/ppermute | solution.py:32
  13.2 2.3 %copy-start.5 = (bf16[1536,1536]{1,0:T(8,128)(2,1)S(1)}, bf16[1536,1536]{1,0:T(8,128)(2,1)}, u32[]{:S(2)}) copy-start(bf16[1536,1536]{1,0:T(8,128)(2,1)} %teacher_proj.1) | copy-start | bytes 14155780
  17.4 0.7 copy-start.4
  18.1 42.7 %collective-permute-start.4 = (bf16[272,2304]{1,0:T(8,128)(2,1)S(1)}, bf16[272,2304]{1,0:T(8,128)(2,1)}, u32[]{:S(2)}, u32[]{:S(2)}) collective-permute-start(bf16[272,2304]{1,0:T(8,128)(2,1)S(1)} %get-tuple-element.30.own), channel_id=1, source_target_pairs={{0,1},{1,0},{2,3},{3,2},{4,5},{5,4},{6,7},{7,6},{8,9},{9,8},{10,11... | collective-permute-start | bytes 3760136 | tf_op jit(solution)/shard_map/ppermute | solution.py:28
  21.0 1.0 copy-start.8
  36.3 1.0 copy-start.6
  37.3 29.2 %collective-permute-start.7 = (bf16[272,2304]{1,0:T(8,128)(2,1)}, bf16[272,2304]{1,0:T(8,128)(2,1)}, u32[]{:S(2)}, u32[]{:S(2)}) collective-permute-start(bf16[272,2304]{1,0:T(8,128)(2,1)} %collective-permute-done.1.direct), channel_id=1, source_target_pairs={{2,0},{4,6},{6,4},{8,10},{10,8},{12,14},{14,12},{16,18},{18,16},{2... | collective-permute-start | bytes 3760136 | tf_op jit(solution)/shard_map/ppermute | solution.py:32
  41.9 24.6 %collective-permute-start.6 = (bf16[272,2304]{1,0:T(8,128)(2,1)}, bf16[272,2304]{1,0:T(8,128)(2,1)}, u32[]{:S(2)}, u32[]{:S(2)}) collective-permute-start(bf16[272,2304]{1,0:T(8,128)(2,1)} %collective-permute-done.2), channel_id=1, source_target_pairs={{112,0},{240,128},{113,1},{241,129}} | collective-permute-start | bytes 3760136 | tf_op jit(solution)/shard_map/ppermute | solution.py:32
  43.6 50.1 %collective-permute-start.8 = (bf16[272,2304]{1,0:T(8,128)(2,1)}, bf16[272,2304]{1,0:T(8,128)(2,1)}, u32[]{:S(2)}, u32[]{:S(2)}) collective-permute-start(bf16[272,2304]{1,0:T(8,128)(2,1)} %collective-permute-done.2), channel_id=1, source_target_pairs={{112,2},{240,130},{113,3},{241,131}} | collective-permute-start | bytes 3760136 | tf_op jit(solution)/shard_map/ppermute | solution.py:32
  44.9 55.2 %collective-permute-start.5 = (bf16[272,2304]{1,0:T(8,128)(2,1)}, bf16[272,2304]{1,0:T(8,128)(2,1)}, u32[]{:S(2)}, u32[]{:S(2)}) collective-permute-start(bf16[272,2304]{1,0:T(8,128)(2,1)} %collective-permute-done.1.direct), channel_id=1, source_target_pairs={{2,4},{6,8},{10,12},{14,16},{18,20},{22,24},{26,28},{30,32},{34,36... | collective-permute-start | bytes 3760136 | tf_op jit(solution)/shard_map/ppermute | solution.py:32
  60.8 1.3 copy-start.9
  62.1 1.3 copy-start.12
  63.4 30.3 %copy-start.10 = (bf16[272,2304]{1,0:T(8,128)(2,1)S(1)}, bf16[272,2304]{1,0:T(8,128)(2,1)}, u32[]{:S(2)}) copy-start(bf16[272,2304]{1,0:T(8,128)(2,1)} %copy-done.8) | copy-start | bytes 3760132
  93.7 6.4 %copy-start.7 = (bf16[272,2304]{1,0:T(8,128)(2,1)S(1)}, bf16[272,2304]{1,0:T(8,128)(2,1)}, u32[]{:S(2)}) copy-start(bf16[272,2304]{1,0:T(8,128)(2,1)} %copy-done.6) | copy-start | bytes 3760132
  100.0 7.5 %collective-permute-start.10 = (bf16[256,768]{1,0:T(8,128)(2,1)S(1)}, bf16[256,768]{1,0:T(8,128)(2,1)S(1)}, u32[]{:S(2)}, u32[]{:S(2)}) collective-permute-start(bf16[256,768]{1,0:T(8,128)(2,1)S(1)} %get-tuple-element.42), channel_id=1, source_target_pairs={{0,2},{2,0},{1,3},{3,1},{4,6},{6,4},{5,7},{7,5},{8,10},{10,8},{9,1... | collective-permute-start | bytes 1179656 | tf_op jit(solution)/shard_map/ppermute | solution.py:28
  104.4 3.9 %copy-start.2 = (bf16[256,768]{1,0:T(8,128)(2,1)S(1)}, bf16[256,768]{1,0:T(8,128)(2,1)}, u32[]{:S(2)}) copy-start(bf16[256,768]{1,0:T(8,128)(2,1)} %feats.1) | copy-start | bytes 1179652
  104.4 14.2 %collective-permute-start.12 = (bf16[256,768]{1,0:T(8,128)(2,1)}, bf16[256,768]{1,0:T(8,128)(2,1)}, u32[]{:S(2)}, u32[]{:S(2)}) collective-permute-start(bf16[256,768]{1,0:T(8,128)(2,1)} %get-tuple-element.43), channel_id=1, source_target_pairs={{0,250},{2,0},{4,254},{6,4},{8,2},{10,8},{12,6},{14,12},{16,10},{1... | collective-permute-start | bytes 1179656 | tf_op jit(solution)/shard_map/ppermute | solution.py:32
  104.8 12.5 %collective-permute-start.9 = (bf16[256,768]{1,0:T(8,128)(2,1)}, bf16[256,768]{1,0:T(8,128)(2,1)}, u32[]{:S(2)}, u32[]{:S(2)}) collective-permute-start(bf16[256,768]{1,0:T(8,128)(2,1)} %get-tuple-element.37), channel_id=1, source_target_pairs={{0,1},{1,0},{2,3},{3,2},{4,5},{5,4},{6,7},{7,6},{8,9},{9,8},{10,11... | collective-permute-start | bytes 1179656 | tf_op jit(solution)/shard_map/ppermute | solution.py:28
  108.3 10.7 %collective-permute-start.11 = (bf16[256,768]{1,0:T(8,128)(2,1)}, bf16[256,768]{1,0:T(8,128)(2,1)}, u32[]{:S(2)}, u32[]{:S(2)}) collective-permute-start(bf16[256,768]{1,0:T(8,128)(2,1)} %add_convert_fusion), channel_id=1, source_target_pairs={{0,252},{2,254},{4,0},{6,2},{8,4},{10,6},{12,8},{14,10},{16,12},{1... | collective-permute-start | bytes 1179656 | tf_op jit(solution)/shard_map/ppermute | solution.py:32
  109.3 14.3 %collective-permute-start = (bf16[256,768]{1,0:T(8,128)(2,1)}, bf16[256,768]{1,0:T(8,128)(2,1)S(1)}, u32[]{:S(2)}, u32[]{:S(2)}) collective-permute-start(bf16[256,768]{1,0:T(8,128)(2,1)} %get-tuple-element.60), channel_id=1, source_target_pairs={{0,2},{2,0},{1,3},{3,1},{4,6},{6,4},{5,7},{7,5},{8,10},{10,8},{9,1... | collective-permute-start | bytes 1179656 | tf_op jit(solution)/shard_map/ppermute | solution.py:28
  122.0 2.8 %copy-start.19 = (bf16[256,768]{1,0:T(8,128)(2,1)S(1)}, bf16[256,768]{1,0:T(8,128)(2,1)}, u32[]{:S(2)}) copy-start(bf16[256,768]{1,0:T(8,128)(2,1)} %get-tuple-element.59) | copy-start | bytes 1179652
  122.2 2.6 %collective-permute-start.14 = (bf16[256,768]{1,0:T(8,128)(2,1)S(1)}, bf16[256,768]{1,0:T(8,128)(2,1)S(1)}, u32[]{:S(2)}, u32[]{:S(2)}) collective-permute-start(bf16[256,768]{1,0:T(8,128)(2,1)S(1)} %get-tuple-element.56), channel_id=1, source_target_pairs={{0,2},{2,0},{1,3},{3,1},{4,6},{6,4},{5,7},{7,5},{8,10},{10,8},{9,1... | collective-permute-start | bytes 1179656 | tf_op jit(solution)/shard_map/ppermute | solution.py:28
  123.4 2.2 %collective-permute-start.13 = (bf16[256,768]{1,0:T(8,128)(2,1)S(1)}, bf16[256,768]{1,0:T(8,128)(2,1)S(1)}, u32[]{:S(2)}, u32[]{:S(2)}) collective-permute-start(bf16[256,768]{1,0:T(8,128)(2,1)S(1)} %get-tuple-element.54), channel_id=1, source_target_pairs={{0,2},{2,0},{1,3},{3,1},{4,6},{6,4},{5,7},{7,5},{8,10},{10,8},{9,1... | collective-permute-start | bytes 1179656 | tf_op jit(solution)/shard_map/ppermute | solution.py:28
  123.5 2.1 copy-start.20
  165.4 4.0 %collective-permute-start.15 = (f32[32,768]{1,0:T(8,128)S(1)}, f32[32,768]{1,0:T(8,128)S(1)}, u32[]{:S(2)}, u32[]{:S(2)}) collective-permute-start(f32[32,768]{1,0:T(8,128)S(1)} %pad_maximum_fusion.4), channel_id=1, source_target_pairs={{0,128},{128,0},{1,129},{129,1},{2,130},{130,2},{3,131},{131,3},{4... | collective-permute-start | bytes 294920 | tf_op jit(solution)/shard_map/ppermute | solution.py:28
  166.7 5.7 %collective-permute-start.16 = (f32[32,768]{1,0:T(8,128)S(1)}, f32[32,768]{1,0:T(8,128)S(1)}, u32[]{:S(2)}, u32[]{:S(2)}) collective-permute-start(f32[32,768]{1,0:T(8,128)S(1)} %pad_maximum_fusion.4), channel_id=1, source_target_pairs={{0,1},{1,0},{2,3},{3,2},{4,5},{5,4},{6,7},{7,6},{8,9},{9,8},{10,11... | collective-permute-start | bytes 294920 | tf_op jit(solution)/shard_map/ppermute | solution.py:28
  169.4 4.7 %collective-permute-start.17 = (f32[32,768]{1,0:T(8,128)S(1)}, f32[32,768]{1,0:T(8,128)S(1)}, u32[]{:S(2)}, u32[]{:S(2)}) collective-permute-start(f32[32,768]{1,0:T(8,128)S(1)} %pad_maximum_fusion.4), channel_id=1, source_target_pairs={{0,129},{1,128},{128,1},{129,0},{2,131},{3,130},{130,3},{131,2},{4... | collective-permute-start | bytes 294920 | tf_op jit(solution)/shard_map/ppermute | solution.py:202
  202.7 8.0 %collective-permute-start.18 = (f16[768,768]{1,0:T(8,128)(2,1)S(1)}, f16[768,768]{1,0:T(8,128)(2,1)S(1)}, u32[]{:S(2)}, u32[]{:S(2)}) collective-permute-start(f16[768,768]{1,0:T(8,128)(2,1)S(1)} %bitcast.17), channel_id=1, source_target_pairs={{0,2},{2,0},{1,3},{3,1},{4,6},{6,4},{5,7},{7,5},{8,10},{10,8},{9,1... | collective-permute-start | bytes 3538952 | tf_op jit(solution)/shard_map/ppermute | solution.py:28
  208.1 2.5 %collective-permute-start.19 = (f32[8,768]{1,0:T(8,128)S(1)}, f32[8,768]{1,0:T(8,128)S(1)}, u32[]{:S(2)}, u32[]{:S(2)}) collective-permute-start(f32[8,768]{1,0:T(8,128)S(1)} %broadcast_in_dim.51), channel_id=1, source_target_pairs={{0,2},{2,0},{1,3},{3,1},{4,6},{6,4},{5,7},{7,5},{8,10},{10,8},{9,1... | collective-permute-start | bytes 73736 | tf_op jit(solution)/shard_map/ppermute | solution.py:28

commit v8 on v7

--- a/solution.py
+++ b/solution.py
@@ -36,10 +36,13 @@
     return along_dp(block, [(i, (i + 2 * step) % N_DP) for i in range(N_DP)])
 
 
-def forward(block):
-    direct = along_dp(block, [(i, (i + 2) % N_DP) for i in range(N_DP) if i not in (62, 126)])
-    aside = along_dp(block, [(126, 56), (62, 120)])
-    return direct, aside
+EVEN_ON = [(i, i + 2) for i in range(0, N_DP, 2) if i not in (62, 126)] + [(126, 57), (62, 121)]
+ODD_ON = [(i, (i + 2) % N_DP) for i in range(1, N_DP, 2)]
+EVEN_OVER = [(i, i + 1) for i in range(0, N_DP, 2) if i not in (0, 64)] + [(57, 1), (121, 65)]
+ODD_OVER = [(i, i - 1) for i in range(1, N_DP, 2)]
+LAST_HOP = [(57, 0), (121, 64)]
+EVEN_STEP = [(i, i + 1) for i in range(0, N_DP, 2)]
+ODD_STEP = [(i, (i + 1) % N_DP) for i in range(1, N_DP, 2)]
 
 
 VMEM = pl.BlockSpec(memory_space=pltpu.VMEM)
@@ -48,6 +51,7 @@
 DT = 1536
 DS = 768
 PAD = 16
+VMEM_ALL = 61 * 2**20
 FAR_COST = 40
 OWN_COST = 2
 
@@ -88,7 +92,7 @@
             jax.ShapeDtypeStruct((ROWS, DS), f32),
             jax.ShapeDtypeStruct((ROWS, 1), f32),
         ],
-        compiler_params=pltpu.CompilerParams(vmem_limit_bytes=28 * 2**20),
+        compiler_params=pltpu.CompilerParams(vmem_limit_bytes=VMEM_ALL),
         cost_estimate=pl.CostEstimate(flops=flops, bytes_accessed=5 * 2**20, transcendentals=0),
     )(*args)
 
@@ -128,14 +132,16 @@
 
 
 def near_kernel(
-    flags, own, other, direct, aside, exch, aside_exch, before, rows, col1, col2, recv, swapped
+    kind, own, other, even, odd, aside, even_over, odd_over, before, rows, col1, col2, recv, exch
 ):
-    recv[...] = jnp.where(flags[0] == 1, aside[...], direct[...])
-    swapped[...] = jnp.where(flags[1] == 1, aside_exch[...], exch[...])
-    row_a, col_a = tile(own, swapped)
+    recv[...] = jnp.where(
+        kind[0] == 2, odd[...], jnp.where(kind[0] == 1, aside[...], even[...])
+    )
+    exch[...] = jnp.where(kind[0] == 2, even_over[...], odd_over[...])
+    row_a, col_a = tile(own, exch)
     row_b, col_b = tile(own, recv)
     rows[:ROWS] = row_a + row_b + before[:ROWS]
-    row_a, col_c = tile(other, swapped)
+    row_a, col_c = tile(other, exch)
     row_b, col_d = tile(other, recv)
     rows[ROWS:] = row_a + row_b + before[ROWS:]
     col2[...] = (col_a + col_c).astype(bf16)
@@ -233,17 +239,19 @@
     ids, image_feats, teacher_image, text_own = lax.optimization_barrier(
         (ids, image_feats, teacher_image, text_own)
     )
-    recv, aside = forward(text_own)
-    beside = along_dp(text_own, [(i, i + 1) for i in range(0, N_DP, 2)])
+    even = along_dp(text_own, EVEN_ON)
+    odd = along_dp(text_own, ODD_ON)
+    beside = along_dp(text_own, EVEN_STEP)
     image_own, image_unit, image_len = embed(
         image_kernel, 2 * 10**9, ids, image_feats, image_proj, teacher_image, teacher_proj
     )
     image_y = swap(image_own, "yh")
-    recv, aside, beside, image_later = lax.optimization_barrier((recv, aside, beside, image_own))
-    aside_exch = along_dp(aside, [(56, 1), (120, 65)])
-    aside = along_dp(aside, [(56, 0), (120, 64)])
-    behind = along_dp(recv, [(i, (i + 1) % N_DP) for i in range(1, N_DP, 2)])
-    exch = along_dp(recv, [(i, i ^ 1) for i in range(N_DP) if i not in (0, 64)])
+    even, beside, image_later = lax.optimization_barrier((even, beside, image_own))
+    even_over = along_dp(even, EVEN_OVER)
+    aside = along_dp(even, LAST_HOP)
+    odd, _ = lax.optimization_barrier((odd, image_own))
+    behind = along_dp(odd, ODD_STEP)
+    odd_over = along_dp(odd, ODD_OVER)
 
     sent_feats = jnp.where(first, text_feats, image_feats)
     kept_feats = jnp.where(first, image_feats, text_feats)
@@ -256,17 +264,18 @@
     place = pltpu.VMEM((ROWS + PAD, DT + DS), bf16)
     rows, col1, col2 = pairs(
         near_kernel,
-        [SMEM] + [VMEM] * 7,
+        [SMEM] + [VMEM] * 8,
         [wide, block, narrow],
         [place] * 2,
         4,
-        jnp.stack([dp == 0, dp == 1]).astype(jnp.int32),
+        jnp.where(first, (dp == 0).astype(jnp.int32), 2)[None],
         image_later,
         image_y,
-        recv,
+        even,
+        odd,
         aside,
-        exch,
-        aside_exch,
+        even_over,
+        odd_over,
         rows,
     )
     both = (col1 + swap(col2, "core").astype(f32)).astype(bf16)

time: 214 us -> 210 us (0.981)
  local copies, waits for them, and re-layouts: 12.8 us -> 6.65 us
  Pallas kernels: 16.3 us -> 21.5 us
  other arithmetic: 11.8 us -> 9.17 us
    pallas_call x2, Pallas kernels: 2.62 us -> 9.78 us  [embed(): pl.pallas_call(kernel, in_specs=[VMEM] * len(args), out_specs=[VMEM] * 3,...]
    ppermute x9, waiting for transfers between devices: 41.8 us -> 35.1 us  [along_dp(): return lax.ppermute(block, DP, route)]
    unnamed x43 -> x29, local copies, waits for them, and re-layouts: 12.4 us -> 6.26 us
    ppermute x10, waiting for transfers between devices: 24 us -> 29.2 us  [swap(): return lax.ppermute(block, axis, [(0, 1), (1, 0)])]
  transfers between devices with their start and end apart: 20 -> 20, of which waited for: 9 -> 9; matrix products, arithmetic and copies ran while one was open for 4% -> 4% of each run, Pallas kernels for 7% -> 8%
where the time goes in v8:
time: 210 us
  waiting for transfers between devices  65.9 us (31%)
  blocking collectives  64.5 us (31%)
  starting transfers between devices  36 us (17%)
  Pallas kernels  21.5 us (10%)
  other arithmetic  9.17 us (4%)
  local copies, waits for them, and re-layouts  6.65 us (3%)
  matrix products  4.29 us (2%)
    ppermute x9, waiting for transfers between devices, along_dp(): return lax.ppermute(block, DP, route)  35.1 us
    ppermute x10, waiting for transfers between devices, swap(): return lax.ppermute(block, axis, [(0, 1), (1, 0)])  29.2 us
    ppermute x9, starting transfers between devices, along_dp(): return lax.ppermute(block, DP, route)  19.3 us
    all_to_all x1, blocking collectives, sum_everywhere(): blocks = lax.all_to_all(blocks, 'x', 0, 0, tiled=True)  18.9 us
    all_to_all x1, blocking collectives, sum_everywhere(): blocks = lax.all_to_all(blocks, 'z', 0, 0, tiled=True)  17.1 us
    ppermute x10, starting transfers between devices, swap(): return lax.ppermute(block, axis, [(0, 1), (1, 0)])  15.9 us
    all_to_all x1, blocking collectives, sum_everywhere(): own_total = lax.all_to_all(spread, 'x', 0, 0, tiled=True).reshape(ds, ds)  14.5 us
    all_to_all x1, blocking collectives, sum_everywhere(): lax.all_to_all(spread, 'z', 0, 0, tiled=True).reshape(ds // 4, ds)  14 us
  transfers between devices with their start and end apart: 20, of which 9 were waited for; matrix products, arithmetic and copies ran while one was open for 4% of the time, Pallas kernels for 8%

profile of v8, /device:TPU:1, one launch (start us, length us, event | category | flops | bytes accessed | tf_op | source)
XLA Modules:
  0.0 209.7 jit_solution(12652165248931230420)
XLA Ops:
  0.6 3.8 %shard_map.95 = (bf16[272,2304]{1,0:T(8,128)(2,1)}, f32[256,768]{1,0:T(8,128)}, f32[256,1]{1,0:T(8,128)}) custom-call(s32[1,256]{1,0:T(1,128)} %bitcast.19, bf16[256,768]{1,0:T(8,128)(2,1)} %feats.1, bf16[768,768]{1,0:T(8,128)(2,1)} %proj.2, bf16[256,1536]{1,0:T(8,128)(2,1)} %teacher.1), custom_call_target="tpu_custom_call" | custom-call | flops 1000000000 | bytes 5242880 | tf_op jit(solution)/shard_map/pallas_call | solution.py:86
  4.4 1.7 collective-permute-start.1
  6.1 1.3 collective-permute-start.2
  7.4 3.9 %collective-permute-start.4 = (bf16[272,2304]{1,0:T(8,128)(2,1)}, bf16[272,2304]{1,0:T(8,128)(2,1)}, u32[]{:S(2)}, u32[]{:S(2)}) collective-permute-start(bf16[272,2304]{1,0:T(8,128)(2,1)} %get-tuple-element.26.text), channel_id=1, source_target_pairs={{2,6},{6,10},{10,14},{14,18},{18,22},{22,26},{26,30},{30,34},{34,3... | collective-permute-start | bytes 3760136 | tf_op jit(solution)/shard_map/ppermute | solution.py:32
  11.4 6.0 %shard_map.96 = (bf16[272,2304]{1,0:T(8,128)(2,1)}, f32[256,768]{1,0:T(8,128)}, f32[256,1]{1,0:T(8,128)}) custom-call(s32[1,256]{1,0:T(1,128)} %bitcast.20, bf16[256,768]{1,0:T(8,128)(2,1)} %feats.2, bf16[768,768]{1,0:T(8,128)(2,1)} %proj.3, bf16[256,1536]{1,0:T(8,128)(2,1)} %teacher.2, bf16[1536,1536]{1,0:T(8,128)(2,1)} %teacher_proj.1), custom_call_target="tpu_custom_call" | custom-call | flops 2000000000 | bytes 5242880 | tf_op jit(solution)/shard_map/pallas_call | solution.py:86
  17.4 2.9 %collective-permute-start.3 = (bf16[272,2304]{1,0:T(8,128)(2,1)}, bf16[272,2304]{1,0:T(8,128)(2,1)S(1)}, u32[]{:S(2)}, u32[]{:S(2)}) collective-permute-start(bf16[272,2304]{1,0:T(8,128)(2,1)} %get-tuple-element.30.own), channel_id=1, source_target_pairs={{0,1},{1,0},{2,3},{3,2},{4,5},{5,4},{6,7},{7,6},{8,9},{9,8},{10,11... | collective-permute-start | bytes 3760136 | tf_op jit(solution)/shard_map/ppermute | solution.py:28
  20.3 1.7 collective-permute-start.6
  22.0 1.3 collective-permute-start.7
  23.3 13.8 %collective-permute-done.4.odd = bf16[272,2304]{1,0:T(8,128)(2,1)} collective-permute-done((bf16[272,2304]{1,0:T(8,128)(2,1)}, bf16[272,2304]{1,0:T(8,128)(2,1)}, u32[]{:S(2)}, u32[]{:S(2)}) %collective-permute-start.4) | collective-permute-done | bytes 1253408 | tf_op jit(solution)/shard_map/ppermute | solution.py:32
  37.1 4.5 %collective-permute-start.8 = (bf16[272,2304]{1,0:T(8,128)(2,1)}, bf16[272,2304]{1,0:T(8,128)(2,1)}, u32[]{:S(2)}, u32[]{:S(2)}) collective-permute-start(bf16[272,2304]{1,0:T(8,128)(2,1)} %collective-permute-done.4.odd), channel_id=1, source_target_pairs={{2,0},{6,4},{10,8},{14,12},{18,16},{22,20},{26,24},{30,28},{34,32}... | collective-permute-start | bytes 3760136 | tf_op jit(solution)/shard_map/ppermute | solution.py:32
  41.7 4.4 %collective-permute-start.5 = (bf16[272,2304]{1,0:T(8,128)(2,1)}, bf16[272,2304]{1,0:T(8,128)(2,1)}, u32[]{:S(2)}, u32[]{:S(2)}) collective-permute-start(bf16[272,2304]{1,0:T(8,128)(2,1)} %collective-permute-done.4.odd), channel_id=1, source_target_pairs={{2,4},{6,8},{10,12},{14,16},{18,20},{22,24},{26,28},{30,32},{34,36... | collective-permute-start | bytes 3760136 | tf_op jit(solution)/shard_map/ppermute | solution.py:32
  46.0 15.7 %collective-permute-done.3.other = bf16[272,2304]{1,0:T(8,128)(2,1)S(1)} collective-permute-done((bf16[272,2304]{1,0:T(8,128)(2,1)}, bf16[272,2304]{1,0:T(8,128)(2,1)S(1)}, u32[]{:S(2)}, u32[]{:S(2)}) %collective-permute-start.3) | collective-permute-done | bytes 1253408 | tf_op jit(solution)/shard_map/ppermute | solution.py:28
  61.8 1.0 copy-done.2
  62.8 1.3 copy-done
  64.1 1.3 copy-done.3
  65.4 1.3 copy-done.6
  66.7 1.7 shard_map.97
  68.5 19.8 %collective-permute-done.7.even_over = bf16[272,2304]{1,0:T(8,128)(2,1)} collective-permute-done((bf16[272,2304]{1,0:T(8,128)(2,1)}, bf16[272,2304]{1,0:T(8,128)(2,1)}, u32[]{:S(2)}, u32[]{:S(2)}) %collective-permute-start.7) | collective-permute-done | bytes 1253408 | tf_op jit(solution)/shard_map/ppermute | solution.py:32
  88.2 1.3 copy-done.4
  89.5 6.3 %shard_map.98 = (f32[512,768]{1,0:T(8,128)S(1)}, f32[256,768]{1,0:T(8,128)S(1)}, bf16[256,768]{1,0:T(8,128)(2,1)S(1)}) custom-call(s32[1]{0:T(128)} %bitcast.2.kind, bf16[272,2304]{1,0:T(8,128)(2,1)S(1)} %copy-done.1, bf16[272,2304]{1,0:T(8,128)(2,1)S(1)} %copy-done.4, bf16[272,2304]{1,0:T(8,128)(2,1)} %collective-permute-done.1.even, ...), custom_call_target="tpu_custom_call" | custom-call | flops 4000000000 | bytes 12582912 | tf_op jit(solution)/shard_map/pallas_call | solution.py:161
  96.0 3.7 %shard_map.99 = (f32[256,768]{1,0:T(8,128)S(1)}, bf16[256,768]{1,0:T(8,128)(2,1)}, bf16[256,768]{1,0:T(8,128)(2,1)S(1)}) custom-call(s32[1]{0:T(128)} %bitcast.1.flag, bf16[272,2304]{1,0:T(8,128)(2,1)S(1)} %copy-done.1, bf16[272,2304]{1,0:T(8,128)(2,1)S(1)} %copy-done.5, bf16[272,2304]{1,0:T(8,128)(2,1)S(1)} %collective-permute-done.2.beside, ...), custom_call_target="tpu_custom_call" | custom-call | flops 40000000000 | bytes 125829120 | tf_op jit(solution)/shard_map/pallas_call | solution.py:161
  99.7 0.5 collective-permute-start.12
  100.2 2.6 %collective-permute-start.9 = (bf16[256,768]{1,0:T(8,128)(2,1)}, bf16[256,768]{1,0:T(8,128)(2,1)S(1)}, u32[]{:S(2)}, u32[]{:S(2)}) collective-permute-start(bf16[256,768]{1,0:T(8,128)(2,1)} %get-tuple-element.37), channel_id=1, source_target_pairs={{0,1},{1,0},{2,3},{3,2},{4,5},{5,4},{6,7},{7,6},{8,9},{9,8},{10,11... | collective-permute-start | bytes 1179656 | tf_op jit(solution)/shard_map/ppermute | solution.py:28
  102.8 0.8 add_convert_fusion
  103.6 1.0 broadcast_select_fusion.5
  104.6 0.4 collective-permute-start
  105.2 7.4 %collective-permute-done.9 = bf16[256,768]{1,0:T(8,128)(2,1)S(1)} collective-permute-done((bf16[256,768]{1,0:T(8,128)(2,1)}, bf16[256,768]{1,0:T(8,128)(2,1)S(1)}, u32[]{:S(2)}, u32[]{:S(2)}) %collective-permute-start.9) | collective-permute-done | bytes 393248 | tf_op jit(solution)/shard_map/ppermute | solution.py:28
  112.8 1.4 collective-permute-done.11
  114.3 1.6 multiply_reduce_fusion.1
  115.9 1.6 broadcast_select_fusion.3
  117.7 1.3 collective-permute-start.14
  119.1 1.2 collective-permute-done.14
  120.3 1.8 fusion.5
  122.1 2.5 %abs_reduce_fusion = (f32[]{:T(128)}, f32[768,768]{1,0:T(8,128)S(1)}) fusion(f32[768,768]{1,0:T(8,128)S(1)} %fusion.5, bf16[256,768]{1,0:T(8,128)(2,1)S(1)} %collective-permute-done.13, bf16[256,768]{1,0:T(8,128)(2,1)S(1)} %get-tuple-element.49, bf16[256,768]{1,0:T(8,128)(2,1)} %collective-permute-done, bf16[256,768]{1,0:T(8,128)(2,1)S(1)} %copy-done.9), kind=kOutput, calls=%fused_computation.6 | convolution fusion | flops 608894976 | bytes 6291460 | tf_op jit(solution)/shard_map/dot_general | solution.py:311
  125.6 0.2 concatenate.21
  125.8 18.9 %all_to_all.20 = f16[4,200,768]{2,1,0:T(8,128)(2,1)S(1)} all-to-all(f16[4,200,768]{2,1,0:T(8,128)(2,1)S(1)} %concatenate.21), channel_id=1, replica_groups=mesh['yl'=2,'z'=8,'x'=4,'core'=2,'yh'=2] {'x'}, dimensions={0} | all-to-all | bytes 2457600 | tf_op jit(solution)/shard_map/all_to_all | solution.py:199
  144.8 0.2 multiply_reduce_fusion
  145.2 17.1 %all_to_all.21 = f16[8,32,768]{2,1,0:T(8,128)(2,1)S(1)} all-to-all(f16[8,32,768]{2,1,0:T(8,128)(2,1)S(1)} %pad_maximum_fusion.3), channel_id=1, replica_groups=mesh['yl'=2,'z'=8,'x'=4,'core'=2,'yh'=2] {'z'}, dimensions={0} | all-to-all | bytes 786432 | tf_op jit(solution)/shard_map/all_to_all | solution.py:203
  162.5 0.6 collective-permute-start.15
  163.1 2.6 %collective-permute-start.16 = (f32[32,768]{1,0:T(8,128)S(1)}, f32[32,768]{1,0:T(8,128)S(1)}, u32[]{:S(2)}, u32[]{:S(2)}) collective-permute-start(f32[32,768]{1,0:T(8,128)S(1)} %pad_maximum_fusion.4), channel_id=1, source_target_pairs={{0,1},{1,0},{2,3},{3,2},{4,5},{5,4},{6,7},{7,6},{8,9},{9,8},{10,11... | collective-permute-start | bytes 294920 | tf_op jit(solution)/shard_map/ppermute | solution.py:28
  165.7 0.8 collective-permute-start.17
  166.4 2.3 %collective-permute-done.16 = f32[32,768]{1,0:T(8,128)S(1)} collective-permute-done((f32[32,768]{1,0:T(8,128)S(1)}, f32[32,768]{1,0:T(8,128)S(1)}, u32[]{:S(2)}, u32[]{:S(2)}) %collective-permute-start.16) | collective-permute-done | bytes 98336 | tf_op jit(solution)/shard_map/ppermute | solution.py:28
  168.7 1.6 collective-permute-done.17
  170.5 14.0 %all_to_all.22 = f16[8,24,768]{2,1,0:T(8,128)(2,1)S(1)} all-to-all(f16[8,24,768]{2,1,0:T(8,128)(2,1)S(1)} %broadcast_in_dim.51), channel_id=1, replica_groups=mesh['yl'=2,'z'=8,'x'=4,'core'=2,'yh'=2] {'z'}, dimensions={0} | all-to-all | bytes 589824 | tf_op jit(solution)/shard_map/all_to_all | solution.py:216
  184.5 14.5 %all_to_all.23 = f16[4,192,768]{2,1,0:T(8,128)(2,1)S(1)} all-to-all(f16[4,192,768]{2,1,0:T(8,128)(2,1)S(1)} %broadcast_in_dim.53), channel_id=1, replica_groups=mesh['yl'=2,'z'=8,'x'=4,'core'=2,'yh'=2] {'x'}, dimensions={0} | all-to-all | bytes 2359296 | tf_op jit(solution)/shard_map/all_to_all | solution.py:218
  199.0 5.4 %collective-permute-start.18 = (f16[768,768]{1,0:T(8,128)(2,1)S(1)}, f16[768,768]{1,0:T(8,128)(2,1)S(1)}, u32[]{:S(2)}, u32[]{:S(2)}) collective-permute-start(f16[768,768]{1,0:T(8,128)(2,1)S(1)} %bitcast.14), channel_id=1, source_target_pairs={{0,2},{2,0},{1,3},{3,1},{4,6},{6,4},{5,7},{7,5},{8,10},{10,8},{9,1... | collective-permute-start | bytes 3538952 | tf_op jit(solution)/shard_map/ppermute | solution.py:28
  204.4 2.5 %collective-permute-done.19 = f32[8,768]{1,0:T(8,128)S(1)} collective-permute-done((f32[8,768]{1,0:T(8,128)S(1)}, f32[8,768]{1,0:T(8,128)S(1)}, u32[]{:S(2)}, u32[]{:S(2)}) %collective-permute-start.19) | collective-permute-done | bytes 24608 | tf_op jit(solution)/shard_map/ppermute | solution.py:28
  206.9 2.7 %fusion = (f32[768,768]{1,0:T(8,128)}, f32[768,768]{1,0:T(8,128)}) fusion(f16[768,768]{1,0:T(8,128)(2,1)S(1)} %collective-permute-done.18, f32[768]{0:T(1024)S(1)} %fusion.21, f32[768]{0:T(1024)S(1)} %get-tuple-element.46, pred[]{:T(512)S(6)} %eq.8, f16[4,192,768]{2,1,0:T(8,128)(2,1)S(1)} %all_to_all.23), kind=kLoop, calls=%fused_computation.1 | loop fusion | flops 3538944 | bytes 7084033 | tf_op jit(solution)/shard_map/jit(_where)/select_n | solution.py:319
  (60 shorter events, 1.6 us)
Async XLA Ops:
  4.4 15.9 %collective-permute-start.1 = (bf16[272,2304]{1,0:T(8,128)(2,1)}, bf16[272,2304]{1,0:T(8,128)(2,1)}, u32[]{:S(2)}, u32[]{:S(2)}) collective-permute-start(bf16[272,2304]{1,0:T(8,128)(2,1)} %get-tuple-element.26.text), channel_id=1, source_target_pairs={{0,4},{4,8},{8,12},{12,16},{16,20},{20,24},{24,28},{28,32},{32,36}... | collective-permute-start | bytes 3760136 | tf_op jit(solution)/shard_map/ppermute | solution.py:32
  6.1 14.2 %collective-permute-start.2 = (bf16[272,2304]{1,0:T(8,128)(2,1)}, bf16[272,2304]{1,0:T(8,128)(2,1)S(1)}, u32[]{:S(2)}, u32[]{:S(2)}) collective-permute-start(bf16[272,2304]{1,0:T(8,128)(2,1)} %get-tuple-element.26.text), channel_id=1, source_target_pairs={{0,2},{4,6},{8,10},{12,14},{16,18},{20,22},{24,26},{28,30},{32,34}... | collective-permute-start | bytes 3760136 | tf_op jit(solution)/shard_map/ppermute | solution.py:32
  7.4 29.7 %collective-permute-start.4 = (bf16[272,2304]{1,0:T(8,128)(2,1)}, bf16[272,2304]{1,0:T(8,128)(2,1)}, u32[]{:S(2)}, u32[]{:S(2)}) collective-permute-start(bf16[272,2304]{1,0:T(8,128)(2,1)} %get-tuple-element.26.text), channel_id=1, source_target_pairs={{2,6},{6,10},{10,14},{14,18},{18,22},{22,26},{26,30},{30,34},{34,3... | collective-permute-start | bytes 3760136 | tf_op jit(solution)/shard_map/ppermute | solution.py:32
  17.4 44.4 %collective-permute-start.3 = (bf16[272,2304]{1,0:T(8,128)(2,1)}, bf16[272,2304]{1,0:T(8,128)(2,1)S(1)}, u32[]{:S(2)}, u32[]{:S(2)}) collective-permute-start(bf16[272,2304]{1,0:T(8,128)(2,1)} %get-tuple-element.30.own), channel_id=1, source_target_pairs={{0,1},{1,0},{2,3},{3,2},{4,5},{5,4},{6,7},{7,6},{8,9},{9,8},{10,11... | collective-permute-start | bytes 3760136 | tf_op jit(solution)/shard_map/ppermute | solution.py:28
  20.3 48.2 %collective-permute-start.6 = (bf16[272,2304]{1,0:T(8,128)(2,1)}, bf16[272,2304]{1,0:T(8,128)(2,1)}, u32[]{:S(2)}, u32[]{:S(2)}) collective-permute-start(bf16[272,2304]{1,0:T(8,128)(2,1)} %collective-permute-done.1.even), channel_id=1, source_target_pairs={{114,0},{242,128},{115,1},{243,129}} | collective-permute-start | bytes 3760136 | tf_op jit(solution)/shard_map/ppermute | solution.py:32
  22.0 66.2 %collective-permute-start.7 = (bf16[272,2304]{1,0:T(8,128)(2,1)}, bf16[272,2304]{1,0:T(8,128)(2,1)}, u32[]{:S(2)}, u32[]{:S(2)}) collective-permute-start(bf16[272,2304]{1,0:T(8,128)(2,1)} %collective-permute-done.1.even), channel_id=1, source_target_pairs={{4,6},{8,10},{12,14},{16,18},{20,22},{24,26},{28,30},{32,34},{36,3... | collective-permute-start | bytes 3760136 | tf_op jit(solution)/shard_map/ppermute | solution.py:32
  37.1 51.1 %collective-permute-start.8 = (bf16[272,2304]{1,0:T(8,128)(2,1)}, bf16[272,2304]{1,0:T(8,128)(2,1)}, u32[]{:S(2)}, u32[]{:S(2)}) collective-permute-start(bf16[272,2304]{1,0:T(8,128)(2,1)} %collective-permute-done.4.odd), channel_id=1, source_target_pairs={{2,0},{6,4},{10,8},{14,12},{18,16},{22,20},{26,24},{30,28},{34,32}... | collective-permute-start | bytes 3760136 | tf_op jit(solution)/shard_map/ppermute | solution.py:32
  41.7 54.3 %collective-permute-start.5 = (bf16[272,2304]{1,0:T(8,128)(2,1)}, bf16[272,2304]{1,0:T(8,128)(2,1)}, u32[]{:S(2)}, u32[]{:S(2)}) collective-permute-start(bf16[272,2304]{1,0:T(8,128)(2,1)} %collective-permute-done.4.odd), channel_id=1, source_target_pairs={{2,4},{6,8},{10,12},{14,16},{18,20},{22,24},{26,28},{30,32},{34,36... | collective-permute-start | bytes 3760136 | tf_op jit(solution)/shard_map/ppermute | solution.py:32
  61.8 1.0 copy-start.2
  62.8 1.3 copy-start
  64.1 1.3 copy-start.3
  65.4 1.3 copy-start.6
  66.7 21.5 %copy-start.1 = (bf16[272,2304]{1,0:T(8,128)(2,1)S(1)}, bf16[272,2304]{1,0:T(8,128)(2,1)}, u32[]{:S(2)}) copy-start(bf16[272,2304]{1,0:T(8,128)(2,1)} %get-tuple-element.30.own) | copy-start | bytes 3760132
  88.2 1.3 copy-start.4
  89.5 6.4 %copy-start.5 = (bf16[272,2304]{1,0:T(8,128)(2,1)S(1)}, bf16[272,2304]{1,0:T(8,128)(2,1)}, u32[]{:S(2)}) copy-start(bf16[272,2304]{1,0:T(8,128)(2,1)} %copy-done.2) | copy-start | bytes 3760132
  95.8 6.9 %collective-permute-start.10 = (bf16[256,768]{1,0:T(8,128)(2,1)S(1)}, bf16[256,768]{1,0:T(8,128)(2,1)S(1)}, u32[]{:S(2)}, u32[]{:S(2)}) collective-permute-start(bf16[256,768]{1,0:T(8,128)(2,1)S(1)} %get-tuple-element.42), channel_id=1, source_target_pairs={{0,2},{2,0},{1,3},{3,1},{4,6},{6,4},{5,7},{7,5},{8,10},{10,8},{9,1... | collective-permute-start | bytes 1179656 | tf_op jit(solution)/shard_map/ppermute | solution.py:28
  99.7 3.9 %copy-start.10 = (bf16[256,768]{1,0:T(8,128)(2,1)S(1)}, bf16[256,768]{1,0:T(8,128)(2,1)}, u32[]{:S(2)}) copy-start(bf16[256,768]{1,0:T(8,128)(2,1)} %feats.2) | copy-start | bytes 1179652
  99.7 3.9 %copy-start.11 = (bf16[256,768]{1,0:T(8,128)(2,1)S(1)}, bf16[256,768]{1,0:T(8,128)(2,1)}, u32[]{:S(2)}) copy-start(bf16[256,768]{1,0:T(8,128)(2,1)} %feats.1) | copy-start | bytes 1179652
  99.7 13.1 %collective-permute-start.12 = (bf16[256,768]{1,0:T(8,128)(2,1)S(1)}, bf16[256,768]{1,0:T(8,128)(2,1)}, u32[]{:S(2)}, u32[]{:S(2)}) collective-permute-start(bf16[256,768]{1,0:T(8,128)(2,1)S(1)} %get-tuple-element.43), channel_id=1, source_target_pairs={{0,250},{2,0},{4,254},{6,4},{8,2},{10,8},{12,6},{14,12},{16,10},{1... | collective-permute-start | bytes 1179656 | tf_op jit(solution)/shard_map/ppermute | solution.py:32
  100.2 12.4 %collective-permute-start.9 = (bf16[256,768]{1,0:T(8,128)(2,1)}, bf16[256,768]{1,0:T(8,128)(2,1)S(1)}, u32[]{:S(2)}, u32[]{:S(2)}) collective-permute-start(bf16[256,768]{1,0:T(8,128)(2,1)} %get-tuple-element.37), channel_id=1, source_target_pairs={{0,1},{1,0},{2,3},{3,2},{4,5},{5,4},{6,7},{7,6},{8,9},{9,8},{10,11... | collective-permute-start | bytes 1179656 | tf_op jit(solution)/shard_map/ppermute | solution.py:28
  102.8 2.2 %copy-start.13 = (f32[256,1]{1,0:T(8,128)S(1)}, f32[256,1]{1,0:T(8,128)}, u32[]{:S(2)}) copy-start(f32[256,1]{1,0:T(8,128)} %get-tuple-element.39) | copy-start | bytes 3076
  102.8 2.3 %copy-start.12 = (f32[256,1]{1,0:T(8,128)S(1)}, f32[256,1]{1,0:T(8,128)}, u32[]{:S(2)}) copy-start(f32[256,1]{1,0:T(8,128)} %get-tuple-element.45) | copy-start | bytes 3076
  102.8 9.8 %copy-start.7 = (f32[256,768]{1,0:T(8,128)S(1)}, f32[256,768]{1,0:T(8,128)}, u32[]{:S(2)}) copy-start(f32[256,768]{1,0:T(8,128)} %get-tuple-element.38) | copy-start | bytes 2359300
  103.6 10.7 %collective-permute-start.11 = (bf16[256,768]{1,0:T(8,128)(2,1)}, bf16[256,768]{1,0:T(8,128)(2,1)}, u32[]{:S(2)}, u32[]{:S(2)}) collective-permute-start(bf16[256,768]{1,0:T(8,128)(2,1)} %add_convert_fusion), channel_id=1, source_target_pairs={{0,252},{2,254},{4,0},{6,2},{8,4},{10,6},{12,8},{14,10},{16,12},{1... | collective-permute-start | bytes 1179656 | tf_op jit(solution)/shard_map/ppermute | solution.py:32
  104.6 14.5 %collective-permute-start = (bf16[256,768]{1,0:T(8,128)(2,1)}, bf16[256,768]{1,0:T(8,128)(2,1)}, u32[]{:S(2)}, u32[]{:S(2)}) collective-permute-start(bf16[256,768]{1,0:T(8,128)(2,1)} %get-tuple-element.60), channel_id=1, source_target_pairs={{0,2},{2,0},{1,3},{3,1},{4,6},{6,4},{5,7},{7,5},{8,10},{10,8},{9,1... | collective-permute-start | bytes 1179656 | tf_op jit(solution)/shard_map/ppermute | solution.py:28
  112.8 3.1 %copy-start.8 = (f32[256,768]{1,0:T(8,128)S(1)}, f32[256,768]{1,0:T(8,128)}, u32[]{:S(2)}) copy-start(f32[256,768]{1,0:T(8,128)} %get-tuple-element.44) | copy-start | bytes 2359300
  117.5 2.8 %copy-start.9 = (bf16[256,768]{1,0:T(8,128)(2,1)S(1)}, bf16[256,768]{1,0:T(8,128)(2,1)}, u32[]{:S(2)}) copy-start(bf16[256,768]{1,0:T(8,128)(2,1)} %get-tuple-element.59) | copy-start | bytes 1179652
  117.7 2.6 %collective-permute-start.14 = (bf16[256,768]{1,0:T(8,128)(2,1)S(1)}, bf16[256,768]{1,0:T(8,128)(2,1)S(1)}, u32[]{:S(2)}, u32[]{:S(2)}) collective-permute-start(bf16[256,768]{1,0:T(8,128)(2,1)S(1)} %get-tuple-element.56), channel_id=1, source_target_pairs={{0,2},{2,0},{1,3},{3,1},{4,6},{6,4},{5,7},{7,5},{8,10},{10,8},{9,1... | collective-permute-start | bytes 1179656 | tf_op jit(solution)/shard_map/ppermute | solution.py:28
  119.0 3.2 %collective-permute-start.13 = (bf16[256,768]{1,0:T(8,128)(2,1)S(1)}, bf16[256,768]{1,0:T(8,128)(2,1)S(1)}, u32[]{:S(2)}, u32[]{:S(2)}) collective-permute-start(bf16[256,768]{1,0:T(8,128)(2,1)S(1)} %get-tuple-element.54), channel_id=1, source_target_pairs={{0,2},{2,0},{1,3},{3,1},{4,6},{6,4},{5,7},{7,5},{8,10},{10,8},{9,1... | collective-permute-start | bytes 1179656 | tf_op jit(solution)/shard_map/ppermute | solution.py:28
  162.5 3.9 %collective-permute-start.15 = (f32[32,768]{1,0:T(8,128)S(1)}, f32[32,768]{1,0:T(8,128)S(1)}, u32[]{:S(2)}, u32[]{:S(2)}) collective-permute-start(f32[32,768]{1,0:T(8,128)S(1)} %pad_maximum_fusion.4), channel_id=1, source_target_pairs={{0,128},{128,0},{1,129},{129,1},{2,130},{130,2},{3,131},{131,3},{4... | collective-permute-start | bytes 294920 | tf_op jit(solution)/shard_map/ppermute | solution.py:28
  163.1 5.6 %collective-permute-start.16 = (f32[32,768]{1,0:T(8,128)S(1)}, f32[32,768]{1,0:T(8,128)S(1)}, u32[]{:S(2)}, u32[]{:S(2)}) collective-permute-start(f32[32,768]{1,0:T(8,128)S(1)} %pad_maximum_fusion.4), channel_id=1, source_target_pairs={{0,1},{1,0},{2,3},{3,2},{4,5},{5,4},{6,7},{7,6},{8,9},{9,8},{10,11... | collective-permute-start | bytes 294920 | tf_op jit(solution)/shard_map/ppermute | solution.py:28
  165.7 4.7 %collective-permute-start.17 = (f32[32,768]{1,0:T(8,128)S(1)}, f32[32,768]{1,0:T(8,128)S(1)}, u32[]{:S(2)}, u32[]{:S(2)}) collective-permute-start(f32[32,768]{1,0:T(8,128)S(1)} %pad_maximum_fusion.4), channel_id=1, source_target_pairs={{0,129},{1,128},{128,1},{129,0},{2,131},{3,130},{130,3},{131,2},{4... | collective-permute-start | bytes 294920 | tf_op jit(solution)/shard_map/ppermute | solution.py:208
  199.0 8.0 %collective-permute-start.18 = (f16[768,768]{1,0:T(8,128)(2,1)S(1)}, f16[768,768]{1,0:T(8,128)(2,1)S(1)}, u32[]{:S(2)}, u32[]{:S(2)}) collective-permute-start(f16[768,768]{1,0:T(8,128)(2,1)S(1)} %bitcast.14), channel_id=1, source_target_pairs={{0,2},{2,0},{1,3},{3,1},{4,6},{6,4},{5,7},{7,5},{8,10},{10,8},{9,1... | collective-permute-start | bytes 3538952 | tf_op jit(solution)/shard_map/ppermute | solution.py:28
  204.4 2.5 %collective-permute-start.19 = (f32[8,768]{1,0:T(8,128)S(1)}, f32[8,768]{1,0:T(8,128)S(1)}, u32[]{:S(2)}, u32[]{:S(2)}) collective-permute-start(f32[8,768]{1,0:T(8,128)S(1)} %broadcast_in_dim.55), channel_id=1, source_target_pairs={{0,2},{2,0},{1,3},{3,1},{4,6},{6,4},{5,7},{7,5},{8,10},{10,8},{9,1... | collective-permute-start | bytes 73736 | tf_op jit(solution)/shard_map/ppermute | solution.py:28

commit v9 on v5

--- a/solution.py
+++ b/solution.py
@@ -36,13 +36,6 @@
 
 def chip_shift(block, step):
     return along_dp(block, [(i, (i + 2 * step) % N_DP) for i in range(N_DP)])
-
-
-def forward(block):
-    direct = along_dp(block, [(i, (i + 2) % N_DP) for i in range(N_DP) if i not in (62, 126)])
-    aside = along_dp(block, [(126, 56), (62, 120)])
-    aside = along_dp(aside, [(56, 0), (120, 64)])
-    return direct, aside
 
 
 def hand_on_kernel(flag, own, got, onward):
@@ -161,7 +154,7 @@
     back_route = [(i, i - 1 if i % 2 else (i - 3) % N_DP) for i in range(N_DP)]
     step_route = [(i, (i + 1) % N_DP) for i in range(N_DP)]
 
-    teach_direct, teach_aside = forward(teacher_text)
+    teach_recv = chip_shift(teacher_text, 1)
     teach_y = swap(teacher_image, "yh")
     text_unit, text_len = unit_rows(jnp.dot(text_feats, text_proj, preferred_element_type=f32))
     text_own = with_ids(text_unit.astype(bf16), class_ids)
@@ -173,10 +166,11 @@
     image_own = with_ids(image_unit.astype(bf16), class_ids)
     teacher_later, image_own = lax.optimization_barrier((teacher_image, image_own))
     image_y = swap(image_own, "yh")
-    teach_far = along_dp(hand_on(first, teacher_text, teach_direct, COST2), step_route)
-    text_far = along_dp(hand_on(first, text_own, text_recv, COST1), step_route)
-    crossed = lax.axis_index(DP) % 64 == 0
-    teach_recv = jnp.where(crossed, teach_aside, teach_direct)
+    teach_on = hand_on(first, teacher_text, teach_recv, COST2)
+    text_on = hand_on(first, text_own, text_recv, COST1)
+    teach_far = along_dp(teach_on, step_route)
+    text_far = along_dp(text_on, step_route)
+    teach_y, image_y, _, _ = lax.optimization_barrier((teach_y, image_y, teach_on, text_on))
     text_exch = swap(text_recv, "core")
     teach_exch = swap(teach_recv, "core")
 

time: 205 us -> 213 us (1.039)
  waiting for transfers between devices: 43.4 us -> 53.5 us
  starting transfers between devices: 39.8 us -> 31.2 us
  blocking collectives: 68.2 us -> 73.7 us
    ppermute x8 -> x6, waiting for transfers between devices: 9.04 us -> 20.3 us  [along_dp(): return lax.ppermute(block, DP, route)]
    all_to_all x1, blocking collectives: 15.6 us -> 26.4 us  [sum_everywhere(): blocks = lax.all_to_all(blocks, 'z', 0, 0, tiled=True)]
    ppermute x13, starting transfers between devices: 26.5 us -> 21.5 us  [swap(): return lax.ppermute(block, axis, [(0, 1), (1, 0)])]
    ppermute x8 -> x6, starting transfers between devices: 11.6 us -> 8.98 us  [along_dp(): return lax.ppermute(block, DP, route)]
    dot_general x4, matrix products: 2.71 us -> 5.02 us  [pair_tile(): lax.dot_general(teach_rows, teach_cols, (((1,), (1,)), ((), ())), preferr...]
  transfers between devices with their start and end apart: 22 -> 20, of which waited for: 8 -> 9; matrix products, arithmetic and copies ran while one was open for 20% -> 18% of each run, Pallas kernels for 2% -> 2%
where the time goes in v9:
time: 213 us; the launch traced here: 212 us
  blocking collectives  73.7 us (35%)
  waiting for transfers between devices  53.5 us (25%)
  starting transfers between devices  31.2 us (15%)
  matrix products  30.6 us (14%)
  other arithmetic  10.2 us (5%)
  local copies, waits for them, and re-layouts  7.04 us (3%)
  Pallas kernels  4.09 us (2%)
    ppermute x13, waiting for transfers between devices, swap(): return lax.ppermute(block, axis, [(0, 1), (1, 0)])  31.6 us
    all_to_all x1, blocking collectives, sum_everywhere(): blocks = lax.all_to_all(blocks, 'z', 0, 0, tiled=True)  26.4 us
    ppermute x13, starting transfers between devices, swap(): return lax.ppermute(block, axis, [(0, 1), (1, 0)])  21.5 us
    ppermute x6, waiting for transfers between devices, along_dp(): return lax.ppermute(block, DP, route)  20.3 us
    all_to_all x1, blocking collectives, sum_everywhere(): blocks = lax.all_to_all(blocks, 'x', 0, 0, tiled=True)  18.9 us
    all_to_all x1, blocking collectives, sum_everywhere(): own_total = lax.all_to_all(spread, 'x', 0, 0, tiled=True).reshape(ds, ds)  14.5 us
    all_to_all x1, blocking collectives, sum_everywhere(): lax.all_to_all(spread, 'z', 0, 0, tiled=True).reshape(ds // 4, ds)  13.9 us
    ppermute x6, starting transfers between devices, along_dp(): return lax.ppermute(block, DP, route)  8.98 us
  transfers between devices with their start and end apart: 20, of which 9 were waited for; matrix products, arithmetic and copies ran while one was open for 18% of the time, Pallas kernels for 2%

profile of v9, /device:TPU:1, one launch (start us, length us, event | category | flops | bytes accessed | tf_op | source)
XLA Modules:
  0.0 212.2 jit_solution(2751290015057746049)
XLA Ops:
  0.7 1.3 copy-done
  1.9 1.6 multiply_reduce_fusion.10
  3.7 0.8 fusion.76.own
  4.4 2.0 collective-permute-start.4
  6.5 2.9 %collective-permute-start.1 = (bf16[256,1536]{1,0:T(8,128)(2,1)}, bf16[256,1536]{1,0:T(8,128)(2,1)}, u32[]{:S(2)}, u32[]{:S(2)}) collective-permute-start(bf16[256,1536]{1,0:T(8,128)(2,1)} %param.8), channel_id=1, source_target_pairs={{0,1},{1,0},{2,3},{3,2},{4,5},{5,4},{6,7},{7,6},{8,9},{9,8},{10,11... | collective-permute-start | bytes 2359304 | tf_op jit(solution)/shard_map/ppermute | solution.py:30
  10.3 1.2 collective-permute-start.3
  13.0 1.4 multiply_reduce_fusion.4
  14.4 4.0 %multiply_reduce_fusion.6 = (f32[256]{0:T(256)S(1)}, f32[256,1536]{1,0:T(8,128)S(1)}) fusion(bf16[256,1536]{1,0:T(8,128)(2,1)} %param.8, bf16[1536,1536]{1,0:T(8,128)(2,1)} %param.9), kind=kOutput, calls=%fused_computation.17 | convolution fusion | flops 1208745728 | bytes 7078912 | tf_op jit(solution)/shard_map/dot_general | solution.py:178
  18.5 1.1 divide_convert_fusion.1
  19.5 4.2 %collective-permute-done.4.got = bf16[272,768]{1,0:T(8,128)(2,1)} collective-permute-done((bf16[272,768]{1,0:T(8,128)(2,1)}, bf16[272,768]{1,0:T(8,128)(2,1)}, u32[]{:S(2)}, u32[]{:S(2)}) %collective-permute-start.4) | collective-permute-done | bytes 417824 | tf_op jit(solution)/shard_map/ppermute | solution.py:34
  23.7 1.9 shard_map.96
  25.7 2.2 %collective-permute-start.5 = (bf16[272,768]{1,0:T(8,128)(2,1)}, bf16[272,768]{1,0:T(8,128)(2,1)}, u32[]{:S(2)}, u32[]{:S(2)}) collective-permute-start(bf16[272,768]{1,0:T(8,128)(2,1)} %collective-permute-done.4.got), channel_id=1, source_target_pairs={{0,2},{2,0},{1,3},{3,1},{4,6},{6,4},{5,7},{7,5},{8,10},{10,8},{9,1... | collective-permute-start | bytes 1253384 | tf_op jit(solution)/shard_map/ppermute | solution.py:30
  28.5 12.0 %collective-permute-done.3.got = bf16[256,1536]{1,0:T(8,128)(2,1)} collective-permute-done((bf16[256,1536]{1,0:T(8,128)(2,1)}, bf16[256,1536]{1,0:T(8,128)(2,1)}, u32[]{:S(2)}, u32[]{:S(2)}) %collective-permute-start.3) | collective-permute-done | bytes 786464 | tf_op jit(solution)/shard_map/ppermute | solution.py:34
  40.6 2.1 %shard_map.95 = bf16[256,1536]{1,0:T(8,128)(2,1)} custom-call(s32[1]{0:T(128)} %bitcast.flag, bf16[256,1536]{1,0:T(8,128)(2,1)} %own.1, bf16[256,1536]{1,0:T(8,128)(2,1)} %collective-permute-done.3.got), custom_call_target="tpu_custom_call" | custom-call | flops 20000000000 | bytes 2359296 | tf_op jit(solution)/shard_map/pallas_call | solution.py:47
  42.7 22.6 %collective-permute-done.2 = bf16[272,768]{1,0:T(8,128)(2,1)} collective-permute-done((bf16[272,768]{1,0:T(8,128)(2,1)S(1)}, bf16[272,768]{1,0:T(8,128)(2,1)}, u32[]{:S(2)}, u32[]{:S(2)}) %collective-permute-start.2) | collective-permute-done | bytes 417824 | tf_op jit(solution)/shard_map/ppermute | solution.py:30
  66.1 1.0 slice.65
  67.2 4.0 %multiply_reduce_fusion.5 = (f32[256]{0:T(256)S(1)}, f32[256,1536]{1,0:T(8,128)S(1)}) fusion(bf16[256,1536]{1,0:T(8,128)(2,1)} %collective-permute-done.1, bf16[1536,1536]{1,0:T(8,128)(2,1)} %param.9), kind=kOutput, calls=%fused_computation.15 | convolution fusion | flops 1208745728 | bytes 7078912 | tf_op jit(solution)/shard_map/dot_general | solution.py:178
  71.2 1.4 multiply_reduce_fusion.3
  72.9 1.5 fusion.8
  74.4 1.8 fusion.67
  76.3 2.4 %collective-permute-start.6 = (bf16[256,1536]{1,0:T(8,128)(2,1)}, bf16[256,1536]{1,0:T(8,128)(2,1)S(1)}, u32[]{:S(2)}, u32[]{:S(2)}) collective-permute-start(bf16[256,1536]{1,0:T(8,128)(2,1)} %collective-permute-done.3.got), channel_id=1, source_target_pairs={{0,2},{2,0},{1,3},{3,1},{4,6},{6,4},{5,7},{7,5},{8,10},{10,8},{9,1... | collective-permute-start | bytes 2359304 | tf_op jit(solution)/shard_map/ppermute | solution.py:30
  78.7 1.8 fusion.47
  80.5 1.4 fusion.86
  81.9 1.4 fusion.64
  83.3 1.4 fusion.83
  87.0 1.4 fusion.65
  89.9 1.4 fusion.66
  92.3 1.4 fusion.78
  93.7 1.4 add_multiply_fusion
  95.2 3.0 %collective-permute-start.9 = (bf16[256,768]{1,0:T(8,128)(2,1)S(1)}, bf16[256,768]{1,0:T(8,128)(2,1)S(1)}, u32[]{:S(2)}, u32[]{:S(2)}) collective-permute-start(bf16[256,768]{1,0:T(8,128)(2,1)S(1)} %slice.194), channel_id=1, source_target_pairs={{0,1},{1,0},{2,3},{3,2},{4,5},{5,4},{6,7},{7,6},{8,9},{9,8},{10,11... | collective-permute-start | bytes 1179656 | tf_op jit(solution)/shard_map/ppermute | solution.py:30
  98.6 5.0 %collective-permute-start.11 = (bf16[256,768]{1,0:T(8,128)(2,1)S(1)}, bf16[256,768]{1,0:T(8,128)(2,1)S(1)}, u32[]{:S(2)}, u32[]{:S(2)}) collective-permute-start(bf16[256,768]{1,0:T(8,128)(2,1)S(1)} %add_convert_fusion), channel_id=1, source_target_pairs={{0,252},{2,254},{4,0},{6,2},{8,4},{10,6},{12,8},{14,10},{16,12},{1... | collective-permute-start | bytes 1179656 | tf_op jit(solution)/shard_map/ppermute | solution.py:34
  104.3 3.2 %collective-permute-done.9 = bf16[256,768]{1,0:T(8,128)(2,1)S(1)} collective-permute-done((bf16[256,768]{1,0:T(8,128)(2,1)S(1)}, bf16[256,768]{1,0:T(8,128)(2,1)S(1)}, u32[]{:S(2)}, u32[]{:S(2)}) %collective-permute-start.9) | collective-permute-done | bytes 393248 | tf_op jit(solution)/shard_map/ppermute | solution.py:30
  107.8 4.0 %collective-permute-done.11 = bf16[256,768]{1,0:T(8,128)(2,1)S(1)} collective-permute-done((bf16[256,768]{1,0:T(8,128)(2,1)S(1)}, bf16[256,768]{1,0:T(8,128)(2,1)S(1)}, u32[]{:S(2)}, u32[]{:S(2)}) %collective-permute-start.11) | collective-permute-done | bytes 393248 | tf_op jit(solution)/shard_map/ppermute | solution.py:34
  113.1 1.2 collective-permute-start.14
  114.6 1.0 collective-permute-done.14
  115.6 0.8 fusion.72
  116.5 1.5 abs_reduce_fusion
  119.2 18.9 %all_to_all.20 = f16[4,200,768]{2,1,0:T(8,128)(2,1)S(1)} all-to-all(f16[4,200,768]{2,1,0:T(8,128)(2,1)S(1)} %concatenate.41), channel_id=1, replica_groups=mesh['yl'=2,'z'=8,'x'=4,'core'=2,'yh'=2] {'x'}, dimensions={0} | all-to-all | bytes 2457600 | tf_op jit(solution)/shard_map/all_to_all | solution.py:119
  138.5 26.4 %all_to_all.21 = f16[8,32,768]{2,1,0:T(8,128)(2,1)S(1)} all-to-all(f16[8,32,768]{2,1,0:T(8,128)(2,1)S(1)} %pad_maximum_fusion.5), channel_id=1, replica_groups=mesh['yl'=2,'z'=8,'x'=4,'core'=2,'yh'=2] {'z'}, dimensions={0} | all-to-all | bytes 786432 | tf_op jit(solution)/shard_map/all_to_all | solution.py:123
  165.3 2.9 %collective-permute-start.16 = (f32[32,768]{1,0:T(8,128)S(1)}, f32[32,768]{1,0:T(8,128)S(1)}, u32[]{:S(2)}, u32[]{:S(2)}) collective-permute-start(f32[32,768]{1,0:T(8,128)S(1)} %pad_maximum_fusion.6), channel_id=1, source_target_pairs={{0,1},{1,0},{2,3},{3,2},{4,5},{5,4},{6,7},{7,6},{8,9},{9,8},{10,11... | collective-permute-start | bytes 294920 | tf_op jit(solution)/shard_map/ppermute | solution.py:30
  168.2 0.8 collective-permute-start.17
  169.0 2.3 %collective-permute-done.16 = f32[32,768]{1,0:T(8,128)S(1)} collective-permute-done((f32[32,768]{1,0:T(8,128)S(1)}, f32[32,768]{1,0:T(8,128)S(1)}, u32[]{:S(2)}, u32[]{:S(2)}) %collective-permute-start.16) | collective-permute-done | bytes 98336 | tf_op jit(solution)/shard_map/ppermute | solution.py:30
  171.3 1.6 collective-permute-done.17
  173.0 13.9 %all_to_all.22 = f16[8,24,768]{2,1,0:T(8,128)(2,1)S(1)} all-to-all(f16[8,24,768]{2,1,0:T(8,128)(2,1)S(1)} %broadcast_in_dim.25), channel_id=1, replica_groups=mesh['yl'=2,'z'=8,'x'=4,'core'=2,'yh'=2] {'z'}, dimensions={0} | all-to-all | bytes 589824 | tf_op jit(solution)/shard_map/all_to_all | solution.py:136
  187.0 14.5 %all_to_all.23 = f16[4,192,768]{2,1,0:T(8,128)(2,1)S(1)} all-to-all(f16[4,192,768]{2,1,0:T(8,128)(2,1)S(1)} %broadcast_in_dim.27), channel_id=1, replica_groups=mesh['yl'=2,'z'=8,'x'=4,'core'=2,'yh'=2] {'x'}, dimensions={0} | all-to-all | bytes 2359296 | tf_op jit(solution)/shard_map/all_to_all | solution.py:138
  201.5 5.4 %collective-permute-start.18 = (f16[768,768]{1,0:T(8,128)(2,1)S(1)}, f16[768,768]{1,0:T(8,128)(2,1)S(1)}, u32[]{:S(2)}, u32[]{:S(2)}) collective-permute-start(f16[768,768]{1,0:T(8,128)(2,1)S(1)} %bitcast.32), channel_id=1, source_target_pairs={{0,2},{2,0},{1,3},{3,1},{4,6},{6,4},{5,7},{7,5},{8,10},{10,8},{9,1... | collective-permute-start | bytes 3538952 | tf_op jit(solution)/shard_map/ppermute | solution.py:30
  206.9 2.5 %collective-permute-done.19 = f32[8,768]{1,0:T(8,128)S(1)} collective-permute-done((f32[8,768]{1,0:T(8,128)S(1)}, f32[8,768]{1,0:T(8,128)S(1)}, u32[]{:S(2)}, u32[]{:S(2)}) %collective-permute-start.19) | collective-permute-done | bytes 24608 | tf_op jit(solution)/shard_map/ppermute | solution.py:30
  209.5 2.7 %fusion = (f32[768,768]{1,0:T(8,128)}, f32[768,768]{1,0:T(8,128)}) fusion(f16[768,768]{1,0:T(8,128)(2,1)S(1)} %collective-permute-done.18, f32[768]{0:T(1024)S(1)} %fusion.101, f32[768]{0:T(1024)S(1)} %get-tuple-element.14, pred[]{:T(512)S(6)} %eq.28, f16[4,192,768]{2,1,0:T(8,128)(2,1)S(1)} %all_to_all.23), kind=kLoop, calls=%fused_computation.1 | loop fusion | flops 3538944 | bytes 7084033 | tf_op jit(solution)/shard_map/jit(_where)/select_n | solution.py:225
  (91 shorter events, 13.4 us)
Async XLA Ops:
  0.6 1.3 copy-start
  0.6 2.9 %copy-start.7 = (s32[256]{0:T(256)S(1)}, s32[256]{0:T(256)}, u32[]{:S(2)}) copy-start(s32[256]{0:T(256)} %param.15) | copy-start | bytes 3076
  3.5 5.9 %copy-start.2 = (bf16[256,768]{1,0:T(8,128)(2,1)S(1)}, bf16[256,768]{1,0:T(8,128)(2,1)}, u32[]{:S(2)}) copy-start(bf16[256,768]{1,0:T(8,128)(2,1)} %param.11) | copy-start | bytes 1179652
  3.5 5.9 %copy-start.4 = (bf16[768,768]{1,0:T(8,128)(2,1)S(1)}, bf16[768,768]{1,0:T(8,128)(2,1)}, u32[]{:S(2)}) copy-start(bf16[768,768]{1,0:T(8,128)(2,1)} %param.13) | copy-start | bytes 3538948
  4.4 19.3 %collective-permute-start.4 = (bf16[272,768]{1,0:T(8,128)(2,1)}, bf16[272,768]{1,0:T(8,128)(2,1)}, u32[]{:S(2)}, u32[]{:S(2)}) collective-permute-start(bf16[272,768]{1,0:T(8,128)(2,1)} %fusion.76.own), channel_id=1, source_target_pairs={{0,4},{2,6},{4,8},{6,10},{8,12},{10,14},{12,16},{14,18},{16,20},{1... | collective-permute-start | bytes 1253384 | tf_op jit(solution)/shard_map/ppermute | solution.py:34
  6.5 58.9 %collective-permute-start.1 = (bf16[256,1536]{1,0:T(8,128)(2,1)}, bf16[256,1536]{1,0:T(8,128)(2,1)}, u32[]{:S(2)}, u32[]{:S(2)}) collective-permute-start(bf16[256,1536]{1,0:T(8,128)(2,1)} %param.8), channel_id=1, source_target_pairs={{0,1},{1,0},{2,3},{3,2},{4,5},{5,4},{6,7},{7,6},{8,9},{9,8},{10,11... | collective-permute-start | bytes 2359304 | tf_op jit(solution)/shard_map/ppermute | solution.py:30
  10.1 55.2 %collective-permute-start.2 = (bf16[272,768]{1,0:T(8,128)(2,1)S(1)}, bf16[272,768]{1,0:T(8,128)(2,1)}, u32[]{:S(2)}, u32[]{:S(2)}) collective-permute-start(bf16[272,768]{1,0:T(8,128)(2,1)S(1)} %fusion.77), channel_id=1, source_target_pairs={{0,1},{1,0},{2,3},{3,2},{4,5},{5,4},{6,7},{7,6},{8,9},{9,8},{10,11... | collective-permute-start | bytes 1253384 | tf_op jit(solution)/shard_map/ppermute | solution.py:30
  10.3 30.3 %collective-permute-start.3 = (bf16[256,1536]{1,0:T(8,128)(2,1)}, bf16[256,1536]{1,0:T(8,128)(2,1)}, u32[]{:S(2)}, u32[]{:S(2)}) collective-permute-start(bf16[256,1536]{1,0:T(8,128)(2,1)} %own.1), channel_id=1, source_target_pairs={{0,4},{2,6},{4,8},{6,10},{8,12},{10,14},{12,16},{14,18},{16,20},{1... | collective-permute-start | bytes 2359304 | tf_op jit(solution)/shard_map/ppermute | solution.py:34
  25.7 59.7 %collective-permute-start.7 = (bf16[272,768]{1,0:T(8,128)(2,1)}, bf16[272,768]{1,0:T(8,128)(2,1)}, u32[]{:S(2)}, u32[]{:S(2)}) collective-permute-start(bf16[272,768]{1,0:T(8,128)(2,1)} %shard_map.96), channel_id=1, source_target_pairs={{0,2},{2,4},{4,6},{6,8},{8,10},{10,12},{12,14},{14,16},{16,18},{18... | collective-permute-start | bytes 1253384 | tf_op jit(solution)/shard_map/ppermute | solution.py:34
  25.7 59.0 %collective-permute-start.5 = (bf16[272,768]{1,0:T(8,128)(2,1)}, bf16[272,768]{1,0:T(8,128)(2,1)}, u32[]{:S(2)}, u32[]{:S(2)}) collective-permute-start(bf16[272,768]{1,0:T(8,128)(2,1)} %collective-permute-done.4.got), channel_id=1, source_target_pairs={{0,2},{2,0},{1,3},{3,1},{4,6},{6,4},{5,7},{7,5},{8,10},{10,8},{9,1... | collective-permute-start | bytes 1253384 | tf_op jit(solution)/shard_map/ppermute | solution.py:30
  67.1 21.9 %collective-permute-start.8 = (bf16[256,1536]{1,0:T(8,128)(2,1)}, bf16[256,1536]{1,0:T(8,128)(2,1)S(1)}, u32[]{:S(2)}, u32[]{:S(2)}) collective-permute-start(bf16[256,1536]{1,0:T(8,128)(2,1)} %shard_map.95), channel_id=1, source_target_pairs={{0,2},{2,4},{4,6},{6,8},{8,10},{10,12},{12,14},{14,16},{16,18},{18... | collective-permute-start | bytes 2359304 | tf_op jit(solution)/shard_map/ppermute | solution.py:34
  71.2 1.7 copy-start.6
  72.9 1.5 copy-start.5
  76.3 9.8 %collective-permute-start.6 = (bf16[256,1536]{1,0:T(8,128)(2,1)}, bf16[256,1536]{1,0:T(8,128)(2,1)S(1)}, u32[]{:S(2)}, u32[]{:S(2)}) collective-permute-start(bf16[256,1536]{1,0:T(8,128)(2,1)} %collective-permute-done.3.got), channel_id=1, source_target_pairs={{0,2},{2,0},{1,3},{3,1},{4,6},{6,4},{5,7},{7,5},{8,10},{10,8},{9,1... | collective-permute-start | bytes 2359304 | tf_op jit(solution)/shard_map/ppermute | solution.py:30
  88.9 9.3 %collective-permute-start.10 = (bf16[256,768]{1,0:T(8,128)(2,1)S(1)}, bf16[256,768]{1,0:T(8,128)(2,1)S(1)}, u32[]{:S(2)}, u32[]{:S(2)}) collective-permute-start(bf16[256,768]{1,0:T(8,128)(2,1)S(1)} %fusion.2), channel_id=1, source_target_pairs={{0,2},{2,0},{1,3},{3,1},{4,6},{6,4},{5,7},{7,5},{8,10},{10,8},{9,1... | collective-permute-start | bytes 1179656 | tf_op jit(solution)/shard_map/ppermute | solution.py:30
  91.8 16.0 %collective-permute-start.12 = (bf16[256,768]{1,0:T(8,128)(2,1)S(1)}, bf16[256,768]{1,0:T(8,128)(2,1)S(1)}, u32[]{:S(2)}, u32[]{:S(2)}) collective-permute-start(bf16[256,768]{1,0:T(8,128)(2,1)S(1)} %fusion.3), channel_id=1, source_target_pairs={{0,250},{2,0},{4,254},{6,4},{8,2},{10,8},{12,6},{14,12},{16,10},{1... | collective-permute-start | bytes 1179656 | tf_op jit(solution)/shard_map/ppermute | solution.py:34
  95.1 8.5 %copy-start.1 = (bf16[256,768]{1,0:T(8,128)(2,1)S(1)}, bf16[256,768]{1,0:T(8,128)(2,1)}, u32[]{:S(2)}) copy-start(bf16[256,768]{1,0:T(8,128)(2,1)} %param.12) | copy-start | bytes 1179652
  95.1 8.5 %copy-start.3 = (bf16[256,768]{1,0:T(8,128)(2,1)S(1)}, bf16[256,768]{1,0:T(8,128)(2,1)}, u32[]{:S(2)}) copy-start(bf16[256,768]{1,0:T(8,128)(2,1)} %param.11) | copy-start | bytes 1179652
  95.2 12.3 %collective-permute-start.9 = (bf16[256,768]{1,0:T(8,128)(2,1)S(1)}, bf16[256,768]{1,0:T(8,128)(2,1)S(1)}, u32[]{:S(2)}, u32[]{:S(2)}) collective-permute-start(bf16[256,768]{1,0:T(8,128)(2,1)S(1)} %slice.194), channel_id=1, source_target_pairs={{0,1},{1,0},{2,3},{3,2},{4,5},{5,4},{6,7},{7,6},{8,9},{9,8},{10,11... | collective-permute-start | bytes 1179656 | tf_op jit(solution)/shard_map/ppermute | solution.py:30
  98.6 13.3 %collective-permute-start.11 = (bf16[256,768]{1,0:T(8,128)(2,1)S(1)}, bf16[256,768]{1,0:T(8,128)(2,1)S(1)}, u32[]{:S(2)}, u32[]{:S(2)}) collective-permute-start(bf16[256,768]{1,0:T(8,128)(2,1)S(1)} %add_convert_fusion), channel_id=1, source_target_pairs={{0,252},{2,254},{4,0},{6,2},{8,4},{10,6},{12,8},{14,10},{16,12},{1... | collective-permute-start | bytes 1179656 | tf_op jit(solution)/shard_map/ppermute | solution.py:34
  103.7 11.0 %collective-permute-start = (bf16[256,768]{1,0:T(8,128)(2,1)S(1)}, bf16[256,768]{1,0:T(8,128)(2,1)S(1)}, u32[]{:S(2)}, u32[]{:S(2)}) collective-permute-start(bf16[256,768]{1,0:T(8,128)(2,1)S(1)} %get-tuple-element.28), channel_id=1, source_target_pairs={{0,2},{2,0},{1,3},{3,1},{4,6},{6,4},{5,7},{7,5},{8,10},{10,8},{9,1... | collective-permute-start | bytes 1179656 | tf_op jit(solution)/shard_map/ppermute | solution.py:30
  113.1 2.5 %collective-permute-start.14 = (bf16[256,768]{1,0:T(8,128)(2,1)S(1)}, bf16[256,768]{1,0:T(8,128)(2,1)S(1)}, u32[]{:S(2)}, u32[]{:S(2)}) collective-permute-start(bf16[256,768]{1,0:T(8,128)(2,1)S(1)} %get-tuple-element.24), channel_id=1, source_target_pairs={{0,2},{2,0},{1,3},{3,1},{4,6},{6,4},{5,7},{7,5},{8,10},{10,8},{9,1... | collective-permute-start | bytes 1179656 | tf_op jit(solution)/shard_map/ppermute | solution.py:30
  114.3 2.2 %collective-permute-start.13 = (bf16[256,768]{1,0:T(8,128)(2,1)S(1)}, bf16[256,768]{1,0:T(8,128)(2,1)S(1)}, u32[]{:S(2)}, u32[]{:S(2)}) collective-permute-start(bf16[256,768]{1,0:T(8,128)(2,1)S(1)} %get-tuple-element.22), channel_id=1, source_target_pairs={{0,2},{2,0},{1,3},{3,1},{4,6},{6,4},{5,7},{7,5},{8,10},{10,8},{9,1... | collective-permute-start | bytes 1179656 | tf_op jit(solution)/shard_map/ppermute | solution.py:30
  165.1 3.9 %collective-permute-start.15 = (f32[32,768]{1,0:T(8,128)S(1)}, f32[32,768]{1,0:T(8,128)S(1)}, u32[]{:S(2)}, u32[]{:S(2)}) collective-permute-start(f32[32,768]{1,0:T(8,128)S(1)} %pad_maximum_fusion.6), channel_id=1, source_target_pairs={{0,128},{128,0},{1,129},{129,1},{2,130},{130,2},{3,131},{131,3},{4... | collective-permute-start | bytes 294920 | tf_op jit(solution)/shard_map/ppermute | solution.py:30
  165.3 6.0 %collective-permute-start.16 = (f32[32,768]{1,0:T(8,128)S(1)}, f32[32,768]{1,0:T(8,128)S(1)}, u32[]{:S(2)}, u32[]{:S(2)}) collective-permute-start(f32[32,768]{1,0:T(8,128)S(1)} %pad_maximum_fusion.6), channel_id=1, source_target_pairs={{0,1},{1,0},{2,3},{3,2},{4,5},{5,4},{6,7},{7,6},{8,9},{9,8},{10,11... | collective-permute-start | bytes 294920 | tf_op jit(solution)/shard_map/ppermute | solution.py:30
  168.2 4.7 %collective-permute-start.17 = (f32[32,768]{1,0:T(8,128)S(1)}, f32[32,768]{1,0:T(8,128)S(1)}, u32[]{:S(2)}, u32[]{:S(2)}) collective-permute-start(f32[32,768]{1,0:T(8,128)S(1)} %pad_maximum_fusion.6), channel_id=1, source_target_pairs={{0,129},{1,128},{128,1},{129,0},{2,131},{3,130},{130,3},{131,2},{4... | collective-permute-start | bytes 294920 | tf_op jit(solution)/shard_map/ppermute | solution.py:128
  201.5 8.0 %collective-permute-start.18 = (f16[768,768]{1,0:T(8,128)(2,1)S(1)}, f16[768,768]{1,0:T(8,128)(2,1)S(1)}, u32[]{:S(2)}, u32[]{:S(2)}) collective-permute-start(f16[768,768]{1,0:T(8,128)(2,1)S(1)} %bitcast.32), channel_id=1, source_target_pairs={{0,2},{2,0},{1,3},{3,1},{4,6},{6,4},{5,7},{7,5},{8,10},{10,8},{9,1... | collective-permute-start | bytes 3538952 | tf_op jit(solution)/shard_map/ppermute | solution.py:30
  206.9 2.5 %collective-permute-start.19 = (f32[8,768]{1,0:T(8,128)S(1)}, f32[8,768]{1,0:T(8,128)S(1)}, u32[]{:S(2)}, u32[]{:S(2)}) collective-permute-start(f32[8,768]{1,0:T(8,128)S(1)} %broadcast_in_dim.29), channel_id=1, source_target_pairs={{0,2},{2,0},{1,3},{3,1},{4,6},{6,4},{5,7},{7,5},{8,10},{10,8},{9,1... | collective-permute-start | bytes 73736 | tf_op jit(solution)/shard_map/ppermute | solution.py:30

commit v10 on v2

--- a/solution.py
+++ b/solution.py
@@ -64,34 +64,37 @@
 
 def packed(values, exponent):
     scaled = (values * jnp.exp2(-exponent)).astype(f16)
-    note = jnp.full((values.shape[0], 8, values.shape[2]), exponent, f32).astype(f16)
+    shape = (values.shape[0], 8, values.shape[2])
+    note = jnp.broadcast_to(exponent.astype(f16), shape)
     return jnp.concatenate([scaled, note], axis=1)
 
 
 def unpacked_sum(blocks):
-    exponents = blocks[:, -8, 0].astype(f32)
-    scales = jnp.exp2(exponents)[:, None, None]
-    return (blocks[:, :-8].astype(f32) * scales).sum(axis=0), exponents.max()
+    exponents = blocks[:, -8:-7, :].astype(f32)
+    summed = (blocks[:, :-8].astype(f32) * jnp.exp2(exponents)).sum(axis=0)
+    return summed, exponents.max(axis=0)
 
 
 def sum_everywhere(part):
     ds = part.shape[0]
     biggest = jnp.log2(jnp.maximum(jnp.max(jnp.abs(part)), 1e-30))
     exponent = jnp.clip(jnp.ceil(biggest) - 14.0, -110.0, 110.0)
-    blocks = lax.all_to_all(packed(part.reshape(4, ds // 4, ds), exponent), "x", 0, 0, tiled=True)
+    blocks = packed(part.reshape(4, ds // 4, ds), exponent)
+    blocks = lax.all_to_all(blocks, "x", 0, 0, tiled=True)
     summed, exponent = unpacked_sum(blocks)
     exponent = exponent + 2.0
     blocks = packed(summed.reshape(8, ds // 32, ds), exponent)
     blocks = lax.all_to_all(blocks, "z", 0, 0, tiled=True)
     summed, exponent = unpacked_sum(blocks)
-    noted = jnp.concatenate([summed, jnp.full((8, ds), exponent, f32)], axis=0)
+    noted = jnp.concatenate([summed, jnp.broadcast_to(exponent, (8, ds))], axis=0)
     other_l = swap(noted, "yl")
     other_h = swap(noted, "yh")
     other_b = lax.ppermute(noted, ("yl", "yh"), [(0, 3), (1, 2), (2, 1), (3, 0)])
     summed = ((noted + other_l) + (other_h + other_b))[:-8]
-    exponent = jnp.maximum(exponent, jnp.maximum(other_l[-8, 0], other_h[-8, 0]))
-    exponent = jnp.maximum(exponent, other_b[-8, 0]) + 5.0
-    other_e = swap(jnp.full((8, 128), exponent, f32), "core")[0, 0]
+    exponent = jnp.maximum(
+        jnp.maximum(noted, other_l), jnp.maximum(other_h, other_b)
+    )[-8:-7] + 5.0
+    other_e = swap(jnp.broadcast_to(exponent, (8, ds)), "core")[0:1]
     block = (summed * jnp.exp2(-exponent)).astype(f16)
     spread = jnp.broadcast_to(block[None], (8,) + block.shape)
     gathered = lax.all_to_all(spread, "z", 0, 0, tiled=True).reshape(ds // 4, ds)

time: 203 us -> 197 us (0.970)
  between operations: 5.86 us -> 1.84 us
  local copies, waits for them, and re-layouts: 3.27 us -> 0.51 us
  waiting for transfers between devices: 62.7 us -> 65 us
    slice x4 -> x1, local copies, waits for them, and re-layouts: 2.1 us -> 0.02 us  [unpacked_sum(): exponents = blocks[:, -8:-7, :].astype(f32)]
  transfers between devices with their start and end apart: 24 -> 24, of which waited for: 8 -> 9; matrix products, arithmetic and copies ran while one was open for 15% -> 15% of each run, Pallas kernels for 0% -> 0%
where the time goes in v10:
time: 197 us
  blocking collectives  65.1 us (33%)
  waiting for transfers between devices  65 us (33%)
  starting transfers between devices  30.1 us (15%)
  matrix products  18.8 us (10%)
  other arithmetic  15.4 us (8%)
    ppermute x14, waiting for transfers between devices, swap(): return lax.ppermute(block, axis, [(0, 1), (1, 0)])  43.9 us
    ppermute x14, starting transfers between devices, swap(): return lax.ppermute(block, axis, [(0, 1), (1, 0)])  22.3 us
    ppermute x9, waiting for transfers between devices, along_dp(): return lax.ppermute(block, DP, route)  19.4 us
    all_to_all x1, blocking collectives, sum_everywhere(): blocks = lax.all_to_all(blocks, 'x', 0, 0, tiled=True)  18.9 us
    all_to_all x1, blocking collectives, sum_everywhere(): blocks = lax.all_to_all(blocks, 'z', 0, 0, tiled=True)  16.5 us
    all_to_all x1, blocking collectives, sum_everywhere(): own_total = lax.all_to_all(spread, 'x', 0, 0, tiled=True).reshape(ds, ds)  15.2 us
    all_to_all x1, blocking collectives, sum_everywhere(): lax.all_to_all(spread, 'z', 0, 0, tiled=True).reshape(ds // 4, ds)  14.5 us
    ppermute x9, starting transfers between devices, along_dp(): return lax.ppermute(block, DP, route)  7.56 us
  transfers between devices with their start and end apart: 24, of which 9 were waited for; matrix products, arithmetic and copies ran while one was open for 15% of the time, Pallas kernels for 0%

profile of v10, /device:TPU:1, one launch (start us, length us, event | category | flops | bytes accessed | tf_op | source)
XLA Modules:
  0.0 196.7 jit_solution(17582682404573081789)
XLA Ops:
  0.7 4.2 %collective-permute-start.10 = (s32[256]{0:T(256)}, s32[256]{0:T(256)}, u32[]{:S(2)}, u32[]{:S(2)}) collective-permute-start(s32[256]{0:T(256)} %param.15), channel_id=1, source_target_pairs={{0,6},{2,8},{4,10},{6,12},{8,14},{10,16},{12,18},{14,20},{16,22},{... | collective-permute-start | bytes 3080 | tf_op jit(solution)/shard_map/ppermute | solution.py:30
  4.9 2.9 %collective-permute-start.3 = (s32[256]{0:T(256)}, s32[256]{0:T(256)}, u32[]{:S(2)}, u32[]{:S(2)}) collective-permute-start(s32[256]{0:T(256)} %param.15), channel_id=1, source_target_pairs={{0,1},{1,0},{2,3},{3,2},{4,5},{5,4},{6,7},{7,6},{8,9},{9,8},{10,11... | collective-permute-start | bytes 3080 | tf_op jit(solution)/shard_map/ppermute | solution.py:26
  7.8 1.4 fusion.2
  9.2 2.5 %fusion.3 = bf16[256,1536]{1,0:T(8,128)(2,1)} fusion(bf16[256,1536]{1,0:T(8,128)(2,1)} %param.10, f32[256]{0:T(256)S(1)} %add_sqrt_fusion), kind=kLoop, calls=%fused_computation.11 | loop fusion | flops 1179648 | bytes 1573888 | tf_op jit(solution)/shard_map/convert_element_type | solution.py:135
  12.6 0.9 fusion.94
  13.5 1.6 collective-permute-start.4
  15.1 1.5 multiply_reduce_fusion.1
  17.1 1.1 divide_convert_fusion
  18.2 0.9 fusion.93
  19.1 1.2 collective-permute-start.6
  20.3 0.7 pad_add_fusion
  21.1 2.9 %collective-permute-start.1 = (bf16[256,768]{1,0:T(8,128)(2,1)}, bf16[256,768]{1,0:T(8,128)(2,1)S(1)}, u32[]{:S(2)}, u32[]{:S(2)}) collective-permute-start(bf16[256,768]{1,0:T(8,128)(2,1)} %fusion.93), channel_id=1, source_target_pairs={{0,1},{1,0},{2,3},{3,2},{4,5},{5,4},{6,7},{7,6},{8,9},{9,8},{10,11... | collective-permute-start | bytes 1179656 | tf_op jit(solution)/shard_map/ppermute | solution.py:26
  24.1 0.7 broadcast_select_fusion.9
  24.7 18.2 %collective-permute-done.4 = bf16[256,768]{1,0:T(8,128)(2,1)} collective-permute-done((bf16[256,768]{1,0:T(8,128)(2,1)}, bf16[256,768]{1,0:T(8,128)(2,1)}, u32[]{:S(2)}, u32[]{:S(2)}) %collective-permute-start.4) | collective-permute-done | bytes 393248 | tf_op jit(solution)/shard_map/ppermute | solution.py:30
  42.9 1.2 broadcast_select_fusion.5
  44.2 0.9 collective-permute-start.7
  45.1 1.6 broadcast_select_fusion
  46.7 18.9 %collective-permute-done.2 = bf16[256,1536]{1,0:T(8,128)(2,1)S(1)} collective-permute-done((bf16[256,1536]{1,0:T(8,128)(2,1)}, bf16[256,1536]{1,0:T(8,128)(2,1)S(1)}, u32[]{:S(2)}, u32[]{:S(2)}) %collective-permute-start.2) | collective-permute-done | bytes 786464 | tf_op jit(solution)/shard_map/ppermute | solution.py:26
  65.6 1.8 fusion.57
  67.4 0.9 collective-permute-start.8
  68.3 1.8 fusion.50
  70.1 10.2 %collective-permute-done.1 = bf16[256,768]{1,0:T(8,128)(2,1)S(1)} collective-permute-done((bf16[256,768]{1,0:T(8,128)(2,1)}, bf16[256,768]{1,0:T(8,128)(2,1)S(1)}, u32[]{:S(2)}, u32[]{:S(2)}) %collective-permute-start.1) | collective-permute-done | bytes 393248 | tf_op jit(solution)/shard_map/ppermute | solution.py:26
  80.3 1.4 fusion.67
  81.7 1.4 fusion.66
  83.2 1.4 fusion.95
  84.5 1.4 fusion.96
  85.9 0.6 fusion.43
  87.4 0.6 collective-permute-start.14
  88.0 0.7 fusion.36
  90.5 3.7 %collective-permute-start.13 = (bf16[256,768]{1,0:T(8,128)(2,1)S(1)}, bf16[256,768]{1,0:T(8,128)(2,1)S(1)}, u32[]{:S(2)}, u32[]{:S(2)}) collective-permute-start(bf16[256,768]{1,0:T(8,128)(2,1)S(1)} %slice.118), channel_id=1, source_target_pairs={{0,1},{1,0},{2,3},{3,2},{4,5},{5,4},{6,7},{7,6},{8,9},{9,8},{10,11... | collective-permute-start | bytes 1179656 | tf_op jit(solution)/shard_map/ppermute | solution.py:26
  95.1 8.5 %collective-permute-done.13 = bf16[256,768]{1,0:T(8,128)(2,1)S(1)} collective-permute-done((bf16[256,768]{1,0:T(8,128)(2,1)S(1)}, bf16[256,768]{1,0:T(8,128)(2,1)S(1)}, u32[]{:S(2)}, u32[]{:S(2)}) %collective-permute-start.13) | collective-permute-done | bytes 393248 | tf_op jit(solution)/shard_map/ppermute | solution.py:26
  103.9 1.1 collective-permute-done.15
  105.1 0.6 multiply_reduce_fusion.2
  106.3 1.2 collective-permute-start.18
  107.8 1.0 collective-permute-done.18
  108.8 0.8 fusion.73
  109.7 1.5 abs_reduce_fusion
  112.3 18.9 %all_to_all.20 = f16[4,200,768]{2,1,0:T(8,128)(2,1)S(1)} all-to-all(f16[4,200,768]{2,1,0:T(8,128)(2,1)S(1)} %concatenate.33), channel_id=1, replica_groups=mesh['yl'=2,'z'=8,'x'=4,'core'=2,'yh'=2] {'x'}, dimensions={0} | all-to-all | bytes 2457600 | tf_op jit(solution)/shard_map/all_to_all | solution.py:83
  131.7 16.5 %all_to_all.21 = f16[8,32,768]{2,1,0:T(8,128)(2,1)S(1)} all-to-all(f16[8,32,768]{2,1,0:T(8,128)(2,1)S(1)} %pad_maximum_fusion.5), channel_id=1, replica_groups=mesh['yl'=2,'z'=8,'x'=4,'core'=2,'yh'=2] {'z'}, dimensions={0} | all-to-all | bytes 786432 | tf_op jit(solution)/shard_map/all_to_all | solution.py:87
  148.3 0.6 collective-permute-start.19
  148.9 3.2 %collective-permute-start.20 = (f32[32,768]{1,0:T(8,128)S(1)}, f32[32,768]{1,0:T(8,128)S(1)}, u32[]{:S(2)}, u32[]{:S(2)}) collective-permute-start(f32[32,768]{1,0:T(8,128)S(1)} %pad_maximum_fusion.6), channel_id=1, source_target_pairs={{0,1},{1,0},{2,3},{3,2},{4,5},{5,4},{6,7},{7,6},{8,9},{9,8},{10,11... | collective-permute-start | bytes 294920 | tf_op jit(solution)/shard_map/ppermute | solution.py:26
  152.3 2.8 %collective-permute-done.20 = f32[32,768]{1,0:T(8,128)S(1)} collective-permute-done((f32[32,768]{1,0:T(8,128)S(1)}, f32[32,768]{1,0:T(8,128)S(1)}, u32[]{:S(2)}, u32[]{:S(2)}) %collective-permute-start.20) | collective-permute-done | bytes 98336 | tf_op jit(solution)/shard_map/ppermute | solution.py:26
  155.1 1.7 collective-permute-done.21
  156.9 14.5 %all_to_all.22 = f16[8,24,768]{2,1,0:T(8,128)(2,1)S(1)} all-to-all(f16[8,24,768]{2,1,0:T(8,128)(2,1)S(1)} %broadcast_in_dim.16), channel_id=1, replica_groups=mesh['yl'=2,'z'=8,'x'=4,'core'=2,'yh'=2] {'z'}, dimensions={0} | all-to-all | bytes 589824 | tf_op jit(solution)/shard_map/all_to_all | solution.py:100
  171.5 15.2 %all_to_all.23 = f16[4,192,768]{2,1,0:T(8,128)(2,1)S(1)} all-to-all(f16[4,192,768]{2,1,0:T(8,128)(2,1)S(1)} %broadcast_in_dim.18), channel_id=1, replica_groups=mesh['yl'=2,'z'=8,'x'=4,'core'=2,'yh'=2] {'x'}, dimensions={0} | all-to-all | bytes 2359296 | tf_op jit(solution)/shard_map/all_to_all | solution.py:102
  186.7 4.7 %collective-permute-start.22 = (f16[768,768]{1,0:T(8,128)(2,1)S(1)}, f16[768,768]{1,0:T(8,128)(2,1)S(1)}, u32[]{:S(2)}, u32[]{:S(2)}) collective-permute-start(f16[768,768]{1,0:T(8,128)(2,1)S(1)} %bitcast.37), channel_id=1, source_target_pairs={{0,2},{2,0},{1,3},{3,1},{4,6},{6,4},{5,7},{7,5},{8,10},{10,8},{9,1... | collective-permute-start | bytes 3538952 | tf_op jit(solution)/shard_map/ppermute | solution.py:26
  191.4 2.5 %collective-permute-done.23 = f32[8,768]{1,0:T(8,128)S(1)} collective-permute-done((f32[8,768]{1,0:T(8,128)S(1)}, f32[8,768]{1,0:T(8,128)S(1)}, u32[]{:S(2)}, u32[]{:S(2)}) %collective-permute-start.23) | collective-permute-done | bytes 24608 | tf_op jit(solution)/shard_map/ppermute | solution.py:26
  193.9 2.7 %fusion = (f32[768,768]{1,0:T(8,128)}, f32[768,768]{1,0:T(8,128)}) fusion(f16[768,768]{1,0:T(8,128)(2,1)S(1)} %collective-permute-done.22, f32[768]{0:T(1024)S(1)} %fusion.89, f32[768]{0:T(1024)S(1)} %get-tuple-element.2, pred[]{:T(512)S(6)} %eq.20, f16[4,192,768]{2,1,0:T(8,128)(2,1)S(1)} %all_to_all.23), kind=kLoop, calls=%fused_computation.1 | loop fusion | flops 3538944 | bytes 7084033 | tf_op jit(solution)/shard_map/jit(_where)/select_n | solution.py:185
  (88 shorter events, 7.9 us)
Async XLA Ops:
  0.6 11.4 %copy-start = (bf16[768,768]{1,0:T(8,128)(2,1)S(1)}, bf16[768,768]{1,0:T(8,128)(2,1)}, u32[]{:S(2)}) copy-start(bf16[768,768]{1,0:T(8,128)(2,1)} %param.14) | copy-start | bytes 3538948
  0.6 11.4 %copy-start.2 = (bf16[256,768]{1,0:T(8,128)(2,1)S(1)}, bf16[256,768]{1,0:T(8,128)(2,1)}, u32[]{:S(2)}) copy-start(bf16[256,768]{1,0:T(8,128)(2,1)} %param.12) | copy-start | bytes 1179652
  0.7 20.4 %collective-permute-start.10 = (s32[256]{0:T(256)}, s32[256]{0:T(256)}, u32[]{:S(2)}, u32[]{:S(2)}) collective-permute-start(s32[256]{0:T(256)} %param.15), channel_id=1, source_target_pairs={{0,6},{2,8},{4,10},{6,12},{8,14},{10,16},{12,18},{14,20},{16,22},{... | collective-permute-start | bytes 3080 | tf_op jit(solution)/shard_map/ppermute | solution.py:30
  4.9 16.3 %collective-permute-start.9 = (s32[256]{0:T(256)}, s32[256]{0:T(256)}, u32[]{:S(2)}, u32[]{:S(2)}) collective-permute-start(s32[256]{0:T(256)} %param.15), channel_id=1, source_target_pairs={{0,2},{2,4},{4,6},{6,8},{8,10},{10,12},{12,14},{14,16},{16,18},{18... | collective-permute-start | bytes 3080 | tf_op jit(solution)/shard_map/ppermute | solution.py:30
  4.9 14.2 %collective-permute-start.3 = (s32[256]{0:T(256)}, s32[256]{0:T(256)}, u32[]{:S(2)}, u32[]{:S(2)}) collective-permute-start(s32[256]{0:T(256)} %param.15), channel_id=1, source_target_pairs={{0,1},{1,0},{2,3},{3,2},{4,5},{5,4},{6,7},{7,6},{8,9},{9,8},{10,11... | collective-permute-start | bytes 3080 | tf_op jit(solution)/shard_map/ppermute | solution.py:26
  7.8 7.3 %copy-start.11 = (bf16[256,1536]{1,0:T(8,128)(2,1)S(1)}, bf16[256,1536]{1,0:T(8,128)(2,1)}, u32[]{:S(2)}) copy-start(bf16[256,1536]{1,0:T(8,128)(2,1)} %param.8) | copy-start | bytes 2359300
  9.2 5.8 %copy-start.10 = (bf16[1536,1536]{1,0:T(8,128)(2,1)S(1)}, bf16[1536,1536]{1,0:T(8,128)(2,1)}, u32[]{:S(2)}) copy-start(bf16[1536,1536]{1,0:T(8,128)(2,1)} %param.9) | copy-start | bytes 14155780
  11.7 32.5 %collective-permute-start.5 = (bf16[256,1536]{1,0:T(8,128)(2,1)}, bf16[256,1536]{1,0:T(8,128)(2,1)}, u32[]{:S(2)}, u32[]{:S(2)}) collective-permute-start(bf16[256,1536]{1,0:T(8,128)(2,1)} %fusion.3), channel_id=1, source_target_pairs={{0,4},{2,6},{4,8},{6,10},{8,12},{10,14},{12,16},{14,18},{16,20},{1... | collective-permute-start | bytes 2359304 | tf_op jit(solution)/shard_map/ppermute | solution.py:30
  13.5 3.1 %copy-start.4 = (bf16[256,768]{1,0:T(8,128)(2,1)S(1)}, bf16[256,768]{1,0:T(8,128)(2,1)}, u32[]{:S(2)}) copy-start(bf16[256,768]{1,0:T(8,128)(2,1)} %param.11) | copy-start | bytes 1179652
  13.5 3.1 %copy-start.6 = (bf16[768,768]{1,0:T(8,128)(2,1)S(1)}, bf16[768,768]{1,0:T(8,128)(2,1)}, u32[]{:S(2)}) copy-start(bf16[768,768]{1,0:T(8,128)(2,1)} %param.13) | copy-start | bytes 3538948
  13.5 29.5 %collective-permute-start.4 = (bf16[256,768]{1,0:T(8,128)(2,1)}, bf16[256,768]{1,0:T(8,128)(2,1)}, u32[]{:S(2)}, u32[]{:S(2)}) collective-permute-start(bf16[256,768]{1,0:T(8,128)(2,1)} %fusion.94), channel_id=1, source_target_pairs={{0,4},{2,6},{4,8},{6,10},{8,12},{10,14},{12,16},{14,18},{16,20},{1... | collective-permute-start | bytes 1179656 | tf_op jit(solution)/shard_map/ppermute | solution.py:30
  17.1 2.0 copy-start.9
  18.2 26.9 %copy-start.1 = (bf16[256,1536]{1,0:T(8,128)(2,1)S(1)}, bf16[256,1536]{1,0:T(8,128)(2,1)}, u32[]{:S(2)}) copy-start(bf16[256,1536]{1,0:T(8,128)(2,1)} %param.10) | copy-start | bytes 2359300
  19.1 48.3 %collective-permute-start.6 = (s32[256]{0:T(256)S(1)}, s32[256]{0:T(256)S(1)}, u32[]{:S(2)}, u32[]{:S(2)}) collective-permute-start(s32[256]{0:T(256)S(1)} %copy-done.9), channel_id=1, source_target_pairs={{0,4},{2,6},{4,8},{6,10},{8,12},{10,14},{12,16},{14,18},{16,20},{1... | collective-permute-start | bytes 3080 | tf_op jit(solution)/shard_map/ppermute | solution.py:30
  21.0 44.6 %collective-permute-start.2 = (bf16[256,1536]{1,0:T(8,128)(2,1)}, bf16[256,1536]{1,0:T(8,128)(2,1)S(1)}, u32[]{:S(2)}, u32[]{:S(2)}) collective-permute-start(bf16[256,1536]{1,0:T(8,128)(2,1)} %divide_convert_fusion), channel_id=1, source_target_pairs={{0,1},{1,0},{2,3},{3,2},{4,5},{5,4},{6,7},{7,6},{8,9},{9,8},{10,11... | collective-permute-start | bytes 2359304 | tf_op jit(solution)/shard_map/ppermute | solution.py:26
  21.1 59.1 %collective-permute-start.1 = (bf16[256,768]{1,0:T(8,128)(2,1)}, bf16[256,768]{1,0:T(8,128)(2,1)S(1)}, u32[]{:S(2)}, u32[]{:S(2)}) collective-permute-start(bf16[256,768]{1,0:T(8,128)(2,1)} %fusion.93), channel_id=1, source_target_pairs={{0,1},{1,0},{2,3},{3,2},{4,5},{5,4},{6,7},{7,6},{8,9},{9,8},{10,11... | collective-permute-start | bytes 1179656 | tf_op jit(solution)/shard_map/ppermute | solution.py:26
  44.1 21.5 %copy-start.7 = (bf16[256,1536]{1,0:T(8,128)(2,1)S(1)}, bf16[256,1536]{1,0:T(8,128)(2,1)}, u32[]{:S(2)}) copy-start(bf16[256,1536]{1,0:T(8,128)(2,1)} %divide_convert_fusion) | copy-start | bytes 2359300
  44.1 44.6 %collective-permute-start.11 = (bf16[256,768]{1,0:T(8,128)(2,1)S(1)}, bf16[256,768]{1,0:T(8,128)(2,1)S(1)}, u32[]{:S(2)}, u32[]{:S(2)}) collective-permute-start(bf16[256,768]{1,0:T(8,128)(2,1)S(1)} %broadcast_select_fusion.5), channel_id=1, source_target_pairs={{0,2},{2,4},{4,6},{6,8},{8,10},{10,12},{12,14},{14,16},{16,18},{18... | collective-permute-start | bytes 1179656 | tf_op jit(solution)/shard_map/ppermute | solution.py:30
  44.2 42.3 %collective-permute-start.7 = (bf16[256,768]{1,0:T(8,128)(2,1)}, bf16[256,768]{1,0:T(8,128)(2,1)S(1)}, u32[]{:S(2)}, u32[]{:S(2)}) collective-permute-start(bf16[256,768]{1,0:T(8,128)(2,1)} %collective-permute-done.4), channel_id=1, source_target_pairs={{0,2},{2,0},{1,3},{3,1},{4,6},{6,4},{5,7},{7,5},{8,10},{10,8},{9,1... | collective-permute-start | bytes 1179656 | tf_op jit(solution)/shard_map/ppermute | solution.py:26
  65.6 22.4 %collective-permute-start.12 = (bf16[256,1536]{1,0:T(8,128)(2,1)S(1)}, bf16[256,1536]{1,0:T(8,128)(2,1)S(1)}, u32[]{:S(2)}, u32[]{:S(2)}) collective-permute-start(bf16[256,1536]{1,0:T(8,128)(2,1)S(1)} %broadcast_select_fusion), channel_id=1, source_target_pairs={{0,2},{2,4},{4,6},{6,8},{8,10},{10,12},{12,14},{14,16},{16,18},{18... | collective-permute-start | bytes 2359304 | tf_op jit(solution)/shard_map/ppermute | solution.py:30
  67.4 12.9 %copy-start.8 = (bf16[256,768]{1,0:T(8,128)(2,1)S(1)}, bf16[256,768]{1,0:T(8,128)(2,1)}, u32[]{:S(2)}) copy-start(bf16[256,768]{1,0:T(8,128)(2,1)} %fusion.93) | copy-start | bytes 1179652
  67.4 18.5 %collective-permute-start.8 = (bf16[256,1536]{1,0:T(8,128)(2,1)}, bf16[256,1536]{1,0:T(8,128)(2,1)S(1)}, u32[]{:S(2)}, u32[]{:S(2)}) collective-permute-start(bf16[256,1536]{1,0:T(8,128)(2,1)} %collective-permute-done.5), channel_id=1, source_target_pairs={{0,2},{2,0},{1,3},{3,1},{4,6},{6,4},{5,7},{7,5},{8,10},{10,8},{9,1... | collective-permute-start | bytes 2359304 | tf_op jit(solution)/shard_map/ppermute | solution.py:26
  87.4 6.8 %collective-permute-start.14 = (bf16[256,768]{1,0:T(8,128)(2,1)S(1)}, bf16[256,768]{1,0:T(8,128)(2,1)S(1)}, u32[]{:S(2)}, u32[]{:S(2)}) collective-permute-start(bf16[256,768]{1,0:T(8,128)(2,1)S(1)} %fusion.8), channel_id=1, source_target_pairs={{0,2},{2,0},{1,3},{3,1},{4,6},{6,4},{5,7},{7,5},{8,10},{10,8},{9,1... | collective-permute-start | bytes 1179656 | tf_op jit(solution)/shard_map/ppermute | solution.py:26
  89.5 14.4 %collective-permute-start.16 = (bf16[256,768]{1,0:T(8,128)(2,1)S(1)}, bf16[256,768]{1,0:T(8,128)(2,1)S(1)}, u32[]{:S(2)}, u32[]{:S(2)}) collective-permute-start(bf16[256,768]{1,0:T(8,128)(2,1)S(1)} %fusion.9), channel_id=1, source_target_pairs={{0,250},{2,0},{4,254},{6,4},{8,2},{10,8},{12,6},{14,12},{16,10},{1... | collective-permute-start | bytes 1179656 | tf_op jit(solution)/shard_map/ppermute | solution.py:30
  90.4 4.3 %copy-start.3 = (bf16[256,768]{1,0:T(8,128)(2,1)S(1)}, bf16[256,768]{1,0:T(8,128)(2,1)}, u32[]{:S(2)}) copy-start(bf16[256,768]{1,0:T(8,128)(2,1)} %param.12) | copy-start | bytes 1179652
  90.4 4.3 %copy-start.5 = (bf16[256,768]{1,0:T(8,128)(2,1)S(1)}, bf16[256,768]{1,0:T(8,128)(2,1)}, u32[]{:S(2)}) copy-start(bf16[256,768]{1,0:T(8,128)(2,1)} %param.11) | copy-start | bytes 1179652
  90.5 13.2 %collective-permute-start.13 = (bf16[256,768]{1,0:T(8,128)(2,1)S(1)}, bf16[256,768]{1,0:T(8,128)(2,1)S(1)}, u32[]{:S(2)}, u32[]{:S(2)}) collective-permute-start(bf16[256,768]{1,0:T(8,128)(2,1)S(1)} %slice.118), channel_id=1, source_target_pairs={{0,1},{1,0},{2,3},{3,2},{4,5},{5,4},{6,7},{7,6},{8,9},{9,8},{10,11... | collective-permute-start | bytes 1179656 | tf_op jit(solution)/shard_map/ppermute | solution.py:26
  94.6 10.5 %collective-permute-start.15 = (bf16[256,768]{1,0:T(8,128)(2,1)S(1)}, bf16[256,768]{1,0:T(8,128)(2,1)S(1)}, u32[]{:S(2)}, u32[]{:S(2)}) collective-permute-start(bf16[256,768]{1,0:T(8,128)(2,1)S(1)} %fusion.7), channel_id=1, source_target_pairs={{0,252},{2,254},{4,0},{6,2},{8,4},{10,6},{12,8},{14,10},{16,12},{1... | collective-permute-start | bytes 1179656 | tf_op jit(solution)/shard_map/ppermute | solution.py:30
  94.8 13.0 %collective-permute-start = (bf16[256,768]{1,0:T(8,128)(2,1)S(1)}, bf16[256,768]{1,0:T(8,128)(2,1)S(1)}, u32[]{:S(2)}, u32[]{:S(2)}) collective-permute-start(bf16[256,768]{1,0:T(8,128)(2,1)S(1)} %get-tuple-element.16), channel_id=1, source_target_pairs={{0,2},{2,0},{1,3},{3,1},{4,6},{6,4},{5,7},{7,5},{8,10},{10,8},{9,1... | collective-permute-start | bytes 1179656 | tf_op jit(solution)/shard_map/ppermute | solution.py:26
  106.3 2.6 %collective-permute-start.18 = (bf16[256,768]{1,0:T(8,128)(2,1)S(1)}, bf16[256,768]{1,0:T(8,128)(2,1)S(1)}, u32[]{:S(2)}, u32[]{:S(2)}) collective-permute-start(bf16[256,768]{1,0:T(8,128)(2,1)S(1)} %get-tuple-element.12), channel_id=1, source_target_pairs={{0,2},{2,0},{1,3},{3,1},{4,6},{6,4},{5,7},{7,5},{8,10},{10,8},{9,1... | collective-permute-start | bytes 1179656 | tf_op jit(solution)/shard_map/ppermute | solution.py:26
  107.5 2.2 %collective-permute-start.17 = (bf16[256,768]{1,0:T(8,128)(2,1)S(1)}, bf16[256,768]{1,0:T(8,128)(2,1)S(1)}, u32[]{:S(2)}, u32[]{:S(2)}) collective-permute-start(bf16[256,768]{1,0:T(8,128)(2,1)S(1)} %get-tuple-element.10), channel_id=1, source_target_pairs={{0,2},{2,0},{1,3},{3,1},{4,6},{6,4},{5,7},{7,5},{8,10},{10,8},{9,1... | collective-permute-start | bytes 1179656 | tf_op jit(solution)/shard_map/ppermute | solution.py:26
  148.3 4.0 %collective-permute-start.19 = (f32[32,768]{1,0:T(8,128)S(1)}, f32[32,768]{1,0:T(8,128)S(1)}, u32[]{:S(2)}, u32[]{:S(2)}) collective-permute-start(f32[32,768]{1,0:T(8,128)S(1)} %pad_maximum_fusion.6), channel_id=1, source_target_pairs={{0,128},{128,0},{1,129},{129,1},{2,130},{130,2},{3,131},{131,3},{4... | collective-permute-start | bytes 294920 | tf_op jit(solution)/shard_map/ppermute | solution.py:26
  148.9 6.1 %collective-permute-start.20 = (f32[32,768]{1,0:T(8,128)S(1)}, f32[32,768]{1,0:T(8,128)S(1)}, u32[]{:S(2)}, u32[]{:S(2)}) collective-permute-start(f32[32,768]{1,0:T(8,128)S(1)} %pad_maximum_fusion.6), channel_id=1, source_target_pairs={{0,1},{1,0},{2,3},{3,2},{4,5},{5,4},{6,7},{7,6},{8,9},{9,8},{10,11... | collective-permute-start | bytes 294920 | tf_op jit(solution)/shard_map/ppermute | solution.py:26
  152.1 4.7 %collective-permute-start.21 = (f32[32,768]{1,0:T(8,128)S(1)}, f32[32,768]{1,0:T(8,128)S(1)}, u32[]{:S(2)}, u32[]{:S(2)}) collective-permute-start(f32[32,768]{1,0:T(8,128)S(1)} %pad_maximum_fusion.6), channel_id=1, source_target_pairs={{0,129},{1,128},{128,1},{129,0},{2,131},{3,130},{130,3},{131,2},{4... | collective-permute-start | bytes 294920 | tf_op jit(solution)/shard_map/ppermute | solution.py:92
  186.7 7.2 %collective-permute-start.22 = (f16[768,768]{1,0:T(8,128)(2,1)S(1)}, f16[768,768]{1,0:T(8,128)(2,1)S(1)}, u32[]{:S(2)}, u32[]{:S(2)}) collective-permute-start(f16[768,768]{1,0:T(8,128)(2,1)S(1)} %bitcast.37), channel_id=1, source_target_pairs={{0,2},{2,0},{1,3},{3,1},{4,6},{6,4},{5,7},{7,5},{8,10},{10,8},{9,1... | collective-permute-start | bytes 3538952 | tf_op jit(solution)/shard_map/ppermute | solution.py:26
  191.4 2.5 %collective-permute-start.23 = (f32[8,768]{1,0:T(8,128)S(1)}, f32[8,768]{1,0:T(8,128)S(1)}, u32[]{:S(2)}, u32[]{:S(2)}) collective-permute-start(f32[8,768]{1,0:T(8,128)S(1)} %broadcast_in_dim.20), channel_id=1, source_target_pairs={{0,2},{2,0},{1,3},{3,1},{4,6},{6,4},{5,7},{7,5},{8,10},{10,8},{9,1... | collective-permute-start | bytes 73736 | tf_op jit(solution)/shard_map/ppermute | solution.py:26

commit v11 on v10

--- a/solution.py
+++ b/solution.py
@@ -35,7 +35,9 @@
 
 
 def pair_tile(target_rows, image_rows, row_ids, target_cols, text_cols, col_ids):
-    teacher_dot = lax.dot_general(
+    wide = target_cols.astype(f32)
+    inverse = 1.0 / jnp.sqrt(jnp.sum(wide * wide, axis=1) + epsilon)
+    teacher_dot = inverse[None, :] * lax.dot_general(
         target_rows, target_cols, (((1,), (1,)), ((), ())), preferred_element_type=f32
     )
     labels = (row_ids[:, None] == col_ids[None, :]).astype(f32)
@@ -131,16 +133,14 @@
     )
     image_emb = image_unit.astype(bf16)
     image_y = swap(image_emb, "yh")
-    written_unit, _ = unit_rows(teacher_text.astype(f32))
-    teacher_txt = written_unit.astype(bf16)
-    teach_recv = chip_shift(teacher_txt, 1)
+    teach_recv = chip_shift(teacher_text, 1)
     teacher_unit, _ = unit_rows(jnp.dot(teacher_image, teacher_proj, preferred_element_type=f32))
     teacher_img = teacher_unit.astype(bf16)
     teach_y = swap(teacher_img, "yh")
     text_exch = swap(text_recv, "core")
     text_far = along_dp(jnp.where(first, text_emb, text_recv), step_route)
     teach_exch = swap(teach_recv, "core")
-    teach_far = along_dp(jnp.where(first, teacher_txt, teach_recv), step_route)
+    teach_far = along_dp(jnp.where(first, teacher_text, teach_recv), step_route)
 
     sent_feats = jnp.where(first, text_feats, image_feats)
     kept_feats = jnp.where(first, image_feats, text_feats)
@@ -149,7 +149,7 @@
     image_rows = jnp.concatenate([image_emb, image_y], axis=0)
     teach_rows = jnp.concatenate([teacher_img, teach_y], axis=0)
     row_ids = jnp.concatenate([class_ids, ids_y], axis=0)
-    row0, col0 = pair_tile(teach_rows, image_rows, row_ids, teacher_txt, text_emb, class_ids)
+    row0, col0 = pair_tile(teach_rows, image_rows, row_ids, teacher_text, text_emb, class_ids)
     row1, col1 = pair_tile(teach_rows, image_rows, row_ids, teach_recv, text_recv, ids2)
     ids_exch = jnp.where(first, ids1, ids3)
     row2, col2 = pair_tile(teach_rows, image_rows, row_ids, teach_exch, text_exch, ids_exch)

time: 197 us -> 204 us (1.036)
  blocking collectives: 65.1 us -> 73.9 us
  waiting for transfers between devices: 65 us -> 60.6 us
  matrix products: 18.8 us -> 21.2 us
  other arithmetic: 15.4 us -> 13.2 us
    all_to_all x1, blocking collectives: 16.5 us -> 23.8 us  [sum_everywhere(): blocks = lax.all_to_all(blocks, 'z', 0, 0, tiled=True)]
    ppermute x9, starting transfers between devices: 7.56 us -> 12.2 us  [along_dp(): return lax.ppermute(block, DP, route)]
    ppermute x14, starting transfers between devices: 22.3 us -> 18.8 us  [swap(): return lax.ppermute(block, axis, [(0, 1), (1, 0)])]
    convert_element_type x1 -> x0, other arithmetic: 2.46 us -> none  [local(): teacher_txt = written_unit.astype(bf16)]
    dot_general x1, matrix products: 1.48 us -> 3.81 us  [local(): jnp.dot(teacher_image, teacher_proj, preferred_element_type=f32)]
    ppermute x14, waiting for transfers between devices: 43.9 us -> 41.7 us  [swap(): return lax.ppermute(block, axis, [(0, 1), (1, 0)])]
  transfers between devices with their start and end apart: 24 -> 24, of which waited for: 9 -> 9; matrix products, arithmetic and copies ran while one was open for 15% -> 14% of each run, Pallas kernels for 0% -> 0%
where the time goes in v11:
time: 204 us; the launch traced here: 203 us
  blocking collectives  73.9 us (36%)
  waiting for transfers between devices  60.6 us (30%)
  starting transfers between devices  31.8 us (16%)
  matrix products  21.2 us (10%)
  other arithmetic  13.2 us (6%)
    ppermute x14, waiting for transfers between devices, swap(): return lax.ppermute(block, axis, [(0, 1), (1, 0)])  41.7 us
    all_to_all x1, blocking collectives, sum_everywhere(): blocks = lax.all_to_all(blocks, 'z', 0, 0, tiled=True)  23.8 us
    all_to_all x1, blocking collectives, sum_everywhere(): blocks = lax.all_to_all(blocks, 'x', 0, 0, tiled=True)  18.9 us
    ppermute x14, starting transfers between devices, swap(): return lax.ppermute(block, axis, [(0, 1), (1, 0)])  18.8 us
    ppermute x9, waiting for transfers between devices, along_dp(): return lax.ppermute(block, DP, route)  17.5 us
    all_to_all x1, blocking collectives, sum_everywhere(): own_total = lax.all_to_all(spread, 'x', 0, 0, tiled=True).reshape(ds, ds)  15.7 us
    all_to_all x1, blocking collectives, sum_everywhere(): lax.all_to_all(spread, 'z', 0, 0, tiled=True).reshape(ds // 4, ds)  15.5 us
    ppermute x9, starting transfers between devices, along_dp(): return lax.ppermute(block, DP, route)  12.2 us
  transfers between devices with their start and end apart: 24, of which 9 were waited for; matrix products, arithmetic and copies ran while one was open for 14% of the time, Pallas kernels for 0%

profile of v11, /device:TPU:1, one launch (start us, length us, event | category | flops | bytes accessed | tf_op | source)
XLA Modules:
  0.0 203.0 jit_solution(2500707199852561573)
XLA Ops:
  0.7 4.2 %collective-permute-start.10 = (s32[256]{0:T(256)}, s32[256]{0:T(256)}, u32[]{:S(2)}, u32[]{:S(2)}) collective-permute-start(s32[256]{0:T(256)} %param.15), channel_id=1, source_target_pairs={{0,6},{2,8},{4,10},{6,12},{8,14},{10,16},{12,18},{14,20},{16,22},{... | collective-permute-start | bytes 3080 | tf_op jit(solution)/shard_map/ppermute | solution.py:30
  4.9 2.9 %collective-permute-start.3 = (s32[256]{0:T(256)}, s32[256]{0:T(256)}, u32[]{:S(2)}, u32[]{:S(2)}) collective-permute-start(s32[256]{0:T(256)} %param.15), channel_id=1, source_target_pairs={{0,1},{1,0},{2,3},{3,2},{4,5},{5,4},{6,7},{7,6},{8,9},{9,8},{10,11... | collective-permute-start | bytes 3080 | tf_op jit(solution)/shard_map/ppermute | solution.py:26
  8.1 1.6 multiply_reduce_fusion.8
  9.7 0.9 fusion.75
  10.6 1.6 collective-permute-start.4
  12.9 3.8 %multiply_reduce_fusion.4 = (f32[256]{0:T(256)S(1)}, f32[256,1536]{1,0:T(8,128)S(1)}) fusion(bf16[256,1536]{1,0:T(8,128)(2,1)S(1)} %copy-done.9, bf16[1536,1536]{1,0:T(8,128)(2,1)} %param.9), kind=kOutput, calls=%fused_computation.14 | convolution fusion | flops 1208745728 | bytes 7078912 | tf_op jit(solution)/shard_map/dot_general | solution.py:137
  16.8 0.9 fusion.74
  17.7 1.1 divide_convert_fusion
  18.8 1.3 collective-permute-start.6
  20.1 0.7 pad_add_fusion
  20.9 2.9 %collective-permute-start.2 = (bf16[256,1536]{1,0:T(8,128)(2,1)}, bf16[256,1536]{1,0:T(8,128)(2,1)S(1)}, u32[]{:S(2)}, u32[]{:S(2)}) collective-permute-start(bf16[256,1536]{1,0:T(8,128)(2,1)} %divide_convert_fusion), channel_id=1, source_target_pairs={{0,1},{1,0},{2,3},{3,2},{4,5},{5,4},{6,7},{7,6},{8,9},{9,8},{10,11... | collective-permute-start | bytes 2359304 | tf_op jit(solution)/shard_map/ppermute | solution.py:26
  23.8 0.7 broadcast_select_fusion.9
  24.5 14.6 %collective-permute-done.4 = bf16[256,768]{1,0:T(8,128)(2,1)} collective-permute-done((bf16[256,768]{1,0:T(8,128)(2,1)}, bf16[256,768]{1,0:T(8,128)(2,1)}, u32[]{:S(2)}, u32[]{:S(2)}) %collective-permute-start.4) | collective-permute-done | bytes 393248 | tf_op jit(solution)/shard_map/ppermute | solution.py:30
  39.0 1.2 broadcast_select_fusion.5
  40.3 0.9 collective-permute-start.7
  41.2 1.2 broadcast_select_fusion
  42.4 27.7 %collective-permute-done.2 = bf16[256,1536]{1,0:T(8,128)(2,1)S(1)} collective-permute-done((bf16[256,1536]{1,0:T(8,128)(2,1)}, bf16[256,1536]{1,0:T(8,128)(2,1)S(1)}, u32[]{:S(2)}, u32[]{:S(2)}) %collective-permute-start.2) | collective-permute-done | bytes 786464 | tf_op jit(solution)/shard_map/ppermute | solution.py:26
  70.1 0.7 fusion.35
  70.8 1.4 fusion.44
  72.3 1.4 fusion.76
  73.6 0.8 collective-permute-start.8
  74.4 1.7 fusion.73
  76.2 1.4 multiply_reduce_fusion.3
  77.5 1.6 fusion.45
  79.1 1.4 fusion.77
  82.4 0.8 collective-permute-done.12
  85.1 3.0 %collective-permute-start.16 = (bf16[256,768]{1,0:T(8,128)(2,1)S(1)}, bf16[256,768]{1,0:T(8,128)(2,1)S(1)}, u32[]{:S(2)}, u32[]{:S(2)}) collective-permute-start(bf16[256,768]{1,0:T(8,128)(2,1)S(1)} %fusion.7), channel_id=1, source_target_pairs={{0,250},{2,0},{4,254},{6,4},{8,2},{10,8},{12,6},{14,12},{16,10},{1... | collective-permute-start | bytes 1179656 | tf_op jit(solution)/shard_map/ppermute | solution.py:30
  89.0 1.5 collective-permute-start.13
  90.9 1.7 collective-permute-start.15
  92.7 0.7 collective-permute-start
  93.4 8.0 %collective-permute-done.13 = bf16[256,768]{1,0:T(8,128)(2,1)S(1)} collective-permute-done((bf16[256,768]{1,0:T(8,128)(2,1)S(1)}, bf16[256,768]{1,0:T(8,128)(2,1)S(1)}, u32[]{:S(2)}, u32[]{:S(2)}) %collective-permute-start.13) | collective-permute-done | bytes 393248 | tf_op jit(solution)/shard_map/ppermute | solution.py:26
  101.6 2.1 %collective-permute-done.15 = bf16[256,768]{1,0:T(8,128)(2,1)S(1)} collective-permute-done((bf16[256,768]{1,0:T(8,128)(2,1)S(1)}, bf16[256,768]{1,0:T(8,128)(2,1)S(1)}, u32[]{:S(2)}, u32[]{:S(2)}) %collective-permute-start.15) | collective-permute-done | bytes 393248 | tf_op jit(solution)/shard_map/ppermute | solution.py:30
  104.9 1.2 collective-permute-start.18
  106.4 1.0 collective-permute-done.18
  107.4 0.8 fusion.51
  108.3 1.5 abs_reduce_fusion
  111.0 18.9 %all_to_all.20 = f16[4,200,768]{2,1,0:T(8,128)(2,1)S(1)} all-to-all(f16[4,200,768]{2,1,0:T(8,128)(2,1)S(1)} %concatenate.33), channel_id=1, replica_groups=mesh['yl'=2,'z'=8,'x'=4,'core'=2,'yh'=2] {'x'}, dimensions={0} | all-to-all | bytes 2457600 | tf_op jit(solution)/shard_map/all_to_all | solution.py:85
  130.3 23.8 %all_to_all.21 = f16[8,32,768]{2,1,0:T(8,128)(2,1)S(1)} all-to-all(f16[8,32,768]{2,1,0:T(8,128)(2,1)S(1)} %pad_maximum_fusion.5), channel_id=1, replica_groups=mesh['yl'=2,'z'=8,'x'=4,'core'=2,'yh'=2] {'z'}, dimensions={0} | all-to-all | bytes 786432 | tf_op jit(solution)/shard_map/all_to_all | solution.py:89
  154.3 1.4 collective-permute-start.19
  155.8 1.7 collective-permute-start.20
  157.5 0.8 collective-permute-start.21
  158.3 2.5 %collective-permute-done.20 = f32[32,768]{1,0:T(8,128)S(1)} collective-permute-done((f32[32,768]{1,0:T(8,128)S(1)}, f32[32,768]{1,0:T(8,128)S(1)}, u32[]{:S(2)}, u32[]{:S(2)}) %collective-permute-start.20) | collective-permute-done | bytes 98336 | tf_op jit(solution)/shard_map/ppermute | solution.py:26
  160.7 1.4 collective-permute-done.21
  162.3 15.5 %all_to_all.22 = f16[8,24,768]{2,1,0:T(8,128)(2,1)S(1)} all-to-all(f16[8,24,768]{2,1,0:T(8,128)(2,1)S(1)} %broadcast_in_dim.16), channel_id=1, replica_groups=mesh['yl'=2,'z'=8,'x'=4,'core'=2,'yh'=2] {'z'}, dimensions={0} | all-to-all | bytes 589824 | tf_op jit(solution)/shard_map/all_to_all | solution.py:102
  177.9 15.7 %all_to_all.23 = f16[4,192,768]{2,1,0:T(8,128)(2,1)S(1)} all-to-all(f16[4,192,768]{2,1,0:T(8,128)(2,1)S(1)} %broadcast_in_dim.18), channel_id=1, replica_groups=mesh['yl'=2,'z'=8,'x'=4,'core'=2,'yh'=2] {'x'}, dimensions={0} | all-to-all | bytes 2359296 | tf_op jit(solution)/shard_map/all_to_all | solution.py:104
  193.5 4.2 %collective-permute-start.22 = (f16[768,768]{1,0:T(8,128)(2,1)S(1)}, f16[768,768]{1,0:T(8,128)(2,1)S(1)}, u32[]{:S(2)}, u32[]{:S(2)}) collective-permute-start(f16[768,768]{1,0:T(8,128)(2,1)S(1)} %bitcast.37), channel_id=1, source_target_pairs={{0,2},{2,0},{1,3},{3,1},{4,6},{6,4},{5,7},{7,5},{8,10},{10,8},{9,1... | collective-permute-start | bytes 3538952 | tf_op jit(solution)/shard_map/ppermute | solution.py:26
  197.8 2.5 %collective-permute-done.23 = f32[8,768]{1,0:T(8,128)S(1)} collective-permute-done((f32[8,768]{1,0:T(8,128)S(1)}, f32[8,768]{1,0:T(8,128)S(1)}, u32[]{:S(2)}, u32[]{:S(2)}) %collective-permute-start.23) | collective-permute-done | bytes 24608 | tf_op jit(solution)/shard_map/ppermute | solution.py:26
  200.3 2.7 %fusion = (f32[768,768]{1,0:T(8,128)}, f32[768,768]{1,0:T(8,128)}) fusion(f16[768,768]{1,0:T(8,128)(2,1)S(1)} %collective-permute-done.22, f32[768]{0:T(1024)S(1)} %fusion.67, f32[768]{0:T(1024)S(1)} %get-tuple-element.2, pred[]{:T(512)S(6)} %eq.20, f16[4,192,768]{2,1,0:T(8,128)(2,1)S(1)} %all_to_all.23), kind=kLoop, calls=%fused_computation.1 | loop fusion | flops 3538944 | bytes 7084033 | tf_op jit(solution)/shard_map/jit(_where)/select_n | solution.py:185
  (89 shorter events, 9.4 us)
Async XLA Ops:
  0.6 7.5 %copy-start = (bf16[768,768]{1,0:T(8,128)(2,1)S(1)}, bf16[768,768]{1,0:T(8,128)(2,1)}, u32[]{:S(2)}) copy-start(bf16[768,768]{1,0:T(8,128)(2,1)} %param.14) | copy-start | bytes 3538948
  0.6 11.5 %copy-start.1 = (bf16[256,1536]{1,0:T(8,128)(2,1)S(1)}, bf16[256,1536]{1,0:T(8,128)(2,1)}, u32[]{:S(2)}) copy-start(bf16[256,1536]{1,0:T(8,128)(2,1)} %param.10) | copy-start | bytes 2359300
  0.7 20.1 %collective-permute-start.10 = (s32[256]{0:T(256)}, s32[256]{0:T(256)}, u32[]{:S(2)}, u32[]{:S(2)}) collective-permute-start(s32[256]{0:T(256)} %param.15), channel_id=1, source_target_pairs={{0,6},{2,8},{4,10},{6,12},{8,14},{10,16},{12,18},{14,20},{16,22},{... | collective-permute-start | bytes 3080 | tf_op jit(solution)/shard_map/ppermute | solution.py:30
  4.9 16.0 %collective-permute-start.9 = (s32[256]{0:T(256)}, s32[256]{0:T(256)}, u32[]{:S(2)}, u32[]{:S(2)}) collective-permute-start(s32[256]{0:T(256)} %param.15), channel_id=1, source_target_pairs={{0,2},{2,4},{4,6},{6,8},{8,10},{10,12},{12,14},{14,16},{16,18},{18... | collective-permute-start | bytes 3080 | tf_op jit(solution)/shard_map/ppermute | solution.py:30
  4.9 13.9 %collective-permute-start.3 = (s32[256]{0:T(256)}, s32[256]{0:T(256)}, u32[]{:S(2)}, u32[]{:S(2)}) collective-permute-start(s32[256]{0:T(256)} %param.15), channel_id=1, source_target_pairs={{0,1},{1,0},{2,3},{3,2},{4,5},{5,4},{6,7},{7,6},{8,9},{9,8},{10,11... | collective-permute-start | bytes 3080 | tf_op jit(solution)/shard_map/ppermute | solution.py:26
  7.8 32.5 %collective-permute-start.5 = (bf16[256,1536]{1,0:T(8,128)(2,1)}, bf16[256,1536]{1,0:T(8,128)(2,1)}, u32[]{:S(2)}, u32[]{:S(2)}) collective-permute-start(bf16[256,1536]{1,0:T(8,128)(2,1)} %param.10), channel_id=1, source_target_pairs={{0,4},{2,6},{4,8},{6,10},{8,12},{10,14},{12,16},{14,18},{16,20},{1... | collective-permute-start | bytes 2359304 | tf_op jit(solution)/shard_map/ppermute | solution.py:30
  9.7 2.7 %copy-start.3 = (bf16[256,768]{1,0:T(8,128)(2,1)S(1)}, bf16[256,768]{1,0:T(8,128)(2,1)}, u32[]{:S(2)}) copy-start(bf16[256,768]{1,0:T(8,128)(2,1)} %param.11) | copy-start | bytes 1179652
  9.7 2.7 %copy-start.5 = (bf16[768,768]{1,0:T(8,128)(2,1)S(1)}, bf16[768,768]{1,0:T(8,128)(2,1)}, u32[]{:S(2)}) copy-start(bf16[768,768]{1,0:T(8,128)(2,1)} %param.13) | copy-start | bytes 3538948
  10.6 2.4 %copy-start.9 = (bf16[256,1536]{1,0:T(8,128)(2,1)S(1)}, bf16[256,1536]{1,0:T(8,128)(2,1)}, u32[]{:S(2)}) copy-start(bf16[256,1536]{1,0:T(8,128)(2,1)} %param.8) | copy-start | bytes 2359300
  10.6 28.5 %collective-permute-start.4 = (bf16[256,768]{1,0:T(8,128)(2,1)}, bf16[256,768]{1,0:T(8,128)(2,1)}, u32[]{:S(2)}, u32[]{:S(2)}) collective-permute-start(bf16[256,768]{1,0:T(8,128)(2,1)} %fusion.75), channel_id=1, source_target_pairs={{0,4},{2,6},{4,8},{6,10},{8,12},{10,14},{12,16},{14,18},{16,20},{1... | collective-permute-start | bytes 1179656 | tf_op jit(solution)/shard_map/ppermute | solution.py:30
  16.8 2.0 copy-start.8
  18.8 58.8 %collective-permute-start.6 = (s32[256]{0:T(256)S(1)}, s32[256]{0:T(256)S(1)}, u32[]{:S(2)}, u32[]{:S(2)}) collective-permute-start(s32[256]{0:T(256)S(1)} %copy-done.8), channel_id=1, source_target_pairs={{0,4},{2,6},{4,8},{6,10},{8,12},{10,14},{12,16},{14,18},{16,20},{1... | collective-permute-start | bytes 3080 | tf_op jit(solution)/shard_map/ppermute | solution.py:30
  20.7 50.1 %collective-permute-start.1 = (bf16[256,768]{1,0:T(8,128)(2,1)}, bf16[256,768]{1,0:T(8,128)(2,1)S(1)}, u32[]{:S(2)}, u32[]{:S(2)}) collective-permute-start(bf16[256,768]{1,0:T(8,128)(2,1)} %fusion.74), channel_id=1, source_target_pairs={{0,1},{1,0},{2,3},{3,2},{4,5},{5,4},{6,7},{7,6},{8,9},{9,8},{10,11... | collective-permute-start | bytes 1179656 | tf_op jit(solution)/shard_map/ppermute | solution.py:26
  20.9 49.3 %collective-permute-start.2 = (bf16[256,1536]{1,0:T(8,128)(2,1)}, bf16[256,1536]{1,0:T(8,128)(2,1)S(1)}, u32[]{:S(2)}, u32[]{:S(2)}) collective-permute-start(bf16[256,1536]{1,0:T(8,128)(2,1)} %divide_convert_fusion), channel_id=1, source_target_pairs={{0,1},{1,0},{2,3},{3,2},{4,5},{5,4},{6,7},{7,6},{8,9},{9,8},{10,11... | collective-permute-start | bytes 2359304 | tf_op jit(solution)/shard_map/ppermute | solution.py:26
  40.2 29.9 %copy-start.6 = (bf16[256,1536]{1,0:T(8,128)(2,1)S(1)}, bf16[256,1536]{1,0:T(8,128)(2,1)}, u32[]{:S(2)}) copy-start(bf16[256,1536]{1,0:T(8,128)(2,1)} %divide_convert_fusion) | copy-start | bytes 2359300
  40.2 43.9 %collective-permute-start.11 = (bf16[256,768]{1,0:T(8,128)(2,1)S(1)}, bf16[256,768]{1,0:T(8,128)(2,1)S(1)}, u32[]{:S(2)}, u32[]{:S(2)}) collective-permute-start(bf16[256,768]{1,0:T(8,128)(2,1)S(1)} %broadcast_select_fusion.5), channel_id=1, source_target_pairs={{0,2},{2,4},{4,6},{6,8},{8,10},{10,12},{12,14},{14,16},{16,18},{18... | collective-permute-start | bytes 1179656 | tf_op jit(solution)/shard_map/ppermute | solution.py:30
  40.3 41.0 %collective-permute-start.7 = (bf16[256,768]{1,0:T(8,128)(2,1)}, bf16[256,768]{1,0:T(8,128)(2,1)S(1)}, u32[]{:S(2)}, u32[]{:S(2)}) collective-permute-start(bf16[256,768]{1,0:T(8,128)(2,1)} %collective-permute-done.4), channel_id=1, source_target_pairs={{0,2},{2,0},{1,3},{3,1},{4,6},{6,4},{5,7},{7,5},{8,10},{10,8},{9,1... | collective-permute-start | bytes 1179656 | tf_op jit(solution)/shard_map/ppermute | solution.py:26
  42.4 28.4 %copy-start.7 = (bf16[256,768]{1,0:T(8,128)(2,1)S(1)}, bf16[256,768]{1,0:T(8,128)(2,1)}, u32[]{:S(2)}) copy-start(bf16[256,768]{1,0:T(8,128)(2,1)} %fusion.74) | copy-start | bytes 1179652
  70.1 13.2 %collective-permute-start.12 = (bf16[256,1536]{1,0:T(8,128)(2,1)S(1)}, bf16[256,1536]{1,0:T(8,128)(2,1)S(1)}, u32[]{:S(2)}, u32[]{:S(2)}) collective-permute-start(bf16[256,1536]{1,0:T(8,128)(2,1)S(1)} %broadcast_select_fusion), channel_id=1, source_target_pairs={{0,2},{2,4},{4,6},{6,8},{8,10},{10,12},{12,14},{14,16},{16,18},{18... | collective-permute-start | bytes 2359304 | tf_op jit(solution)/shard_map/ppermute | solution.py:30
  73.6 6.8 %collective-permute-start.8 = (bf16[256,1536]{1,0:T(8,128)(2,1)}, bf16[256,1536]{1,0:T(8,128)(2,1)S(1)}, u32[]{:S(2)}, u32[]{:S(2)}) collective-permute-start(bf16[256,1536]{1,0:T(8,128)(2,1)} %collective-permute-done.5), channel_id=1, source_target_pairs={{0,2},{2,0},{1,3},{3,1},{4,6},{6,4},{5,7},{7,5},{8,10},{10,8},{9,1... | collective-permute-start | bytes 2359304 | tf_op jit(solution)/shard_map/ppermute | solution.py:26
  82.3 8.2 %collective-permute-start.14 = (bf16[256,768]{1,0:T(8,128)(2,1)S(1)}, bf16[256,768]{1,0:T(8,128)(2,1)S(1)}, u32[]{:S(2)}, u32[]{:S(2)}) collective-permute-start(bf16[256,768]{1,0:T(8,128)(2,1)S(1)} %fusion.6), channel_id=1, source_target_pairs={{0,2},{2,0},{1,3},{3,1},{4,6},{6,4},{5,7},{7,5},{8,10},{10,8},{9,1... | collective-permute-start | bytes 1179656 | tf_op jit(solution)/shard_map/ppermute | solution.py:26
  85.1 16.5 %collective-permute-start.16 = (bf16[256,768]{1,0:T(8,128)(2,1)S(1)}, bf16[256,768]{1,0:T(8,128)(2,1)S(1)}, u32[]{:S(2)}, u32[]{:S(2)}) collective-permute-start(bf16[256,768]{1,0:T(8,128)(2,1)S(1)} %fusion.7), channel_id=1, source_target_pairs={{0,250},{2,0},{4,254},{6,4},{8,2},{10,8},{12,6},{14,12},{16,10},{1... | collective-permute-start | bytes 1179656 | tf_op jit(solution)/shard_map/ppermute | solution.py:30
  88.9 3.7 %copy-start.2 = (bf16[256,768]{1,0:T(8,128)(2,1)S(1)}, bf16[256,768]{1,0:T(8,128)(2,1)}, u32[]{:S(2)}) copy-start(bf16[256,768]{1,0:T(8,128)(2,1)} %param.12) | copy-start | bytes 1179652
  88.9 3.7 %copy-start.4 = (bf16[256,768]{1,0:T(8,128)(2,1)S(1)}, bf16[256,768]{1,0:T(8,128)(2,1)}, u32[]{:S(2)}) copy-start(bf16[256,768]{1,0:T(8,128)(2,1)} %param.11) | copy-start | bytes 1179652
  89.0 12.3 %collective-permute-start.13 = (bf16[256,768]{1,0:T(8,128)(2,1)S(1)}, bf16[256,768]{1,0:T(8,128)(2,1)S(1)}, u32[]{:S(2)}, u32[]{:S(2)}) collective-permute-start(bf16[256,768]{1,0:T(8,128)(2,1)S(1)} %slice.118), channel_id=1, source_target_pairs={{0,1},{1,0},{2,3},{3,2},{4,5},{5,4},{6,7},{7,6},{8,9},{9,8},{10,11... | collective-permute-start | bytes 1179656 | tf_op jit(solution)/shard_map/ppermute | solution.py:26
  90.9 12.8 %collective-permute-start.15 = (bf16[256,768]{1,0:T(8,128)(2,1)S(1)}, bf16[256,768]{1,0:T(8,128)(2,1)S(1)}, u32[]{:S(2)}, u32[]{:S(2)}) collective-permute-start(bf16[256,768]{1,0:T(8,128)(2,1)S(1)} %fusion.5), channel_id=1, source_target_pairs={{0,252},{2,254},{4,0},{6,2},{8,4},{10,6},{12,8},{14,10},{16,12},{1... | collective-permute-start | bytes 1179656 | tf_op jit(solution)/shard_map/ppermute | solution.py:30
  92.7 13.7 %collective-permute-start = (bf16[256,768]{1,0:T(8,128)(2,1)S(1)}, bf16[256,768]{1,0:T(8,128)(2,1)S(1)}, u32[]{:S(2)}, u32[]{:S(2)}) collective-permute-start(bf16[256,768]{1,0:T(8,128)(2,1)S(1)} %get-tuple-element.16), channel_id=1, source_target_pairs={{0,2},{2,0},{1,3},{3,1},{4,6},{6,4},{5,7},{7,5},{8,10},{10,8},{9,1... | collective-permute-start | bytes 1179656 | tf_op jit(solution)/shard_map/ppermute | solution.py:26
  104.9 2.5 %collective-permute-start.18 = (bf16[256,768]{1,0:T(8,128)(2,1)S(1)}, bf16[256,768]{1,0:T(8,128)(2,1)S(1)}, u32[]{:S(2)}, u32[]{:S(2)}) collective-permute-start(bf16[256,768]{1,0:T(8,128)(2,1)S(1)} %get-tuple-element.12), channel_id=1, source_target_pairs={{0,2},{2,0},{1,3},{3,1},{4,6},{6,4},{5,7},{7,5},{8,10},{10,8},{9,1... | collective-permute-start | bytes 1179656 | tf_op jit(solution)/shard_map/ppermute | solution.py:26
  106.1 2.2 %collective-permute-start.17 = (bf16[256,768]{1,0:T(8,128)(2,1)S(1)}, bf16[256,768]{1,0:T(8,128)(2,1)S(1)}, u32[]{:S(2)}, u32[]{:S(2)}) collective-permute-start(bf16[256,768]{1,0:T(8,128)(2,1)S(1)} %get-tuple-element.10), channel_id=1, source_target_pairs={{0,2},{2,0},{1,3},{3,1},{4,6},{6,4},{5,7},{7,5},{8,10},{10,8},{9,1... | collective-permute-start | bytes 1179656 | tf_op jit(solution)/shard_map/ppermute | solution.py:26
  154.3 3.9 %collective-permute-start.19 = (f32[32,768]{1,0:T(8,128)S(1)}, f32[32,768]{1,0:T(8,128)S(1)}, u32[]{:S(2)}, u32[]{:S(2)}) collective-permute-start(f32[32,768]{1,0:T(8,128)S(1)} %pad_maximum_fusion.6), channel_id=1, source_target_pairs={{0,128},{128,0},{1,129},{129,1},{2,130},{130,2},{3,131},{131,3},{4... | collective-permute-start | bytes 294920 | tf_op jit(solution)/shard_map/ppermute | solution.py:26
  155.8 5.0 %collective-permute-start.20 = (f32[32,768]{1,0:T(8,128)S(1)}, f32[32,768]{1,0:T(8,128)S(1)}, u32[]{:S(2)}, u32[]{:S(2)}) collective-permute-start(f32[32,768]{1,0:T(8,128)S(1)} %pad_maximum_fusion.6), channel_id=1, source_target_pairs={{0,1},{1,0},{2,3},{3,2},{4,5},{5,4},{6,7},{7,6},{8,9},{9,8},{10,11... | collective-permute-start | bytes 294920 | tf_op jit(solution)/shard_map/ppermute | solution.py:26
  157.5 4.7 %collective-permute-start.21 = (f32[32,768]{1,0:T(8,128)S(1)}, f32[32,768]{1,0:T(8,128)S(1)}, u32[]{:S(2)}, u32[]{:S(2)}) collective-permute-start(f32[32,768]{1,0:T(8,128)S(1)} %pad_maximum_fusion.6), channel_id=1, source_target_pairs={{0,129},{1,128},{128,1},{129,0},{2,131},{3,130},{130,3},{131,2},{4... | collective-permute-start | bytes 294920 | tf_op jit(solution)/shard_map/ppermute | solution.py:94
  193.5 6.8 %collective-permute-start.22 = (f16[768,768]{1,0:T(8,128)(2,1)S(1)}, f16[768,768]{1,0:T(8,128)(2,1)S(1)}, u32[]{:S(2)}, u32[]{:S(2)}) collective-permute-start(f16[768,768]{1,0:T(8,128)(2,1)S(1)} %bitcast.37), channel_id=1, source_target_pairs={{0,2},{2,0},{1,3},{3,1},{4,6},{6,4},{5,7},{7,5},{8,10},{10,8},{9,1... | collective-permute-start | bytes 3538952 | tf_op jit(solution)/shard_map/ppermute | solution.py:26
  197.8 2.5 %collective-permute-start.23 = (f32[8,768]{1,0:T(8,128)S(1)}, f32[8,768]{1,0:T(8,128)S(1)}, u32[]{:S(2)}, u32[]{:S(2)}) collective-permute-start(f32[8,768]{1,0:T(8,128)S(1)} %broadcast_in_dim.20), channel_id=1, source_target_pairs={{0,2},{2,0},{1,3},{3,1},{4,6},{6,4},{5,7},{7,5},{8,10},{10,8},{9,1... | collective-permute-start | bytes 73736 | tf_op jit(solution)/shard_map/ppermute | solution.py:26

commit v12 on v4

--- a/solution.py
+++ b/solution.py
@@ -44,17 +44,14 @@
     return noted[:count], noted[count, :count]
 
 
-def pair_tile(teach_rows, image_rows, row_ids, teach_cols, noted_cols):
+def pair_tile(target_rows, image_rows, row_ids, target_cols, noted_cols):
     text_cols, col_ids = without_ids(noted_cols)
-    wide = teach_cols.astype(f32)
+    wide = target_cols.astype(f32)
     inverse = 1.0 / jnp.sqrt(jnp.sum(wide * wide, axis=1) + epsilon)
-    teacher_dot = (
-        lax.dot_general(
-            teach_rows, teach_cols, (((1,), (1,)), ((), ())), preferred_element_type=f32
-        )
-        * inverse[None, :]
-    )
-    labels = (row_ids == col_ids[None, :]).astype(f32)
+    teacher_dot = inverse[None, :] * lax.dot_general(
+        target_rows, target_cols, (((1,), (1,)), ((), ())), preferred_element_type=f32
+    )
+    labels = (row_ids[:, None] == col_ids[None, :]).astype(f32)
     target = 0.5 * jax.nn.sigmoid(scale * teacher_dot + shift) + 0.5 * labels
     logits = (
         scale
@@ -134,29 +131,25 @@
     back_route = [(i, i - 1 if i % 2 else (i - 3) % N_DP) for i in range(N_DP)]
     step_route = [(i, (i + 1) % N_DP) for i in range(N_DP)]
 
-    teach_recv = chip_shift(teacher_text, 1)
-    teach_y = swap(teacher_image, "yh")
     text_unit, text_len = unit_rows(jnp.dot(text_feats, text_proj, preferred_element_type=f32))
     text_own = with_ids(text_unit.astype(bf16), class_ids)
-    image_first, text_own = lax.optimization_barrier((image_feats, text_own))
     text_recv = chip_shift(text_own, 1)
+    teacher_later, text_own = lax.optimization_barrier((teacher_image, text_own))
+    teacher_unit, _ = unit_rows(jnp.dot(teacher_later, teacher_proj, preferred_element_type=f32))
+    teacher_img = teacher_unit.astype(bf16)
+    image_later, teacher_img = lax.optimization_barrier((image_feats, teacher_img))
+    teach_y = swap(teacher_img, "yh")
     image_unit, image_len = unit_rows(
-        jnp.dot(image_first, image_proj, preferred_element_type=f32)
+        jnp.dot(image_later, image_proj, preferred_element_type=f32)
     )
     image_own = with_ids(image_unit.astype(bf16), class_ids)
-    teacher_later, image_own = lax.optimization_barrier((teacher_image, image_own))
+    image_own, _ = lax.optimization_barrier((image_own, text_own))
     image_y = swap(image_own, "yh")
+    teach_recv = chip_shift(teacher_text, 1)
+    text_exch = swap(text_recv, "core")
+    text_far = along_dp(jnp.where(first, text_own, text_recv), step_route)
     teach_exch = swap(teach_recv, "core")
     teach_far = along_dp(jnp.where(first, teacher_text, teach_recv), step_route)
-    text_exch = swap(text_recv, "core")
-    text_far = along_dp(jnp.where(first, text_own, text_recv), step_route)
-
-    def teacher_rows(rows):
-        unit, _ = unit_rows(jnp.dot(rows, teacher_proj, preferred_element_type=f32))
-        return unit.astype(bf16)
-
-    teacher_img = teacher_rows(teacher_later)
-    teacher_img_y = teacher_rows(teach_y)
 
     sent_feats = jnp.where(first, text_feats, image_feats)
     kept_feats = jnp.where(first, image_feats, text_feats)
@@ -165,15 +158,14 @@
     image_emb, ids = without_ids(image_own)
     image_emb_y, ids_y = without_ids(image_y)
     image_rows = jnp.concatenate([image_emb, image_emb_y], axis=0)
-    teach_rows = jnp.concatenate([teacher_img, teacher_img_y], axis=0)
-    row_ids = jnp.concatenate([ids, ids_y], axis=0)[:, None]
-    rows = (teach_rows, image_rows, row_ids)
-    row0, col0 = pair_tile(*rows, teacher_text, text_own)
-    row1, col1 = pair_tile(*rows, teach_recv, text_recv)
-    row2, col2 = pair_tile(*rows, teach_exch, text_exch)
+    teach_rows = jnp.concatenate([teacher_img, teach_y], axis=0)
+    row_ids = jnp.concatenate([ids, ids_y], axis=0)
+    row0, col0 = pair_tile(teach_rows, image_rows, row_ids, teacher_text, text_own)
+    row1, col1 = pair_tile(teach_rows, image_rows, row_ids, teach_recv, text_recv)
+    row2, col2 = pair_tile(teach_rows, image_rows, row_ids, teach_exch, text_exch)
     both = col1 + swap(col2.astype(bf16), "core").astype(f32)
     both_back = chip_shift(both.astype(bf16), -1)
-    row3, col3 = pair_tile(*rows, teach_far, text_far)
+    row3, col3 = pair_tile(teach_rows, image_rows, row_ids, teach_far, text_far)
     far_back = along_dp(col3.astype(bf16), back_route)
     grad_rows = row0 + row1 + row2 + row3
     half = image_emb.shape[0]

time: 203 us -> 204 us (level)
  waiting for transfers between devices: 55.1 us -> 67.8 us
  starting transfers between devices: 32.5 us -> 20 us
  blocking collectives: 71.3 us -> 66.1 us
  local copies, waits for them, and re-layouts: 6.62 us -> 11.5 us
    ppermute x13, waiting for transfers between devices: 44.1 us -> 66.5 us  [swap(): return lax.ppermute(block, axis, [(0, 1), (1, 0)])]
    ppermute x13, starting transfers between devices: 23.4 us -> 11.5 us  [swap(): return lax.ppermute(block, axis, [(0, 1), (1, 0)])]
    ppermute x6, waiting for transfers between devices: 9.42 us -> 0.35 us  [along_dp(): return lax.ppermute(block, DP, route)]
    all_to_all x1, blocking collectives: 24 us -> 17.5 us  [sum_everywhere(): blocks = lax.all_to_all(blocks, 'z', 0, 0, tiled=True)]
    unnamed x21 -> x22, local copies, waits for them, and re-layouts: 1.22 us -> 4.29 us
    dot_general x7 -> x6, matrix products: 12.2 us -> 9.1 us  [the longest x4 4.74 us: pair_tile(): lax.dot_general(target_rows, target_cols, (((1,), (1,)), ((), ())), prefe...]
    ppermute x6, starting transfers between devices: 8.35 us -> 6.29 us  [along_dp(): return lax.ppermute(block, DP, route)]
  transfers between devices with their start and end apart: 20 -> 20, of which waited for: 8 -> 8; matrix products, arithmetic and copies ran while one was open for 17% -> 18% of each run, Pallas kernels for 0% -> 0%
where the time goes in v12:
time: 204 us; the launch traced here: 203 us
  waiting for transfers between devices  67.8 us (33%)
  blocking collectives  66.1 us (32%)
  matrix products  22.3 us (11%)
  starting transfers between devices  20 us (10%)
  other arithmetic  12.9 us (6%)
  local copies, waits for them, and re-layouts  11.5 us (6%)
    ppermute x13, waiting for transfers between devices, swap(): return lax.ppermute(block, axis, [(0, 1), (1, 0)])  66.5 us
    all_to_all x1, blocking collectives, sum_everywhere(): blocks = lax.all_to_all(blocks, 'x', 0, 0, tiled=True)  18.9 us
    all_to_all x1, blocking collectives, sum_everywhere(): blocks = lax.all_to_all(blocks, 'z', 0, 0, tiled=True)  17.5 us
    all_to_all x1, blocking collectives, sum_everywhere(): own_total = lax.all_to_all(spread, 'x', 0, 0, tiled=True).reshape(ds, ds)  15.2 us
    all_to_all x1, blocking collectives, sum_everywhere(): lax.all_to_all(spread, 'z', 0, 0, tiled=True).reshape(ds // 4, ds)  14.5 us
    ppermute x13, starting transfers between devices, swap(): return lax.ppermute(block, axis, [(0, 1), (1, 0)])  11.5 us
    ppermute x6, starting transfers between devices, along_dp(): return lax.ppermute(block, DP, route)  6.29 us
    slice x8, local copies, waits for them, and re-layouts, without_ids(): return (noted[:count], noted[count, :count])  5.63 us
  transfers between devices with their start and end apart: 20, of which 8 were waited for; matrix products, arithmetic and copies ran while one was open for 18% of the time, Pallas kernels for 0%

profile of v12, /device:TPU:1, one launch (start us, length us, event | category | flops | bytes accessed | tf_op | source)
XLA Modules:
  0.0 202.6 jit_solution(5722140168002887628)
XLA Ops:
  0.7 1.3 copy-done
  1.9 1.6 multiply_reduce_fusion.9
  3.5 0.8 copy-done.1
  4.5 0.8 fusion.56
  5.2 2.0 %collective-permute-start.3 = (bf16[272,768]{1,0:T(8,128)(2,1)}, bf16[272,768]{1,0:T(8,128)(2,1)}, u32[]{:S(2)}, u32[]{:S(2)}) collective-permute-start(bf16[272,768]{1,0:T(8,128)(2,1)} %fusion.56), channel_id=1, source_target_pairs={{0,4},{2,6},{4,8},{6,10},{8,12},{10,14},{12,16},{14,18},{16,20},{1... | collective-permute-start | bytes 1253384 | tf_op jit(solution)/shard_map/ppermute | solution.py:30
  7.3 3.8 %multiply_reduce_fusion.5 = (f32[256]{0:T(256)S(1)}, f32[256,1536]{1,0:T(8,128)S(1)}) fusion(bf16[256,1536]{1,0:T(8,128)(2,1)S(1)} %copy-done.8, bf16[1536,1536]{1,0:T(8,128)(2,1)} %param.9), kind=kOutput, calls=%fused_computation.14 | convolution fusion | flops 1208745728 | bytes 7078912 | tf_op jit(solution)/shard_map/dot_general | solution.py:138
  11.1 1.1 divide_convert_fusion
  13.5 0.8 fusion.57
  14.3 2.9 %collective-permute-start.1 = (bf16[272,768]{1,0:T(8,128)(2,1)}, bf16[272,768]{1,0:T(8,128)(2,1)}, u32[]{:S(2)}, u32[]{:S(2)}) collective-permute-start(bf16[272,768]{1,0:T(8,128)(2,1)} %fusion.57), channel_id=1, source_target_pairs={{0,1},{1,0},{2,3},{3,2},{4,5},{5,4},{6,7},{7,6},{8,9},{9,8},{10,11... | collective-permute-start | bytes 1253384 | tf_op jit(solution)/shard_map/ppermute | solution.py:26
  17.2 1.2 collective-permute-start.4
  18.5 1.2 constant_dynamic-update-slice_fusion.1
  19.6 1.4 multiply_reduce_fusion.4
  21.0 0.7 slice_reduce_fusion.5
  21.7 1.8 slice.64
  23.5 0.7 slice_reduce_fusion.4
  24.5 1.0 broadcast_select_fusion.1
  25.6 2.3 %collective-permute-start.7 = (bf16[272,768]{1,0:T(8,128)(2,1)S(1)}, bf16[272,768]{1,0:T(8,128)(2,1)S(1)}, u32[]{:S(2)}, u32[]{:S(2)}) collective-permute-start(bf16[272,768]{1,0:T(8,128)(2,1)S(1)} %broadcast_select_fusion.1), channel_id=1, source_target_pairs={{0,2},{2,4},{4,6},{6,8},{8,10},{10,12},{12,14},{14,16},{16,18},{18... | collective-permute-start | bytes 1253384 | tf_op jit(solution)/shard_map/ppermute | solution.py:30
  27.9 29.2 %collective-permute-done.1 = bf16[272,768]{1,0:T(8,128)(2,1)} collective-permute-done((bf16[272,768]{1,0:T(8,128)(2,1)}, bf16[272,768]{1,0:T(8,128)(2,1)}, u32[]{:S(2)}, u32[]{:S(2)}) %collective-permute-start.1) | collective-permute-done | bytes 417824 | tf_op jit(solution)/shard_map/ppermute | solution.py:26
  57.2 1.0 slice.85
  58.2 0.7 slice_reduce_fusion.3
  58.9 0.7 slice_reduce_fusion.2
  59.6 1.2 broadcast_select_fusion
  60.9 1.4 multiply_reduce_fusion.3
  62.3 20.1 %collective-permute-done.2 = bf16[256,1536]{1,0:T(8,128)(2,1)} collective-permute-done((bf16[256,1536]{1,0:T(8,128)(2,1)}, bf16[256,1536]{1,0:T(8,128)(2,1)}, u32[]{:S(2)}, u32[]{:S(2)}) %collective-permute-start.2) | collective-permute-done | bytes 786464 | tf_op jit(solution)/shard_map/ppermute | solution.py:26
  82.5 1.2 constant_dynamic-update-slice_fusion
  83.6 1.8 fusion.35
  86.1 1.7 fusion.87
  87.8 1.6 fusion.45
  89.4 1.4 fusion.44
  90.8 1.4 fusion.66
  92.2 1.4 fusion.63
  96.0 0.6 fusion.89
  100.2 11.1 %collective-permute-done.9 = bf16[256,768]{1,0:T(8,128)(2,1)S(1)} collective-permute-done((bf16[256,768]{1,0:T(8,128)(2,1)S(1)}, bf16[256,768]{1,0:T(8,128)(2,1)S(1)}, u32[]{:S(2)}, u32[]{:S(2)}) %collective-permute-start.9) | collective-permute-done | bytes 393248 | tf_op jit(solution)/shard_map/ppermute | solution.py:26
  112.9 0.9 collective-permute-start.14
  113.8 1.2 collective-permute-done.14
  115.1 0.8 fusion.52
  115.9 1.5 abs_reduce_fusion
  118.6 18.9 %all_to_all.20 = f16[4,200,768]{2,1,0:T(8,128)(2,1)S(1)} all-to-all(f16[4,200,768]{2,1,0:T(8,128)(2,1)S(1)} %concatenate.41), channel_id=1, replica_groups=mesh['yl'=2,'z'=8,'x'=4,'core'=2,'yh'=2] {'x'}, dimensions={0} | all-to-all | bytes 2457600 | tf_op jit(solution)/shard_map/all_to_all | solution.py:96
  138.0 17.5 %all_to_all.21 = f16[8,32,768]{2,1,0:T(8,128)(2,1)S(1)} all-to-all(f16[8,32,768]{2,1,0:T(8,128)(2,1)S(1)} %pad_maximum_fusion.4), channel_id=1, replica_groups=mesh['yl'=2,'z'=8,'x'=4,'core'=2,'yh'=2] {'z'}, dimensions={0} | all-to-all | bytes 786432 | tf_op jit(solution)/shard_map/all_to_all | solution.py:100
  155.6 1.1 collective-permute-start.15
  157.3 2.2 %collective-permute-start.17 = (f32[32,768]{1,0:T(8,128)S(1)}, f32[32,768]{1,0:T(8,128)S(1)}, u32[]{:S(2)}, u32[]{:S(2)}) collective-permute-start(f32[32,768]{1,0:T(8,128)S(1)} %pad_maximum_fusion.5), channel_id=1, source_target_pairs={{0,129},{1,128},{128,1},{129,0},{2,131},{3,130},{130,3},{131,2},{4... | collective-permute-start | bytes 294920 | tf_op jit(solution)/shard_map/ppermute | solution.py:105
  159.5 2.3 %collective-permute-done.16 = f32[32,768]{1,0:T(8,128)S(1)} collective-permute-done((f32[32,768]{1,0:T(8,128)S(1)}, f32[32,768]{1,0:T(8,128)S(1)}, u32[]{:S(2)}, u32[]{:S(2)}) %collective-permute-start.16) | collective-permute-done | bytes 98336 | tf_op jit(solution)/shard_map/ppermute | solution.py:26
  161.8 1.0 collective-permute-done.17
  162.9 14.5 %all_to_all.22 = f16[8,24,768]{2,1,0:T(8,128)(2,1)S(1)} all-to-all(f16[8,24,768]{2,1,0:T(8,128)(2,1)S(1)} %broadcast_in_dim.19), channel_id=1, replica_groups=mesh['yl'=2,'z'=8,'x'=4,'core'=2,'yh'=2] {'z'}, dimensions={0} | all-to-all | bytes 589824 | tf_op jit(solution)/shard_map/all_to_all | solution.py:113
  177.4 15.2 %all_to_all.23 = f16[4,192,768]{2,1,0:T(8,128)(2,1)S(1)} all-to-all(f16[4,192,768]{2,1,0:T(8,128)(2,1)S(1)} %broadcast_in_dim.21), channel_id=1, replica_groups=mesh['yl'=2,'z'=8,'x'=4,'core'=2,'yh'=2] {'x'}, dimensions={0} | all-to-all | bytes 2359296 | tf_op jit(solution)/shard_map/all_to_all | solution.py:115
  192.7 4.6 %collective-permute-start.18 = (f16[768,768]{1,0:T(8,128)(2,1)S(1)}, f16[768,768]{1,0:T(8,128)(2,1)S(1)}, u32[]{:S(2)}, u32[]{:S(2)}) collective-permute-start(f16[768,768]{1,0:T(8,128)(2,1)S(1)} %bitcast.33), channel_id=1, source_target_pairs={{0,2},{2,0},{1,3},{3,1},{4,6},{6,4},{5,7},{7,5},{8,10},{10,8},{9,1... | collective-permute-start | bytes 3538952 | tf_op jit(solution)/shard_map/ppermute | solution.py:26
  197.3 2.5 %collective-permute-done.19 = f32[8,768]{1,0:T(8,128)S(1)} collective-permute-done((f32[8,768]{1,0:T(8,128)S(1)}, f32[8,768]{1,0:T(8,128)S(1)}, u32[]{:S(2)}, u32[]{:S(2)}) %collective-permute-start.19) | collective-permute-done | bytes 24608 | tf_op jit(solution)/shard_map/ppermute | solution.py:26
  199.9 2.7 %fusion = (f32[768,768]{1,0:T(8,128)}, f32[768,768]{1,0:T(8,128)}) fusion(f16[768,768]{1,0:T(8,128)(2,1)S(1)} %collective-permute-done.18, f32[768]{0:T(1024)S(1)} %fusion.81, f32[768]{0:T(1024)S(1)} %get-tuple-element.12, pred[]{:T(512)S(6)} %eq.28, f16[4,192,768]{2,1,0:T(8,128)(2,1)S(1)} %all_to_all.23), kind=kLoop, calls=%fused_computation.1 | loop fusion | flops 3538944 | bytes 7084033 | tf_op jit(solution)/shard_map/jit(_where)/select_n | solution.py:194
  (94 shorter events, 11.9 us)
Async XLA Ops:
  0.6 1.3 copy-start
  0.6 2.9 %copy-start.9 = (s32[256]{0:T(256)S(1)}, s32[256]{0:T(256)}, u32[]{:S(2)}) copy-start(s32[256]{0:T(256)} %param.15) | copy-start | bytes 3076
  3.5 0.9 copy-start.1
  3.5 3.8 %copy-start.8 = (bf16[256,1536]{1,0:T(8,128)(2,1)S(1)}, bf16[256,1536]{1,0:T(8,128)(2,1)}, u32[]{:S(2)}) copy-start(bf16[256,1536]{1,0:T(8,128)(2,1)} %param.8) | copy-start | bytes 2359300
  5.2 19.3 %collective-permute-start.3 = (bf16[272,768]{1,0:T(8,128)(2,1)}, bf16[272,768]{1,0:T(8,128)(2,1)}, u32[]{:S(2)}, u32[]{:S(2)}) collective-permute-start(bf16[272,768]{1,0:T(8,128)(2,1)} %fusion.56), channel_id=1, source_target_pairs={{0,4},{2,6},{4,8},{6,10},{8,12},{10,14},{12,16},{14,18},{16,20},{1... | collective-permute-start | bytes 1253384 | tf_op jit(solution)/shard_map/ppermute | solution.py:30
  11.1 1.1 copy-start.4
  11.1 1.7 copy-start.6
  14.3 42.9 %collective-permute-start.1 = (bf16[272,768]{1,0:T(8,128)(2,1)}, bf16[272,768]{1,0:T(8,128)(2,1)}, u32[]{:S(2)}, u32[]{:S(2)}) collective-permute-start(bf16[272,768]{1,0:T(8,128)(2,1)} %fusion.57), channel_id=1, source_target_pairs={{0,1},{1,0},{2,3},{3,2},{4,5},{5,4},{6,7},{7,6},{8,9},{9,8},{10,11... | collective-permute-start | bytes 1253384 | tf_op jit(solution)/shard_map/ppermute | solution.py:26
  17.2 65.3 %collective-permute-start.2 = (bf16[256,1536]{1,0:T(8,128)(2,1)}, bf16[256,1536]{1,0:T(8,128)(2,1)}, u32[]{:S(2)}, u32[]{:S(2)}) collective-permute-start(bf16[256,1536]{1,0:T(8,128)(2,1)} %divide_convert_fusion), channel_id=1, source_target_pairs={{0,1},{1,0},{2,3},{3,2},{4,5},{5,4},{6,7},{7,6},{8,9},{9,8},{10,11... | collective-permute-start | bytes 2359304 | tf_op jit(solution)/shard_map/ppermute | solution.py:26
  17.2 42.4 %collective-permute-start.4 = (bf16[256,1536]{1,0:T(8,128)(2,1)}, bf16[256,1536]{1,0:T(8,128)(2,1)}, u32[]{:S(2)}, u32[]{:S(2)}) collective-permute-start(bf16[256,1536]{1,0:T(8,128)(2,1)} %param.10), channel_id=1, source_target_pairs={{0,4},{2,6},{4,8},{6,10},{8,12},{10,14},{12,16},{14,18},{16,20},{1... | collective-permute-start | bytes 2359304 | tf_op jit(solution)/shard_map/ppermute | solution.py:30
  25.6 68.0 %collective-permute-start.7 = (bf16[272,768]{1,0:T(8,128)(2,1)S(1)}, bf16[272,768]{1,0:T(8,128)(2,1)S(1)}, u32[]{:S(2)}, u32[]{:S(2)}) collective-permute-start(bf16[272,768]{1,0:T(8,128)(2,1)S(1)} %broadcast_select_fusion.1), channel_id=1, source_target_pairs={{0,2},{2,4},{4,6},{6,8},{8,10},{10,12},{12,14},{14,16},{16,18},{18... | collective-permute-start | bytes 1253384 | tf_op jit(solution)/shard_map/ppermute | solution.py:30
  27.9 65.6 %collective-permute-start.5 = (bf16[272,768]{1,0:T(8,128)(2,1)}, bf16[272,768]{1,0:T(8,128)(2,1)S(1)}, u32[]{:S(2)}, u32[]{:S(2)}) collective-permute-start(bf16[272,768]{1,0:T(8,128)(2,1)} %collective-permute-done.3), channel_id=1, source_target_pairs={{0,2},{2,0},{1,3},{3,1},{4,6},{6,4},{5,7},{7,5},{8,10},{10,8},{9,1... | collective-permute-start | bytes 1253384 | tf_op jit(solution)/shard_map/ppermute | solution.py:26
  60.8 35.0 %collective-permute-start.8 = (bf16[256,1536]{1,0:T(8,128)(2,1)S(1)}, bf16[256,1536]{1,0:T(8,128)(2,1)S(1)}, u32[]{:S(2)}, u32[]{:S(2)}) collective-permute-start(bf16[256,1536]{1,0:T(8,128)(2,1)S(1)} %broadcast_select_fusion), channel_id=1, source_target_pairs={{0,2},{2,4},{4,6},{6,8},{8,10},{10,12},{12,14},{14,16},{16,18},{18... | collective-permute-start | bytes 2359304 | tf_op jit(solution)/shard_map/ppermute | solution.py:30
  85.4 2.4 %copy-start.7 = (bf16[256,768]{1,0:T(8,128)(2,1)S(1)}, bf16[256,768]{1,0:T(8,128)(2,1)}, u32[]{:S(2)}) copy-start(bf16[256,768]{1,0:T(8,128)(2,1)} %slice.64) | copy-start | bytes 1179652
  85.5 8.2 %collective-permute-start.6 = (bf16[256,1536]{1,0:T(8,128)(2,1)}, bf16[256,1536]{1,0:T(8,128)(2,1)S(1)}, u32[]{:S(2)}, u32[]{:S(2)}) collective-permute-start(bf16[256,1536]{1,0:T(8,128)(2,1)} %collective-permute-done.4), channel_id=1, source_target_pairs={{0,2},{2,0},{1,3},{3,1},{4,6},{6,4},{5,7},{7,5},{8,10},{10,8},{9,1... | collective-permute-start | bytes 2359304 | tf_op jit(solution)/shard_map/ppermute | solution.py:26
  95.5 3.7 %collective-permute-start.10 = (bf16[256,768]{1,0:T(8,128)(2,1)S(1)}, bf16[256,768]{1,0:T(8,128)(2,1)S(1)}, u32[]{:S(2)}, u32[]{:S(2)}) collective-permute-start(bf16[256,768]{1,0:T(8,128)(2,1)S(1)} %fusion.6), channel_id=1, source_target_pairs={{0,2},{2,0},{1,3},{3,1},{4,6},{6,4},{5,7},{7,5},{8,10},{10,8},{9,1... | collective-permute-start | bytes 1179656 | tf_op jit(solution)/shard_map/ppermute | solution.py:26
  97.6 14.0 %collective-permute-start.12 = (bf16[256,768]{1,0:T(8,128)(2,1)S(1)}, bf16[256,768]{1,0:T(8,128)(2,1)S(1)}, u32[]{:S(2)}, u32[]{:S(2)}) collective-permute-start(bf16[256,768]{1,0:T(8,128)(2,1)S(1)} %fusion.7), channel_id=1, source_target_pairs={{0,250},{2,0},{4,254},{6,4},{8,2},{10,8},{12,6},{14,12},{16,10},{1... | collective-permute-start | bytes 1179656 | tf_op jit(solution)/shard_map/ppermute | solution.py:30
  98.9 1.0 copy-start.3
  98.9 1.1 copy-start.5
  99.0 12.3 %collective-permute-start.9 = (bf16[256,768]{1,0:T(8,128)(2,1)S(1)}, bf16[256,768]{1,0:T(8,128)(2,1)S(1)}, u32[]{:S(2)}, u32[]{:S(2)}) collective-permute-start(bf16[256,768]{1,0:T(8,128)(2,1)S(1)} %slice.196), channel_id=1, source_target_pairs={{0,1},{1,0},{2,3},{3,2},{4,5},{5,4},{6,7},{7,6},{8,9},{9,8},{10,11... | collective-permute-start | bytes 1179656 | tf_op jit(solution)/shard_map/ppermute | solution.py:26
  99.5 12.1 %copy-start.2 = (f32[256,768]{1,0:T(8,128)S(1)}, f32[256,768]{1,0:T(8,128)}, u32[]{:S(2)}) copy-start(f32[256,768]{1,0:T(8,128)} %copy-done.1) | copy-start | bytes 2359300
  99.6 12.1 %collective-permute-start.11 = (bf16[256,768]{1,0:T(8,128)(2,1)S(1)}, bf16[256,768]{1,0:T(8,128)(2,1)S(1)}, u32[]{:S(2)}, u32[]{:S(2)}) collective-permute-start(bf16[256,768]{1,0:T(8,128)(2,1)S(1)} %fusion.5), channel_id=1, source_target_pairs={{0,252},{2,254},{4,0},{6,2},{8,4},{10,6},{12,8},{14,10},{16,12},{1... | collective-permute-start | bytes 1179656 | tf_op jit(solution)/shard_map/ppermute | solution.py:30
  100.1 13.7 %collective-permute-start = (bf16[256,768]{1,0:T(8,128)(2,1)S(1)}, bf16[256,768]{1,0:T(8,128)(2,1)S(1)}, u32[]{:S(2)}, u32[]{:S(2)}) collective-permute-start(bf16[256,768]{1,0:T(8,128)(2,1)S(1)} %get-tuple-element.26), channel_id=1, source_target_pairs={{0,2},{2,0},{1,3},{3,1},{4,6},{6,4},{5,7},{7,5},{8,10},{10,8},{9,1... | collective-permute-start | bytes 1179656 | tf_op jit(solution)/shard_map/ppermute | solution.py:26
  112.9 2.2 %collective-permute-start.14 = (bf16[256,768]{1,0:T(8,128)(2,1)S(1)}, bf16[256,768]{1,0:T(8,128)(2,1)S(1)}, u32[]{:S(2)}, u32[]{:S(2)}) collective-permute-start(bf16[256,768]{1,0:T(8,128)(2,1)S(1)} %get-tuple-element.22), channel_id=1, source_target_pairs={{0,2},{2,0},{1,3},{3,1},{4,6},{6,4},{5,7},{7,5},{8,10},{10,8},{9,1... | collective-permute-start | bytes 1179656 | tf_op jit(solution)/shard_map/ppermute | solution.py:26
  113.7 2.2 %collective-permute-start.13 = (bf16[256,768]{1,0:T(8,128)(2,1)S(1)}, bf16[256,768]{1,0:T(8,128)(2,1)S(1)}, u32[]{:S(2)}, u32[]{:S(2)}) collective-permute-start(bf16[256,768]{1,0:T(8,128)(2,1)S(1)} %get-tuple-element.20), channel_id=1, source_target_pairs={{0,2},{2,0},{1,3},{3,1},{4,6},{6,4},{5,7},{7,5},{8,10},{10,8},{9,1... | collective-permute-start | bytes 1179656 | tf_op jit(solution)/shard_map/ppermute | solution.py:26
  155.6 3.9 %collective-permute-start.15 = (f32[32,768]{1,0:T(8,128)S(1)}, f32[32,768]{1,0:T(8,128)S(1)}, u32[]{:S(2)}, u32[]{:S(2)}) collective-permute-start(f32[32,768]{1,0:T(8,128)S(1)} %pad_maximum_fusion.5), channel_id=1, source_target_pairs={{0,128},{128,0},{1,129},{129,1},{2,130},{130,2},{3,131},{131,3},{4... | collective-permute-start | bytes 294920 | tf_op jit(solution)/shard_map/ppermute | solution.py:26
  156.7 5.1 %collective-permute-start.16 = (f32[32,768]{1,0:T(8,128)S(1)}, f32[32,768]{1,0:T(8,128)S(1)}, u32[]{:S(2)}, u32[]{:S(2)}) collective-permute-start(f32[32,768]{1,0:T(8,128)S(1)} %pad_maximum_fusion.5), channel_id=1, source_target_pairs={{0,1},{1,0},{2,3},{3,2},{4,5},{5,4},{6,7},{7,6},{8,9},{9,8},{10,11... | collective-permute-start | bytes 294920 | tf_op jit(solution)/shard_map/ppermute | solution.py:26
  157.3 5.4 %collective-permute-start.17 = (f32[32,768]{1,0:T(8,128)S(1)}, f32[32,768]{1,0:T(8,128)S(1)}, u32[]{:S(2)}, u32[]{:S(2)}) collective-permute-start(f32[32,768]{1,0:T(8,128)S(1)} %pad_maximum_fusion.5), channel_id=1, source_target_pairs={{0,129},{1,128},{128,1},{129,0},{2,131},{3,130},{130,3},{131,2},{4... | collective-permute-start | bytes 294920 | tf_op jit(solution)/shard_map/ppermute | solution.py:105
  192.7 7.2 %collective-permute-start.18 = (f16[768,768]{1,0:T(8,128)(2,1)S(1)}, f16[768,768]{1,0:T(8,128)(2,1)S(1)}, u32[]{:S(2)}, u32[]{:S(2)}) collective-permute-start(f16[768,768]{1,0:T(8,128)(2,1)S(1)} %bitcast.33), channel_id=1, source_target_pairs={{0,2},{2,0},{1,3},{3,1},{4,6},{6,4},{5,7},{7,5},{8,10},{10,8},{9,1... | collective-permute-start | bytes 3538952 | tf_op jit(solution)/shard_map/ppermute | solution.py:26
  197.3 2.5 %collective-permute-start.19 = (f32[8,768]{1,0:T(8,128)S(1)}, f32[8,768]{1,0:T(8,128)S(1)}, u32[]{:S(2)}, u32[]{:S(2)}) collective-permute-start(f32[8,768]{1,0:T(8,128)S(1)} %broadcast_in_dim.23), channel_id=1, source_target_pairs={{0,2},{2,0},{1,3},{3,1},{4,6},{6,4},{5,7},{7,5},{8,10},{10,8},{9,1... | collective-permute-start | bytes 73736 | tf_op jit(solution)/shard_map/ppermute | solution.py:26

commit v13 on v10

--- a/solution.py
+++ b/solution.py
@@ -131,6 +131,7 @@
     )
     image_emb = image_unit.astype(bf16)
     image_y = swap(image_emb, "yh")
+    teacher_text, text_emb = lax.optimization_barrier((teacher_text, text_emb))
     written_unit, _ = unit_rows(teacher_text.astype(f32))
     teacher_txt = written_unit.astype(bf16)
     teach_recv = chip_shift(teacher_txt, 1)

time: 197 us -> 196 us (level)
  waiting for transfers between devices: 65 us -> 58.4 us
  starting transfers between devices: 30.1 us -> 35.7 us
  other arithmetic: 15.4 us -> 12.8 us
  matrix products: 18.8 us -> 21.1 us
    ppermute x9, waiting for transfers between devices: 19.4 us -> 13.6 us  [along_dp(): return lax.ppermute(block, DP, route)]
    ppermute x9, starting transfers between devices: 7.56 us -> 11.2 us  [along_dp(): return lax.ppermute(block, DP, route)]
    ppermute x14, starting transfers between devices: 22.3 us -> 24.3 us  [swap(): return lax.ppermute(block, axis, [(0, 1), (1, 0)])]
  transfers between devices with their start and end apart: 24 -> 24, of which waited for: 9 -> 10; matrix products, arithmetic and copies ran while one was open for 15% -> 15% of each run, Pallas kernels for 0% -> 0%
where the time goes in v13:
time: 196 us; the launch traced here: 195 us
  blocking collectives  65.1 us (33%)
  waiting for transfers between devices  58.4 us (30%)
  starting transfers between devices  35.7 us (18%)
  matrix products  21.1 us (11%)
  other arithmetic  12.8 us (7%)
    ppermute x14, waiting for transfers between devices, swap(): return lax.ppermute(block, axis, [(0, 1), (1, 0)])  43.1 us
    ppermute x14, starting transfers between devices, swap(): return lax.ppermute(block, axis, [(0, 1), (1, 0)])  24.3 us
    all_to_all x1, blocking collectives, sum_everywhere(): blocks = lax.all_to_all(blocks, 'x', 0, 0, tiled=True)  18.9 us
    all_to_all x1, blocking collectives, sum_everywhere(): blocks = lax.all_to_all(blocks, 'z', 0, 0, tiled=True)  16.5 us
    all_to_all x1, blocking collectives, sum_everywhere(): own_total = lax.all_to_all(spread, 'x', 0, 0, tiled=True).reshape(ds, ds)  15.2 us
    all_to_all x1, blocking collectives, sum_everywhere(): lax.all_to_all(spread, 'z', 0, 0, tiled=True).reshape(ds // 4, ds)  14.5 us
    ppermute x9, waiting for transfers between devices, along_dp(): return lax.ppermute(block, DP, route)  13.6 us
    ppermute x9, starting transfers between devices, along_dp(): return lax.ppermute(block, DP, route)  11.2 us
  transfers between devices with their start and end apart: 24, of which 10 were waited for; matrix products, arithmetic and copies ran while one was open for 15% of the time, Pallas kernels for 0%

profile of v13, /device:TPU:1, one launch (start us, length us, event | category | flops | bytes accessed | tf_op | source)
XLA Modules:
  0.0 195.4 jit_solution(14294187073003004374)
XLA Ops:
  0.7 4.2 %collective-permute-start.10 = (s32[256]{0:T(256)}, s32[256]{0:T(256)}, u32[]{:S(2)}, u32[]{:S(2)}) collective-permute-start(s32[256]{0:T(256)} %param.15), channel_id=1, source_target_pairs={{0,6},{2,8},{4,10},{6,12},{8,14},{10,16},{12,18},{14,20},{16,22},{... | collective-permute-start | bytes 3080 | tf_op jit(solution)/shard_map/ppermute | solution.py:30
  4.9 2.9 %collective-permute-start.3 = (s32[256]{0:T(256)}, s32[256]{0:T(256)}, u32[]{:S(2)}, u32[]{:S(2)}) collective-permute-start(s32[256]{0:T(256)} %param.15), channel_id=1, source_target_pairs={{0,1},{1,0},{2,3},{3,2},{4,5},{5,4},{6,7},{7,6},{8,9},{9,8},{10,11... | collective-permute-start | bytes 3080 | tf_op jit(solution)/shard_map/ppermute | solution.py:26
  7.8 1.7 multiply_reduce_fusion.4
  9.5 0.9 fusion.94
  11.0 1.2 fusion.3
  12.2 1.6 collective-permute-start.5
  13.7 2.6 %multiply_reduce_fusion.1 = (f32[256]{0:T(256)S(1)}, f32[256,1536]{1,0:T(8,128)S(1)}) fusion(bf16[256,1536]{1,0:T(8,128)(2,1)} %param.8, bf16[1536,1536]{1,0:T(8,128)(2,1)S(1)} %copy-done.9), kind=kOutput, calls=%fused_computation.15 | convolution fusion | flops 1208745728 | bytes 7078912 | tf_op jit(solution)/shard_map/dot_general | solution.py:138
  16.9 1.1 divide_convert_fusion
  18.0 0.9 fusion.93
  18.9 1.2 collective-permute-start.6
  20.2 0.7 broadcast_select_fusion.9
  20.8 2.9 %collective-permute-start.1 = (bf16[256,768]{1,0:T(8,128)(2,1)}, bf16[256,768]{1,0:T(8,128)(2,1)S(1)}, u32[]{:S(2)}, u32[]{:S(2)}) collective-permute-start(bf16[256,768]{1,0:T(8,128)(2,1)} %fusion.93), channel_id=1, source_target_pairs={{0,1},{1,0},{2,3},{3,2},{4,5},{5,4},{6,7},{7,6},{8,9},{9,8},{10,11... | collective-permute-start | bytes 1179656 | tf_op jit(solution)/shard_map/ppermute | solution.py:26
  23.7 0.7 pad_add_fusion
  24.8 1.0 broadcast_select_fusion.5
  25.8 3.7 %collective-permute-start.11 = (bf16[256,768]{1,0:T(8,128)(2,1)S(1)}, bf16[256,768]{1,0:T(8,128)(2,1)S(1)}, u32[]{:S(2)}, u32[]{:S(2)}) collective-permute-start(bf16[256,768]{1,0:T(8,128)(2,1)S(1)} %broadcast_select_fusion.5), channel_id=1, source_target_pairs={{0,2},{2,4},{4,6},{6,8},{8,10},{10,12},{12,14},{14,16},{16,18},{18... | collective-permute-start | bytes 1179656 | tf_op jit(solution)/shard_map/ppermute | solution.py:30
  29.5 12.1 %collective-permute-done.5 = bf16[256,1536]{1,0:T(8,128)(2,1)} collective-permute-done((bf16[256,1536]{1,0:T(8,128)(2,1)}, bf16[256,1536]{1,0:T(8,128)(2,1)}, u32[]{:S(2)}, u32[]{:S(2)}) %collective-permute-start.5) | collective-permute-done | bytes 786464 | tf_op jit(solution)/shard_map/ppermute | solution.py:30
  41.6 3.1 %collective-permute-start.7 = (bf16[256,768]{1,0:T(8,128)(2,1)}, bf16[256,768]{1,0:T(8,128)(2,1)S(1)}, u32[]{:S(2)}, u32[]{:S(2)}) collective-permute-start(bf16[256,768]{1,0:T(8,128)(2,1)} %collective-permute-done.4), channel_id=1, source_target_pairs={{0,2},{2,0},{1,3},{3,1},{4,6},{6,4},{5,7},{7,5},{8,10},{10,8},{9,1... | collective-permute-start | bytes 1179656 | tf_op jit(solution)/shard_map/ppermute | solution.py:26
  44.7 1.6 broadcast_select_fusion
  46.3 18.0 %collective-permute-done.2 = bf16[256,1536]{1,0:T(8,128)(2,1)S(1)} collective-permute-done((bf16[256,1536]{1,0:T(8,128)(2,1)}, bf16[256,1536]{1,0:T(8,128)(2,1)S(1)}, u32[]{:S(2)}, u32[]{:S(2)}) %collective-permute-start.2) | collective-permute-done | bytes 786464 | tf_op jit(solution)/shard_map/ppermute | solution.py:26
  64.3 1.8 fusion.57
  66.1 0.8 collective-permute-start.8
  67.0 1.8 fusion.50
  68.8 10.2 %collective-permute-done.1 = bf16[256,768]{1,0:T(8,128)(2,1)S(1)} collective-permute-done((bf16[256,768]{1,0:T(8,128)(2,1)}, bf16[256,768]{1,0:T(8,128)(2,1)S(1)}, u32[]{:S(2)}, u32[]{:S(2)}) %collective-permute-start.1) | collective-permute-done | bytes 393248 | tf_op jit(solution)/shard_map/ppermute | solution.py:26
  79.0 1.4 fusion.67
  80.4 1.4 fusion.66
  81.9 1.4 fusion.95
  83.2 1.4 fusion.96
  84.6 0.7 fusion.43
  86.1 0.6 collective-permute-start.14
  86.7 0.7 fusion.36
  89.2 3.7 %collective-permute-start.13 = (bf16[256,768]{1,0:T(8,128)(2,1)S(1)}, bf16[256,768]{1,0:T(8,128)(2,1)S(1)}, u32[]{:S(2)}, u32[]{:S(2)}) collective-permute-start(bf16[256,768]{1,0:T(8,128)(2,1)S(1)} %slice.118), channel_id=1, source_target_pairs={{0,1},{1,0},{2,3},{3,2},{4,5},{5,4},{6,7},{7,6},{8,9},{9,8},{10,11... | collective-permute-start | bytes 1179656 | tf_op jit(solution)/shard_map/ppermute | solution.py:26
  93.8 8.5 %collective-permute-done.13 = bf16[256,768]{1,0:T(8,128)(2,1)S(1)} collective-permute-done((bf16[256,768]{1,0:T(8,128)(2,1)S(1)}, bf16[256,768]{1,0:T(8,128)(2,1)S(1)}, u32[]{:S(2)}, u32[]{:S(2)}) %collective-permute-start.13) | collective-permute-done | bytes 393248 | tf_op jit(solution)/shard_map/ppermute | solution.py:26
  102.6 1.1 collective-permute-done.15
  103.8 0.6 multiply_reduce_fusion.2
  105.0 1.2 collective-permute-start.18
  106.5 1.0 collective-permute-done.18
  107.5 0.8 fusion.73
  108.4 1.5 abs_reduce_fusion
  111.0 18.9 %all_to_all.20 = f16[4,200,768]{2,1,0:T(8,128)(2,1)S(1)} all-to-all(f16[4,200,768]{2,1,0:T(8,128)(2,1)S(1)} %concatenate.33), channel_id=1, replica_groups=mesh['yl'=2,'z'=8,'x'=4,'core'=2,'yh'=2] {'x'}, dimensions={0} | all-to-all | bytes 2457600 | tf_op jit(solution)/shard_map/all_to_all | solution.py:83
  130.4 16.5 %all_to_all.21 = f16[8,32,768]{2,1,0:T(8,128)(2,1)S(1)} all-to-all(f16[8,32,768]{2,1,0:T(8,128)(2,1)S(1)} %pad_maximum_fusion.5), channel_id=1, replica_groups=mesh['yl'=2,'z'=8,'x'=4,'core'=2,'yh'=2] {'z'}, dimensions={0} | all-to-all | bytes 786432 | tf_op jit(solution)/shard_map/all_to_all | solution.py:87
  147.6 3.2 %collective-permute-start.20 = (f32[32,768]{1,0:T(8,128)S(1)}, f32[32,768]{1,0:T(8,128)S(1)}, u32[]{:S(2)}, u32[]{:S(2)}) collective-permute-start(f32[32,768]{1,0:T(8,128)S(1)} %pad_maximum_fusion.6), channel_id=1, source_target_pairs={{0,1},{1,0},{2,3},{3,2},{4,5},{5,4},{6,7},{7,6},{8,9},{9,8},{10,11... | collective-permute-start | bytes 294920 | tf_op jit(solution)/shard_map/ppermute | solution.py:26
  151.1 2.8 %collective-permute-done.20 = f32[32,768]{1,0:T(8,128)S(1)} collective-permute-done((f32[32,768]{1,0:T(8,128)S(1)}, f32[32,768]{1,0:T(8,128)S(1)}, u32[]{:S(2)}, u32[]{:S(2)}) %collective-permute-start.20) | collective-permute-done | bytes 98336 | tf_op jit(solution)/shard_map/ppermute | solution.py:26
  153.8 1.7 collective-permute-done.21
  155.6 14.5 %all_to_all.22 = f16[8,24,768]{2,1,0:T(8,128)(2,1)S(1)} all-to-all(f16[8,24,768]{2,1,0:T(8,128)(2,1)S(1)} %broadcast_in_dim.16), channel_id=1, replica_groups=mesh['yl'=2,'z'=8,'x'=4,'core'=2,'yh'=2] {'z'}, dimensions={0} | all-to-all | bytes 589824 | tf_op jit(solution)/shard_map/all_to_all | solution.py:100
  170.2 15.2 %all_to_all.23 = f16[4,192,768]{2,1,0:T(8,128)(2,1)S(1)} all-to-all(f16[4,192,768]{2,1,0:T(8,128)(2,1)S(1)} %broadcast_in_dim.18), channel_id=1, replica_groups=mesh['yl'=2,'z'=8,'x'=4,'core'=2,'yh'=2] {'x'}, dimensions={0} | all-to-all | bytes 2359296 | tf_op jit(solution)/shard_map/all_to_all | solution.py:102
  185.5 4.6 %collective-permute-start.22 = (f16[768,768]{1,0:T(8,128)(2,1)S(1)}, f16[768,768]{1,0:T(8,128)(2,1)S(1)}, u32[]{:S(2)}, u32[]{:S(2)}) collective-permute-start(f16[768,768]{1,0:T(8,128)(2,1)S(1)} %bitcast.37), channel_id=1, source_target_pairs={{0,2},{2,0},{1,3},{3,1},{4,6},{6,4},{5,7},{7,5},{8,10},{10,8},{9,1... | collective-permute-start | bytes 3538952 | tf_op jit(solution)/shard_map/ppermute | solution.py:26
  190.1 2.5 %collective-permute-done.23 = f32[8,768]{1,0:T(8,128)S(1)} collective-permute-done((f32[8,768]{1,0:T(8,128)S(1)}, f32[8,768]{1,0:T(8,128)S(1)}, u32[]{:S(2)}, u32[]{:S(2)}) %collective-permute-start.23) | collective-permute-done | bytes 24608 | tf_op jit(solution)/shard_map/ppermute | solution.py:26
  192.7 2.7 %fusion = (f32[768,768]{1,0:T(8,128)}, f32[768,768]{1,0:T(8,128)}) fusion(f16[768,768]{1,0:T(8,128)(2,1)S(1)} %collective-permute-done.22, f32[768]{0:T(1024)S(1)} %fusion.89, f32[768]{0:T(1024)S(1)} %get-tuple-element.6, pred[]{:T(512)S(6)} %eq.20, f16[4,192,768]{2,1,0:T(8,128)(2,1)S(1)} %all_to_all.23), kind=kLoop, calls=%fused_computation.1 | loop fusion | flops 3538944 | bytes 7084033 | tf_op jit(solution)/shard_map/jit(_where)/select_n | solution.py:186
  (84 shorter events, 8.3 us)
Async XLA Ops:
  0.6 7.2 %copy-start = (bf16[768,768]{1,0:T(8,128)(2,1)S(1)}, bf16[768,768]{1,0:T(8,128)(2,1)}, u32[]{:S(2)}) copy-start(bf16[768,768]{1,0:T(8,128)(2,1)} %param.14) | copy-start | bytes 3538948
  0.6 10.1 %copy-start.1 = (bf16[256,1536]{1,0:T(8,128)(2,1)S(1)}, bf16[256,1536]{1,0:T(8,128)(2,1)}, u32[]{:S(2)}) copy-start(bf16[256,1536]{1,0:T(8,128)(2,1)} %param.10) | copy-start | bytes 2359300
  0.7 18.2 %collective-permute-start.10 = (s32[256]{0:T(256)}, s32[256]{0:T(256)}, u32[]{:S(2)}, u32[]{:S(2)}) collective-permute-start(s32[256]{0:T(256)} %param.15), channel_id=1, source_target_pairs={{0,6},{2,8},{4,10},{6,12},{8,14},{10,16},{12,18},{14,20},{16,22},{... | collective-permute-start | bytes 3080 | tf_op jit(solution)/shard_map/ppermute | solution.py:30
  4.9 15.2 %collective-permute-start.9 = (s32[256]{0:T(256)}, s32[256]{0:T(256)}, u32[]{:S(2)}, u32[]{:S(2)}) collective-permute-start(s32[256]{0:T(256)} %param.15), channel_id=1, source_target_pairs={{0,2},{2,4},{4,6},{6,8},{8,10},{10,12},{12,14},{14,16},{16,18},{18... | collective-permute-start | bytes 3080 | tf_op jit(solution)/shard_map/ppermute | solution.py:30
  4.9 16.0 %collective-permute-start.3 = (s32[256]{0:T(256)}, s32[256]{0:T(256)}, u32[]{:S(2)}, u32[]{:S(2)}) collective-permute-start(s32[256]{0:T(256)} %param.15), channel_id=1, source_target_pairs={{0,1},{1,0},{2,3},{3,2},{4,5},{5,4},{6,7},{7,6},{8,9},{9,8},{10,11... | collective-permute-start | bytes 3080 | tf_op jit(solution)/shard_map/ppermute | solution.py:26
  7.8 5.9 %copy-start.9 = (bf16[1536,1536]{1,0:T(8,128)(2,1)S(1)}, bf16[1536,1536]{1,0:T(8,128)(2,1)}, u32[]{:S(2)}) copy-start(bf16[1536,1536]{1,0:T(8,128)(2,1)} %param.9) | copy-start | bytes 14155780
  10.4 14.4 %collective-permute-start.4 = (bf16[256,768]{1,0:T(8,128)(2,1)}, bf16[256,768]{1,0:T(8,128)(2,1)}, u32[]{:S(2)}, u32[]{:S(2)}) collective-permute-start(bf16[256,768]{1,0:T(8,128)(2,1)} %fusion.94), channel_id=1, source_target_pairs={{0,4},{2,6},{4,8},{6,10},{8,12},{10,14},{12,16},{14,18},{16,20},{1... | collective-permute-start | bytes 1179656 | tf_op jit(solution)/shard_map/ppermute | solution.py:30
  12.2 4.2 %copy-start.3 = (bf16[256,768]{1,0:T(8,128)(2,1)S(1)}, bf16[256,768]{1,0:T(8,128)(2,1)}, u32[]{:S(2)}) copy-start(bf16[256,768]{1,0:T(8,128)(2,1)} %param.11) | copy-start | bytes 1179652
  12.2 4.2 %copy-start.5 = (bf16[768,768]{1,0:T(8,128)(2,1)S(1)}, bf16[768,768]{1,0:T(8,128)(2,1)}, u32[]{:S(2)}) copy-start(bf16[768,768]{1,0:T(8,128)(2,1)} %param.13) | copy-start | bytes 3538948
  12.2 29.5 %collective-permute-start.5 = (bf16[256,1536]{1,0:T(8,128)(2,1)}, bf16[256,1536]{1,0:T(8,128)(2,1)}, u32[]{:S(2)}, u32[]{:S(2)}) collective-permute-start(bf16[256,1536]{1,0:T(8,128)(2,1)} %fusion.3), channel_id=1, source_target_pairs={{0,4},{2,6},{4,8},{6,10},{8,12},{10,14},{12,16},{14,18},{16,20},{1... | collective-permute-start | bytes 2359304 | tf_op jit(solution)/shard_map/ppermute | solution.py:30
  16.9 2.0 %copy-start.8 = (s32[256]{0:T(256)S(1)}, s32[256]{0:T(256)}, u32[]{:S(2)}) copy-start(s32[256]{0:T(256)} %param.15) | copy-start | bytes 3076
  18.9 47.2 %collective-permute-start.6 = (s32[256]{0:T(256)S(1)}, s32[256]{0:T(256)S(1)}, u32[]{:S(2)}, u32[]{:S(2)}) collective-permute-start(s32[256]{0:T(256)S(1)} %copy-done.8), channel_id=1, source_target_pairs={{0,4},{2,6},{4,8},{6,10},{8,12},{10,14},{12,16},{14,18},{16,20},{1... | collective-permute-start | bytes 3080 | tf_op jit(solution)/shard_map/ppermute | solution.py:30
  20.1 44.2 %collective-permute-start.2 = (bf16[256,1536]{1,0:T(8,128)(2,1)}, bf16[256,1536]{1,0:T(8,128)(2,1)S(1)}, u32[]{:S(2)}, u32[]{:S(2)}) collective-permute-start(bf16[256,1536]{1,0:T(8,128)(2,1)} %divide_convert_fusion), channel_id=1, source_target_pairs={{0,1},{1,0},{2,3},{3,2},{4,5},{5,4},{6,7},{7,6},{8,9},{9,8},{10,11... | collective-permute-start | bytes 2359304 | tf_op jit(solution)/shard_map/ppermute | solution.py:26
  20.8 58.1 %collective-permute-start.1 = (bf16[256,768]{1,0:T(8,128)(2,1)}, bf16[256,768]{1,0:T(8,128)(2,1)S(1)}, u32[]{:S(2)}, u32[]{:S(2)}) collective-permute-start(bf16[256,768]{1,0:T(8,128)(2,1)} %fusion.93), channel_id=1, source_target_pairs={{0,1},{1,0},{2,3},{3,2},{4,5},{5,4},{6,7},{7,6},{8,9},{9,8},{10,11... | collective-permute-start | bytes 1179656 | tf_op jit(solution)/shard_map/ppermute | solution.py:26
  24.4 39.9 %copy-start.6 = (bf16[256,1536]{1,0:T(8,128)(2,1)S(1)}, bf16[256,1536]{1,0:T(8,128)(2,1)}, u32[]{:S(2)}) copy-start(bf16[256,1536]{1,0:T(8,128)(2,1)} %divide_convert_fusion) | copy-start | bytes 2359300
  25.8 61.6 %collective-permute-start.11 = (bf16[256,768]{1,0:T(8,128)(2,1)S(1)}, bf16[256,768]{1,0:T(8,128)(2,1)S(1)}, u32[]{:S(2)}, u32[]{:S(2)}) collective-permute-start(bf16[256,768]{1,0:T(8,128)(2,1)S(1)} %broadcast_select_fusion.5), channel_id=1, source_target_pairs={{0,2},{2,4},{4,6},{6,8},{8,10},{10,12},{12,14},{14,16},{16,18},{18... | collective-permute-start | bytes 1179656 | tf_op jit(solution)/shard_map/ppermute | solution.py:30
  41.6 43.6 %collective-permute-start.7 = (bf16[256,768]{1,0:T(8,128)(2,1)}, bf16[256,768]{1,0:T(8,128)(2,1)S(1)}, u32[]{:S(2)}, u32[]{:S(2)}) collective-permute-start(bf16[256,768]{1,0:T(8,128)(2,1)} %collective-permute-done.4), channel_id=1, source_target_pairs={{0,2},{2,0},{1,3},{3,1},{4,6},{6,4},{5,7},{7,5},{8,10},{10,8},{9,1... | collective-permute-start | bytes 1179656 | tf_op jit(solution)/shard_map/ppermute | solution.py:26
  64.3 22.4 %collective-permute-start.12 = (bf16[256,1536]{1,0:T(8,128)(2,1)S(1)}, bf16[256,1536]{1,0:T(8,128)(2,1)S(1)}, u32[]{:S(2)}, u32[]{:S(2)}) collective-permute-start(bf16[256,1536]{1,0:T(8,128)(2,1)S(1)} %broadcast_select_fusion), channel_id=1, source_target_pairs={{0,2},{2,4},{4,6},{6,8},{8,10},{10,12},{12,14},{14,16},{16,18},{18... | collective-permute-start | bytes 2359304 | tf_op jit(solution)/shard_map/ppermute | solution.py:30
  66.1 12.9 %copy-start.7 = (bf16[256,768]{1,0:T(8,128)(2,1)S(1)}, bf16[256,768]{1,0:T(8,128)(2,1)}, u32[]{:S(2)}) copy-start(bf16[256,768]{1,0:T(8,128)(2,1)} %fusion.93) | copy-start | bytes 1179652
  66.1 18.5 %collective-permute-start.8 = (bf16[256,1536]{1,0:T(8,128)(2,1)}, bf16[256,1536]{1,0:T(8,128)(2,1)S(1)}, u32[]{:S(2)}, u32[]{:S(2)}) collective-permute-start(bf16[256,1536]{1,0:T(8,128)(2,1)} %collective-permute-done.5), channel_id=1, source_target_pairs={{0,2},{2,0},{1,3},{3,1},{4,6},{6,4},{5,7},{7,5},{8,10},{10,8},{9,1... | collective-permute-start | bytes 2359304 | tf_op jit(solution)/shard_map/ppermute | solution.py:26
  86.1 6.7 %collective-permute-start.14 = (bf16[256,768]{1,0:T(8,128)(2,1)S(1)}, bf16[256,768]{1,0:T(8,128)(2,1)S(1)}, u32[]{:S(2)}, u32[]{:S(2)}) collective-permute-start(bf16[256,768]{1,0:T(8,128)(2,1)S(1)} %fusion.8), channel_id=1, source_target_pairs={{0,2},{2,0},{1,3},{3,1},{4,6},{6,4},{5,7},{7,5},{8,10},{10,8},{9,1... | collective-permute-start | bytes 1179656 | tf_op jit(solution)/shard_map/ppermute | solution.py:26
  88.3 14.4 %collective-permute-start.16 = (bf16[256,768]{1,0:T(8,128)(2,1)S(1)}, bf16[256,768]{1,0:T(8,128)(2,1)S(1)}, u32[]{:S(2)}, u32[]{:S(2)}) collective-permute-start(bf16[256,768]{1,0:T(8,128)(2,1)S(1)} %fusion.9), channel_id=1, source_target_pairs={{0,250},{2,0},{4,254},{6,4},{8,2},{10,8},{12,6},{14,12},{16,10},{1... | collective-permute-start | bytes 1179656 | tf_op jit(solution)/shard_map/ppermute | solution.py:30
  89.1 4.3 %copy-start.2 = (bf16[256,768]{1,0:T(8,128)(2,1)S(1)}, bf16[256,768]{1,0:T(8,128)(2,1)}, u32[]{:S(2)}) copy-start(bf16[256,768]{1,0:T(8,128)(2,1)} %param.12) | copy-start | bytes 1179652
  89.1 4.2 %copy-start.4 = (bf16[256,768]{1,0:T(8,128)(2,1)S(1)}, bf16[256,768]{1,0:T(8,128)(2,1)}, u32[]{:S(2)}) copy-start(bf16[256,768]{1,0:T(8,128)(2,1)} %param.11) | copy-start | bytes 1179652
  89.2 13.2 %collective-permute-start.13 = (bf16[256,768]{1,0:T(8,128)(2,1)S(1)}, bf16[256,768]{1,0:T(8,128)(2,1)S(1)}, u32[]{:S(2)}, u32[]{:S(2)}) collective-permute-start(bf16[256,768]{1,0:T(8,128)(2,1)S(1)} %slice.118), channel_id=1, source_target_pairs={{0,1},{1,0},{2,3},{3,2},{4,5},{5,4},{6,7},{7,6},{8,9},{9,8},{10,11... | collective-permute-start | bytes 1179656 | tf_op jit(solution)/shard_map/ppermute | solution.py:26
  93.3 10.5 %collective-permute-start.15 = (bf16[256,768]{1,0:T(8,128)(2,1)S(1)}, bf16[256,768]{1,0:T(8,128)(2,1)S(1)}, u32[]{:S(2)}, u32[]{:S(2)}) collective-permute-start(bf16[256,768]{1,0:T(8,128)(2,1)S(1)} %fusion.7), channel_id=1, source_target_pairs={{0,252},{2,254},{4,0},{6,2},{8,4},{10,6},{12,8},{14,10},{16,12},{1... | collective-permute-start | bytes 1179656 | tf_op jit(solution)/shard_map/ppermute | solution.py:30
  93.5 13.0 %collective-permute-start = (bf16[256,768]{1,0:T(8,128)(2,1)S(1)}, bf16[256,768]{1,0:T(8,128)(2,1)S(1)}, u32[]{:S(2)}, u32[]{:S(2)}) collective-permute-start(bf16[256,768]{1,0:T(8,128)(2,1)S(1)} %get-tuple-element.20), channel_id=1, source_target_pairs={{0,2},{2,0},{1,3},{3,1},{4,6},{6,4},{5,7},{7,5},{8,10},{10,8},{9,1... | collective-permute-start | bytes 1179656 | tf_op jit(solution)/shard_map/ppermute | solution.py:26
  105.0 2.5 %collective-permute-start.18 = (bf16[256,768]{1,0:T(8,128)(2,1)S(1)}, bf16[256,768]{1,0:T(8,128)(2,1)S(1)}, u32[]{:S(2)}, u32[]{:S(2)}) collective-permute-start(bf16[256,768]{1,0:T(8,128)(2,1)S(1)} %get-tuple-element.16), channel_id=1, source_target_pairs={{0,2},{2,0},{1,3},{3,1},{4,6},{6,4},{5,7},{7,5},{8,10},{10,8},{9,1... | collective-permute-start | bytes 1179656 | tf_op jit(solution)/shard_map/ppermute | solution.py:26
  106.2 2.2 %collective-permute-start.17 = (bf16[256,768]{1,0:T(8,128)(2,1)S(1)}, bf16[256,768]{1,0:T(8,128)(2,1)S(1)}, u32[]{:S(2)}, u32[]{:S(2)}) collective-permute-start(bf16[256,768]{1,0:T(8,128)(2,1)S(1)} %get-tuple-element.14), channel_id=1, source_target_pairs={{0,2},{2,0},{1,3},{3,1},{4,6},{6,4},{5,7},{7,5},{8,10},{10,8},{9,1... | collective-permute-start | bytes 1179656 | tf_op jit(solution)/shard_map/ppermute | solution.py:26
  147.1 4.0 %collective-permute-start.19 = (f32[32,768]{1,0:T(8,128)S(1)}, f32[32,768]{1,0:T(8,128)S(1)}, u32[]{:S(2)}, u32[]{:S(2)}) collective-permute-start(f32[32,768]{1,0:T(8,128)S(1)} %pad_maximum_fusion.6), channel_id=1, source_target_pairs={{0,128},{128,0},{1,129},{129,1},{2,130},{130,2},{3,131},{131,3},{4... | collective-permute-start | bytes 294920 | tf_op jit(solution)/shard_map/ppermute | solution.py:26
  147.6 6.2 %collective-permute-start.20 = (f32[32,768]{1,0:T(8,128)S(1)}, f32[32,768]{1,0:T(8,128)S(1)}, u32[]{:S(2)}, u32[]{:S(2)}) collective-permute-start(f32[32,768]{1,0:T(8,128)S(1)} %pad_maximum_fusion.6), channel_id=1, source_target_pairs={{0,1},{1,0},{2,3},{3,2},{4,5},{5,4},{6,7},{7,6},{8,9},{9,8},{10,11... | collective-permute-start | bytes 294920 | tf_op jit(solution)/shard_map/ppermute | solution.py:26
  150.9 4.7 %collective-permute-start.21 = (f32[32,768]{1,0:T(8,128)S(1)}, f32[32,768]{1,0:T(8,128)S(1)}, u32[]{:S(2)}, u32[]{:S(2)}) collective-permute-start(f32[32,768]{1,0:T(8,128)S(1)} %pad_maximum_fusion.6), channel_id=1, source_target_pairs={{0,129},{1,128},{128,1},{129,0},{2,131},{3,130},{130,3},{131,2},{4... | collective-permute-start | bytes 294920 | tf_op jit(solution)/shard_map/ppermute | solution.py:92
  185.5 7.2 %collective-permute-start.22 = (f16[768,768]{1,0:T(8,128)(2,1)S(1)}, f16[768,768]{1,0:T(8,128)(2,1)S(1)}, u32[]{:S(2)}, u32[]{:S(2)}) collective-permute-start(f16[768,768]{1,0:T(8,128)(2,1)S(1)} %bitcast.37), channel_id=1, source_target_pairs={{0,2},{2,0},{1,3},{3,1},{4,6},{6,4},{5,7},{7,5},{8,10},{10,8},{9,1... | collective-permute-start | bytes 3538952 | tf_op jit(solution)/shard_map/ppermute | solution.py:26
  190.1 2.5 %collective-permute-start.23 = (f32[8,768]{1,0:T(8,128)S(1)}, f32[8,768]{1,0:T(8,128)S(1)}, u32[]{:S(2)}, u32[]{:S(2)}) collective-permute-start(f32[8,768]{1,0:T(8,128)S(1)} %broadcast_in_dim.20), channel_id=1, source_target_pairs={{0,2},{2,0},{1,3},{3,1},{4,6},{6,4},{5,7},{7,5},{8,10},{10,8},{9,1... | collective-permute-start | bytes 73736 | tf_op jit(solution)/shard_map/ppermute | solution.py:26
